TPU v7x, 32 devices: a whole 2x2x4 slice. The times are simulated.
32 devices in a mesh: groups: 2 (over y), wide: 8 (over z, x), heads: 2 (over core).
Axes of the slice: x: 2, y: 2, z: 4, core: 2. Of those that a mesh axis runs over, the one named last changes fastest.
Arguments:
- queries: bfloat16 [2048, 2048], P(('groups', 'wide'), 'heads'), parts along dimension 0, may hold values from -160 to 160
- encodings: bfloat16 [1024, 3584], P(('groups', 'wide')), parts along dimension 0, may hold values from -6 to 6
- w_key: bfloat16 [896, 2048], P(None, 'heads'), may hold values from -0.1875 to 0.1875
- w_value: bfloat16 [896, 2048], P(None, 'heads'), may hold values from -0.1875 to 0.1875
- block_owner: int32 [32, 64, 1], P(('groups', 'wide')), parts along dimension 0, may hold values from 0 to 7; in each aligned block of 128 rows (0 to 127, 128 to 255, ..., all dimensions but the last counted through in order) at most 32 rows name the same one
- block_row: int32 [32, 64], P(('groups', 'wide')), parts along dimension 0, may hold values from 0 to 63
Outputs:
- attended: bfloat16 [2048, 2048], P(('groups', 'wide'), 'heads'), parts along dimension 0
There are 2 independent parts, one for each index of `groups`. A program takes and returns all parts, laid end to end along the dimension named above; an argument that names none is the same for every part. Nothing has to cross between parts.
Inputs may be any that keep to these rules, and one draw needn't show every extreme that they name: `block_owner`: within the requests of one index of wide, no owner is named more than 32 times, a bound that some block reaches.
All inputs are finite; a program needn't handle non-finite values.
Results may differ from a plain program's by a relative error of at most 0.0065.
The roundings to bfloat16 on the way count: a program that leaves them out, or rounds other values in their place, can miss the bound.
Values may be sent and summed in bfloat16 or wider, within the bound.
No kernel may reach another device: no remote copies, remote signals or barrier semaphores. Data moves between devices by JAX's collectives and lax.ppermute only.
A program may use at most 64 MiB of HBM per device.

v0:
```python
import functools

import jax
import jax.numpy as jnp
from jax import lax
from jax.experimental import pallas as pl
from jax.experimental.pallas import tpu as pltpu
from jax.sharding import PartitionSpec as P

HD = 128
SPAN = 64
SIDE = 2
LIMIT = 24 * 1024 * 1024
STREAMS = 2
EXPONENT = HD ** (-0.5) * 1.4426950408889634
VMEM = pl.BlockSpec(memory_space=pltpu.VMEM)


def params():
    return pltpu.CompilerParams(vmem_limit_bytes=LIMIT)


def half_kernel(enc_ref, *refs):
    outs, sems = refs[:-1], refs[-1]
    width = outs[0].shape[1]
    start = lax.axis_index("heads") * len(outs) * width
    copies = [
        pltpu.make_async_copy(enc_ref.at[:, pl.ds(pl.multiple_of(start + n * width, 128), width)], out, sems.at[n])
        for n, out in enumerate(outs)
    ]
    for copy in copies:
        copy.start()
    for copy in copies:
        copy.wait()


def half_columns(encodings):
    rows, columns = encodings.shape
    width = columns // lax.axis_size("heads") // STREAMS
    return pl.pallas_call(
        half_kernel,
        out_shape=[jax.ShapeDtypeStruct((rows, width), encodings.dtype)] * STREAMS,
        in_specs=[VMEM],
        out_specs=[VMEM] * STREAMS,
        scratch_shapes=[pltpu.SemaphoreType.DMA((STREAMS,))],
        compiler_params=params(),
    )(encodings)


def chosen_rows(index, sources, first):
    chunks = len(sources) // STREAMS
    rows = sources[0].shape[0]
    places = lax.broadcasted_iota(jnp.int32, (index.shape[0], chunks * rows), 1) + first
    chosen = jnp.where(places == index, 1.0, 0.0).astype(sources[0].dtype)
    parts = []
    for n in range(STREAMS):
        held = jnp.concatenate([ref[...] for ref in sources[n * chunks : (n + 1) * chunks]], axis=0)
        parts.append(jnp.dot(chosen, held, preferred_element_type=jnp.float32))
    return jnp.concatenate(parts, axis=1)


def early_kernel(index_ref, *refs):
    refs[-1][...] = chosen_rows(index_ref[...], refs[:-1], 0).astype(refs[-1].dtype)


def early(index, streams):
    sources = [chunk for stream in streams for chunk in stream]
    rows, width = sources[0].shape
    return pl.pallas_call(
        early_kernel,
        out_shape=jax.ShapeDtypeStruct((index.shape[0], STREAMS * width), sources[0].dtype),
        in_specs=[VMEM] * (1 + len(sources)),
        out_specs=VMEM,
        compiler_params=params(),
        cost_estimate=pl.CostEstimate(
            flops=2 * index.shape[0] * width * rows * len(sources),
            bytes_accessed=2 * index.shape[0] * width * STREAMS,
            transcendentals=0,
        ),
    )(index, *sources)


def pick_kernel(first, index_ref, begun_ref, *refs):
    picked = chosen_rows(index_ref[...], refs[:-1], first)
    refs[-1][...] = (picked + begun_ref[...].astype(jnp.float32)).astype(begun_ref.dtype)


def pick(index, begun, streams, first):
    sources = [chunk for stream in streams for chunk in stream]
    return pl.pallas_call(
        functools.partial(pick_kernel, first),
        out_shape=jax.ShapeDtypeStruct(begun.shape, begun.dtype),
        in_specs=[VMEM] * (2 + len(sources)),
        out_specs=VMEM,
        compiler_params=params(),
    )(index, begun, *sources)


def by_span(picked, spans, channels):
    per = picked.shape[0] // spans
    parts = []
    for c in range(spans):
        for t in range(picked.shape[1] // channels):
            parts.append(picked[c * per : (c + 1) * per, t * channels : (t + 1) * channels])
    return jnp.concatenate(parts, axis=0)


def project_kernel(spans, picked_ref, wk_ref, wv_ref, keys_ref, values_ref):
    source = by_span(picked_ref[...], spans, wk_ref.shape[0])
    keys_ref[...] = jnp.dot(source, wk_ref[...], preferred_element_type=jnp.float32).astype(keys_ref.dtype)
    values_ref[...] = jnp.dot(source, wv_ref[...], preferred_element_type=jnp.float32).astype(values_ref.dtype)


def project(picked, w_key, w_value, spans):
    rows = picked.size // w_key.shape[0]
    shape = jax.ShapeDtypeStruct((rows, w_key.shape[1]), picked.dtype)
    return pl.pallas_call(
        functools.partial(project_kernel, spans),
        out_shape=(shape, shape),
        in_specs=[VMEM] * 3,
        out_specs=(VMEM, VMEM),
        compiler_params=params(),
    )(picked, w_key, w_value)


def attend_kernel(spans, picked_ref, wk_ref, wv_ref, keys_ref, values_ref, query_ref, out_ref, scores_ref, probs_ref):
    source = by_span(picked_ref[...], spans, wk_ref.shape[0])
    keys_more = jnp.dot(source, wk_ref[...], preferred_element_type=jnp.float32).astype(jnp.bfloat16)
    values_more = jnp.dot(source, wv_ref[...], preferred_element_type=jnp.float32).astype(jnp.bfloat16)
    per = keys_more.shape[0] // spans
    heads = wk_ref.shape[1] // HD
    places = [(c, slice(h * HD, (h + 1) * HD), c * heads + h) for c in range(spans) for h in range(heads)]

    def joined(ref, more, c, lanes):
        return jnp.concatenate([ref[c * per : (c + 1) * per, lanes], more[c * per : (c + 1) * per, lanes]], axis=0)

    for c, lanes, n in places:
        scores_ref[n] = lax.dot_general(
            query_ref[c * SPAN : (c + 1) * SPAN, lanes],
            joined(keys_ref, keys_more, c, lanes),
            (((1,), (1,)), ((), ())),
            preferred_element_type=jnp.float32,
        )
    for c, lanes, n in places:
        scores = scores_ref[n]
        raised = jnp.exp2((scores - jnp.max(scores, axis=-1, keepdims=True)) * EXPONENT)
        probs_ref[n] = (raised * (1.0 / jnp.sum(raised, axis=-1, keepdims=True))).astype(jnp.bfloat16)
    for c, lanes, n in places:
        mixed = jnp.dot(probs_ref[n], joined(values_ref, values_more, c, lanes), preferred_element_type=jnp.float32)
        out_ref[c * SPAN : (c + 1) * SPAN, lanes] = mixed.astype(out_ref.dtype)


def attend(picked, w_key, w_value, keys, values, queries, spans):
    each = spans * (queries.shape[1] // HD), SPAN, 2 * keys.shape[0] // spans
    return pl.pallas_call(
        functools.partial(attend_kernel, spans),
        out_shape=jax.ShapeDtypeStruct(queries.shape, queries.dtype),
        in_specs=[VMEM] * 6,
        out_specs=VMEM,
        scratch_shapes=[pltpu.VMEM(each, jnp.float32), pltpu.VMEM(each, jnp.bfloat16)],
        compiler_params=params(),
    )(picked, w_key, w_value, keys, values, queries)


def gathered_plan(queries, encodings, w_key, w_value, owners, stored):
    wide_count = lax.axis_size("wide")
    turns = wide_count // SIDE
    me = lax.axis_index("wide")
    rows = encodings.shape[0]
    spans = queries.shape[0] // SPAN
    ring = [(n, (n + SIDE) % wide_count) for n in range(wide_count)]
    across = [(n, n + 1 if n % SIDE == 0 else n - 1) for n in range(wide_count)]
    held = [[piece] for piece in half_columns(encodings)]
    crossed = [[] for _ in held]
    for k in range(turns - 1):
        for straight, side in zip(held, crossed):
            onward = lax.ppermute(straight[k], "wide", ring)
            aside = lax.ppermute(straight[k], "wide", across)
            onward, aside = lax.optimization_barrier((onward, aside))
            straight.append(onward)
            side.append(aside)
    last = [
        lax.ppermute(held[n][-1], "wide", across) if n % 2 == 0 else lax.ppermute(crossed[n][-1], "wide", ring)
        for n in range(STREAMS)
    ]
    back = (me // SIDE - owners // SIDE) % turns
    straight = jnp.where(back == 0, 0, 2 * back - 1)
    place = jnp.where(owners % SIDE == me % SIDE, straight, jnp.where(back == turns - 1, wide_count - 1, 2 * back + 2))
    index = (place * rows + stored)[:, None]
    order = [
        [straight[0]] + [chunk for pair in zip(straight[1:], side) for chunk in pair]
        for straight, side in zip(held, crossed)
    ]
    there = len(order[0]) - 2
    begun = early(index, [chunks[:there] for chunks in order])
    picked = pick(index, begun, [chunks[there:] + [final] for chunks, final in zip(order, last)], there * rows)
    other = lax.ppermute(picked, "heads", [(0, 1), (1, 0)])
    keys, values = project(picked, w_key, w_value, spans)
    return attend(other, w_key, w_value, keys, values, queries, spans)


def exchange(encodings, owners, stored, capacity):
    wide_count = lax.axis_size("wide")
    requests = owners.shape[0]
    order = jnp.arange(requests, dtype=jnp.int32)
    earlier = (owners[:, None] == owners[None, :]) & (order[None, :] < order[:, None])
    rank = jnp.sum(earlier.astype(jnp.int32), axis=1)
    slot = owners * capacity + rank
    table = jnp.full((wide_count * capacity,), -1, jnp.int32).at[slot].set(stored)
    table = table.reshape(wide_count, capacity)
    asked = lax.all_to_all(table, "wide", split_axis=0, concat_axis=0, tiled=True)
    wanted = jnp.maximum(asked, 0)
    picked = encodings[wanted]
    returned = lax.all_to_all(picked, "wide", split_axis=0, concat_axis=0, tiled=True)
    return returned.reshape(wide_count * capacity, encodings.shape[1])[slot]


def exchanged_plan(queries, encodings, w_key, w_value, owners, stored, capacity):
    fetched = exchange(encodings, owners, stored, capacity)
    channels = w_key.shape[0]
    source = fetched.reshape(-1, channels)
    keys = jnp.dot(source, w_key, preferred_element_type=jnp.float32).astype(jnp.bfloat16)
    values = jnp.dot(source, w_value, preferred_element_type=jnp.float32).astype(jnp.bfloat16)
    span_count = queries.shape[0] // SPAN
    heads_local = w_key.shape[1] // HD
    keys = keys.reshape(span_count, -1, heads_local, HD)
    values = values.reshape(span_count, -1, heads_local, HD)
    query_part = queries.reshape(span_count, SPAN, heads_local, HD)
    scores = jnp.einsum(
        "cqhd,ckhd->chqk", query_part, keys, preferred_element_type=jnp.float32
    ) * HD ** (-0.5)
    probs = jax.nn.softmax(scores, axis=-1).astype(jnp.bfloat16)
    mixed = jnp.einsum("chqk,ckhd->cqhd", probs, values, preferred_element_type=jnp.float32)
    return mixed.astype(jnp.bfloat16).reshape(queries.shape)


def on_device(queries, encodings, w_key, w_value, block_owner, block_row):
    wide_count = lax.axis_size("wide")
    owners = block_owner.reshape(-1)
    stored = block_row.reshape(-1)
    requests = owners.shape[0]
    capacity = 2 * ((requests + wide_count - 1) // wide_count)
    if encodings.shape[0] <= 2 * capacity:
        return gathered_plan(queries, encodings, w_key, w_value, owners, stored)
    return exchanged_plan(queries, encodings, w_key, w_value, owners, stored, capacity)


def solution(mesh):
    placed = (
        P(("groups", "wide"), "heads"),
        P(("groups", "wide"), None),
        P(None, "heads"),
        P(None, "heads"),
        P(("groups", "wide"), None, None),
        P(("groups", "wide"), None),
    )
    return jax.shard_map(
        on_device,
        mesh=mesh,
        in_specs=placed,
        out_specs=P(("groups", "wide"), "heads"),
        check_vma=False,
    )
```

profile of v0, /device:TPU:0, one launch (start us, length us, event | category | flops | bytes accessed | tf_op | source)
XLA Modules:
  0.0 39.0 jit_solution(9088441028724881152)
XLA Ops:
  0.0 1.0 %copy-done.2 = bf16[64,3584]{1,0:T(8,128)(2,1)S(1)} copy-done((bf16[64,3584]{1,0:T(8,128)(2,1)S(1)}, bf16[64,3584]{1,0:T(8,128)(2,1)}, u32[]{:S(2)}) %copy-start.2) | copy-done | bytes 458776
  1.1 3.1 %collective-permute-start = (bf16[64,896]{1,0:T(8,128)(2,1)S(1)}, bf16[64,896]{1,0:T(8,128)(2,1)S(1)}, u32[]{:S(2)}, u32[]{:S(2)}) collective-permute-start(bf16[64,896]{1,0:T(8,128)(2,1)S(1)} %get-tuple-element.21.refs_0_), channel_id=1, source_target_pairs={{0,4},{2,6},{4,8},{6,10},{8,12},{10,14},{12,0},{14,2},{1,5},{3,7},... | collective-permute-start | bytes 344072 | tf_op jit(solution)/shard_map/ppermute | solution.py:177
  4.2 1.5 %collective-permute-start.1 = (bf16[64,896]{1,0:T(8,128)(2,1)S(1)}, bf16[64,896]{1,0:T(8,128)(2,1)S(1)}, u32[]{:S(2)}, u32[]{:S(2)}) collective-permute-start(bf16[64,896]{1,0:T(8,128)(2,1)S(1)} %get-tuple-element.21.refs_0_), channel_id=1, source_target_pairs={{0,2},{2,0},{4,6},{6,4},{8,10},{10,8},{12,14},{14,12},{1,3},{3,1},... | collective-permute-start | bytes 344072 | tf_op jit(solution)/shard_map/ppermute | solution.py:178
  5.6 1.6 %collective-permute-start.4 = (bf16[64,896]{1,0:T(8,128)(2,1)S(1)}, bf16[64,896]{1,0:T(8,128)(2,1)S(1)}, u32[]{:S(2)}, u32[]{:S(2)}) collective-permute-start(bf16[64,896]{1,0:T(8,128)(2,1)S(1)} %get-tuple-element.26.refs_5_), channel_id=1, source_target_pairs={{0,4},{2,6},{4,8},{6,10},{8,12},{10,14},{12,0},{14,2},{1,5},{3,7},... | collective-permute-start | bytes 344072 | tf_op jit(solution)/shard_map/ppermute | solution.py:177
  7.8 1.6 %collective-permute-done.refs_1_ = bf16[64,896]{1,0:T(8,128)(2,1)S(1)} collective-permute-done((bf16[64,896]{1,0:T(8,128)(2,1)S(1)}, bf16[64,896]{1,0:T(8,128)(2,1)S(1)}, u32[]{:S(2)}, u32[]{:S(2)}) %collective-permute-start) | collective-permute-done | bytes 114720 | tf_op jit(solution)/shard_map/ppermute | solution.py:177
  9.3 1.3 %collective-permute-start.2 = (bf16[64,896]{1,0:T(8,128)(2,1)S(1)}, bf16[64,896]{1,0:T(8,128)(2,1)S(1)}, u32[]{:S(2)}, u32[]{:S(2)}) collective-permute-start(bf16[64,896]{1,0:T(8,128)(2,1)S(1)} %collective-permute-done.refs_1_), channel_id=1, source_target_pairs={{0,4},{2,6},{4,8},{6,10},{8,12},{10,14},{12,0},{14,2},{1,5},{3,7},... | collective-permute-start | bytes 344072 | tf_op jit(solution)/shard_map/ppermute | solution.py:177
  10.6 2.5 %collective-permute-start.3 = (bf16[64,896]{1,0:T(8,128)(2,1)S(1)}, bf16[64,896]{1,0:T(8,128)(2,1)S(1)}, u32[]{:S(2)}, u32[]{:S(2)}) collective-permute-start(bf16[64,896]{1,0:T(8,128)(2,1)S(1)} %collective-permute-done.refs_1_), channel_id=1, source_target_pairs={{0,2},{2,0},{4,6},{6,4},{8,10},{10,8},{12,14},{14,12},{1,3},{3,1},... | collective-permute-start | bytes 344072 | tf_op jit(solution)/shard_map/ppermute | solution.py:178
  13.1 1.5 %collective-permute-start.6 = (bf16[64,896]{1,0:T(8,128)(2,1)S(1)}, bf16[64,896]{1,0:T(8,128)(2,1)S(1)}, u32[]{:S(2)}, u32[]{:S(2)}) collective-permute-start(bf16[64,896]{1,0:T(8,128)(2,1)S(1)} %collective-permute-done.4.refs_6_), channel_id=1, source_target_pairs={{0,4},{2,6},{4,8},{6,10},{8,12},{10,14},{12,0},{14,2},{1,5},{3,7},... | collective-permute-start | bytes 344072 | tf_op jit(solution)/shard_map/ppermute | solution.py:177
  14.6 0.6 %collective-permute-start.7 = (bf16[64,896]{1,0:T(8,128)(2,1)S(1)}, bf16[64,896]{1,0:T(8,128)(2,1)S(1)}, u32[]{:S(2)}, u32[]{:S(2)}) collective-permute-start(bf16[64,896]{1,0:T(8,128)(2,1)S(1)} %collective-permute-done.4.refs_6_), channel_id=1, source_target_pairs={{0,2},{2,0},{4,6},{6,4},{8,10},{10,8},{12,14},{14,12},{1,3},{3,1},... | collective-permute-start | bytes 344072 | tf_op jit(solution)/shard_map/ppermute | solution.py:178
  15.2 1.8 %collective-permute-done.2.refs_3_ = bf16[64,896]{1,0:T(8,128)(2,1)S(1)} collective-permute-done((bf16[64,896]{1,0:T(8,128)(2,1)S(1)}, bf16[64,896]{1,0:T(8,128)(2,1)S(1)}, u32[]{:S(2)}, u32[]{:S(2)}) %collective-permute-start.2) | collective-permute-done | bytes 114720 | tf_op jit(solution)/shard_map/ppermute | solution.py:177
  17.1 1.1 %collective-permute-start.8 = (bf16[64,896]{1,0:T(8,128)(2,1)S(1)}, bf16[64,896]{1,0:T(8,128)(2,1)S(1)}, u32[]{:S(2)}, u32[]{:S(2)}) collective-permute-start(bf16[64,896]{1,0:T(8,128)(2,1)S(1)} %collective-permute-done.2.refs_3_), channel_id=1, source_target_pairs={{0,4},{2,6},{4,8},{6,10},{8,12},{10,14},{12,0},{14,2},{1,5},{3,7},... | collective-permute-start | bytes 344072 | tf_op jit(solution)/shard_map/ppermute | solution.py:177
  18.2 1.4 %collective-permute-start.9 = (bf16[64,896]{1,0:T(8,128)(2,1)S(1)}, bf16[64,896]{1,0:T(8,128)(2,1)S(1)}, u32[]{:S(2)}, u32[]{:S(2)}) collective-permute-start(bf16[64,896]{1,0:T(8,128)(2,1)S(1)} %collective-permute-done.2.refs_3_), channel_id=1, source_target_pairs={{0,2},{2,0},{4,6},{6,4},{8,10},{10,8},{12,14},{14,12},{1,3},{3,1},... | collective-permute-start | bytes 344072 | tf_op jit(solution)/shard_map/ppermute | solution.py:178
  19.6 1.3 %collective-permute-done.6.refs_8_ = bf16[64,896]{1,0:T(8,128)(2,1)S(1)} collective-permute-done((bf16[64,896]{1,0:T(8,128)(2,1)S(1)}, bf16[64,896]{1,0:T(8,128)(2,1)S(1)}, u32[]{:S(2)}, u32[]{:S(2)}) %collective-permute-start.6) | collective-permute-done | bytes 114720 | tf_op jit(solution)/shard_map/ppermute | solution.py:177
  20.9 1.2 %collective-permute-start.12 = (bf16[64,896]{1,0:T(8,128)(2,1)S(1)}, bf16[64,896]{1,0:T(8,128)(2,1)S(1)}, u32[]{:S(2)}, u32[]{:S(2)}) collective-permute-start(bf16[64,896]{1,0:T(8,128)(2,1)S(1)} %collective-permute-done.6.refs_8_), channel_id=1, source_target_pairs={{0,2},{2,0},{4,6},{6,4},{8,10},{10,8},{12,14},{14,12},{1,3},{3,1},... | collective-permute-start | bytes 344072 | tf_op jit(solution)/shard_map/ppermute | solution.py:178
  22.1 0.9 %reshape.180 = s32[128,1]{1,0:T(8,128)S(1)} reshape(s32[2,64]{1,0:T(2,128)} %param.11) | data formatting | bytes 1024 | tf_op jit(solution)/shard_map/reshape | solution.py:240
  23.6 1.3 %reduce.3 = s32[2,64]{1,0:T(2,128)S(1)} reduce(s32[2,64,1]{1,2,0:T(1,128)} %param.10, s32[]{:T(128)} %broadcast.196), dimensions={2}, to_apply=%param.10.reduce_sub_computation.3 | reduce | bytes 1028 | tf_op args[4]
  24.9 0.8 %reshape.179 = s32[128,1]{1,0:T(8,128)} reshape(s32[2,64]{1,0:T(2,128)S(1)} %reduce.3) | data formatting | bytes 1024 | tf_op jit(solution)/shard_map/reshape | solution.py:239
  25.7 0.9 %collective-permute-start.10 = (bf16[64,896]{1,0:T(8,128)(2,1)S(1)}, bf16[64,896]{1,0:T(8,128)(2,1)S(1)}, u32[]{:S(2)}, u32[]{:S(2)}) collective-permute-start(bf16[64,896]{1,0:T(8,128)(2,1)S(1)} %collective-permute-done.8.refs_0_), channel_id=1, source_target_pairs={{0,2},{2,0},{4,6},{6,4},{8,10},{10,8},{12,14},{14,12},{1,3},{3,1},... | collective-permute-start | bytes 344072 | tf_op jit(solution)/shard_map/ppermute | solution.py:183
  26.6 0.9 %collective-permute-done.11.refs_3_ = bf16[64,896]{1,0:T(8,128)(2,1)S(1)} collective-permute-done((bf16[64,896]{1,0:T(8,128)(2,1)S(1)}, bf16[64,896]{1,0:T(8,128)(2,1)S(1)}, u32[]{:S(2)}, u32[]{:S(2)}) %collective-permute-start.11) | collective-permute-done | bytes 114720 | tf_op jit(solution)/shard_map/ppermute | solution.py:177
  27.8 1.0 %multiply_add_fusion.index_ref = s32[128,1]{1,0:T(8,128)S(1)} fusion(s32[128,1]{1,0:T(8,128)S(1)} %reshape.180, s32[128,1]{1,0:T(8,128)} %reshape.179, s32[]{:T(128)S(6)} %select_n.80, s32[]{:T(128)S(6)} %select_n.79), kind=kLoop, calls=%fused_computation.11 | loop fusion | flops 5376 | bytes 1544 | tf_op jit(solution)/shard_map/add | solution.py:189
  29.3 1.3 %collective-permute-done.10.refs_2_ = bf16[64,896]{1,0:T(8,128)(2,1)S(1)} collective-permute-done((bf16[64,896]{1,0:T(8,128)(2,1)S(1)}, bf16[64,896]{1,0:T(8,128)(2,1)S(1)}, u32[]{:S(2)}, u32[]{:S(2)}) %collective-permute-start.10) | collective-permute-done | bytes 114720 | tf_op jit(solution)/shard_map/ppermute | solution.py:183
  30.5 3.5 %collective-permute-done.13.refs_5_ = bf16[64,896]{1,0:T(8,128)(2,1)S(1)} collective-permute-done((bf16[64,896]{1,0:T(8,128)(2,1)S(1)}, bf16[64,896]{1,0:T(8,128)(2,1)S(1)}, u32[]{:S(2)}, u32[]{:S(2)}) %collective-permute-start.13) | collective-permute-done | bytes 114720 | tf_op jit(solution)/shard_map/ppermute | solution.py:183
  34.5 1.2 %shard_map.67 = (bf16[256,1024]{1,0:T(8,128)(2,1)S(1)}, bf16[256,1024]{1,0:T(8,128)(2,1)S(1)}) custom-call(bf16[128,1792]{1,0:T(8,128)(2,1)S(1)} %shard_map.66.picked_ref, bf16[896,1024]{1,0:T(8,128)(2,1)S(1)} %copy-done, bf16[896,1024]{1,0:T(8,128)(2,1)S(1)} %copy-done.1), custom_call_target="tpu_custom_call" | custom-call | tf_op jit(solution)/shard_map/pallas_call | solution.py:117
  36.3 2.7 %shard_map.68 = bf16[128,1024]{1,0:T(8,128)(2,1)} custom-call(bf16[128,1792]{1,0:T(8,128)(2,1)S(1)} %collective-permute-done.14.picked_ref, bf16[896,1024]{1,0:T(8,128)(2,1)S(1)} %copy-done, bf16[896,1024]{1,0:T(8,128)(2,1)S(1)} %copy-done.1, bf16[256,1024]{1,0:T(8,128)(2,1)S(1)} %get-tuple-element.35.keys_ref, ...), custom_call_target="tpu_custom_call" | custom-call | tf_op jit(solution)/shard_map/pallas_call | solution.py:155
  (24 shorter events, 2.9 us)
Async XLA Ops:
  0.0 1.0 %copy-start.2 = (bf16[64,3584]{1,0:T(8,128)(2,1)S(1)}, bf16[64,3584]{1,0:T(8,128)(2,1)}, u32[]{:S(2)}) copy-start(bf16[64,3584]{1,0:T(8,128)(2,1)} %enc_ref.1) | copy-start | bytes 1376260
  1.1 8.2 %collective-permute-start = (bf16[64,896]{1,0:T(8,128)(2,1)S(1)}, bf16[64,896]{1,0:T(8,128)(2,1)S(1)}, u32[]{:S(2)}, u32[]{:S(2)}) collective-permute-start(bf16[64,896]{1,0:T(8,128)(2,1)S(1)} %get-tuple-element.21.refs_0_), channel_id=1, source_target_pairs={{0,4},{2,6},{4,8},{6,10},{8,12},{10,14},{12,0},{14,2},{1,5},{3,7},... | collective-permute-start | bytes 344072 | tf_op jit(solution)/shard_map/ppermute | solution.py:177
  4.2 5.2 %collective-permute-start.1 = (bf16[64,896]{1,0:T(8,128)(2,1)S(1)}, bf16[64,896]{1,0:T(8,128)(2,1)S(1)}, u32[]{:S(2)}, u32[]{:S(2)}) collective-permute-start(bf16[64,896]{1,0:T(8,128)(2,1)S(1)} %get-tuple-element.21.refs_0_), channel_id=1, source_target_pairs={{0,2},{2,0},{4,6},{6,4},{8,10},{10,8},{12,14},{14,12},{1,3},{3,1},... | collective-permute-start | bytes 344072 | tf_op jit(solution)/shard_map/ppermute | solution.py:178
  5.6 7.5 %collective-permute-start.4 = (bf16[64,896]{1,0:T(8,128)(2,1)S(1)}, bf16[64,896]{1,0:T(8,128)(2,1)S(1)}, u32[]{:S(2)}, u32[]{:S(2)}) collective-permute-start(bf16[64,896]{1,0:T(8,128)(2,1)S(1)} %get-tuple-element.26.refs_5_), channel_id=1, source_target_pairs={{0,4},{2,6},{4,8},{6,10},{8,12},{10,14},{12,0},{14,2},{1,5},{3,7},... | collective-permute-start | bytes 344072 | tf_op jit(solution)/shard_map/ppermute | solution.py:177
  7.2 5.9 %collective-permute-start.5 = (bf16[64,896]{1,0:T(8,128)(2,1)S(1)}, bf16[64,896]{1,0:T(8,128)(2,1)S(1)}, u32[]{:S(2)}, u32[]{:S(2)}) collective-permute-start(bf16[64,896]{1,0:T(8,128)(2,1)S(1)} %get-tuple-element.26.refs_5_), channel_id=1, source_target_pairs={{0,2},{2,0},{4,6},{6,4},{8,10},{10,8},{12,14},{14,12},{1,3},{3,1},... | collective-permute-start | bytes 344072 | tf_op jit(solution)/shard_map/ppermute | solution.py:178
  9.3 7.7 %collective-permute-start.2 = (bf16[64,896]{1,0:T(8,128)(2,1)S(1)}, bf16[64,896]{1,0:T(8,128)(2,1)S(1)}, u32[]{:S(2)}, u32[]{:S(2)}) collective-permute-start(bf16[64,896]{1,0:T(8,128)(2,1)S(1)} %collective-permute-done.refs_1_), channel_id=1, source_target_pairs={{0,4},{2,6},{4,8},{6,10},{8,12},{10,14},{12,0},{14,2},{1,5},{3,7},... | collective-permute-start | bytes 344072 | tf_op jit(solution)/shard_map/ppermute | solution.py:177
  10.6 6.4 %collective-permute-start.3 = (bf16[64,896]{1,0:T(8,128)(2,1)S(1)}, bf16[64,896]{1,0:T(8,128)(2,1)S(1)}, u32[]{:S(2)}, u32[]{:S(2)}) collective-permute-start(bf16[64,896]{1,0:T(8,128)(2,1)S(1)} %collective-permute-done.refs_1_), channel_id=1, source_target_pairs={{0,2},{2,0},{4,6},{6,4},{8,10},{10,8},{12,14},{14,12},{1,3},{3,1},... | collective-permute-start | bytes 344072 | tf_op jit(solution)/shard_map/ppermute | solution.py:178
  13.1 7.8 %collective-permute-start.6 = (bf16[64,896]{1,0:T(8,128)(2,1)S(1)}, bf16[64,896]{1,0:T(8,128)(2,1)S(1)}, u32[]{:S(2)}, u32[]{:S(2)}) collective-permute-start(bf16[64,896]{1,0:T(8,128)(2,1)S(1)} %collective-permute-done.4.refs_6_), channel_id=1, source_target_pairs={{0,4},{2,6},{4,8},{6,10},{8,12},{10,14},{12,0},{14,2},{1,5},{3,7},... | collective-permute-start | bytes 344072 | tf_op jit(solution)/shard_map/ppermute | solution.py:177
  14.6 6.3 %collective-permute-start.7 = (bf16[64,896]{1,0:T(8,128)(2,1)S(1)}, bf16[64,896]{1,0:T(8,128)(2,1)S(1)}, u32[]{:S(2)}, u32[]{:S(2)}) collective-permute-start(bf16[64,896]{1,0:T(8,128)(2,1)S(1)} %collective-permute-done.4.refs_6_), channel_id=1, source_target_pairs={{0,2},{2,0},{4,6},{6,4},{8,10},{10,8},{12,14},{14,12},{1,3},{3,1},... | collective-permute-start | bytes 344072 | tf_op jit(solution)/shard_map/ppermute | solution.py:178
  17.1 8.6 %collective-permute-start.8 = (bf16[64,896]{1,0:T(8,128)(2,1)S(1)}, bf16[64,896]{1,0:T(8,128)(2,1)S(1)}, u32[]{:S(2)}, u32[]{:S(2)}) collective-permute-start(bf16[64,896]{1,0:T(8,128)(2,1)S(1)} %collective-permute-done.2.refs_3_), channel_id=1, source_target_pairs={{0,4},{2,6},{4,8},{6,10},{8,12},{10,14},{12,0},{14,2},{1,5},{3,7},... | collective-permute-start | bytes 344072 | tf_op jit(solution)/shard_map/ppermute | solution.py:177
  18.2 7.5 %collective-permute-start.9 = (bf16[64,896]{1,0:T(8,128)(2,1)S(1)}, bf16[64,896]{1,0:T(8,128)(2,1)S(1)}, u32[]{:S(2)}, u32[]{:S(2)}) collective-permute-start(bf16[64,896]{1,0:T(8,128)(2,1)S(1)} %collective-permute-done.2.refs_3_), channel_id=1, source_target_pairs={{0,2},{2,0},{4,6},{6,4},{8,10},{10,8},{12,14},{14,12},{1,3},{3,1},... | collective-permute-start | bytes 344072 | tf_op jit(solution)/shard_map/ppermute | solution.py:178
  20.9 6.6 %collective-permute-start.11 = (bf16[64,896]{1,0:T(8,128)(2,1)S(1)}, bf16[64,896]{1,0:T(8,128)(2,1)S(1)}, u32[]{:S(2)}, u32[]{:S(2)}) collective-permute-start(bf16[64,896]{1,0:T(8,128)(2,1)S(1)} %collective-permute-done.6.refs_8_), channel_id=1, source_target_pairs={{0,4},{2,6},{4,8},{6,10},{8,12},{10,14},{12,0},{14,2},{1,5},{3,7},... | collective-permute-start | bytes 344072 | tf_op jit(solution)/shard_map/ppermute | solution.py:177
  20.9 6.6 %collective-permute-start.12 = (bf16[64,896]{1,0:T(8,128)(2,1)S(1)}, bf16[64,896]{1,0:T(8,128)(2,1)S(1)}, u32[]{:S(2)}, u32[]{:S(2)}) collective-permute-start(bf16[64,896]{1,0:T(8,128)(2,1)S(1)} %collective-permute-done.6.refs_8_), channel_id=1, source_target_pairs={{0,2},{2,0},{4,6},{6,4},{8,10},{10,8},{12,14},{14,12},{1,3},{3,1},... | collective-permute-start | bytes 344072 | tf_op jit(solution)/shard_map/ppermute | solution.py:178
  22.1 12.4 %copy-start = (bf16[896,1024]{1,0:T(8,128)(2,1)S(1)}, bf16[896,1024]{1,0:T(8,128)(2,1)}, u32[]{:S(2)}) copy-start(bf16[896,1024]{1,0:T(8,128)(2,1)} %wk_ref.3) | copy-start | bytes 5505028
  25.7 8.9 %copy-start.1 = (bf16[896,1024]{1,0:T(8,128)(2,1)S(1)}, bf16[896,1024]{1,0:T(8,128)(2,1)}, u32[]{:S(2)}) copy-start(bf16[896,1024]{1,0:T(8,128)(2,1)} %wv_ref.3) | copy-start | bytes 5505028
  25.7 4.9 %collective-permute-start.10 = (bf16[64,896]{1,0:T(8,128)(2,1)S(1)}, bf16[64,896]{1,0:T(8,128)(2,1)S(1)}, u32[]{:S(2)}, u32[]{:S(2)}) collective-permute-start(bf16[64,896]{1,0:T(8,128)(2,1)S(1)} %collective-permute-done.8.refs_0_), channel_id=1, source_target_pairs={{0,2},{2,0},{4,6},{6,4},{8,10},{10,8},{12,14},{14,12},{1,3},{3,1},... | collective-permute-start | bytes 344072 | tf_op jit(solution)/shard_map/ppermute | solution.py:183
  27.5 6.6 %collective-permute-start.13 = (bf16[64,896]{1,0:T(8,128)(2,1)S(1)}, bf16[64,896]{1,0:T(8,128)(2,1)S(1)}, u32[]{:S(2)}, u32[]{:S(2)}) collective-permute-start(bf16[64,896]{1,0:T(8,128)(2,1)S(1)} %collective-permute-done.12.refs_4_), channel_id=1, source_target_pairs={{0,4},{2,6},{4,8},{6,10},{8,12},{10,14},{12,0},{14,2},{1,5},{3,7},... | collective-permute-start | bytes 344072 | tf_op jit(solution)/shard_map/ppermute | solution.py:183
  34.4 1.9 %copy-start.3 = (bf16[128,1024]{1,0:T(8,128)(2,1)S(1)}, bf16[128,1024]{1,0:T(8,128)(2,1)}, u32[]{:S(2)}) copy-start(bf16[128,1024]{1,0:T(8,128)(2,1)} %query_ref.1) | copy-start | bytes 786436
  34.5 1.9 %collective-permute-start.14 = (bf16[128,1792]{1,0:T(8,128)(2,1)S(1)}, bf16[128,1792]{1,0:T(8,128)(2,1)S(1)}, u32[]{:S(2)}, u32[]{:S(2)}) collective-permute-start(bf16[128,1792]{1,0:T(8,128)(2,1)S(1)} %shard_map.66.picked_ref), channel_id=1, source_target_pairs={{0,1},{1,0},{2,3},{3,2},{4,5},{5,4},{6,7},{7,6},{8,9},{9,8},{10,11... | collective-permute-start | bytes 1376264 | tf_op jit(solution)/shard_map/ppermute | solution.py:197
where the time goes:
time: 39.2 us; the launch traced here: 39 us
  starting transfers between devices  17.6 us (45%)
  waiting for transfers between devices  10.9 us (28%)
  Pallas kernels  4.79 us (12%)
  local copies, waits for them, and re-layouts  3.26 us (8%)
  other arithmetic  2.29 us (6%)
    ppermute x6, starting transfers between devices, gathered_plan(): onward = lax.ppermute(straight[k], 'wide', ring)  8.6 us
    ppermute x6, starting transfers between devices, gathered_plan(): aside = lax.ppermute(straight[k], 'wide', across)  7.72 us
    ppermute x6, waiting for transfers between devices, gathered_plan(): onward = lax.ppermute(straight[k], 'wide', ring)  5.58 us
    ppermute x1, waiting for transfers between devices, gathered_plan(): lax.ppermute(crossed[n][-1], 'wide', ring)  3.54 us
    pallas_call x1, Pallas kernels, attend(): pl.pallas_call(functools.partial(attend_kernel, spans), out_shape=jax.Sha...  2.67 us
    unnamed x9, local copies, waits for them, and re-layouts  1.54 us
    unnamed x1, other arithmetic  1.34 us
    ppermute x1, waiting for transfers between devices, gathered_plan(): lax.ppermute(held[n][-1], 'wide', across)  1.25 us
  transfers between devices with their start and end apart: 15, of which 7 were waited for; matrix products, arithmetic and copies ran while one was open for 12% of the time, Pallas kernels for 4%

commit v1 on v0

--- a/solution.py
+++ b/solution.py
@@ -59,25 +59,57 @@
     return jnp.concatenate(parts, axis=1)
 
 
-def early_kernel(index_ref, *refs):
-    refs[-1][...] = chosen_rows(index_ref[...], refs[:-1], 0).astype(refs[-1].dtype)
-
-
-def early(index, streams):
+def ring_order(turns):
+    return [0] + list(range(1, turns, 2)) + list(range(turns - 2 + turns % 2, 0, -2))
+
+
+def ring_place(line, turns):
+    return jnp.where(line % 2 == 1, (line + 1) // 2, jnp.where(line == 0, 0, turns - line // 2))
+
+
+def wanted_rows(wide_count, rows, owner_ref, stored_ref):
+    turns = wide_count // SIDE
+    me = lax.axis_index("wide")
+    columns = []
+    for c in range(stored_ref.shape[0]):
+        owner, stored = owner_ref[c], stored_ref[c : c + 1, :]
+        back = ring_place(me // SIDE, turns) - ring_place(owner // SIDE, turns)
+        back = jnp.where(back < 0, back + turns, back)
+        straight = jnp.where(back == 0, 0, 2 * back - 1)
+        crossed = jnp.where(back == turns - 1, wide_count - 1, 2 * back + 2)
+        place = jnp.where(owner % SIDE == me % SIDE, straight, crossed) * rows + stored
+        square = (place.shape[1], place.shape[1])
+        own = lax.broadcasted_iota(jnp.int32, square, 0) == lax.broadcasted_iota(jnp.int32, square, 1)
+        spread = jnp.where(own, jnp.broadcast_to(place.astype(jnp.float32), square), 0.0)
+        columns.append(jnp.sum(spread, axis=1, keepdims=True))
+    return jnp.concatenate(columns, axis=0).astype(jnp.int32)
+
+
+def early_kernel(wide_count, owner_ref, stored_ref, *refs):
+    sources, index_ref, out_ref = refs[:-2], refs[-2], refs[-1]
+    index_ref[...] = wanted_rows(wide_count, sources[0].shape[0], owner_ref, stored_ref)
+    out_ref[...] = chosen_rows(index_ref[...], sources, 0).astype(out_ref.dtype)
+
+
+def early(owners, stored, streams):
     sources = [chunk for stream in streams for chunk in stream]
     rows, width = sources[0].shape
-    return pl.pallas_call(
-        early_kernel,
-        out_shape=jax.ShapeDtypeStruct((index.shape[0], STREAMS * width), sources[0].dtype),
-        in_specs=[VMEM] * (1 + len(sources)),
-        out_specs=VMEM,
+    requests = stored.size
+    return pl.pallas_call(
+        functools.partial(early_kernel, lax.axis_size("wide")),
+        out_shape=(
+            jax.ShapeDtypeStruct((requests, 1), jnp.int32),
+            jax.ShapeDtypeStruct((requests, STREAMS * width), sources[0].dtype),
+        ),
+        in_specs=[VMEM] * (2 + len(sources)),
+        out_specs=(VMEM, VMEM),
         compiler_params=params(),
         cost_estimate=pl.CostEstimate(
-            flops=2 * index.shape[0] * width * rows * len(sources),
-            bytes_accessed=2 * index.shape[0] * width * STREAMS,
+            flops=2 * requests * width * rows * len(sources),
+            bytes_accessed=2 * requests * width * STREAMS,
             transcendentals=0,
         ),
-    )(index, *sources)
+    )(owners, stored, *sources)
 
 
 def pick_kernel(first, index_ref, begun_ref, *refs):
@@ -105,70 +137,83 @@
     return jnp.concatenate(parts, axis=0)
 
 
-def project_kernel(spans, picked_ref, wk_ref, wv_ref, keys_ref, values_ref):
-    source = by_span(picked_ref[...], spans, wk_ref.shape[0])
-    keys_ref[...] = jnp.dot(source, wk_ref[...], preferred_element_type=jnp.float32).astype(keys_ref.dtype)
-    values_ref[...] = jnp.dot(source, wv_ref[...], preferred_element_type=jnp.float32).astype(values_ref.dtype)
-
-
-def project(picked, w_key, w_value, spans):
-    rows = picked.size // w_key.shape[0]
-    shape = jax.ShapeDtypeStruct((rows, w_key.shape[1]), picked.dtype)
-    return pl.pallas_call(
-        functools.partial(project_kernel, spans),
-        out_shape=(shape, shape),
-        in_specs=[VMEM] * 3,
-        out_specs=(VMEM, VMEM),
-        compiler_params=params(),
-    )(picked, w_key, w_value)
-
-
-def attend_kernel(spans, picked_ref, wk_ref, wv_ref, keys_ref, values_ref, query_ref, out_ref, scores_ref, probs_ref):
-    source = by_span(picked_ref[...], spans, wk_ref.shape[0])
-    keys_more = jnp.dot(source, wk_ref[...], preferred_element_type=jnp.float32).astype(jnp.bfloat16)
-    values_more = jnp.dot(source, wv_ref[...], preferred_element_type=jnp.float32).astype(jnp.bfloat16)
-    per = keys_more.shape[0] // spans
-    heads = wk_ref.shape[1] // HD
-    places = [(c, slice(h * HD, (h + 1) * HD), c * heads + h) for c in range(spans) for h in range(heads)]
-
-    def joined(ref, more, c, lanes):
-        return jnp.concatenate([ref[c * per : (c + 1) * per, lanes], more[c * per : (c + 1) * per, lanes]], axis=0)
-
-    for c, lanes, n in places:
+def head_places(spans, columns):
+    heads = columns // HD
+    return [(c, slice(h * HD, (h + 1) * HD), c * heads + h) for c in range(spans) for h in range(heads)]
+
+
+def score(spans, source, wk_ref, query_ref, scores_ref):
+    keys = jnp.dot(source, wk_ref[...], preferred_element_type=jnp.float32).astype(jnp.bfloat16)
+    per = keys.shape[0] // spans
+    for c, lanes, n in head_places(spans, keys.shape[1]):
         scores_ref[n] = lax.dot_general(
             query_ref[c * SPAN : (c + 1) * SPAN, lanes],
-            joined(keys_ref, keys_more, c, lanes),
+            keys[c * per : (c + 1) * per, lanes],
             (((1,), (1,)), ((), ())),
             preferred_element_type=jnp.float32,
         )
+
+
+def score_kernel(spans, picked_ref, wk_ref, query_ref, scores_ref):
+    score(spans, by_span(picked_ref[...], spans, wk_ref.shape[0]), wk_ref, query_ref, scores_ref)
+
+
+def scores_shape(picked, queries, channels, spans):
+    return spans * (queries.shape[1] // HD), SPAN, picked.size // channels // spans
+
+
+def own_scores(picked, w_key, queries, spans):
+    return pl.pallas_call(
+        functools.partial(score_kernel, spans),
+        out_shape=jax.ShapeDtypeStruct(scores_shape(picked, queries, w_key.shape[0], spans), jnp.float32),
+        in_specs=[VMEM] * 3,
+        out_specs=VMEM,
+        compiler_params=params(),
+    )(picked, w_key, queries)
+
+
+def attend_kernel(spans, own_ref, other_ref, wk_ref, wv_ref, query_ref, first_ref, out_ref, second_ref, probs_ref):
+    channels = wk_ref.shape[0]
+    other = by_span(other_ref[...], spans, channels)
+    score(spans, other, wk_ref, query_ref, second_ref)
+    per = other.shape[0] // spans
+    own = by_span(own_ref[...], spans, channels)
+    source = []
+    for c in range(spans):
+        source += [own[c * per : (c + 1) * per], other[c * per : (c + 1) * per]]
+    source = jnp.concatenate(source, axis=0)
+    values = jnp.dot(source, wv_ref[...], preferred_element_type=jnp.float32).astype(jnp.bfloat16)
+    places = head_places(spans, values.shape[1])
     for c, lanes, n in places:
-        scores = scores_ref[n]
+        scores = jnp.concatenate([first_ref[n], second_ref[n]], axis=1)
         raised = jnp.exp2((scores - jnp.max(scores, axis=-1, keepdims=True)) * EXPONENT)
         probs_ref[n] = (raised * (1.0 / jnp.sum(raised, axis=-1, keepdims=True))).astype(jnp.bfloat16)
     for c, lanes, n in places:
-        mixed = jnp.dot(probs_ref[n], joined(values_ref, values_more, c, lanes), preferred_element_type=jnp.float32)
+        mixed = jnp.dot(probs_ref[n], values[2 * c * per : 2 * (c + 1) * per, lanes], preferred_element_type=jnp.float32)
         out_ref[c * SPAN : (c + 1) * SPAN, lanes] = mixed.astype(out_ref.dtype)
 
 
-def attend(picked, w_key, w_value, keys, values, queries, spans):
-    each = spans * (queries.shape[1] // HD), SPAN, 2 * keys.shape[0] // spans
+def attend(picked, other, w_key, w_value, queries, first, spans):
+    each = scores_shape(picked, queries, w_key.shape[0], spans)
     return pl.pallas_call(
         functools.partial(attend_kernel, spans),
         out_shape=jax.ShapeDtypeStruct(queries.shape, queries.dtype),
         in_specs=[VMEM] * 6,
         out_specs=VMEM,
-        scratch_shapes=[pltpu.VMEM(each, jnp.float32), pltpu.VMEM(each, jnp.bfloat16)],
-        compiler_params=params(),
-    )(picked, w_key, w_value, keys, values, queries)
-
-
-def gathered_plan(queries, encodings, w_key, w_value, owners, stored):
+        scratch_shapes=[pltpu.VMEM(each, jnp.float32), pltpu.VMEM(each[:2] + (2 * each[2],), jnp.bfloat16)],
+        compiler_params=params(),
+    )(picked, other, w_key, w_value, queries, first)
+
+
+def gathered_plan(queries, encodings, w_key, w_value, block_owner, block_row):
     wide_count = lax.axis_size("wide")
     turns = wide_count // SIDE
-    me = lax.axis_index("wide")
     rows = encodings.shape[0]
     spans = queries.shape[0] // SPAN
-    ring = [(n, (n + SIDE) % wide_count) for n in range(wide_count)]
+    line = ring_order(turns)
+    ring = [
+        (here * SIDE + x, there * SIDE + x) for here, there in zip(line, line[1:] + line[:1]) for x in range(SIDE)
+    ]
     across = [(n, n + 1 if n % SIDE == 0 else n - 1) for n in range(wide_count)]
     held = [[piece] for piece in half_columns(encodings)]
     crossed = [[] for _ in held]
@@ -183,20 +228,16 @@
         lax.ppermute(held[n][-1], "wide", across) if n % 2 == 0 else lax.ppermute(crossed[n][-1], "wide", ring)
         for n in range(STREAMS)
     ]
-    back = (me // SIDE - owners // SIDE) % turns
-    straight = jnp.where(back == 0, 0, 2 * back - 1)
-    place = jnp.where(owners % SIDE == me % SIDE, straight, jnp.where(back == turns - 1, wide_count - 1, 2 * back + 2))
-    index = (place * rows + stored)[:, None]
     order = [
         [straight[0]] + [chunk for pair in zip(straight[1:], side) for chunk in pair]
         for straight, side in zip(held, crossed)
     ]
     there = len(order[0]) - 2
-    begun = early(index, [chunks[:there] for chunks in order])
+    index, begun = early(jnp.transpose(block_owner, (0, 2, 1)), block_row, [chunks[:there] for chunks in order])
     picked = pick(index, begun, [chunks[there:] + [final] for chunks, final in zip(order, last)], there * rows)
     other = lax.ppermute(picked, "heads", [(0, 1), (1, 0)])
-    keys, values = project(picked, w_key, w_value, spans)
-    return attend(other, w_key, w_value, keys, values, queries, spans)
+    first = own_scores(picked, w_key, queries, spans)
+    return attend(picked, other, w_key, w_value, queries, first, spans)
 
 
 def exchange(encodings, owners, stored, capacity):
@@ -236,13 +277,13 @@
 
 def on_device(queries, encodings, w_key, w_value, block_owner, block_row):
     wide_count = lax.axis_size("wide")
-    owners = block_owner.reshape(-1)
-    stored = block_row.reshape(-1)
-    requests = owners.shape[0]
+    requests = block_row.size
     capacity = 2 * ((requests + wide_count - 1) // wide_count)
     if encodings.shape[0] <= 2 * capacity:
-        return gathered_plan(queries, encodings, w_key, w_value, owners, stored)
-    return exchanged_plan(queries, encodings, w_key, w_value, owners, stored, capacity)
+        return gathered_plan(queries, encodings, w_key, w_value, block_owner, block_row)
+    return exchanged_plan(
+        queries, encodings, w_key, w_value, block_owner.reshape(-1), block_row.reshape(-1), capacity
+    )
 
 
 def solution(mesh):

time: 39.2 us -> 37 us (0.944)
  starting transfers between devices: 17.6 us -> 21.7 us
  waiting for transfers between devices: 10.9 us -> 7.41 us
  other arithmetic: 2.29 us -> 0 us
  local copies, waits for them, and re-layouts: 3.26 us -> 2.54 us
    ppermute x6, starting transfers between devices: 8.6 us -> 13.1 us  [gathered_plan(): onward = lax.ppermute(straight[k], 'wide', ring)]
    ppermute x1, waiting for transfers between devices: 3.54 us -> 0.01 us  [gathered_plan(): lax.ppermute(crossed[n][-1], 'wide', ring)]
    ppermute x6, waiting for transfers between devices: 5.58 us -> 2.2 us  [gathered_plan(): onward = lax.ppermute(straight[k], 'wide', ring)]
    ppermute x6, waiting for transfers between devices: 0.02 us -> 2.91 us  [gathered_plan(): aside = lax.ppermute(straight[k], 'wide', across)]
    reshape x2 -> x0, local copies, waits for them, and re-layouts: 1.72 us -> none  [the longest x1 0.94 us: on_device(): stored = block_row.reshape(-1)]
    ppermute x6, starting transfers between devices: 7.72 us -> 6.12 us  [gathered_plan(): aside = lax.ppermute(straight[k], 'wide', across)]
    unnamed x1 -> x0, other arithmetic: 1.34 us -> none
    unnamed x9 -> x12, local copies, waits for them, and re-layouts: 1.54 us -> 2.54 us
  transfers between devices with their start and end apart: 15 -> 15, of which waited for: 7 -> 8; matrix products, arithmetic and copies ran while one was open for 12% -> 0% of each run, Pallas kernels for 4% -> 4%
where the time goes in v1:
time: 37 us; the launch traced here: 36.8 us
  starting transfers between devices  21.7 us (59%)
  waiting for transfers between devices  7.41 us (20%)
  Pallas kernels  5.09 us (14%)
  local copies, waits for them, and re-layouts  2.54 us (7%)
    ppermute x6, starting transfers between devices, gathered_plan(): onward = lax.ppermute(straight[k], 'wide', ring)  13.1 us
    ppermute x6, starting transfers between devices, gathered_plan(): aside = lax.ppermute(straight[k], 'wide', across)  6.12 us
    pallas_call x1, Pallas kernels, attend(): pl.pallas_call(functools.partial(attend_kernel, spans), out_shape=jax.Sha...  3.08 us
    ppermute x6, waiting for transfers between devices, gathered_plan(): aside = lax.ppermute(straight[k], 'wide', across)  2.91 us
    unnamed x12, local copies, waits for them, and re-layouts  2.54 us
    ppermute x6, waiting for transfers between devices, gathered_plan(): onward = lax.ppermute(straight[k], 'wide', ring)  2.2 us
    ppermute x1, waiting for transfers between devices, gathered_plan(): lax.ppermute(held[n][-1], 'wide', across)  1.53 us
    ppermute x1, starting transfers between devices, gathered_plan(): lax.ppermute(held[n][-1], 'wide', across)  1.28 us
  transfers between devices with their start and end apart: 15, of which 8 were waited for; matrix products, arithmetic and copies ran while one was open for 0% of the time, Pallas kernels for 4%

profile of v1, /device:TPU:0, one launch (start us, length us, event | category | flops | bytes accessed | tf_op | source)
XLA Modules:
  0.0 36.8 jit_solution(17636455744119672892)
XLA Ops:
  0.0 1.2 %copy-done.3 = bf16[64,3584]{1,0:T(8,128)(2,1)S(1)} copy-done((bf16[64,3584]{1,0:T(8,128)(2,1)S(1)}, bf16[64,3584]{1,0:T(8,128)(2,1)}, u32[]{:S(2)}) %copy-start.3) | copy-done | bytes 458776
  1.2 3.1 %collective-permute-start.4 = (bf16[64,896]{1,0:T(8,128)(2,1)S(1)}, bf16[64,896]{1,0:T(8,128)(2,1)S(1)}, u32[]{:S(2)}, u32[]{:S(2)}) collective-permute-start(bf16[64,896]{1,0:T(8,128)(2,1)S(1)} %get-tuple-element.26.refs_5_), channel_id=1, source_target_pairs={{0,4},{2,6},{4,12},{6,14},{12,8},{14,10},{8,0},{10,2},{1,5},{3,7},... | collective-permute-start | bytes 344072 | tf_op jit(solution)/shard_map/ppermute | solution.py:222
  4.3 1.5 %collective-permute-start.5 = (bf16[64,896]{1,0:T(8,128)(2,1)S(1)}, bf16[64,896]{1,0:T(8,128)(2,1)S(1)}, u32[]{:S(2)}, u32[]{:S(2)}) collective-permute-start(bf16[64,896]{1,0:T(8,128)(2,1)S(1)} %get-tuple-element.26.refs_5_), channel_id=1, source_target_pairs={{0,2},{2,0},{4,6},{6,4},{8,10},{10,8},{12,14},{14,12},{1,3},{3,1},... | collective-permute-start | bytes 344072 | tf_op jit(solution)/shard_map/ppermute | solution.py:223
  5.8 2.6 %collective-permute-start = (bf16[64,896]{1,0:T(8,128)(2,1)S(1)}, bf16[64,896]{1,0:T(8,128)(2,1)S(1)}, u32[]{:S(2)}, u32[]{:S(2)}) collective-permute-start(bf16[64,896]{1,0:T(8,128)(2,1)S(1)} %get-tuple-element.21.refs_0_), channel_id=1, source_target_pairs={{0,4},{2,6},{4,12},{6,14},{12,8},{14,10},{8,0},{10,2},{1,5},{3,7},... | collective-permute-start | bytes 344072 | tf_op jit(solution)/shard_map/ppermute | solution.py:222
  8.4 0.5 %collective-permute-start.1 = (bf16[64,896]{1,0:T(8,128)(2,1)S(1)}, bf16[64,896]{1,0:T(8,128)(2,1)S(1)}, u32[]{:S(2)}, u32[]{:S(2)}) collective-permute-start(bf16[64,896]{1,0:T(8,128)(2,1)S(1)} %get-tuple-element.21.refs_0_), channel_id=1, source_target_pairs={{0,2},{2,0},{4,6},{6,4},{8,10},{10,8},{12,14},{14,12},{1,3},{3,1},... | collective-permute-start | bytes 344072 | tf_op jit(solution)/shard_map/ppermute | solution.py:223
  9.1 3.8 %collective-permute-start.6 = (bf16[64,896]{1,0:T(8,128)(2,1)S(1)}, bf16[64,896]{1,0:T(8,128)(2,1)S(1)}, u32[]{:S(2)}, u32[]{:S(2)}) collective-permute-start(bf16[64,896]{1,0:T(8,128)(2,1)S(1)} %collective-permute-done.4.refs_6_), channel_id=1, source_target_pairs={{0,4},{2,6},{4,12},{6,14},{12,8},{14,10},{8,0},{10,2},{1,5},{3,7},... | collective-permute-start | bytes 344072 | tf_op jit(solution)/shard_map/ppermute | solution.py:222
  12.9 1.3 %collective-permute-start.7 = (bf16[64,896]{1,0:T(8,128)(2,1)S(1)}, bf16[64,896]{1,0:T(8,128)(2,1)S(1)}, u32[]{:S(2)}, u32[]{:S(2)}) collective-permute-start(bf16[64,896]{1,0:T(8,128)(2,1)S(1)} %collective-permute-done.4.refs_6_), channel_id=1, source_target_pairs={{0,2},{2,0},{4,6},{6,4},{8,10},{10,8},{12,14},{14,12},{1,3},{3,1},... | collective-permute-start | bytes 344072 | tf_op jit(solution)/shard_map/ppermute | solution.py:223
  14.2 1.1 %collective-permute-start.2 = (bf16[64,896]{1,0:T(8,128)(2,1)S(1)}, bf16[64,896]{1,0:T(8,128)(2,1)S(1)}, u32[]{:S(2)}, u32[]{:S(2)}) collective-permute-start(bf16[64,896]{1,0:T(8,128)(2,1)S(1)} %collective-permute-done.refs_1_), channel_id=1, source_target_pairs={{0,4},{2,6},{4,12},{6,14},{12,8},{14,10},{8,0},{10,2},{1,5},{3,7},... | collective-permute-start | bytes 344072 | tf_op jit(solution)/shard_map/ppermute | solution.py:222
  15.8 2.2 %collective-permute-done.7.refs_9_ = bf16[64,896]{1,0:T(8,128)(2,1)S(1)} collective-permute-done((bf16[64,896]{1,0:T(8,128)(2,1)S(1)}, bf16[64,896]{1,0:T(8,128)(2,1)S(1)}, u32[]{:S(2)}, u32[]{:S(2)}) %collective-permute-start.7) | collective-permute-done | bytes 114720 | tf_op jit(solution)/shard_map/ppermute | solution.py:223
  18.0 1.4 %collective-permute-start.11 = (bf16[64,896]{1,0:T(8,128)(2,1)S(1)}, bf16[64,896]{1,0:T(8,128)(2,1)S(1)}, u32[]{:S(2)}, u32[]{:S(2)}) collective-permute-start(bf16[64,896]{1,0:T(8,128)(2,1)S(1)} %collective-permute-done.6.refs_8_), channel_id=1, source_target_pairs={{0,4},{2,6},{4,12},{6,14},{12,8},{14,10},{8,0},{10,2},{1,5},{3,7},... | collective-permute-start | bytes 344072 | tf_op jit(solution)/shard_map/ppermute | solution.py:222
  19.4 1.3 %collective-permute-start.12 = (bf16[64,896]{1,0:T(8,128)(2,1)S(1)}, bf16[64,896]{1,0:T(8,128)(2,1)S(1)}, u32[]{:S(2)}, u32[]{:S(2)}) collective-permute-start(bf16[64,896]{1,0:T(8,128)(2,1)S(1)} %collective-permute-done.6.refs_8_), channel_id=1, source_target_pairs={{0,2},{2,0},{4,6},{6,4},{8,10},{10,8},{12,14},{14,12},{1,3},{3,1},... | collective-permute-start | bytes 344072 | tf_op jit(solution)/shard_map/ppermute | solution.py:223
  20.7 1.1 %collective-permute-start.8 = (bf16[64,896]{1,0:T(8,128)(2,1)S(1)}, bf16[64,896]{1,0:T(8,128)(2,1)S(1)}, u32[]{:S(2)}, u32[]{:S(2)}) collective-permute-start(bf16[64,896]{1,0:T(8,128)(2,1)S(1)} %collective-permute-done.2.refs_3_), channel_id=1, source_target_pairs={{0,4},{2,6},{4,12},{6,14},{12,8},{14,10},{8,0},{10,2},{1,5},{3,7},... | collective-permute-start | bytes 344072 | tf_op jit(solution)/shard_map/ppermute | solution.py:222
  21.9 1.0 %collective-permute-start.9 = (bf16[64,896]{1,0:T(8,128)(2,1)S(1)}, bf16[64,896]{1,0:T(8,128)(2,1)S(1)}, u32[]{:S(2)}, u32[]{:S(2)}) collective-permute-start(bf16[64,896]{1,0:T(8,128)(2,1)S(1)} %collective-permute-done.2.refs_3_), channel_id=1, source_target_pairs={{0,2},{2,0},{4,6},{6,4},{8,10},{10,8},{12,14},{14,12},{1,3},{3,1},... | collective-permute-start | bytes 344072 | tf_op jit(solution)/shard_map/ppermute | solution.py:223
  22.8 1.1 %collective-permute-done.11.refs_3_ = bf16[64,896]{1,0:T(8,128)(2,1)S(1)} collective-permute-done((bf16[64,896]{1,0:T(8,128)(2,1)S(1)}, bf16[64,896]{1,0:T(8,128)(2,1)S(1)}, u32[]{:S(2)}, u32[]{:S(2)}) %collective-permute-start.11) | collective-permute-done | bytes 114720 | tf_op jit(solution)/shard_map/ppermute | solution.py:222
  24.2 1.1 %collective-permute-start.13 = (bf16[64,896]{1,0:T(8,128)(2,1)S(1)}, bf16[64,896]{1,0:T(8,128)(2,1)S(1)}, u32[]{:S(2)}, u32[]{:S(2)}) collective-permute-start(bf16[64,896]{1,0:T(8,128)(2,1)S(1)} %collective-permute-done.12.refs_4_), channel_id=1, source_target_pairs={{0,4},{2,6},{4,12},{6,14},{12,8},{14,10},{8,0},{10,2},{1,5},{3,7},... | collective-permute-start | bytes 344072 | tf_op jit(solution)/shard_map/ppermute | solution.py:228
  25.3 1.1 %collective-permute-done.8.refs_0_ = bf16[64,896]{1,0:T(8,128)(2,1)S(1)} collective-permute-done((bf16[64,896]{1,0:T(8,128)(2,1)S(1)}, bf16[64,896]{1,0:T(8,128)(2,1)S(1)}, u32[]{:S(2)}, u32[]{:S(2)}) %collective-permute-start.8) | collective-permute-done | bytes 114720 | tf_op jit(solution)/shard_map/ppermute | solution.py:222
  26.7 1.3 %collective-permute-start.10 = (bf16[64,896]{1,0:T(8,128)(2,1)S(1)}, bf16[64,896]{1,0:T(8,128)(2,1)S(1)}, u32[]{:S(2)}, u32[]{:S(2)}) collective-permute-start(bf16[64,896]{1,0:T(8,128)(2,1)S(1)} %collective-permute-done.8.refs_0_), channel_id=1, source_target_pairs={{0,2},{2,0},{4,6},{6,4},{8,10},{10,8},{12,14},{14,12},{1,3},{3,1},... | collective-permute-start | bytes 344072 | tf_op jit(solution)/shard_map/ppermute | solution.py:228
  28.0 0.7 %copy-done.4 = s32[2,64,1]{1,2,0:T(1,128)S(1)} copy-done((s32[2,64,1]{1,2,0:T(1,128)S(1)}, s32[2,64,1]{1,2,0:T(1,128)}, u32[]{:S(2)}) %copy-start.4) | copy-done | bytes 536
  28.7 0.7 %copy-done.5 = s32[2,64]{1,0:T(2,128)S(1)} copy-done((s32[2,64]{1,0:T(2,128)S(1)}, s32[2,64]{1,0:T(2,128)}, u32[]{:S(2)}) %copy-start.5) | copy-done | bytes 536
  29.3 0.6 %shard_map.65 = (s32[128,1]{1,0:T(8,128)S(1)}, bf16[128,1792]{1,0:T(8,128)(2,1)S(1)}) custom-call(s32[2,1,64]{2,1,0:T(1,128)S(1)} %bitcast.3, s32[2,64]{1,0:T(2,128)S(1)} %copy-done.5, bf16[64,896]{1,0:T(8,128)(2,1)S(1)} %get-tuple-element.21.refs_0_, bf16[64,896]{1,0:T(8,128)(2,1)S(1)} %collective-permute-done.refs_1_, ...), custom_call_target="tpu_custom_call" | custom-call | flops 146800640 | bytes 458752 | tf_op jit(solution)/shard_map/pallas_call | solution.py:98
  30.0 1.5 %collective-permute-done.10.refs_2_ = bf16[64,896]{1,0:T(8,128)(2,1)S(1)} collective-permute-done((bf16[64,896]{1,0:T(8,128)(2,1)S(1)}, bf16[64,896]{1,0:T(8,128)(2,1)S(1)}, u32[]{:S(2)}, u32[]{:S(2)}) %collective-permute-start.10) | collective-permute-done | bytes 114720 | tf_op jit(solution)/shard_map/ppermute | solution.py:228
  31.9 1.0 %shard_map.67.first_ref = f32[16,64,128]{2,1,0:T(8,128)S(1)} custom-call(bf16[128,1792]{1,0:T(8,128)(2,1)S(1)} %shard_map.66.picked_ref.own_ref, bf16[896,1024]{1,0:T(8,128)(2,1)S(1)} %copy-done, bf16[128,1024]{1,0:T(8,128)(2,1)S(1)} %copy-done.2), custom_call_target="tpu_custom_call" | custom-call | tf_op jit(solution)/shard_map/pallas_call | solution.py:166
  33.0 0.8 %collective-permute-done.14.other_ref = bf16[128,1792]{1,0:T(8,128)(2,1)S(1)} collective-permute-done((bf16[128,1792]{1,0:T(8,128)(2,1)S(1)}, bf16[128,1792]{1,0:T(8,128)(2,1)S(1)}, u32[]{:S(2)}, u32[]{:S(2)}) %collective-permute-start.14) | collective-permute-done | bytes 458784 | tf_op jit(solution)/shard_map/ppermute | solution.py:238
  33.7 3.1 %shard_map.68 = bf16[128,1024]{1,0:T(8,128)(2,1)} custom-call(bf16[128,1792]{1,0:T(8,128)(2,1)S(1)} %shard_map.66.picked_ref.own_ref, bf16[128,1792]{1,0:T(8,128)(2,1)S(1)} %collective-permute-done.14.other_ref, bf16[896,1024]{1,0:T(8,128)(2,1)S(1)} %copy-done, bf16[896,1024]{1,0:T(8,128)(2,1)S(1)} %copy-done.1, bf16[128,1024]{1,0:T(8,128)(2,1)S(1)} %copy-done.2, ...), custom_call_target="tpu_custom_call" | custom-call | tf_op jit(solution)/shard_map/pallas_call | solution.py:198
  (23 shorter events, 1.7 us)
Async XLA Ops:
  0.0 31.9 %copy-start.2 = (bf16[128,1024]{1,0:T(8,128)(2,1)S(1)}, bf16[128,1024]{1,0:T(8,128)(2,1)}, u32[]{:S(2)}) copy-start(bf16[128,1024]{1,0:T(8,128)(2,1)} %query_ref.3) | copy-start | bytes 786436
  0.0 31.9 %copy-start = (bf16[896,1024]{1,0:T(8,128)(2,1)S(1)}, bf16[896,1024]{1,0:T(8,128)(2,1)}, u32[]{:S(2)}) copy-start(bf16[896,1024]{1,0:T(8,128)(2,1)} %wk_ref.3) | copy-start | bytes 5505028
  0.0 1.2 %copy-start.3 = (bf16[64,3584]{1,0:T(8,128)(2,1)S(1)}, bf16[64,3584]{1,0:T(8,128)(2,1)}, u32[]{:S(2)}) copy-start(bf16[64,3584]{1,0:T(8,128)(2,1)} %enc_ref.1) | copy-start | bytes 1376260
  1.2 7.7 %collective-permute-start.4 = (bf16[64,896]{1,0:T(8,128)(2,1)S(1)}, bf16[64,896]{1,0:T(8,128)(2,1)S(1)}, u32[]{:S(2)}, u32[]{:S(2)}) collective-permute-start(bf16[64,896]{1,0:T(8,128)(2,1)S(1)} %get-tuple-element.26.refs_5_), channel_id=1, source_target_pairs={{0,4},{2,6},{4,12},{6,14},{12,8},{14,10},{8,0},{10,2},{1,5},{3,7},... | collective-permute-start | bytes 344072 | tf_op jit(solution)/shard_map/ppermute | solution.py:222
  4.3 4.8 %collective-permute-start.5 = (bf16[64,896]{1,0:T(8,128)(2,1)S(1)}, bf16[64,896]{1,0:T(8,128)(2,1)S(1)}, u32[]{:S(2)}, u32[]{:S(2)}) collective-permute-start(bf16[64,896]{1,0:T(8,128)(2,1)S(1)} %get-tuple-element.26.refs_5_), channel_id=1, source_target_pairs={{0,2},{2,0},{4,6},{6,4},{8,10},{10,8},{12,14},{14,12},{1,3},{3,1},... | collective-permute-start | bytes 344072 | tf_op jit(solution)/shard_map/ppermute | solution.py:223
  5.8 8.4 %collective-permute-start = (bf16[64,896]{1,0:T(8,128)(2,1)S(1)}, bf16[64,896]{1,0:T(8,128)(2,1)S(1)}, u32[]{:S(2)}, u32[]{:S(2)}) collective-permute-start(bf16[64,896]{1,0:T(8,128)(2,1)S(1)} %get-tuple-element.21.refs_0_), channel_id=1, source_target_pairs={{0,4},{2,6},{4,12},{6,14},{12,8},{14,10},{8,0},{10,2},{1,5},{3,7},... | collective-permute-start | bytes 344072 | tf_op jit(solution)/shard_map/ppermute | solution.py:222
  8.4 5.8 %collective-permute-start.1 = (bf16[64,896]{1,0:T(8,128)(2,1)S(1)}, bf16[64,896]{1,0:T(8,128)(2,1)S(1)}, u32[]{:S(2)}, u32[]{:S(2)}) collective-permute-start(bf16[64,896]{1,0:T(8,128)(2,1)S(1)} %get-tuple-element.21.refs_0_), channel_id=1, source_target_pairs={{0,2},{2,0},{4,6},{6,4},{8,10},{10,8},{12,14},{14,12},{1,3},{3,1},... | collective-permute-start | bytes 344072 | tf_op jit(solution)/shard_map/ppermute | solution.py:223
  9.1 6.7 %collective-permute-start.6 = (bf16[64,896]{1,0:T(8,128)(2,1)S(1)}, bf16[64,896]{1,0:T(8,128)(2,1)S(1)}, u32[]{:S(2)}, u32[]{:S(2)}) collective-permute-start(bf16[64,896]{1,0:T(8,128)(2,1)S(1)} %collective-permute-done.4.refs_6_), channel_id=1, source_target_pairs={{0,4},{2,6},{4,12},{6,14},{12,8},{14,10},{8,0},{10,2},{1,5},{3,7},... | collective-permute-start | bytes 344072 | tf_op jit(solution)/shard_map/ppermute | solution.py:222
  12.9 5.1 %collective-permute-start.7 = (bf16[64,896]{1,0:T(8,128)(2,1)S(1)}, bf16[64,896]{1,0:T(8,128)(2,1)S(1)}, u32[]{:S(2)}, u32[]{:S(2)}) collective-permute-start(bf16[64,896]{1,0:T(8,128)(2,1)S(1)} %collective-permute-done.4.refs_6_), channel_id=1, source_target_pairs={{0,2},{2,0},{4,6},{6,4},{8,10},{10,8},{12,14},{14,12},{1,3},{3,1},... | collective-permute-start | bytes 344072 | tf_op jit(solution)/shard_map/ppermute | solution.py:223
  14.2 6.5 %collective-permute-start.2 = (bf16[64,896]{1,0:T(8,128)(2,1)S(1)}, bf16[64,896]{1,0:T(8,128)(2,1)S(1)}, u32[]{:S(2)}, u32[]{:S(2)}) collective-permute-start(bf16[64,896]{1,0:T(8,128)(2,1)S(1)} %collective-permute-done.refs_1_), channel_id=1, source_target_pairs={{0,4},{2,6},{4,12},{6,14},{12,8},{14,10},{8,0},{10,2},{1,5},{3,7},... | collective-permute-start | bytes 344072 | tf_op jit(solution)/shard_map/ppermute | solution.py:222
  15.3 5.4 %collective-permute-start.3 = (bf16[64,896]{1,0:T(8,128)(2,1)S(1)}, bf16[64,896]{1,0:T(8,128)(2,1)S(1)}, u32[]{:S(2)}, u32[]{:S(2)}) collective-permute-start(bf16[64,896]{1,0:T(8,128)(2,1)S(1)} %collective-permute-done.refs_1_), channel_id=1, source_target_pairs={{0,2},{2,0},{4,6},{6,4},{8,10},{10,8},{12,14},{14,12},{1,3},{3,1},... | collective-permute-start | bytes 344072 | tf_op jit(solution)/shard_map/ppermute | solution.py:223
  18.0 5.9 %collective-permute-start.11 = (bf16[64,896]{1,0:T(8,128)(2,1)S(1)}, bf16[64,896]{1,0:T(8,128)(2,1)S(1)}, u32[]{:S(2)}, u32[]{:S(2)}) collective-permute-start(bf16[64,896]{1,0:T(8,128)(2,1)S(1)} %collective-permute-done.6.refs_8_), channel_id=1, source_target_pairs={{0,4},{2,6},{4,12},{6,14},{12,8},{14,10},{8,0},{10,2},{1,5},{3,7},... | collective-permute-start | bytes 344072 | tf_op jit(solution)/shard_map/ppermute | solution.py:222
  19.4 4.8 %collective-permute-start.12 = (bf16[64,896]{1,0:T(8,128)(2,1)S(1)}, bf16[64,896]{1,0:T(8,128)(2,1)S(1)}, u32[]{:S(2)}, u32[]{:S(2)}) collective-permute-start(bf16[64,896]{1,0:T(8,128)(2,1)S(1)} %collective-permute-done.6.refs_8_), channel_id=1, source_target_pairs={{0,2},{2,0},{4,6},{6,4},{8,10},{10,8},{12,14},{14,12},{1,3},{3,1},... | collective-permute-start | bytes 344072 | tf_op jit(solution)/shard_map/ppermute | solution.py:223
  20.7 5.7 %collective-permute-start.8 = (bf16[64,896]{1,0:T(8,128)(2,1)S(1)}, bf16[64,896]{1,0:T(8,128)(2,1)S(1)}, u32[]{:S(2)}, u32[]{:S(2)}) collective-permute-start(bf16[64,896]{1,0:T(8,128)(2,1)S(1)} %collective-permute-done.2.refs_3_), channel_id=1, source_target_pairs={{0,4},{2,6},{4,12},{6,14},{12,8},{14,10},{8,0},{10,2},{1,5},{3,7},... | collective-permute-start | bytes 344072 | tf_op jit(solution)/shard_map/ppermute | solution.py:222
  21.9 4.8 %collective-permute-start.9 = (bf16[64,896]{1,0:T(8,128)(2,1)S(1)}, bf16[64,896]{1,0:T(8,128)(2,1)S(1)}, u32[]{:S(2)}, u32[]{:S(2)}) collective-permute-start(bf16[64,896]{1,0:T(8,128)(2,1)S(1)} %collective-permute-done.2.refs_3_), channel_id=1, source_target_pairs={{0,2},{2,0},{4,6},{6,4},{8,10},{10,8},{12,14},{14,12},{1,3},{3,1},... | collective-permute-start | bytes 344072 | tf_op jit(solution)/shard_map/ppermute | solution.py:223
  24.2 5.8 %collective-permute-start.13 = (bf16[64,896]{1,0:T(8,128)(2,1)S(1)}, bf16[64,896]{1,0:T(8,128)(2,1)S(1)}, u32[]{:S(2)}, u32[]{:S(2)}) collective-permute-start(bf16[64,896]{1,0:T(8,128)(2,1)S(1)} %collective-permute-done.12.refs_4_), channel_id=1, source_target_pairs={{0,4},{2,6},{4,12},{6,14},{12,8},{14,10},{8,0},{10,2},{1,5},{3,7},... | collective-permute-start | bytes 344072 | tf_op jit(solution)/shard_map/ppermute | solution.py:228
  26.7 4.8 %collective-permute-start.10 = (bf16[64,896]{1,0:T(8,128)(2,1)S(1)}, bf16[64,896]{1,0:T(8,128)(2,1)S(1)}, u32[]{:S(2)}, u32[]{:S(2)}) collective-permute-start(bf16[64,896]{1,0:T(8,128)(2,1)S(1)} %collective-permute-done.8.refs_0_), channel_id=1, source_target_pairs={{0,2},{2,0},{4,6},{6,4},{8,10},{10,8},{12,14},{14,12},{1,3},{3,1},... | collective-permute-start | bytes 344072 | tf_op jit(solution)/shard_map/ppermute | solution.py:228
  28.0 0.7 %copy-start.4 = (s32[2,64,1]{1,2,0:T(1,128)S(1)}, s32[2,64,1]{1,2,0:T(1,128)}, u32[]{:S(2)}) copy-start(s32[2,64,1]{1,2,0:T(1,128)} %param.10) | copy-start | bytes 1540
  28.7 0.7 %copy-start.5 = (s32[2,64]{1,0:T(2,128)S(1)}, s32[2,64]{1,0:T(2,128)}, u32[]{:S(2)}) copy-start(s32[2,64]{1,0:T(2,128)} %stored_ref.1) | copy-start | bytes 1540
  31.8 1.9 %copy-start.1 = (bf16[896,1024]{1,0:T(8,128)(2,1)S(1)}, bf16[896,1024]{1,0:T(8,128)(2,1)}, u32[]{:S(2)}) copy-start(bf16[896,1024]{1,0:T(8,128)(2,1)} %wv_ref.1) | copy-start | bytes 5505028
  31.8 1.9 %collective-permute-start.14 = (bf16[128,1792]{1,0:T(8,128)(2,1)S(1)}, bf16[128,1792]{1,0:T(8,128)(2,1)S(1)}, u32[]{:S(2)}, u32[]{:S(2)}) collective-permute-start(bf16[128,1792]{1,0:T(8,128)(2,1)S(1)} %shard_map.66.picked_ref.own_ref), channel_id=1, source_target_pairs={{0,1},{1,0},{2,3},{3,2},{4,5},{5,4},{6,7},{7,6},{8,9},{9,8},{10,11... | collective-permute-start | bytes 1376264 | tf_op jit(solution)/shard_map/ppermute | solution.py:238

commit v2 on v1

--- a/solution.py
+++ b/solution.py
@@ -67,17 +67,18 @@
     return jnp.where(line % 2 == 1, (line + 1) // 2, jnp.where(line == 0, 0, turns - line // 2))
 
 
-def wanted_rows(wide_count, rows, owner_ref, stored_ref):
-    turns = wide_count // SIDE
+def wanted_rows(order, turns, rows, owner_ref, stored_ref):
     me = lax.axis_index("wide")
     columns = []
     for c in range(stored_ref.shape[0]):
         owner, stored = owner_ref[c], stored_ref[c : c + 1, :]
         back = ring_place(me // SIDE, turns) - ring_place(owner // SIDE, turns)
         back = jnp.where(back < 0, back + turns, back)
-        straight = jnp.where(back == 0, 0, 2 * back - 1)
-        crossed = jnp.where(back == turns - 1, wide_count - 1, 2 * back + 2)
-        place = jnp.where(owner % SIDE == me % SIDE, straight, crossed) * rows + stored
+        beside = jnp.where(owner % SIDE == me % SIDE, 0, 1)
+        place = jnp.zeros_like(stored)
+        for n, chunk in enumerate(order):
+            place = jnp.where(back * 2 + beside == chunk[0] * 2 + chunk[1], n, place)
+        place = place * rows + stored
         square = (place.shape[1], place.shape[1])
         own = lax.broadcasted_iota(jnp.int32, square, 0) == lax.broadcasted_iota(jnp.int32, square, 1)
         spread = jnp.where(own, jnp.broadcast_to(place.astype(jnp.float32), square), 0.0)
@@ -85,18 +86,18 @@
     return jnp.concatenate(columns, axis=0).astype(jnp.int32)
 
 
-def early_kernel(wide_count, owner_ref, stored_ref, *refs):
+def early_kernel(order, turns, owner_ref, stored_ref, *refs):
     sources, index_ref, out_ref = refs[:-2], refs[-2], refs[-1]
-    index_ref[...] = wanted_rows(wide_count, sources[0].shape[0], owner_ref, stored_ref)
+    index_ref[...] = wanted_rows(order, turns, sources[0].shape[0], owner_ref, stored_ref)
     out_ref[...] = chosen_rows(index_ref[...], sources, 0).astype(out_ref.dtype)
 
 
-def early(owners, stored, streams):
+def early(order, turns, owners, stored, streams):
     sources = [chunk for stream in streams for chunk in stream]
     rows, width = sources[0].shape
     requests = stored.size
     return pl.pallas_call(
-        functools.partial(early_kernel, lax.axis_size("wide")),
+        functools.partial(early_kernel, order, turns),
         out_shape=(
             jax.ShapeDtypeStruct((requests, 1), jnp.int32),
             jax.ShapeDtypeStruct((requests, STREAMS * width), sources[0].dtype),
@@ -172,29 +173,43 @@
     )(picked, w_key, queries)
 
 
-def attend_kernel(spans, own_ref, other_ref, wk_ref, wv_ref, query_ref, first_ref, out_ref, second_ref, probs_ref):
-    channels = wk_ref.shape[0]
-    other = by_span(other_ref[...], spans, channels)
+def values_kernel(spans, picked_ref, wv_ref, values_ref):
+    source = by_span(picked_ref[...], spans, wv_ref.shape[0])
+    values_ref[...] = jnp.dot(source, wv_ref[...], preferred_element_type=jnp.float32).astype(values_ref.dtype)
+
+
+def own_values(picked, w_value, spans):
+    rows = picked.size // w_value.shape[0]
+    return pl.pallas_call(
+        functools.partial(values_kernel, spans),
+        out_shape=jax.ShapeDtypeStruct((rows, w_value.shape[1]), picked.dtype),
+        in_specs=[VMEM] * 2,
+        out_specs=VMEM,
+        compiler_params=params(),
+    )(picked, w_value)
+
+
+def attend_kernel(
+    spans, other_ref, wk_ref, wv_ref, query_ref, first_ref, values_ref, out_ref, second_ref, probs_ref
+):
+    other = by_span(other_ref[...], spans, wk_ref.shape[0])
     score(spans, other, wk_ref, query_ref, second_ref)
     per = other.shape[0] // spans
-    own = by_span(own_ref[...], spans, channels)
-    source = []
-    for c in range(spans):
-        source += [own[c * per : (c + 1) * per], other[c * per : (c + 1) * per]]
-    source = jnp.concatenate(source, axis=0)
-    values = jnp.dot(source, wv_ref[...], preferred_element_type=jnp.float32).astype(jnp.bfloat16)
-    places = head_places(spans, values.shape[1])
+    more = jnp.dot(other, wv_ref[...], preferred_element_type=jnp.float32).astype(jnp.bfloat16)
+    places = head_places(spans, more.shape[1])
     for c, lanes, n in places:
         scores = jnp.concatenate([first_ref[n], second_ref[n]], axis=1)
         raised = jnp.exp2((scores - jnp.max(scores, axis=-1, keepdims=True)) * EXPONENT)
         probs_ref[n] = (raised * (1.0 / jnp.sum(raised, axis=-1, keepdims=True))).astype(jnp.bfloat16)
     for c, lanes, n in places:
-        mixed = jnp.dot(probs_ref[n], values[2 * c * per : 2 * (c + 1) * per, lanes], preferred_element_type=jnp.float32)
+        rows = slice(c * per, (c + 1) * per)
+        values = jnp.concatenate([values_ref[rows, lanes], more[rows, lanes]], axis=0)
+        mixed = jnp.dot(probs_ref[n], values, preferred_element_type=jnp.float32)
         out_ref[c * SPAN : (c + 1) * SPAN, lanes] = mixed.astype(out_ref.dtype)
 
 
-def attend(picked, other, w_key, w_value, queries, first, spans):
-    each = scores_shape(picked, queries, w_key.shape[0], spans)
+def attend(other, w_key, w_value, queries, first, values, spans):
+    each = scores_shape(other, queries, w_key.shape[0], spans)
     return pl.pallas_call(
         functools.partial(attend_kernel, spans),
         out_shape=jax.ShapeDtypeStruct(queries.shape, queries.dtype),
@@ -202,7 +217,11 @@
         out_specs=VMEM,
         scratch_shapes=[pltpu.VMEM(each, jnp.float32), pltpu.VMEM(each[:2] + (2 * each[2],), jnp.bfloat16)],
         compiler_params=params(),
-    )(picked, other, w_key, w_value, queries, first)
+    )(other, w_key, w_value, queries, first, values)
+
+
+def send(chunk, pairs):
+    return lax.ppermute(chunk, "wide", pairs)
 
 
 def gathered_plan(queries, encodings, w_key, w_value, block_owner, block_row):
@@ -211,33 +230,46 @@
     rows = encodings.shape[0]
     spans = queries.shape[0] // SPAN
     line = ring_order(turns)
-    ring = [
+    onward = [
         (here * SIDE + x, there * SIDE + x) for here, there in zip(line, line[1:] + line[:1]) for x in range(SIDE)
     ]
+    backward = [(there, here) for here, there in onward]
     across = [(n, n + 1 if n % SIDE == 0 else n - 1) for n in range(wide_count)]
-    held = [[piece] for piece in half_columns(encodings)]
-    crossed = [[] for _ in held]
-    for k in range(turns - 1):
-        for straight, side in zip(held, crossed):
-            onward = lax.ppermute(straight[k], "wide", ring)
-            aside = lax.ppermute(straight[k], "wide", across)
-            onward, aside = lax.optimization_barrier((onward, aside))
-            straight.append(onward)
-            side.append(aside)
-    last = [
-        lax.ppermute(held[n][-1], "wide", across) if n % 2 == 0 else lax.ppermute(crossed[n][-1], "wide", ring)
-        for n in range(STREAMS)
-    ]
-    order = [
-        [straight[0]] + [chunk for pair in zip(straight[1:], side) for chunk in pair]
-        for straight, side in zip(held, crossed)
-    ]
-    there = len(order[0]) - 2
-    index, begun = early(jnp.transpose(block_owner, (0, 2, 1)), block_row, [chunks[:there] for chunks in order])
-    picked = pick(index, begun, [chunks[there:] + [final] for chunks, final in zip(order, last)], there * rows)
+    ahead = turns // 2
+    pieces = half_columns(encodings)
+    streams = [{(0, 0): piece} for piece in pieces]
+    for k in range(1, ahead + 1):
+        for held in streams:
+            held[k, 0], held[k - 1, 1] = lax.optimization_barrier(
+                (send(held[k - 1, 0], onward), send(held[k - 1, 0], across))
+            )
+    for k in range(turns - 1, ahead, -1):
+        for held in streams:
+            source = held[(k + 1) % turns, 0]
+            if k == turns - 1:
+                source, streams[0][1, 0] = lax.optimization_barrier((source, streams[0][1, 0]))
+            held[k, 0] = send(source, backward)
+            if k < turns - 1:
+                held[k + 1, 1] = send(source, across)
+    for n, held in enumerate(streams):
+        held[ahead, 1] = send(held[ahead, 0], across)
+        k = ahead + 1
+        held[k, 1] = send(held[k, 0], across) if n % 2 == 0 else send(held[(k + 1) % turns, 1], backward)
+    late = [(ahead, 1), (ahead + 1, 1)]
+    order = [chunk for chunk in streams[0] if chunk not in late] + late
+    there = len(order) - len(late)
+    index, begun = early(
+        order,
+        turns,
+        jnp.transpose(block_owner, (0, 2, 1)),
+        block_row,
+        [[held[chunk] for chunk in order[:there]] for held in streams],
+    )
+    picked = pick(index, begun, [[held[chunk] for chunk in late] for held in streams], there * rows)
     other = lax.ppermute(picked, "heads", [(0, 1), (1, 0)])
     first = own_scores(picked, w_key, queries, spans)
-    return attend(picked, other, w_key, w_value, queries, first, spans)
+    values = own_values(picked, w_value, spans)
+    return attend(other, w_key, w_value, queries, first, values, spans)
 
 
 def exchange(encodings, owners, stored, capacity):

time: 37 us -> 39.4 us (1.065)
  waiting for transfers between devices: 7.41 us -> 8.73 us
  starting transfers between devices: 21.7 us -> 22.2 us
    ppermute x14, waiting for transfers between devices: 6.64 us -> 8.73 us  [send(): return lax.ppermute(chunk, 'wide', pairs)]
    ppermute x1, waiting for transfers between devices: 0.77 us -> 0.01 us  [gathered_plan(): other = lax.ppermute(picked, 'heads', [(0, 1), (1, 0)])]
    pallas_call x1 -> x2, Pallas kernels: 0.61 us -> 1.31 us  [the longest x1 0.71 us: own_values(): pl.pallas_call(functools.partial(values_kernel, spans), out_shape=jax.Sha...]
    ppermute x14, starting transfers between devices: 21.6 us -> 22.2 us  [send(): return lax.ppermute(chunk, 'wide', pairs)]
    pallas_call x1, Pallas kernels: 3.08 us -> 2.57 us  [attend(): pl.pallas_call(functools.partial(attend_kernel, spans), out_shape=jax.Sha...]
  transfers between devices with their start and end apart: 15 -> 15, of which waited for: 8 -> 4; matrix products, arithmetic and copies ran while one was open for 0% -> 0% of each run, Pallas kernels for 4% -> 6%
where the time goes in v2:
time: 39.4 us; the launch traced here: 39.2 us
  starting transfers between devices  22.2 us (56%)
  waiting for transfers between devices  8.73 us (22%)
  Pallas kernels  5.27 us (13%)
  local copies, waits for them, and re-layouts  2.88 us (7%)
    ppermute x14, starting transfers between devices, send(): return lax.ppermute(chunk, 'wide', pairs)  22.2 us
    ppermute x14, waiting for transfers between devices, send(): return lax.ppermute(chunk, 'wide', pairs)  8.73 us
    unnamed x12, local copies, waits for them, and re-layouts  2.88 us
    pallas_call x1, Pallas kernels, attend(): pl.pallas_call(functools.partial(attend_kernel, spans), out_shape=jax.Sha...  2.57 us
    pallas_call x1, Pallas kernels, own_scores(): pl.pallas_call(functools.partial(score_kernel, spans), out_shape=jax.Shap...  1.02 us
  transfers between devices with their start and end apart: 15, of which 4 were waited for; matrix products, arithmetic and copies ran while one was open for 0% of the time, Pallas kernels for 6%

profile of v2, /device:TPU:0, one launch (start us, length us, event | category | flops | bytes accessed | tf_op | source)
XLA Modules:
  0.0 39.2 jit_solution(9274487618649389184)
XLA Ops:
  0.0 1.2 %copy-done.3 = bf16[64,3584]{1,0:T(8,128)(2,1)S(1)} copy-done((bf16[64,3584]{1,0:T(8,128)(2,1)S(1)}, bf16[64,3584]{1,0:T(8,128)(2,1)}, u32[]{:S(2)}) %copy-start.3) | copy-done | bytes 458776
  1.2 3.1 %collective-permute-start = (bf16[64,896]{1,0:T(8,128)(2,1)S(1)}, bf16[64,896]{1,0:T(8,128)(2,1)S(1)}, u32[]{:S(2)}, u32[]{:S(2)}) collective-permute-start(bf16[64,896]{1,0:T(8,128)(2,1)S(1)} %get-tuple-element.29.refs_0_), channel_id=1, source_target_pairs={{0,4},{2,6},{4,12},{6,14},{12,8},{14,10},{8,0},{10,2},{1,5},{3,7},... | collective-permute-start | bytes 344072 | tf_op jit(solution)/shard_map/ppermute | solution.py:224
  4.3 1.5 %collective-permute-start.1 = (bf16[64,896]{1,0:T(8,128)(2,1)S(1)}, bf16[64,896]{1,0:T(8,128)(2,1)S(1)}, u32[]{:S(2)}, u32[]{:S(2)}) collective-permute-start(bf16[64,896]{1,0:T(8,128)(2,1)S(1)} %get-tuple-element.29.refs_0_), channel_id=1, source_target_pairs={{0,2},{2,0},{4,6},{6,4},{8,10},{10,8},{12,14},{14,12},{1,3},{3,1},... | collective-permute-start | bytes 344072 | tf_op jit(solution)/shard_map/ppermute | solution.py:224
  5.8 2.6 %collective-permute-start.5 = (bf16[64,896]{1,0:T(8,128)(2,1)S(1)}, bf16[64,896]{1,0:T(8,128)(2,1)S(1)}, u32[]{:S(2)}, u32[]{:S(2)}) collective-permute-start(bf16[64,896]{1,0:T(8,128)(2,1)S(1)} %get-tuple-element.34.refs_6_), channel_id=1, source_target_pairs={{0,4},{2,6},{4,12},{6,14},{12,8},{14,10},{8,0},{10,2},{1,5},{3,7},... | collective-permute-start | bytes 344072 | tf_op jit(solution)/shard_map/ppermute | solution.py:224
  8.4 0.5 %collective-permute-start.6 = (bf16[64,896]{1,0:T(8,128)(2,1)S(1)}, bf16[64,896]{1,0:T(8,128)(2,1)S(1)}, u32[]{:S(2)}, u32[]{:S(2)}) collective-permute-start(bf16[64,896]{1,0:T(8,128)(2,1)S(1)} %get-tuple-element.34.refs_6_), channel_id=1, source_target_pairs={{0,2},{2,0},{4,6},{6,4},{8,10},{10,8},{12,14},{14,12},{1,3},{3,1},... | collective-permute-start | bytes 344072 | tf_op jit(solution)/shard_map/ppermute | solution.py:224
  9.1 3.8 %collective-permute-start.2 = (bf16[64,896]{1,0:T(8,128)(2,1)S(1)}, bf16[64,896]{1,0:T(8,128)(2,1)S(1)}, u32[]{:S(2)}, u32[]{:S(2)}) collective-permute-start(bf16[64,896]{1,0:T(8,128)(2,1)S(1)} %collective-permute-done.refs_1_), channel_id=1, source_target_pairs={{0,4},{2,6},{4,12},{6,14},{12,8},{14,10},{8,0},{10,2},{1,5},{3,7},... | collective-permute-start | bytes 344072 | tf_op jit(solution)/shard_map/ppermute | solution.py:224
  12.9 1.3 %collective-permute-start.3 = (bf16[64,896]{1,0:T(8,128)(2,1)S(1)}, bf16[64,896]{1,0:T(8,128)(2,1)S(1)}, u32[]{:S(2)}, u32[]{:S(2)}) collective-permute-start(bf16[64,896]{1,0:T(8,128)(2,1)S(1)} %collective-permute-done.refs_1_), channel_id=1, source_target_pairs={{0,2},{2,0},{4,6},{6,4},{8,10},{10,8},{12,14},{14,12},{1,3},{3,1},... | collective-permute-start | bytes 344072 | tf_op jit(solution)/shard_map/ppermute | solution.py:224
  14.2 1.1 %collective-permute-start.7 = (bf16[64,896]{1,0:T(8,128)(2,1)S(1)}, bf16[64,896]{1,0:T(8,128)(2,1)S(1)}, u32[]{:S(2)}, u32[]{:S(2)}) collective-permute-start(bf16[64,896]{1,0:T(8,128)(2,1)S(1)} %collective-permute-done.5.refs_7_), channel_id=1, source_target_pairs={{0,4},{2,6},{4,12},{6,14},{12,8},{14,10},{8,0},{10,2},{1,5},{3,7},... | collective-permute-start | bytes 344072 | tf_op jit(solution)/shard_map/ppermute | solution.py:224
  15.3 0.5 %collective-permute-start.8 = (bf16[64,896]{1,0:T(8,128)(2,1)S(1)}, bf16[64,896]{1,0:T(8,128)(2,1)S(1)}, u32[]{:S(2)}, u32[]{:S(2)}) collective-permute-start(bf16[64,896]{1,0:T(8,128)(2,1)S(1)} %collective-permute-done.5.refs_7_), channel_id=1, source_target_pairs={{0,2},{2,0},{4,6},{6,4},{8,10},{10,8},{12,14},{14,12},{1,3},{3,1},... | collective-permute-start | bytes 344072 | tf_op jit(solution)/shard_map/ppermute | solution.py:224
  15.8 2.0 %collective-permute-start.4 = (bf16[64,896]{1,0:T(8,128)(2,1)S(1)}, bf16[64,896]{1,0:T(8,128)(2,1)S(1)}, u32[]{:S(2)}, u32[]{:S(2)}) collective-permute-start(bf16[64,896]{1,0:T(8,128)(2,1)S(1)} %get-tuple-element.29.refs_0_), channel_id=1, source_target_pairs={{4,0},{6,2},{12,4},{14,6},{8,12},{10,14},{0,8},{2,10},{5,1},{7,3},... | collective-permute-start | bytes 344072 | tf_op jit(solution)/shard_map/ppermute | solution.py:224
  17.9 2.9 %collective-permute-start.13 = (bf16[64,896]{1,0:T(8,128)(2,1)S(1)}, bf16[64,896]{1,0:T(8,128)(2,1)S(1)}, u32[]{:S(2)}, u32[]{:S(2)}) collective-permute-start(bf16[64,896]{1,0:T(8,128)(2,1)S(1)} %collective-permute-done.6.refs_8_), channel_id=1, source_target_pairs={{4,0},{6,2},{12,4},{14,6},{8,12},{10,14},{0,8},{2,10},{5,1},{7,3},... | collective-permute-start | bytes 344072 | tf_op jit(solution)/shard_map/ppermute | solution.py:224
  20.8 6.1 %collective-permute-done.7.refs_9_ = bf16[64,896]{1,0:T(8,128)(2,1)S(1)} collective-permute-done((bf16[64,896]{1,0:T(8,128)(2,1)S(1)}, bf16[64,896]{1,0:T(8,128)(2,1)S(1)}, u32[]{:S(2)}, u32[]{:S(2)}) %collective-permute-start.7) | collective-permute-done | bytes 114720 | tf_op jit(solution)/shard_map/ppermute | solution.py:224
  26.8 0.8 %collective-permute-start.10 = (bf16[64,896]{1,0:T(8,128)(2,1)S(1)}, bf16[64,896]{1,0:T(8,128)(2,1)S(1)}, u32[]{:S(2)}, u32[]{:S(2)}) collective-permute-start(bf16[64,896]{1,0:T(8,128)(2,1)S(1)} %collective-permute-done.2.refs_3_), channel_id=1, source_target_pairs={{0,2},{2,0},{4,6},{6,4},{8,10},{10,8},{12,14},{14,12},{1,3},{3,1},... | collective-permute-start | bytes 344072 | tf_op jit(solution)/shard_map/ppermute | solution.py:224
  27.6 1.3 %collective-permute-start.11 = (bf16[64,896]{1,0:T(8,128)(2,1)S(1)}, bf16[64,896]{1,0:T(8,128)(2,1)S(1)}, u32[]{:S(2)}, u32[]{:S(2)}) collective-permute-start(bf16[64,896]{1,0:T(8,128)(2,1)S(1)} %collective-permute-done.4.refs_5_), channel_id=1, source_target_pairs={{0,2},{2,0},{4,6},{6,4},{8,10},{10,8},{12,14},{14,12},{1,3},{3,1},... | collective-permute-start | bytes 344072 | tf_op jit(solution)/shard_map/ppermute | solution.py:224
  28.9 0.8 %collective-permute-start.12 = (bf16[64,896]{1,0:T(8,128)(2,1)S(1)}, bf16[64,896]{1,0:T(8,128)(2,1)S(1)}, u32[]{:S(2)}, u32[]{:S(2)}) collective-permute-start(bf16[64,896]{1,0:T(8,128)(2,1)S(1)} %collective-permute-done.7.refs_9_), channel_id=1, source_target_pairs={{0,2},{2,0},{4,6},{6,4},{8,10},{10,8},{12,14},{14,12},{1,3},{3,1},... | collective-permute-start | bytes 344072 | tf_op jit(solution)/shard_map/ppermute | solution.py:224
  29.6 0.7 %copy-done.4 = s32[2,64,1]{1,2,0:T(1,128)S(1)} copy-done((s32[2,64,1]{1,2,0:T(1,128)S(1)}, s32[2,64,1]{1,2,0:T(1,128)}, u32[]{:S(2)}) %copy-start.4) | copy-done | bytes 536
  30.3 0.7 %copy-done.5 = s32[2,64]{1,0:T(2,128)S(1)} copy-done((s32[2,64]{1,0:T(2,128)S(1)}, s32[2,64]{1,0:T(2,128)}, u32[]{:S(2)}) %copy-start.5) | copy-done | bytes 536
  31.0 0.6 %shard_map.65 = (s32[128,1]{1,0:T(8,128)S(1)}, bf16[128,1792]{1,0:T(8,128)(2,1)S(1)}) custom-call(s32[2,1,64]{2,1,0:T(1,128)S(1)} %bitcast.3, s32[2,64]{1,0:T(2,128)S(1)} %copy-done.5, bf16[64,896]{1,0:T(8,128)(2,1)S(1)} %get-tuple-element.29.refs_0_, bf16[64,896]{1,0:T(8,128)(2,1)S(1)} %collective-permute-done.refs_1_, ...), custom_call_target="tpu_custom_call" | custom-call | flops 176160768 | bytes 458752 | tf_op jit(solution)/shard_map/pallas_call | solution.py:99
  31.6 1.2 %collective-permute-done.11.refs_1_ = bf16[64,896]{1,0:T(8,128)(2,1)S(1)} collective-permute-done((bf16[64,896]{1,0:T(8,128)(2,1)S(1)}, bf16[64,896]{1,0:T(8,128)(2,1)S(1)}, u32[]{:S(2)}, u32[]{:S(2)}) %collective-permute-start.11) | collective-permute-done | bytes 114720 | tf_op jit(solution)/shard_map/ppermute | solution.py:224
  32.9 1.2 %collective-permute-done.12.refs_2_ = bf16[64,896]{1,0:T(8,128)(2,1)S(1)} collective-permute-done((bf16[64,896]{1,0:T(8,128)(2,1)S(1)}, bf16[64,896]{1,0:T(8,128)(2,1)S(1)}, u32[]{:S(2)}, u32[]{:S(2)}) %collective-permute-start.12) | collective-permute-done | bytes 114720 | tf_op jit(solution)/shard_map/ppermute | solution.py:224
  34.5 0.7 %shard_map.68.values_ref = bf16[256,1024]{1,0:T(8,128)(2,1)S(1)} custom-call(bf16[128,1792]{1,0:T(8,128)(2,1)S(1)} %shard_map.66.picked_ref, bf16[896,1024]{1,0:T(8,128)(2,1)S(1)} %copy-done.1), custom_call_target="tpu_custom_call" | custom-call | tf_op jit(solution)/shard_map/pallas_call | solution.py:183
  35.2 0.4 copy-done
  35.6 1.0 %shard_map.67.first_ref = f32[16,64,128]{2,1,0:T(8,128)S(1)} custom-call(bf16[128,1792]{1,0:T(8,128)(2,1)S(1)} %shard_map.66.picked_ref, bf16[896,1024]{1,0:T(8,128)(2,1)S(1)} %copy-done, bf16[128,1024]{1,0:T(8,128)(2,1)S(1)} %copy-done.2), custom_call_target="tpu_custom_call" | custom-call | tf_op jit(solution)/shard_map/pallas_call | solution.py:167
  36.6 2.6 %shard_map.69 = bf16[128,1024]{1,0:T(8,128)(2,1)} custom-call(bf16[128,1792]{1,0:T(8,128)(2,1)S(1)} %collective-permute-done.14.other_ref, bf16[896,1024]{1,0:T(8,128)(2,1)S(1)} %copy-done, bf16[896,1024]{1,0:T(8,128)(2,1)S(1)} %copy-done.1, bf16[128,1024]{1,0:T(8,128)(2,1)S(1)} %copy-done.2, f32[16,64,128]{2,1,0:T(8,128)S(1)} %shard_map.67.first_ref, ...), custom_call_target="tpu_custom_call" | custom-call | tf_op jit(solution)/shard_map/pallas_call | solution.py:213
  (24 shorter events, 0.7 us)
Async XLA Ops:
  0.0 34.5 %copy-start.1 = (bf16[896,1024]{1,0:T(8,128)(2,1)S(1)}, bf16[896,1024]{1,0:T(8,128)(2,1)}, u32[]{:S(2)}) copy-start(bf16[896,1024]{1,0:T(8,128)(2,1)} %wv_ref.3) | copy-start | bytes 5505028
  0.0 1.2 %copy-start.3 = (bf16[64,3584]{1,0:T(8,128)(2,1)S(1)}, bf16[64,3584]{1,0:T(8,128)(2,1)}, u32[]{:S(2)}) copy-start(bf16[64,3584]{1,0:T(8,128)(2,1)} %enc_ref.1) | copy-start | bytes 1376260
  1.2 7.7 %collective-permute-start = (bf16[64,896]{1,0:T(8,128)(2,1)S(1)}, bf16[64,896]{1,0:T(8,128)(2,1)S(1)}, u32[]{:S(2)}, u32[]{:S(2)}) collective-permute-start(bf16[64,896]{1,0:T(8,128)(2,1)S(1)} %get-tuple-element.29.refs_0_), channel_id=1, source_target_pairs={{0,4},{2,6},{4,12},{6,14},{12,8},{14,10},{8,0},{10,2},{1,5},{3,7},... | collective-permute-start | bytes 344072 | tf_op jit(solution)/shard_map/ppermute | solution.py:224
  4.3 4.8 %collective-permute-start.1 = (bf16[64,896]{1,0:T(8,128)(2,1)S(1)}, bf16[64,896]{1,0:T(8,128)(2,1)S(1)}, u32[]{:S(2)}, u32[]{:S(2)}) collective-permute-start(bf16[64,896]{1,0:T(8,128)(2,1)S(1)} %get-tuple-element.29.refs_0_), channel_id=1, source_target_pairs={{0,2},{2,0},{4,6},{6,4},{8,10},{10,8},{12,14},{14,12},{1,3},{3,1},... | collective-permute-start | bytes 344072 | tf_op jit(solution)/shard_map/ppermute | solution.py:224
  5.8 8.4 %collective-permute-start.5 = (bf16[64,896]{1,0:T(8,128)(2,1)S(1)}, bf16[64,896]{1,0:T(8,128)(2,1)S(1)}, u32[]{:S(2)}, u32[]{:S(2)}) collective-permute-start(bf16[64,896]{1,0:T(8,128)(2,1)S(1)} %get-tuple-element.34.refs_6_), channel_id=1, source_target_pairs={{0,4},{2,6},{4,12},{6,14},{12,8},{14,10},{8,0},{10,2},{1,5},{3,7},... | collective-permute-start | bytes 344072 | tf_op jit(solution)/shard_map/ppermute | solution.py:224
  8.4 5.8 %collective-permute-start.6 = (bf16[64,896]{1,0:T(8,128)(2,1)S(1)}, bf16[64,896]{1,0:T(8,128)(2,1)S(1)}, u32[]{:S(2)}, u32[]{:S(2)}) collective-permute-start(bf16[64,896]{1,0:T(8,128)(2,1)S(1)} %get-tuple-element.34.refs_6_), channel_id=1, source_target_pairs={{0,2},{2,0},{4,6},{6,4},{8,10},{10,8},{12,14},{14,12},{1,3},{3,1},... | collective-permute-start | bytes 344072 | tf_op jit(solution)/shard_map/ppermute | solution.py:224
  9.1 8.7 %collective-permute-start.2 = (bf16[64,896]{1,0:T(8,128)(2,1)S(1)}, bf16[64,896]{1,0:T(8,128)(2,1)S(1)}, u32[]{:S(2)}, u32[]{:S(2)}) collective-permute-start(bf16[64,896]{1,0:T(8,128)(2,1)S(1)} %collective-permute-done.refs_1_), channel_id=1, source_target_pairs={{0,4},{2,6},{4,12},{6,14},{12,8},{14,10},{8,0},{10,2},{1,5},{3,7},... | collective-permute-start | bytes 344072 | tf_op jit(solution)/shard_map/ppermute | solution.py:224
  12.9 5.0 %collective-permute-start.3 = (bf16[64,896]{1,0:T(8,128)(2,1)S(1)}, bf16[64,896]{1,0:T(8,128)(2,1)S(1)}, u32[]{:S(2)}, u32[]{:S(2)}) collective-permute-start(bf16[64,896]{1,0:T(8,128)(2,1)S(1)} %collective-permute-done.refs_1_), channel_id=1, source_target_pairs={{0,2},{2,0},{4,6},{6,4},{8,10},{10,8},{12,14},{14,12},{1,3},{3,1},... | collective-permute-start | bytes 344072 | tf_op jit(solution)/shard_map/ppermute | solution.py:224
  14.2 12.6 %collective-permute-start.7 = (bf16[64,896]{1,0:T(8,128)(2,1)S(1)}, bf16[64,896]{1,0:T(8,128)(2,1)S(1)}, u32[]{:S(2)}, u32[]{:S(2)}) collective-permute-start(bf16[64,896]{1,0:T(8,128)(2,1)S(1)} %collective-permute-done.5.refs_7_), channel_id=1, source_target_pairs={{0,4},{2,6},{4,12},{6,14},{12,8},{14,10},{8,0},{10,2},{1,5},{3,7},... | collective-permute-start | bytes 344072 | tf_op jit(solution)/shard_map/ppermute | solution.py:224
  15.3 11.5 %collective-permute-start.8 = (bf16[64,896]{1,0:T(8,128)(2,1)S(1)}, bf16[64,896]{1,0:T(8,128)(2,1)S(1)}, u32[]{:S(2)}, u32[]{:S(2)}) collective-permute-start(bf16[64,896]{1,0:T(8,128)(2,1)S(1)} %collective-permute-done.5.refs_7_), channel_id=1, source_target_pairs={{0,2},{2,0},{4,6},{6,4},{8,10},{10,8},{12,14},{14,12},{1,3},{3,1},... | collective-permute-start | bytes 344072 | tf_op jit(solution)/shard_map/ppermute | solution.py:224
  15.8 11.8 %collective-permute-start.4 = (bf16[64,896]{1,0:T(8,128)(2,1)S(1)}, bf16[64,896]{1,0:T(8,128)(2,1)S(1)}, u32[]{:S(2)}, u32[]{:S(2)}) collective-permute-start(bf16[64,896]{1,0:T(8,128)(2,1)S(1)} %get-tuple-element.29.refs_0_), channel_id=1, source_target_pairs={{4,0},{6,2},{12,4},{14,6},{8,12},{10,14},{0,8},{2,10},{5,1},{7,3},... | collective-permute-start | bytes 344072 | tf_op jit(solution)/shard_map/ppermute | solution.py:224
  17.8 11.8 %collective-permute-start.9 = (bf16[64,896]{1,0:T(8,128)(2,1)S(1)}, bf16[64,896]{1,0:T(8,128)(2,1)S(1)}, u32[]{:S(2)}, u32[]{:S(2)}) collective-permute-start(bf16[64,896]{1,0:T(8,128)(2,1)S(1)} %get-tuple-element.34.refs_6_), channel_id=1, source_target_pairs={{4,0},{6,2},{12,4},{14,6},{8,12},{10,14},{0,8},{2,10},{5,1},{7,3},... | collective-permute-start | bytes 344072 | tf_op jit(solution)/shard_map/ppermute | solution.py:224
  17.9 13.8 %collective-permute-start.13 = (bf16[64,896]{1,0:T(8,128)(2,1)S(1)}, bf16[64,896]{1,0:T(8,128)(2,1)S(1)}, u32[]{:S(2)}, u32[]{:S(2)}) collective-permute-start(bf16[64,896]{1,0:T(8,128)(2,1)S(1)} %collective-permute-done.6.refs_8_), channel_id=1, source_target_pairs={{4,0},{6,2},{12,4},{14,6},{8,12},{10,14},{0,8},{2,10},{5,1},{7,3},... | collective-permute-start | bytes 344072 | tf_op jit(solution)/shard_map/ppermute | solution.py:224
  26.8 4.8 %collective-permute-start.10 = (bf16[64,896]{1,0:T(8,128)(2,1)S(1)}, bf16[64,896]{1,0:T(8,128)(2,1)S(1)}, u32[]{:S(2)}, u32[]{:S(2)}) collective-permute-start(bf16[64,896]{1,0:T(8,128)(2,1)S(1)} %collective-permute-done.2.refs_3_), channel_id=1, source_target_pairs={{0,2},{2,0},{4,6},{6,4},{8,10},{10,8},{12,14},{14,12},{1,3},{3,1},... | collective-permute-start | bytes 344072 | tf_op jit(solution)/shard_map/ppermute | solution.py:224
  27.6 5.3 %collective-permute-start.11 = (bf16[64,896]{1,0:T(8,128)(2,1)S(1)}, bf16[64,896]{1,0:T(8,128)(2,1)S(1)}, u32[]{:S(2)}, u32[]{:S(2)}) collective-permute-start(bf16[64,896]{1,0:T(8,128)(2,1)S(1)} %collective-permute-done.4.refs_5_), channel_id=1, source_target_pairs={{0,2},{2,0},{4,6},{6,4},{8,10},{10,8},{12,14},{14,12},{1,3},{3,1},... | collective-permute-start | bytes 344072 | tf_op jit(solution)/shard_map/ppermute | solution.py:224
  28.9 5.2 %collective-permute-start.12 = (bf16[64,896]{1,0:T(8,128)(2,1)S(1)}, bf16[64,896]{1,0:T(8,128)(2,1)S(1)}, u32[]{:S(2)}, u32[]{:S(2)}) collective-permute-start(bf16[64,896]{1,0:T(8,128)(2,1)S(1)} %collective-permute-done.7.refs_9_), channel_id=1, source_target_pairs={{0,2},{2,0},{4,6},{6,4},{8,10},{10,8},{12,14},{14,12},{1,3},{3,1},... | collective-permute-start | bytes 344072 | tf_op jit(solution)/shard_map/ppermute | solution.py:224
  29.6 0.7 %copy-start.4 = (s32[2,64,1]{1,2,0:T(1,128)S(1)}, s32[2,64,1]{1,2,0:T(1,128)}, u32[]{:S(2)}) copy-start(s32[2,64,1]{1,2,0:T(1,128)} %param.10) | copy-start | bytes 1540
  30.3 0.7 %copy-start.5 = (s32[2,64]{1,0:T(2,128)S(1)}, s32[2,64]{1,0:T(2,128)}, u32[]{:S(2)}) copy-start(s32[2,64]{1,0:T(2,128)} %stored_ref.1) | copy-start | bytes 1540
  34.1 1.5 %copy-start = (bf16[896,1024]{1,0:T(8,128)(2,1)S(1)}, bf16[896,1024]{1,0:T(8,128)(2,1)}, u32[]{:S(2)}) copy-start(bf16[896,1024]{1,0:T(8,128)(2,1)} %wk_ref.3) | copy-start | bytes 5505028
  34.1 1.5 %copy-start.2 = (bf16[128,1024]{1,0:T(8,128)(2,1)S(1)}, bf16[128,1024]{1,0:T(8,128)(2,1)}, u32[]{:S(2)}) copy-start(bf16[128,1024]{1,0:T(8,128)(2,1)} %query_ref.3) | copy-start | bytes 786436
  34.4 2.2 %collective-permute-start.14 = (bf16[128,1792]{1,0:T(8,128)(2,1)S(1)}, bf16[128,1792]{1,0:T(8,128)(2,1)S(1)}, u32[]{:S(2)}, u32[]{:S(2)}) collective-permute-start(bf16[128,1792]{1,0:T(8,128)(2,1)S(1)} %shard_map.66.picked_ref), channel_id=1, source_target_pairs={{0,1},{1,0},{2,3},{3,2},{4,5},{5,4},{6,7},{7,6},{8,9},{9,8},{10,11... | collective-permute-start | bytes 1376264 | tf_op jit(solution)/shard_map/ppermute | solution.py:269

commit v3 on v2

--- a/solution.py
+++ b/solution.py
@@ -233,29 +233,17 @@
     onward = [
         (here * SIDE + x, there * SIDE + x) for here, there in zip(line, line[1:] + line[:1]) for x in range(SIDE)
     ]
-    backward = [(there, here) for here, there in onward]
     across = [(n, n + 1 if n % SIDE == 0 else n - 1) for n in range(wide_count)]
-    ahead = turns // 2
-    pieces = half_columns(encodings)
-    streams = [{(0, 0): piece} for piece in pieces]
-    for k in range(1, ahead + 1):
+    streams = [{(0, 0): piece} for piece in half_columns(encodings)]
+    for k in range(1, turns):
         for held in streams:
-            held[k, 0], held[k - 1, 1] = lax.optimization_barrier(
-                (send(held[k - 1, 0], onward), send(held[k - 1, 0], across))
-            )
-    for k in range(turns - 1, ahead, -1):
-        for held in streams:
-            source = held[(k + 1) % turns, 0]
-            if k == turns - 1:
-                source, streams[0][1, 0] = lax.optimization_barrier((source, streams[0][1, 0]))
-            held[k, 0] = send(source, backward)
-            if k < turns - 1:
-                held[k + 1, 1] = send(source, across)
+            held[k, 0] = send(held[k - 1, 0], onward)
+            held[k - 1, 1] = send(held[k - 1, 0], across)
+            if k > 1:
+                held[k, 0], held[k - 2, 1] = lax.optimization_barrier((held[k, 0], held[k - 2, 1]))
     for n, held in enumerate(streams):
-        held[ahead, 1] = send(held[ahead, 0], across)
-        k = ahead + 1
-        held[k, 1] = send(held[k, 0], across) if n % 2 == 0 else send(held[(k + 1) % turns, 1], backward)
-    late = [(ahead, 1), (ahead + 1, 1)]
+        held[turns - 1, 1] = send(held[turns - 1, 0], across) if n % 2 == 0 else send(held[turns - 2, 1], onward)
+    late = [(turns - 1, 0), (turns - 2, 1), (turns - 1, 1)]
     order = [chunk for chunk in streams[0] if chunk not in late] + late
     there = len(order) - len(late)
     index, begun = early(

time: 39.4 us -> 35.7 us (0.906)
  waiting for transfers between devices: 8.73 us -> 4.98 us
    ppermute x14, waiting for transfers between devices: 8.73 us -> 4.98 us  [send(): return lax.ppermute(chunk, 'wide', pairs)]
  transfers between devices with their start and end apart: 15 -> 15, of which waited for: 4 -> 8; matrix products, arithmetic and copies ran while one was open for 0% -> 0% of each run, Pallas kernels for 6% -> 7%
where the time goes in v3:
time: 35.7 us; the launch traced here: 35.5 us
  starting transfers between devices  22.3 us (62%)
  Pallas kernels  5.28 us (15%)
  waiting for transfers between devices  4.98 us (14%)
  local copies, waits for them, and re-layouts  2.86 us (8%)
    ppermute x14, starting transfers between devices, send(): return lax.ppermute(chunk, 'wide', pairs)  22.2 us
    ppermute x14, waiting for transfers between devices, send(): return lax.ppermute(chunk, 'wide', pairs)  4.98 us
    unnamed x12, local copies, waits for them, and re-layouts  2.86 us
    pallas_call x1, Pallas kernels, attend(): pl.pallas_call(functools.partial(attend_kernel, spans), out_shape=jax.Sha...  2.57 us
    pallas_call x1, Pallas kernels, own_scores(): pl.pallas_call(functools.partial(score_kernel, spans), out_shape=jax.Shap...  1.02 us
  transfers between devices with their start and end apart: 15, of which 8 were waited for; matrix products, arithmetic and copies ran while one was open for 0% of the time, Pallas kernels for 7%

profile of v3, /device:TPU:0, one launch (start us, length us, event | category | flops | bytes accessed | tf_op | source)
XLA Modules:
  0.0 35.5 jit_solution(18345214962915014013)
XLA Ops:
  0.0 1.2 %copy-done.3 = bf16[64,3584]{1,0:T(8,128)(2,1)S(1)} copy-done((bf16[64,3584]{1,0:T(8,128)(2,1)S(1)}, bf16[64,3584]{1,0:T(8,128)(2,1)}, u32[]{:S(2)}) %copy-start.3) | copy-done | bytes 458776
  1.2 3.1 %collective-permute-start = (bf16[64,896]{1,0:T(8,128)(2,1)S(1)}, bf16[64,896]{1,0:T(8,128)(2,1)S(1)}, u32[]{:S(2)}, u32[]{:S(2)}) collective-permute-start(bf16[64,896]{1,0:T(8,128)(2,1)S(1)} %get-tuple-element.17.refs_0_), channel_id=1, source_target_pairs={{0,4},{2,6},{4,12},{6,14},{12,8},{14,10},{8,0},{10,2},{1,5},{3,7},... | collective-permute-start | bytes 344072 | tf_op jit(solution)/shard_map/ppermute | solution.py:224
  4.3 2.6 %collective-permute-start.5 = (bf16[64,896]{1,0:T(8,128)(2,1)S(1)}, bf16[64,896]{1,0:T(8,128)(2,1)S(1)}, u32[]{:S(2)}, u32[]{:S(2)}) collective-permute-start(bf16[64,896]{1,0:T(8,128)(2,1)S(1)} %get-tuple-element.21.refs_5_), channel_id=1, source_target_pairs={{0,4},{2,6},{4,12},{6,14},{12,8},{14,10},{8,0},{10,2},{1,5},{3,7},... | collective-permute-start | bytes 344072 | tf_op jit(solution)/shard_map/ppermute | solution.py:224
  6.9 1.5 %collective-permute-start.2 = (bf16[64,896]{1,0:T(8,128)(2,1)S(1)}, bf16[64,896]{1,0:T(8,128)(2,1)S(1)}, u32[]{:S(2)}, u32[]{:S(2)}) collective-permute-start(bf16[64,896]{1,0:T(8,128)(2,1)S(1)} %get-tuple-element.17.refs_0_), channel_id=1, source_target_pairs={{0,2},{2,0},{4,6},{6,4},{8,10},{10,8},{12,14},{14,12},{1,3},{3,1},... | collective-permute-start | bytes 344072 | tf_op jit(solution)/shard_map/ppermute | solution.py:224
  8.4 0.9 %collective-permute-done.refs_1_ = bf16[64,896]{1,0:T(8,128)(2,1)S(1)} collective-permute-done((bf16[64,896]{1,0:T(8,128)(2,1)S(1)}, bf16[64,896]{1,0:T(8,128)(2,1)S(1)}, u32[]{:S(2)}, u32[]{:S(2)}) %collective-permute-start) | collective-permute-done | bytes 114720 | tf_op jit(solution)/shard_map/ppermute | solution.py:224
  9.3 1.2 %collective-permute-start.1 = (bf16[64,896]{1,0:T(8,128)(2,1)S(1)}, bf16[64,896]{1,0:T(8,128)(2,1)S(1)}, u32[]{:S(2)}, u32[]{:S(2)}) collective-permute-start(bf16[64,896]{1,0:T(8,128)(2,1)S(1)} %collective-permute-done.refs_1_), channel_id=1, source_target_pairs={{0,4},{2,6},{4,12},{6,14},{12,8},{14,10},{8,0},{10,2},{1,5},{3,7},... | collective-permute-start | bytes 344072 | tf_op jit(solution)/shard_map/ppermute | solution.py:224
  10.4 1.5 %collective-permute-start.7 = (bf16[64,896]{1,0:T(8,128)(2,1)S(1)}, bf16[64,896]{1,0:T(8,128)(2,1)S(1)}, u32[]{:S(2)}, u32[]{:S(2)}) collective-permute-start(bf16[64,896]{1,0:T(8,128)(2,1)S(1)} %get-tuple-element.21.refs_5_), channel_id=1, source_target_pairs={{0,2},{2,0},{4,6},{6,4},{8,10},{10,8},{12,14},{14,12},{1,3},{3,1},... | collective-permute-start | bytes 344072 | tf_op jit(solution)/shard_map/ppermute | solution.py:224
  11.9 3.4 %collective-permute-start.6 = (bf16[64,896]{1,0:T(8,128)(2,1)S(1)}, bf16[64,896]{1,0:T(8,128)(2,1)S(1)}, u32[]{:S(2)}, u32[]{:S(2)}) collective-permute-start(bf16[64,896]{1,0:T(8,128)(2,1)S(1)} %collective-permute-done.5.refs_6_), channel_id=1, source_target_pairs={{0,4},{2,6},{4,12},{6,14},{12,8},{14,10},{8,0},{10,2},{1,5},{3,7},... | collective-permute-start | bytes 344072 | tf_op jit(solution)/shard_map/ppermute | solution.py:224
  16.2 0.8 %collective-permute-start.3 = (bf16[64,896]{1,0:T(8,128)(2,1)S(1)}, bf16[64,896]{1,0:T(8,128)(2,1)S(1)}, u32[]{:S(2)}, u32[]{:S(2)}) collective-permute-start(bf16[64,896]{1,0:T(8,128)(2,1)S(1)} %collective-permute-done.1.refs_3_), channel_id=1, source_target_pairs={{0,4},{2,6},{4,12},{6,14},{12,8},{14,10},{8,0},{10,2},{1,5},{3,7},... | collective-permute-start | bytes 344072 | tf_op jit(solution)/shard_map/ppermute | solution.py:224
  17.0 1.6 %collective-permute-done.6.refs_8_ = bf16[64,896]{1,0:T(8,128)(2,1)S(1)} collective-permute-done((bf16[64,896]{1,0:T(8,128)(2,1)S(1)}, bf16[64,896]{1,0:T(8,128)(2,1)S(1)}, u32[]{:S(2)}, u32[]{:S(2)}) %collective-permute-start.6) | collective-permute-done | bytes 114720 | tf_op jit(solution)/shard_map/ppermute | solution.py:224
  18.6 1.0 %collective-permute-start.12 = (bf16[64,896]{1,0:T(8,128)(2,1)S(1)}, bf16[64,896]{1,0:T(8,128)(2,1)S(1)}, u32[]{:S(2)}, u32[]{:S(2)}) collective-permute-start(bf16[64,896]{1,0:T(8,128)(2,1)S(1)} %collective-permute-done.6.refs_8_), channel_id=1, source_target_pairs={{0,2},{2,0},{4,6},{6,4},{8,10},{10,8},{12,14},{14,12},{1,3},{3,1},... | collective-permute-start | bytes 344072 | tf_op jit(solution)/shard_map/ppermute | solution.py:224
  19.6 1.0 %collective-permute-start.9 = (bf16[64,896]{1,0:T(8,128)(2,1)S(1)}, bf16[64,896]{1,0:T(8,128)(2,1)S(1)}, u32[]{:S(2)}, u32[]{:S(2)}) collective-permute-start(bf16[64,896]{1,0:T(8,128)(2,1)S(1)} %collective-permute-done.5.refs_6_), channel_id=1, source_target_pairs={{0,2},{2,0},{4,6},{6,4},{8,10},{10,8},{12,14},{14,12},{1,3},{3,1},... | collective-permute-start | bytes 344072 | tf_op jit(solution)/shard_map/ppermute | solution.py:224
  20.6 1.8 %collective-permute-start.8 = (bf16[64,896]{1,0:T(8,128)(2,1)S(1)}, bf16[64,896]{1,0:T(8,128)(2,1)S(1)}, u32[]{:S(2)}, u32[]{:S(2)}) collective-permute-start(bf16[64,896]{1,0:T(8,128)(2,1)S(1)} %collective-permute-done.6.refs_8_), channel_id=1, source_target_pairs={{0,4},{2,6},{4,12},{6,14},{12,8},{14,10},{8,0},{10,2},{1,5},{3,7},... | collective-permute-start | bytes 344072 | tf_op jit(solution)/shard_map/ppermute | solution.py:224
  22.4 1.5 %collective-permute-start.10 = (bf16[64,896]{1,0:T(8,128)(2,1)S(1)}, bf16[64,896]{1,0:T(8,128)(2,1)S(1)}, u32[]{:S(2)}, u32[]{:S(2)}) collective-permute-start(bf16[64,896]{1,0:T(8,128)(2,1)S(1)} %collective-permute-done.1.refs_3_), channel_id=1, source_target_pairs={{0,2},{2,0},{4,6},{6,4},{8,10},{10,8},{12,14},{14,12},{1,3},{3,1},... | collective-permute-start | bytes 344072 | tf_op jit(solution)/shard_map/ppermute | solution.py:224
  23.9 0.5 %collective-permute-start.11 = (bf16[64,896]{1,0:T(8,128)(2,1)S(1)}, bf16[64,896]{1,0:T(8,128)(2,1)S(1)}, u32[]{:S(2)}, u32[]{:S(2)}) collective-permute-start(bf16[64,896]{1,0:T(8,128)(2,1)S(1)} %collective-permute-done.3.refs_0_), channel_id=1, source_target_pairs={{0,2},{2,0},{4,6},{6,4},{8,10},{10,8},{12,14},{14,12},{1,3},{3,1},... | collective-permute-start | bytes 344072 | tf_op jit(solution)/shard_map/ppermute | solution.py:224
  24.7 1.9 %collective-permute-start.13 = (bf16[64,896]{1,0:T(8,128)(2,1)S(1)}, bf16[64,896]{1,0:T(8,128)(2,1)S(1)}, u32[]{:S(2)}, u32[]{:S(2)}) collective-permute-start(bf16[64,896]{1,0:T(8,128)(2,1)S(1)} %collective-permute-done.12.refs_4_), channel_id=1, source_target_pairs={{0,4},{2,6},{4,12},{6,14},{12,8},{14,10},{8,0},{10,2},{1,5},{3,7},... | collective-permute-start | bytes 344072 | tf_op jit(solution)/shard_map/ppermute | solution.py:224
  26.6 0.6 %collective-permute-done.9.refs_9_ = bf16[64,896]{1,0:T(8,128)(2,1)S(1)} collective-permute-done((bf16[64,896]{1,0:T(8,128)(2,1)S(1)}, bf16[64,896]{1,0:T(8,128)(2,1)S(1)}, u32[]{:S(2)}, u32[]{:S(2)}) %collective-permute-start.9) | collective-permute-done | bytes 114720 | tf_op jit(solution)/shard_map/ppermute | solution.py:224
  27.2 0.7 %copy-done.4 = s32[2,64,1]{1,2,0:T(1,128)S(1)} copy-done((s32[2,64,1]{1,2,0:T(1,128)S(1)}, s32[2,64,1]{1,2,0:T(1,128)}, u32[]{:S(2)}) %copy-start.4) | copy-done | bytes 536
  27.9 0.7 %copy-done.5 = s32[2,64]{1,0:T(2,128)S(1)} copy-done((s32[2,64]{1,0:T(2,128)S(1)}, s32[2,64]{1,0:T(2,128)}, u32[]{:S(2)}) %copy-start.5) | copy-done | bytes 536
  28.6 0.6 %shard_map.65 = (s32[128,1]{1,0:T(8,128)S(1)}, bf16[128,1792]{1,0:T(8,128)(2,1)S(1)}) custom-call(s32[2,1,64]{2,1,0:T(1,128)S(1)} %bitcast.3, s32[2,64]{1,0:T(2,128)S(1)} %copy-done.5, bf16[64,896]{1,0:T(8,128)(2,1)S(1)} %get-tuple-element.17.refs_0_, bf16[64,896]{1,0:T(8,128)(2,1)S(1)} %collective-permute-done.refs_1_, ...), custom_call_target="tpu_custom_call" | custom-call | flops 146800640 | bytes 458752 | tf_op jit(solution)/shard_map/pallas_call | solution.py:99
  29.2 0.6 %collective-permute-done.11.refs_2_ = bf16[64,896]{1,0:T(8,128)(2,1)S(1)} collective-permute-done((bf16[64,896]{1,0:T(8,128)(2,1)S(1)}, bf16[64,896]{1,0:T(8,128)(2,1)S(1)}, u32[]{:S(2)}, u32[]{:S(2)}) %collective-permute-start.11) | collective-permute-done | bytes 114720 | tf_op jit(solution)/shard_map/ppermute | solution.py:224
  30.8 0.7 %shard_map.68.values_ref = bf16[256,1024]{1,0:T(8,128)(2,1)S(1)} custom-call(bf16[128,1792]{1,0:T(8,128)(2,1)S(1)} %shard_map.66.picked_ref, bf16[896,1024]{1,0:T(8,128)(2,1)S(1)} %copy-done.1), custom_call_target="tpu_custom_call" | custom-call | tf_op jit(solution)/shard_map/pallas_call | solution.py:183
  31.9 1.0 %shard_map.67.first_ref = f32[16,64,128]{2,1,0:T(8,128)S(1)} custom-call(bf16[128,1792]{1,0:T(8,128)(2,1)S(1)} %shard_map.66.picked_ref, bf16[896,1024]{1,0:T(8,128)(2,1)S(1)} %copy-done, bf16[128,1024]{1,0:T(8,128)(2,1)S(1)} %copy-done.2), custom_call_target="tpu_custom_call" | custom-call | tf_op jit(solution)/shard_map/pallas_call | solution.py:167
  32.9 2.6 %shard_map.69 = bf16[128,1024]{1,0:T(8,128)(2,1)} custom-call(bf16[128,1792]{1,0:T(8,128)(2,1)S(1)} %collective-permute-done.14.other_ref, bf16[896,1024]{1,0:T(8,128)(2,1)S(1)} %copy-done, bf16[896,1024]{1,0:T(8,128)(2,1)S(1)} %copy-done.1, bf16[128,1024]{1,0:T(8,128)(2,1)S(1)} %copy-done.2, f32[16,64,128]{2,1,0:T(8,128)S(1)} %shard_map.67.first_ref, ...), custom_call_target="tpu_custom_call" | custom-call | tf_op jit(solution)/shard_map/pallas_call | solution.py:213
  (24 shorter events, 2.6 us)
Async XLA Ops:
  0.0 30.8 %copy-start.1 = (bf16[896,1024]{1,0:T(8,128)(2,1)S(1)}, bf16[896,1024]{1,0:T(8,128)(2,1)}, u32[]{:S(2)}) copy-start(bf16[896,1024]{1,0:T(8,128)(2,1)} %wv_ref.3) | copy-start | bytes 5505028
  0.0 1.2 %copy-start.3 = (bf16[64,3584]{1,0:T(8,128)(2,1)S(1)}, bf16[64,3584]{1,0:T(8,128)(2,1)}, u32[]{:S(2)}) copy-start(bf16[64,3584]{1,0:T(8,128)(2,1)} %enc_ref.1) | copy-start | bytes 1376260
  1.2 8.1 %collective-permute-start = (bf16[64,896]{1,0:T(8,128)(2,1)S(1)}, bf16[64,896]{1,0:T(8,128)(2,1)S(1)}, u32[]{:S(2)}, u32[]{:S(2)}) collective-permute-start(bf16[64,896]{1,0:T(8,128)(2,1)S(1)} %get-tuple-element.17.refs_0_), channel_id=1, source_target_pairs={{0,4},{2,6},{4,12},{6,14},{12,8},{14,10},{8,0},{10,2},{1,5},{3,7},... | collective-permute-start | bytes 344072 | tf_op jit(solution)/shard_map/ppermute | solution.py:224
  4.3 7.6 %collective-permute-start.5 = (bf16[64,896]{1,0:T(8,128)(2,1)S(1)}, bf16[64,896]{1,0:T(8,128)(2,1)S(1)}, u32[]{:S(2)}, u32[]{:S(2)}) collective-permute-start(bf16[64,896]{1,0:T(8,128)(2,1)S(1)} %get-tuple-element.21.refs_5_), channel_id=1, source_target_pairs={{0,4},{2,6},{4,12},{6,14},{12,8},{14,10},{8,0},{10,2},{1,5},{3,7},... | collective-permute-start | bytes 344072 | tf_op jit(solution)/shard_map/ppermute | solution.py:224
  6.9 9.0 %collective-permute-start.2 = (bf16[64,896]{1,0:T(8,128)(2,1)S(1)}, bf16[64,896]{1,0:T(8,128)(2,1)S(1)}, u32[]{:S(2)}, u32[]{:S(2)}) collective-permute-start(bf16[64,896]{1,0:T(8,128)(2,1)S(1)} %get-tuple-element.17.refs_0_), channel_id=1, source_target_pairs={{0,2},{2,0},{4,6},{6,4},{8,10},{10,8},{12,14},{14,12},{1,3},{3,1},... | collective-permute-start | bytes 344072 | tf_op jit(solution)/shard_map/ppermute | solution.py:224
  9.3 6.9 %collective-permute-start.1 = (bf16[64,896]{1,0:T(8,128)(2,1)S(1)}, bf16[64,896]{1,0:T(8,128)(2,1)S(1)}, u32[]{:S(2)}, u32[]{:S(2)}) collective-permute-start(bf16[64,896]{1,0:T(8,128)(2,1)S(1)} %collective-permute-done.refs_1_), channel_id=1, source_target_pairs={{0,4},{2,6},{4,12},{6,14},{12,8},{14,10},{8,0},{10,2},{1,5},{3,7},... | collective-permute-start | bytes 344072 | tf_op jit(solution)/shard_map/ppermute | solution.py:224
  10.4 6.5 %collective-permute-start.7 = (bf16[64,896]{1,0:T(8,128)(2,1)S(1)}, bf16[64,896]{1,0:T(8,128)(2,1)S(1)}, u32[]{:S(2)}, u32[]{:S(2)}) collective-permute-start(bf16[64,896]{1,0:T(8,128)(2,1)S(1)} %get-tuple-element.21.refs_5_), channel_id=1, source_target_pairs={{0,2},{2,0},{4,6},{6,4},{8,10},{10,8},{12,14},{14,12},{1,3},{3,1},... | collective-permute-start | bytes 344072 | tf_op jit(solution)/shard_map/ppermute | solution.py:224
  11.9 6.7 %collective-permute-start.6 = (bf16[64,896]{1,0:T(8,128)(2,1)S(1)}, bf16[64,896]{1,0:T(8,128)(2,1)S(1)}, u32[]{:S(2)}, u32[]{:S(2)}) collective-permute-start(bf16[64,896]{1,0:T(8,128)(2,1)S(1)} %collective-permute-done.5.refs_6_), channel_id=1, source_target_pairs={{0,4},{2,6},{4,12},{6,14},{12,8},{14,10},{8,0},{10,2},{1,5},{3,7},... | collective-permute-start | bytes 344072 | tf_op jit(solution)/shard_map/ppermute | solution.py:224
  15.3 7.1 %collective-permute-start.4 = (bf16[64,896]{1,0:T(8,128)(2,1)S(1)}, bf16[64,896]{1,0:T(8,128)(2,1)S(1)}, u32[]{:S(2)}, u32[]{:S(2)}) collective-permute-start(bf16[64,896]{1,0:T(8,128)(2,1)S(1)} %collective-permute-done.refs_1_), channel_id=1, source_target_pairs={{0,2},{2,0},{4,6},{6,4},{8,10},{10,8},{12,14},{14,12},{1,3},{3,1},... | collective-permute-start | bytes 344072 | tf_op jit(solution)/shard_map/ppermute | solution.py:224
  16.2 7.7 %collective-permute-start.3 = (bf16[64,896]{1,0:T(8,128)(2,1)S(1)}, bf16[64,896]{1,0:T(8,128)(2,1)S(1)}, u32[]{:S(2)}, u32[]{:S(2)}) collective-permute-start(bf16[64,896]{1,0:T(8,128)(2,1)S(1)} %collective-permute-done.1.refs_3_), channel_id=1, source_target_pairs={{0,4},{2,6},{4,12},{6,14},{12,8},{14,10},{8,0},{10,2},{1,5},{3,7},... | collective-permute-start | bytes 344072 | tf_op jit(solution)/shard_map/ppermute | solution.py:224
  18.6 6.1 %collective-permute-start.12 = (bf16[64,896]{1,0:T(8,128)(2,1)S(1)}, bf16[64,896]{1,0:T(8,128)(2,1)S(1)}, u32[]{:S(2)}, u32[]{:S(2)}) collective-permute-start(bf16[64,896]{1,0:T(8,128)(2,1)S(1)} %collective-permute-done.6.refs_8_), channel_id=1, source_target_pairs={{0,2},{2,0},{4,6},{6,4},{8,10},{10,8},{12,14},{14,12},{1,3},{3,1},... | collective-permute-start | bytes 344072 | tf_op jit(solution)/shard_map/ppermute | solution.py:224
  19.6 7.6 %collective-permute-start.9 = (bf16[64,896]{1,0:T(8,128)(2,1)S(1)}, bf16[64,896]{1,0:T(8,128)(2,1)S(1)}, u32[]{:S(2)}, u32[]{:S(2)}) collective-permute-start(bf16[64,896]{1,0:T(8,128)(2,1)S(1)} %collective-permute-done.5.refs_6_), channel_id=1, source_target_pairs={{0,2},{2,0},{4,6},{6,4},{8,10},{10,8},{12,14},{14,12},{1,3},{3,1},... | collective-permute-start | bytes 344072 | tf_op jit(solution)/shard_map/ppermute | solution.py:224
  20.6 6.6 %collective-permute-start.8 = (bf16[64,896]{1,0:T(8,128)(2,1)S(1)}, bf16[64,896]{1,0:T(8,128)(2,1)S(1)}, u32[]{:S(2)}, u32[]{:S(2)}) collective-permute-start(bf16[64,896]{1,0:T(8,128)(2,1)S(1)} %collective-permute-done.6.refs_8_), channel_id=1, source_target_pairs={{0,4},{2,6},{4,12},{6,14},{12,8},{14,10},{8,0},{10,2},{1,5},{3,7},... | collective-permute-start | bytes 344072 | tf_op jit(solution)/shard_map/ppermute | solution.py:224
  22.4 6.8 %collective-permute-start.10 = (bf16[64,896]{1,0:T(8,128)(2,1)S(1)}, bf16[64,896]{1,0:T(8,128)(2,1)S(1)}, u32[]{:S(2)}, u32[]{:S(2)}) collective-permute-start(bf16[64,896]{1,0:T(8,128)(2,1)S(1)} %collective-permute-done.1.refs_3_), channel_id=1, source_target_pairs={{0,2},{2,0},{4,6},{6,4},{8,10},{10,8},{12,14},{14,12},{1,3},{3,1},... | collective-permute-start | bytes 344072 | tf_op jit(solution)/shard_map/ppermute | solution.py:224
  23.9 6.0 %collective-permute-start.11 = (bf16[64,896]{1,0:T(8,128)(2,1)S(1)}, bf16[64,896]{1,0:T(8,128)(2,1)S(1)}, u32[]{:S(2)}, u32[]{:S(2)}) collective-permute-start(bf16[64,896]{1,0:T(8,128)(2,1)S(1)} %collective-permute-done.3.refs_0_), channel_id=1, source_target_pairs={{0,2},{2,0},{4,6},{6,4},{8,10},{10,8},{12,14},{14,12},{1,3},{3,1},... | collective-permute-start | bytes 344072 | tf_op jit(solution)/shard_map/ppermute | solution.py:224
  24.7 5.7 %collective-permute-start.13 = (bf16[64,896]{1,0:T(8,128)(2,1)S(1)}, bf16[64,896]{1,0:T(8,128)(2,1)S(1)}, u32[]{:S(2)}, u32[]{:S(2)}) collective-permute-start(bf16[64,896]{1,0:T(8,128)(2,1)S(1)} %collective-permute-done.12.refs_4_), channel_id=1, source_target_pairs={{0,4},{2,6},{4,12},{6,14},{12,8},{14,10},{8,0},{10,2},{1,5},{3,7},... | collective-permute-start | bytes 344072 | tf_op jit(solution)/shard_map/ppermute | solution.py:224
  27.2 0.7 %copy-start.4 = (s32[2,64,1]{1,2,0:T(1,128)S(1)}, s32[2,64,1]{1,2,0:T(1,128)}, u32[]{:S(2)}) copy-start(s32[2,64,1]{1,2,0:T(1,128)} %param.10) | copy-start | bytes 1540
  27.9 0.7 %copy-start.5 = (s32[2,64]{1,0:T(2,128)S(1)}, s32[2,64]{1,0:T(2,128)}, u32[]{:S(2)}) copy-start(s32[2,64]{1,0:T(2,128)} %stored_ref.1) | copy-start | bytes 1540
  30.4 1.5 %copy-start = (bf16[896,1024]{1,0:T(8,128)(2,1)S(1)}, bf16[896,1024]{1,0:T(8,128)(2,1)}, u32[]{:S(2)}) copy-start(bf16[896,1024]{1,0:T(8,128)(2,1)} %wk_ref.3) | copy-start | bytes 5505028
  30.4 1.5 %copy-start.2 = (bf16[128,1024]{1,0:T(8,128)(2,1)S(1)}, bf16[128,1024]{1,0:T(8,128)(2,1)}, u32[]{:S(2)}) copy-start(bf16[128,1024]{1,0:T(8,128)(2,1)} %query_ref.3) | copy-start | bytes 786436
  30.7 2.2 %collective-permute-start.14 = (bf16[128,1792]{1,0:T(8,128)(2,1)S(1)}, bf16[128,1792]{1,0:T(8,128)(2,1)S(1)}, u32[]{:S(2)}, u32[]{:S(2)}) collective-permute-start(bf16[128,1792]{1,0:T(8,128)(2,1)S(1)} %shard_map.66.picked_ref), channel_id=1, source_target_pairs={{0,1},{1,0},{2,3},{3,2},{4,5},{5,4},{6,7},{7,6},{8,9},{9,8},{10,11... | collective-permute-start | bytes 1376264 | tf_op jit(solution)/shard_map/ppermute | solution.py:257

commit v4 on v3

--- a/solution.py
+++ b/solution.py
@@ -236,11 +236,12 @@
     across = [(n, n + 1 if n % SIDE == 0 else n - 1) for n in range(wide_count)]
     streams = [{(0, 0): piece} for piece in half_columns(encodings)]
     for k in range(1, turns):
-        for held in streams:
+        for n, held in enumerate(streams):
             held[k, 0] = send(held[k - 1, 0], onward)
             held[k - 1, 1] = send(held[k - 1, 0], across)
-            if k > 1:
-                held[k, 0], held[k - 2, 1] = lax.optimization_barrier((held[k, 0], held[k - 2, 1]))
+            before, place = streams[n - 1], (k - 1 if n else k - 2, 1)
+            if place in before:
+                held[k, 0], before[place] = lax.optimization_barrier((held[k, 0], before[place]))
     for n, held in enumerate(streams):
         held[turns - 1, 1] = send(held[turns - 1, 0], across) if n % 2 == 0 else send(held[turns - 2, 1], onward)
     late = [(turns - 1, 0), (turns - 2, 1), (turns - 1, 1)]

time: 35.7 us -> 35.6 us (level)
  starting transfers between devices: 22.3 us -> 19.9 us
  waiting for transfers between devices: 4.98 us -> 7.26 us
    ppermute x14, starting transfers between devices: 22.2 us -> 19.8 us  [send(): return lax.ppermute(chunk, 'wide', pairs)]
    ppermute x14, waiting for transfers between devices: 4.98 us -> 7.26 us  [send(): return lax.ppermute(chunk, 'wide', pairs)]
  transfers between devices with their start and end apart: 15 -> 15, of which waited for: 8 -> 9; matrix products, arithmetic and copies ran while one was open for 0% -> 0% of each run, Pallas kernels for 7% -> 7%
where the time goes in v4:
time: 35.6 us; the launch traced here: 35.4 us
  starting transfers between devices  19.9 us (56%)
  waiting for transfers between devices  7.26 us (20%)
  Pallas kernels  5.3 us (15%)
  local copies, waits for them, and re-layouts  2.85 us (8%)
    ppermute x14, starting transfers between devices, send(): return lax.ppermute(chunk, 'wide', pairs)  19.8 us
    ppermute x14, waiting for transfers between devices, send(): return lax.ppermute(chunk, 'wide', pairs)  7.26 us
    unnamed x12, local copies, waits for them, and re-layouts  2.85 us
    pallas_call x1, Pallas kernels, attend(): pl.pallas_call(functools.partial(attend_kernel, spans), out_shape=jax.Sha...  2.57 us
    pallas_call x1, Pallas kernels, own_scores(): pl.pallas_call(functools.partial(score_kernel, spans), out_shape=jax.Shap...  1.02 us
  transfers between devices with their start and end apart: 15, of which 9 were waited for; matrix products, arithmetic and copies ran while one was open for 0% of the time, Pallas kernels for 7%

profile of v4, /device:TPU:0, one launch (start us, length us, event | category | flops | bytes accessed | tf_op | source)
XLA Modules:
  0.0 35.4 jit_solution(4419538978727091127)
XLA Ops:
  0.0 1.2 %copy-done.3 = bf16[64,3584]{1,0:T(8,128)(2,1)S(1)} copy-done((bf16[64,3584]{1,0:T(8,128)(2,1)S(1)}, bf16[64,3584]{1,0:T(8,128)(2,1)}, u32[]{:S(2)}) %copy-start.3) | copy-done | bytes 458776
  1.2 3.1 %collective-permute-start = (bf16[64,896]{1,0:T(8,128)(2,1)S(1)}, bf16[64,896]{1,0:T(8,128)(2,1)S(1)}, u32[]{:S(2)}, u32[]{:S(2)}) collective-permute-start(bf16[64,896]{1,0:T(8,128)(2,1)S(1)} %get-tuple-element.19.refs_0_), channel_id=1, source_target_pairs={{0,4},{2,6},{4,12},{6,14},{12,8},{14,10},{8,0},{10,2},{1,5},{3,7},... | collective-permute-start | bytes 344072 | tf_op jit(solution)/shard_map/ppermute | solution.py:224
  4.3 2.6 %collective-permute-start.1 = (bf16[64,896]{1,0:T(8,128)(2,1)S(1)}, bf16[64,896]{1,0:T(8,128)(2,1)S(1)}, u32[]{:S(2)}, u32[]{:S(2)}) collective-permute-start(bf16[64,896]{1,0:T(8,128)(2,1)S(1)} %get-tuple-element.20.refs_5_), channel_id=1, source_target_pairs={{0,4},{2,6},{4,12},{6,14},{12,8},{14,10},{8,0},{10,2},{1,5},{3,7},... | collective-permute-start | bytes 344072 | tf_op jit(solution)/shard_map/ppermute | solution.py:224
  6.9 1.5 %collective-permute-start.2 = (bf16[64,896]{1,0:T(8,128)(2,1)S(1)}, bf16[64,896]{1,0:T(8,128)(2,1)S(1)}, u32[]{:S(2)}, u32[]{:S(2)}) collective-permute-start(bf16[64,896]{1,0:T(8,128)(2,1)S(1)} %get-tuple-element.19.refs_0_), channel_id=1, source_target_pairs={{0,2},{2,0},{4,6},{6,4},{8,10},{10,8},{12,14},{14,12},{1,3},{3,1},... | collective-permute-start | bytes 344072 | tf_op jit(solution)/shard_map/ppermute | solution.py:224
  9.3 1.2 %collective-permute-start.3 = (bf16[64,896]{1,0:T(8,128)(2,1)S(1)}, bf16[64,896]{1,0:T(8,128)(2,1)S(1)}, u32[]{:S(2)}, u32[]{:S(2)}) collective-permute-start(bf16[64,896]{1,0:T(8,128)(2,1)S(1)} %collective-permute-done.refs_1_), channel_id=1, source_target_pairs={{0,4},{2,6},{4,12},{6,14},{12,8},{14,10},{8,0},{10,2},{1,5},{3,7},... | collective-permute-start | bytes 344072 | tf_op jit(solution)/shard_map/ppermute | solution.py:224
  10.9 1.5 %collective-permute-done.2.refs_2_ = bf16[64,896]{1,0:T(8,128)(2,1)S(1)} collective-permute-done((bf16[64,896]{1,0:T(8,128)(2,1)S(1)}, bf16[64,896]{1,0:T(8,128)(2,1)S(1)}, u32[]{:S(2)}, u32[]{:S(2)}) %collective-permute-start.2) | collective-permute-done | bytes 114720 | tf_op jit(solution)/shard_map/ppermute | solution.py:224
  12.4 1.4 %collective-permute-start.5 = (bf16[64,896]{1,0:T(8,128)(2,1)S(1)}, bf16[64,896]{1,0:T(8,128)(2,1)S(1)}, u32[]{:S(2)}, u32[]{:S(2)}) collective-permute-start(bf16[64,896]{1,0:T(8,128)(2,1)S(1)} %collective-permute-done.1.refs_6_), channel_id=1, source_target_pairs={{0,4},{2,6},{4,12},{6,14},{12,8},{14,10},{8,0},{10,2},{1,5},{3,7},... | collective-permute-start | bytes 344072 | tf_op jit(solution)/shard_map/ppermute | solution.py:224
  13.8 1.5 %collective-permute-start.6 = (bf16[64,896]{1,0:T(8,128)(2,1)S(1)}, bf16[64,896]{1,0:T(8,128)(2,1)S(1)}, u32[]{:S(2)}, u32[]{:S(2)}) collective-permute-start(bf16[64,896]{1,0:T(8,128)(2,1)S(1)} %collective-permute-done.refs_1_), channel_id=1, source_target_pairs={{0,2},{2,0},{4,6},{6,4},{8,10},{10,8},{12,14},{14,12},{1,3},{3,1},... | collective-permute-start | bytes 344072 | tf_op jit(solution)/shard_map/ppermute | solution.py:224
  16.2 1.0 %collective-permute-start.7 = (bf16[64,896]{1,0:T(8,128)(2,1)S(1)}, bf16[64,896]{1,0:T(8,128)(2,1)S(1)}, u32[]{:S(2)}, u32[]{:S(2)}) collective-permute-start(bf16[64,896]{1,0:T(8,128)(2,1)S(1)} %collective-permute-done.3.refs_3_), channel_id=1, source_target_pairs={{0,4},{2,6},{4,12},{6,14},{12,8},{14,10},{8,0},{10,2},{1,5},{3,7},... | collective-permute-start | bytes 344072 | tf_op jit(solution)/shard_map/ppermute | solution.py:224
  17.2 1.4 %collective-permute-done.5.refs_8_ = bf16[64,896]{1,0:T(8,128)(2,1)S(1)} collective-permute-done((bf16[64,896]{1,0:T(8,128)(2,1)S(1)}, bf16[64,896]{1,0:T(8,128)(2,1)S(1)}, u32[]{:S(2)}, u32[]{:S(2)}) %collective-permute-start.5) | collective-permute-done | bytes 114720 | tf_op jit(solution)/shard_map/ppermute | solution.py:224
  18.6 1.8 %collective-permute-start.12 = (bf16[64,896]{1,0:T(8,128)(2,1)S(1)}, bf16[64,896]{1,0:T(8,128)(2,1)S(1)}, u32[]{:S(2)}, u32[]{:S(2)}) collective-permute-start(bf16[64,896]{1,0:T(8,128)(2,1)S(1)} %collective-permute-done.5.refs_8_), channel_id=1, source_target_pairs={{0,2},{2,0},{4,6},{6,4},{8,10},{10,8},{12,14},{14,12},{1,3},{3,1},... | collective-permute-start | bytes 344072 | tf_op jit(solution)/shard_map/ppermute | solution.py:224
  20.4 1.4 %collective-permute-start.9 = (bf16[64,896]{1,0:T(8,128)(2,1)S(1)}, bf16[64,896]{1,0:T(8,128)(2,1)S(1)}, u32[]{:S(2)}, u32[]{:S(2)}) collective-permute-start(bf16[64,896]{1,0:T(8,128)(2,1)S(1)} %collective-permute-done.5.refs_8_), channel_id=1, source_target_pairs={{0,4},{2,6},{4,12},{6,14},{12,8},{14,10},{8,0},{10,2},{1,5},{3,7},... | collective-permute-start | bytes 344072 | tf_op jit(solution)/shard_map/ppermute | solution.py:224
  21.9 0.5 %collective-permute-start.10 = (bf16[64,896]{1,0:T(8,128)(2,1)S(1)}, bf16[64,896]{1,0:T(8,128)(2,1)S(1)}, u32[]{:S(2)}, u32[]{:S(2)}) collective-permute-start(bf16[64,896]{1,0:T(8,128)(2,1)S(1)} %collective-permute-done.3.refs_3_), channel_id=1, source_target_pairs={{0,2},{2,0},{4,6},{6,4},{8,10},{10,8},{12,14},{14,12},{1,3},{3,1},... | collective-permute-start | bytes 344072 | tf_op jit(solution)/shard_map/ppermute | solution.py:224
  22.9 1.0 %collective-permute-start.11 = (bf16[64,896]{1,0:T(8,128)(2,1)S(1)}, bf16[64,896]{1,0:T(8,128)(2,1)S(1)}, u32[]{:S(2)}, u32[]{:S(2)}) collective-permute-start(bf16[64,896]{1,0:T(8,128)(2,1)S(1)} %collective-permute-done.7.refs_0_), channel_id=1, source_target_pairs={{0,2},{2,0},{4,6},{6,4},{8,10},{10,8},{12,14},{14,12},{1,3},{3,1},... | collective-permute-start | bytes 344072 | tf_op jit(solution)/shard_map/ppermute | solution.py:224
  23.9 0.7 %collective-permute-done.12.refs_4_ = bf16[64,896]{1,0:T(8,128)(2,1)S(1)} collective-permute-done((bf16[64,896]{1,0:T(8,128)(2,1)S(1)}, bf16[64,896]{1,0:T(8,128)(2,1)S(1)}, u32[]{:S(2)}, u32[]{:S(2)}) %collective-permute-start.12) | collective-permute-done | bytes 114720 | tf_op jit(solution)/shard_map/ppermute | solution.py:224
  24.6 1.8 %collective-permute-start.13 = (bf16[64,896]{1,0:T(8,128)(2,1)S(1)}, bf16[64,896]{1,0:T(8,128)(2,1)S(1)}, u32[]{:S(2)}, u32[]{:S(2)}) collective-permute-start(bf16[64,896]{1,0:T(8,128)(2,1)S(1)} %collective-permute-done.12.refs_4_), channel_id=1, source_target_pairs={{0,4},{2,6},{4,12},{6,14},{12,8},{14,10},{8,0},{10,2},{1,5},{3,7},... | collective-permute-start | bytes 344072 | tf_op jit(solution)/shard_map/ppermute | solution.py:224
  26.4 0.9 %collective-permute-done.9.refs_3_ = bf16[64,896]{1,0:T(8,128)(2,1)S(1)} collective-permute-done((bf16[64,896]{1,0:T(8,128)(2,1)S(1)}, bf16[64,896]{1,0:T(8,128)(2,1)S(1)}, u32[]{:S(2)}, u32[]{:S(2)}) %collective-permute-start.9) | collective-permute-done | bytes 114720 | tf_op jit(solution)/shard_map/ppermute | solution.py:224
  27.3 0.7 %copy-done.4 = s32[2,64,1]{1,2,0:T(1,128)S(1)} copy-done((s32[2,64,1]{1,2,0:T(1,128)S(1)}, s32[2,64,1]{1,2,0:T(1,128)}, u32[]{:S(2)}) %copy-start.4) | copy-done | bytes 536
  27.9 0.7 %copy-done.5 = s32[2,64]{1,0:T(2,128)S(1)} copy-done((s32[2,64]{1,0:T(2,128)S(1)}, s32[2,64]{1,0:T(2,128)}, u32[]{:S(2)}) %copy-start.5) | copy-done | bytes 536
  28.6 0.6 %shard_map.65 = (s32[128,1]{1,0:T(8,128)S(1)}, bf16[128,1792]{1,0:T(8,128)(2,1)S(1)}) custom-call(s32[2,1,64]{2,1,0:T(1,128)S(1)} %bitcast.3, s32[2,64]{1,0:T(2,128)S(1)} %copy-done.5, bf16[64,896]{1,0:T(8,128)(2,1)S(1)} %get-tuple-element.19.refs_0_, bf16[64,896]{1,0:T(8,128)(2,1)S(1)} %collective-permute-done.refs_1_, ...), custom_call_target="tpu_custom_call" | custom-call | flops 146800640 | bytes 458752 | tf_op jit(solution)/shard_map/pallas_call | solution.py:99
  29.2 1.1 %collective-permute-done.13.refs_5_ = bf16[64,896]{1,0:T(8,128)(2,1)S(1)} collective-permute-done((bf16[64,896]{1,0:T(8,128)(2,1)S(1)}, bf16[64,896]{1,0:T(8,128)(2,1)S(1)}, u32[]{:S(2)}, u32[]{:S(2)}) %collective-permute-start.13) | collective-permute-done | bytes 114720 | tf_op jit(solution)/shard_map/ppermute | solution.py:224
  30.8 0.7 %shard_map.68.values_ref = bf16[256,1024]{1,0:T(8,128)(2,1)S(1)} custom-call(bf16[128,1792]{1,0:T(8,128)(2,1)S(1)} %shard_map.66.picked_ref, bf16[896,1024]{1,0:T(8,128)(2,1)S(1)} %copy-done.1), custom_call_target="tpu_custom_call" | custom-call | tf_op jit(solution)/shard_map/pallas_call | solution.py:183
  31.8 1.0 %shard_map.67.first_ref = f32[16,64,128]{2,1,0:T(8,128)S(1)} custom-call(bf16[128,1792]{1,0:T(8,128)(2,1)S(1)} %shard_map.66.picked_ref, bf16[896,1024]{1,0:T(8,128)(2,1)S(1)} %copy-done, bf16[128,1024]{1,0:T(8,128)(2,1)S(1)} %copy-done.2), custom_call_target="tpu_custom_call" | custom-call | tf_op jit(solution)/shard_map/pallas_call | solution.py:167
  32.8 2.6 %shard_map.69 = bf16[128,1024]{1,0:T(8,128)(2,1)} custom-call(bf16[128,1792]{1,0:T(8,128)(2,1)S(1)} %collective-permute-done.14.other_ref, bf16[896,1024]{1,0:T(8,128)(2,1)S(1)} %copy-done, bf16[896,1024]{1,0:T(8,128)(2,1)S(1)} %copy-done.1, bf16[128,1024]{1,0:T(8,128)(2,1)S(1)} %copy-done.2, f32[16,64,128]{2,1,0:T(8,128)S(1)} %shard_map.67.first_ref, ...), custom_call_target="tpu_custom_call" | custom-call | tf_op jit(solution)/shard_map/pallas_call | solution.py:213
  (24 shorter events, 3.6 us)
Async XLA Ops:
  0.0 30.8 %copy-start.1 = (bf16[896,1024]{1,0:T(8,128)(2,1)S(1)}, bf16[896,1024]{1,0:T(8,128)(2,1)}, u32[]{:S(2)}) copy-start(bf16[896,1024]{1,0:T(8,128)(2,1)} %wv_ref.3) | copy-start | bytes 5505028
  0.0 1.2 %copy-start.3 = (bf16[64,3584]{1,0:T(8,128)(2,1)S(1)}, bf16[64,3584]{1,0:T(8,128)(2,1)}, u32[]{:S(2)}) copy-start(bf16[64,3584]{1,0:T(8,128)(2,1)} %enc_ref.1) | copy-start | bytes 1376260
  1.2 8.1 %collective-permute-start = (bf16[64,896]{1,0:T(8,128)(2,1)S(1)}, bf16[64,896]{1,0:T(8,128)(2,1)S(1)}, u32[]{:S(2)}, u32[]{:S(2)}) collective-permute-start(bf16[64,896]{1,0:T(8,128)(2,1)S(1)} %get-tuple-element.19.refs_0_), channel_id=1, source_target_pairs={{0,4},{2,6},{4,12},{6,14},{12,8},{14,10},{8,0},{10,2},{1,5},{3,7},... | collective-permute-start | bytes 344072 | tf_op jit(solution)/shard_map/ppermute | solution.py:224
  4.3 6.6 %collective-permute-start.1 = (bf16[64,896]{1,0:T(8,128)(2,1)S(1)}, bf16[64,896]{1,0:T(8,128)(2,1)S(1)}, u32[]{:S(2)}, u32[]{:S(2)}) collective-permute-start(bf16[64,896]{1,0:T(8,128)(2,1)S(1)} %get-tuple-element.20.refs_5_), channel_id=1, source_target_pairs={{0,4},{2,6},{4,12},{6,14},{12,8},{14,10},{8,0},{10,2},{1,5},{3,7},... | collective-permute-start | bytes 344072 | tf_op jit(solution)/shard_map/ppermute | solution.py:224
  6.9 5.6 %collective-permute-start.2 = (bf16[64,896]{1,0:T(8,128)(2,1)S(1)}, bf16[64,896]{1,0:T(8,128)(2,1)S(1)}, u32[]{:S(2)}, u32[]{:S(2)}) collective-permute-start(bf16[64,896]{1,0:T(8,128)(2,1)S(1)} %get-tuple-element.19.refs_0_), channel_id=1, source_target_pairs={{0,2},{2,0},{4,6},{6,4},{8,10},{10,8},{12,14},{14,12},{1,3},{3,1},... | collective-permute-start | bytes 344072 | tf_op jit(solution)/shard_map/ppermute | solution.py:224
  8.4 7.5 %collective-permute-start.4 = (bf16[64,896]{1,0:T(8,128)(2,1)S(1)}, bf16[64,896]{1,0:T(8,128)(2,1)S(1)}, u32[]{:S(2)}, u32[]{:S(2)}) collective-permute-start(bf16[64,896]{1,0:T(8,128)(2,1)S(1)} %get-tuple-element.20.refs_5_), channel_id=1, source_target_pairs={{0,2},{2,0},{4,6},{6,4},{8,10},{10,8},{12,14},{14,12},{1,3},{3,1},... | collective-permute-start | bytes 344072 | tf_op jit(solution)/shard_map/ppermute | solution.py:224
  9.3 6.9 %collective-permute-start.3 = (bf16[64,896]{1,0:T(8,128)(2,1)S(1)}, bf16[64,896]{1,0:T(8,128)(2,1)S(1)}, u32[]{:S(2)}, u32[]{:S(2)}) collective-permute-start(bf16[64,896]{1,0:T(8,128)(2,1)S(1)} %collective-permute-done.refs_1_), channel_id=1, source_target_pairs={{0,4},{2,6},{4,12},{6,14},{12,8},{14,10},{8,0},{10,2},{1,5},{3,7},... | collective-permute-start | bytes 344072 | tf_op jit(solution)/shard_map/ppermute | solution.py:224
  12.4 6.2 %collective-permute-start.5 = (bf16[64,896]{1,0:T(8,128)(2,1)S(1)}, bf16[64,896]{1,0:T(8,128)(2,1)S(1)}, u32[]{:S(2)}, u32[]{:S(2)}) collective-permute-start(bf16[64,896]{1,0:T(8,128)(2,1)S(1)} %collective-permute-done.1.refs_6_), channel_id=1, source_target_pairs={{0,4},{2,6},{4,12},{6,14},{12,8},{14,10},{8,0},{10,2},{1,5},{3,7},... | collective-permute-start | bytes 344072 | tf_op jit(solution)/shard_map/ppermute | solution.py:224
  13.8 4.8 %collective-permute-start.6 = (bf16[64,896]{1,0:T(8,128)(2,1)S(1)}, bf16[64,896]{1,0:T(8,128)(2,1)S(1)}, u32[]{:S(2)}, u32[]{:S(2)}) collective-permute-start(bf16[64,896]{1,0:T(8,128)(2,1)S(1)} %collective-permute-done.refs_1_), channel_id=1, source_target_pairs={{0,2},{2,0},{4,6},{6,4},{8,10},{10,8},{12,14},{14,12},{1,3},{3,1},... | collective-permute-start | bytes 344072 | tf_op jit(solution)/shard_map/ppermute | solution.py:224
  15.3 7.1 %collective-permute-start.8 = (bf16[64,896]{1,0:T(8,128)(2,1)S(1)}, bf16[64,896]{1,0:T(8,128)(2,1)S(1)}, u32[]{:S(2)}, u32[]{:S(2)}) collective-permute-start(bf16[64,896]{1,0:T(8,128)(2,1)S(1)} %collective-permute-done.1.refs_6_), channel_id=1, source_target_pairs={{0,2},{2,0},{4,6},{6,4},{8,10},{10,8},{12,14},{14,12},{1,3},{3,1},... | collective-permute-start | bytes 344072 | tf_op jit(solution)/shard_map/ppermute | solution.py:224
  16.2 6.7 %collective-permute-start.7 = (bf16[64,896]{1,0:T(8,128)(2,1)S(1)}, bf16[64,896]{1,0:T(8,128)(2,1)S(1)}, u32[]{:S(2)}, u32[]{:S(2)}) collective-permute-start(bf16[64,896]{1,0:T(8,128)(2,1)S(1)} %collective-permute-done.3.refs_3_), channel_id=1, source_target_pairs={{0,4},{2,6},{4,12},{6,14},{12,8},{14,10},{8,0},{10,2},{1,5},{3,7},... | collective-permute-start | bytes 344072 | tf_op jit(solution)/shard_map/ppermute | solution.py:224
  18.6 6.0 %collective-permute-start.12 = (bf16[64,896]{1,0:T(8,128)(2,1)S(1)}, bf16[64,896]{1,0:T(8,128)(2,1)S(1)}, u32[]{:S(2)}, u32[]{:S(2)}) collective-permute-start(bf16[64,896]{1,0:T(8,128)(2,1)S(1)} %collective-permute-done.5.refs_8_), channel_id=1, source_target_pairs={{0,2},{2,0},{4,6},{6,4},{8,10},{10,8},{12,14},{14,12},{1,3},{3,1},... | collective-permute-start | bytes 344072 | tf_op jit(solution)/shard_map/ppermute | solution.py:224
  20.4 6.8 %collective-permute-start.9 = (bf16[64,896]{1,0:T(8,128)(2,1)S(1)}, bf16[64,896]{1,0:T(8,128)(2,1)S(1)}, u32[]{:S(2)}, u32[]{:S(2)}) collective-permute-start(bf16[64,896]{1,0:T(8,128)(2,1)S(1)} %collective-permute-done.5.refs_8_), channel_id=1, source_target_pairs={{0,4},{2,6},{4,12},{6,14},{12,8},{14,10},{8,0},{10,2},{1,5},{3,7},... | collective-permute-start | bytes 344072 | tf_op jit(solution)/shard_map/ppermute | solution.py:224
  21.9 5.4 %collective-permute-start.10 = (bf16[64,896]{1,0:T(8,128)(2,1)S(1)}, bf16[64,896]{1,0:T(8,128)(2,1)S(1)}, u32[]{:S(2)}, u32[]{:S(2)}) collective-permute-start(bf16[64,896]{1,0:T(8,128)(2,1)S(1)} %collective-permute-done.3.refs_3_), channel_id=1, source_target_pairs={{0,2},{2,0},{4,6},{6,4},{8,10},{10,8},{12,14},{14,12},{1,3},{3,1},... | collective-permute-start | bytes 344072 | tf_op jit(solution)/shard_map/ppermute | solution.py:224
  22.9 6.4 %collective-permute-start.11 = (bf16[64,896]{1,0:T(8,128)(2,1)S(1)}, bf16[64,896]{1,0:T(8,128)(2,1)S(1)}, u32[]{:S(2)}, u32[]{:S(2)}) collective-permute-start(bf16[64,896]{1,0:T(8,128)(2,1)S(1)} %collective-permute-done.7.refs_0_), channel_id=1, source_target_pairs={{0,2},{2,0},{4,6},{6,4},{8,10},{10,8},{12,14},{14,12},{1,3},{3,1},... | collective-permute-start | bytes 344072 | tf_op jit(solution)/shard_map/ppermute | solution.py:224
  24.6 5.7 %collective-permute-start.13 = (bf16[64,896]{1,0:T(8,128)(2,1)S(1)}, bf16[64,896]{1,0:T(8,128)(2,1)S(1)}, u32[]{:S(2)}, u32[]{:S(2)}) collective-permute-start(bf16[64,896]{1,0:T(8,128)(2,1)S(1)} %collective-permute-done.12.refs_4_), channel_id=1, source_target_pairs={{0,4},{2,6},{4,12},{6,14},{12,8},{14,10},{8,0},{10,2},{1,5},{3,7},... | collective-permute-start | bytes 344072 | tf_op jit(solution)/shard_map/ppermute | solution.py:224
  27.2 0.7 %copy-start.4 = (s32[2,64,1]{1,2,0:T(1,128)S(1)}, s32[2,64,1]{1,2,0:T(1,128)}, u32[]{:S(2)}) copy-start(s32[2,64,1]{1,2,0:T(1,128)} %param.10) | copy-start | bytes 1540
  27.9 0.7 %copy-start.5 = (s32[2,64]{1,0:T(2,128)S(1)}, s32[2,64]{1,0:T(2,128)}, u32[]{:S(2)}) copy-start(s32[2,64]{1,0:T(2,128)} %stored_ref.1) | copy-start | bytes 1540
  30.3 1.5 %copy-start = (bf16[896,1024]{1,0:T(8,128)(2,1)S(1)}, bf16[896,1024]{1,0:T(8,128)(2,1)}, u32[]{:S(2)}) copy-start(bf16[896,1024]{1,0:T(8,128)(2,1)} %wk_ref.3) | copy-start | bytes 5505028
  30.3 1.5 %copy-start.2 = (bf16[128,1024]{1,0:T(8,128)(2,1)S(1)}, bf16[128,1024]{1,0:T(8,128)(2,1)}, u32[]{:S(2)}) copy-start(bf16[128,1024]{1,0:T(8,128)(2,1)} %query_ref.3) | copy-start | bytes 786436
  30.7 2.2 %collective-permute-start.14 = (bf16[128,1792]{1,0:T(8,128)(2,1)S(1)}, bf16[128,1792]{1,0:T(8,128)(2,1)S(1)}, u32[]{:S(2)}, u32[]{:S(2)}) collective-permute-start(bf16[128,1792]{1,0:T(8,128)(2,1)S(1)} %shard_map.66.picked_ref), channel_id=1, source_target_pairs={{0,1},{1,0},{2,3},{3,2},{4,5},{5,4},{6,7},{7,6},{8,9},{9,8},{10,11... | collective-permute-start | bytes 1376264 | tf_op jit(solution)/shard_map/ppermute | solution.py:258

commit v5 on v3

--- a/solution.py
+++ b/solution.py
@@ -22,12 +22,12 @@
 
 def half_kernel(enc_ref, *refs):
     outs, sems = refs[:-1], refs[-1]
-    width = outs[0].shape[1]
-    start = lax.axis_index("heads") * len(outs) * width
-    copies = [
-        pltpu.make_async_copy(enc_ref.at[:, pl.ds(pl.multiple_of(start + n * width, 128), width)], out, sems.at[n])
-        for n, out in enumerate(outs)
-    ]
+    first = lax.axis_index("heads") * outs[-1].shape[1]
+    copies = []
+    for n, out in enumerate(outs):
+        width = out.shape[1]
+        start = first + (n * width if n < STREAMS else 0)
+        copies.append(pltpu.make_async_copy(enc_ref.at[:, pl.ds(pl.multiple_of(start, 128), width)], out, sems.at[n]))
     for copy in copies:
         copy.start()
     for copy in copies:
@@ -36,26 +36,31 @@
 
 def half_columns(encodings):
     rows, columns = encodings.shape
-    width = columns // lax.axis_size("heads") // STREAMS
+    whole = columns // lax.axis_size("heads")
+    widths = [whole // STREAMS] * STREAMS + [whole]
     return pl.pallas_call(
         half_kernel,
-        out_shape=[jax.ShapeDtypeStruct((rows, width), encodings.dtype)] * STREAMS,
+        out_shape=[jax.ShapeDtypeStruct((rows, width), encodings.dtype) for width in widths],
         in_specs=[VMEM],
-        out_specs=[VMEM] * STREAMS,
-        scratch_shapes=[pltpu.SemaphoreType.DMA((STREAMS,))],
+        out_specs=[VMEM] * len(widths),
+        scratch_shapes=[pltpu.SemaphoreType.DMA((len(widths),))],
         compiler_params=params(),
     )(encodings)
 
 
-def chosen_rows(index, sources, first):
-    chunks = len(sources) // STREAMS
-    rows = sources[0].shape[0]
-    places = lax.broadcasted_iota(jnp.int32, (index.shape[0], chunks * rows), 1) + first
-    chosen = jnp.where(places == index, 1.0, 0.0).astype(sources[0].dtype)
+def chosen_rows(index, chunks, refs, first):
+    rows = refs[0].shape[0]
+    width = min(ref.shape[1] for ref in refs)
+    places = lax.broadcasted_iota(jnp.int32, (index.shape[0], len(chunks) * rows), 1) + first
+    chosen = jnp.where(places == index, 1.0, 0.0).astype(refs[0].dtype)
+    starts = [sum(chunks[:n]) for n in range(len(chunks))]
     parts = []
     for n in range(STREAMS):
-        held = jnp.concatenate([ref[...] for ref in sources[n * chunks : (n + 1) * chunks]], axis=0)
-        parts.append(jnp.dot(chosen, held, preferred_element_type=jnp.float32))
+        held = [
+            refs[at + n][...] if arrays > 1 else refs[at][:, n * width : (n + 1) * width]
+            for at, arrays in zip(starts, chunks)
+        ]
+        parts.append(jnp.dot(chosen, jnp.concatenate(held, axis=0), preferred_element_type=jnp.float32))
     return jnp.concatenate(parts, axis=1)
 
 
@@ -86,47 +91,47 @@
     return jnp.concatenate(columns, axis=0).astype(jnp.int32)
 
 
-def early_kernel(order, turns, owner_ref, stored_ref, *refs):
+def early_kernel(order, turns, chunks, owner_ref, stored_ref, *refs):
     sources, index_ref, out_ref = refs[:-2], refs[-2], refs[-1]
     index_ref[...] = wanted_rows(order, turns, sources[0].shape[0], owner_ref, stored_ref)
-    out_ref[...] = chosen_rows(index_ref[...], sources, 0).astype(out_ref.dtype)
-
-
-def early(order, turns, owners, stored, streams):
-    sources = [chunk for stream in streams for chunk in stream]
-    rows, width = sources[0].shape
+    out_ref[...] = chosen_rows(index_ref[...], chunks, sources, 0).astype(out_ref.dtype)
+
+
+def early(order, turns, owners, stored, sources, width):
+    rows = sources[0][0].shape[0]
     requests = stored.size
-    return pl.pallas_call(
-        functools.partial(early_kernel, order, turns),
+    arrays = [array for chunk in sources for array in chunk]
+    return pl.pallas_call(
+        functools.partial(early_kernel, order, turns, [len(chunk) for chunk in sources]),
         out_shape=(
             jax.ShapeDtypeStruct((requests, 1), jnp.int32),
-            jax.ShapeDtypeStruct((requests, STREAMS * width), sources[0].dtype),
+            jax.ShapeDtypeStruct((requests, width), arrays[0].dtype),
         ),
-        in_specs=[VMEM] * (2 + len(sources)),
+        in_specs=[VMEM] * (2 + len(arrays)),
         out_specs=(VMEM, VMEM),
         compiler_params=params(),
         cost_estimate=pl.CostEstimate(
             flops=2 * requests * width * rows * len(sources),
-            bytes_accessed=2 * requests * width * STREAMS,
+            bytes_accessed=2 * requests * width,
             transcendentals=0,
         ),
-    )(owners, stored, *sources)
-
-
-def pick_kernel(first, index_ref, begun_ref, *refs):
-    picked = chosen_rows(index_ref[...], refs[:-1], first)
+    )(owners, stored, *arrays)
+
+
+def pick_kernel(chunks, first, index_ref, begun_ref, *refs):
+    picked = chosen_rows(index_ref[...], chunks, refs[:-1], first)
     refs[-1][...] = (picked + begun_ref[...].astype(jnp.float32)).astype(begun_ref.dtype)
 
 
-def pick(index, begun, streams, first):
-    sources = [chunk for stream in streams for chunk in stream]
-    return pl.pallas_call(
-        functools.partial(pick_kernel, first),
+def pick(index, begun, sources, first):
+    arrays = [array for chunk in sources for array in chunk]
+    return pl.pallas_call(
+        functools.partial(pick_kernel, [len(chunk) for chunk in sources], first),
         out_shape=jax.ShapeDtypeStruct(begun.shape, begun.dtype),
-        in_specs=[VMEM] * (2 + len(sources)),
+        in_specs=[VMEM] * (2 + len(arrays)),
         out_specs=VMEM,
         compiler_params=params(),
-    )(index, begun, *sources)
+    )(index, begun, *arrays)
 
 
 def by_span(picked, spans, channels):
@@ -190,22 +195,28 @@
 
 
 def attend_kernel(
-    spans, other_ref, wk_ref, wv_ref, query_ref, first_ref, values_ref, out_ref, second_ref, probs_ref
+    spans, other_ref, wk_ref, wv_ref, query_ref, first_ref, values_ref, out_ref, second_ref
 ):
     other = by_span(other_ref[...], spans, wk_ref.shape[0])
+    per = other.shape[0] // spans
+    columns = wk_ref.shape[1]
+    heads = columns // HD
+    group = 2 if heads % 2 == 0 else 1
     score(spans, other, wk_ref, query_ref, second_ref)
-    per = other.shape[0] // spans
-    more = jnp.dot(other, wv_ref[...], preferred_element_type=jnp.float32).astype(jnp.bfloat16)
-    places = head_places(spans, more.shape[1])
-    for c, lanes, n in places:
-        scores = jnp.concatenate([first_ref[n], second_ref[n]], axis=1)
-        raised = jnp.exp2((scores - jnp.max(scores, axis=-1, keepdims=True)) * EXPONENT)
-        probs_ref[n] = (raised * (1.0 / jnp.sum(raised, axis=-1, keepdims=True))).astype(jnp.bfloat16)
-    for c, lanes, n in places:
-        rows = slice(c * per, (c + 1) * per)
-        values = jnp.concatenate([values_ref[rows, lanes], more[rows, lanes]], axis=0)
-        mixed = jnp.dot(probs_ref[n], values, preferred_element_type=jnp.float32)
-        out_ref[c * SPAN : (c + 1) * SPAN, lanes] = mixed.astype(out_ref.dtype)
+    for at in range(0, heads, group):
+        lanes = slice(at * HD, (at + group) * HD)
+        more = jnp.dot(other, wv_ref[:, lanes], preferred_element_type=jnp.float32).astype(jnp.bfloat16)
+        for c in range(spans):
+            rows = slice(c * per, (c + 1) * per)
+            for h in range(group):
+                n = c * heads + at + h
+                scores = jnp.concatenate([first_ref[n], second_ref[n]], axis=1)
+                raised = jnp.exp2((scores - jnp.max(scores, axis=-1, keepdims=True)) * EXPONENT)
+                probs = (raised * (1.0 / jnp.sum(raised, axis=-1, keepdims=True))).astype(jnp.bfloat16)
+                head = slice((at + h) * HD, (at + h + 1) * HD)
+                values = jnp.concatenate([values_ref[rows, head], more[rows, h * HD : (h + 1) * HD]], axis=0)
+                mixed = jnp.dot(probs, values, preferred_element_type=jnp.float32)
+                out_ref[c * SPAN : (c + 1) * SPAN, head] = mixed.astype(out_ref.dtype)
 
 
 def attend(other, w_key, w_value, queries, first, values, spans):
@@ -215,7 +226,7 @@
         out_shape=jax.ShapeDtypeStruct(queries.shape, queries.dtype),
         in_specs=[VMEM] * 6,
         out_specs=VMEM,
-        scratch_shapes=[pltpu.VMEM(each, jnp.float32), pltpu.VMEM(each[:2] + (2 * each[2],), jnp.bfloat16)],
+        scratch_shapes=[pltpu.VMEM(each, jnp.float32)],
         compiler_params=params(),
     )(other, w_key, w_value, queries, first, values)
 
@@ -234,26 +245,29 @@
         (here * SIDE + x, there * SIDE + x) for here, there in zip(line, line[1:] + line[:1]) for x in range(SIDE)
     ]
     across = [(n, n + 1 if n % SIDE == 0 else n - 1) for n in range(wide_count)]
-    streams = [{(0, 0): piece} for piece in half_columns(encodings)]
+    *pieces, whole = half_columns(encodings)
+    held = {(0, 0): pieces}
     for k in range(1, turns):
-        for held in streams:
-            held[k, 0] = send(held[k - 1, 0], onward)
-            held[k - 1, 1] = send(held[k - 1, 0], across)
-            if k > 1:
-                held[k, 0], held[k - 2, 1] = lax.optimization_barrier((held[k, 0], held[k - 2, 1]))
-    for n, held in enumerate(streams):
-        held[turns - 1, 1] = send(held[turns - 1, 0], across) if n % 2 == 0 else send(held[turns - 2, 1], onward)
+        behind = held[k - 1, 0]
+        steps = [send(piece, onward) for piece in behind]
+        joined = whole if k == 1 else jnp.concatenate(behind, axis=1)
+        held[k - 1, 1] = [send(joined, across)]
+        if k > 1:
+            steps[0], held[k - 2, 1][0] = lax.optimization_barrier((steps[0], held[k - 2, 1][0]))
+        held[k, 0] = steps
+    held[turns - 1, 1] = [send(piece, across) for piece in held[turns - 1, 0]]
     late = [(turns - 1, 0), (turns - 2, 1), (turns - 1, 1)]
-    order = [chunk for chunk in streams[0] if chunk not in late] + late
+    order = [chunk for chunk in held if chunk not in late] + late
     there = len(order) - len(late)
     index, begun = early(
         order,
         turns,
         jnp.transpose(block_owner, (0, 2, 1)),
         block_row,
-        [[held[chunk] for chunk in order[:there]] for held in streams],
+        [held[chunk] for chunk in order[:there]],
+        whole.shape[1],
     )
-    picked = pick(index, begun, [[held[chunk] for chunk in late] for held in streams], there * rows)
+    picked = pick(index, begun, [held[chunk] for chunk in late], there * rows)
     other = lax.ppermute(picked, "heads", [(0, 1), (1, 0)])
     first = own_scores(picked, w_key, queries, spans)
     values = own_values(picked, w_value, spans)

time: 35.7 us -> 36.4 us (1.020)
  starting transfers between devices: 22.3 us -> 19.1 us
  waiting for transfers between devices: 4.98 us -> 8.1 us
  Pallas kernels: 5.28 us -> 6.13 us
    ppermute x14 -> x11, starting transfers between devices: 22.2 us -> 19 us  [send(): return lax.ppermute(chunk, 'wide', pairs)]
    ppermute x14 -> x11, waiting for transfers between devices: 4.98 us -> 8.1 us  [send(): return lax.ppermute(chunk, 'wide', pairs)]
    pallas_call x1, Pallas kernels: 2.57 us -> 3.35 us  [attend(): pl.pallas_call(functools.partial(attend_kernel, spans), out_shape=jax.Sha...]
  transfers between devices with their start and end apart: 15 -> 12, of which waited for: 8 -> 8; matrix products, arithmetic and copies ran while one was open for 0% -> 0% of each run, Pallas kernels for 7% -> 6%
where the time goes in v5:
time: 36.4 us; the launch traced here: 36.2 us
  starting transfers between devices  19.1 us (52%)
  waiting for transfers between devices  8.1 us (22%)
  Pallas kernels  6.13 us (17%)
  local copies, waits for them, and re-layouts  2.71 us (7%)
    ppermute x11, starting transfers between devices, send(): return lax.ppermute(chunk, 'wide', pairs)  19 us
    ppermute x11, waiting for transfers between devices, send(): return lax.ppermute(chunk, 'wide', pairs)  8.1 us
    pallas_call x1, Pallas kernels, attend(): pl.pallas_call(functools.partial(attend_kernel, spans), out_shape=jax.Sha...  3.35 us
    unnamed x12, local copies, waits for them, and re-layouts  2.71 us
    pallas_call x1, Pallas kernels, own_scores(): pl.pallas_call(functools.partial(score_kernel, spans), out_shape=jax.Shap...  1.02 us
  transfers between devices with their start and end apart: 12, of which 8 were waited for; matrix products, arithmetic and copies ran while one was open for 0% of the time, Pallas kernels for 6%

profile of v5, /device:TPU:0, one launch (start us, length us, event | category | flops | bytes accessed | tf_op | source)
XLA Modules:
  0.0 36.2 jit_solution(10330981149332072110)
XLA Ops:
  0.0 1.0 %copy-done.3 = bf16[64,3584]{1,0:T(8,128)(2,1)S(1)} copy-done((bf16[64,3584]{1,0:T(8,128)(2,1)S(1)}, bf16[64,3584]{1,0:T(8,128)(2,1)}, u32[]{:S(2)}) %copy-start.3) | copy-done | bytes 458776
  1.1 3.1 %collective-permute-start = (bf16[64,896]{1,0:T(8,128)(2,1)S(1)}, bf16[64,896]{1,0:T(8,128)(2,1)S(1)}, u32[]{:S(2)}, u32[]{:S(2)}) collective-permute-start(bf16[64,896]{1,0:T(8,128)(2,1)S(1)} %get-tuple-element.14.refs_0_), channel_id=1, source_target_pairs={{0,4},{2,6},{4,12},{6,14},{12,8},{14,10},{8,0},{10,2},{1,5},{3,7},... | collective-permute-start | bytes 344072 | tf_op jit(solution)/shard_map/ppermute | solution.py:235
  4.2 2.6 %collective-permute-start.3 = (bf16[64,896]{1,0:T(8,128)(2,1)S(1)}, bf16[64,896]{1,0:T(8,128)(2,1)S(1)}, u32[]{:S(2)}, u32[]{:S(2)}) collective-permute-start(bf16[64,896]{1,0:T(8,128)(2,1)S(1)} %get-tuple-element.15.refs_1_), channel_id=1, source_target_pairs={{0,4},{2,6},{4,12},{6,14},{12,8},{14,10},{8,0},{10,2},{1,5},{3,7},... | collective-permute-start | bytes 344072 | tf_op jit(solution)/shard_map/ppermute | solution.py:235
  6.8 1.5 %collective-permute-start.2 = (bf16[64,1792]{1,0:T(8,128)(2,1)S(1)}, bf16[64,1792]{1,0:T(8,128)(2,1)S(1)}, u32[]{:S(2)}, u32[]{:S(2)}) collective-permute-start(bf16[64,1792]{1,0:T(8,128)(2,1)S(1)} %get-tuple-element.16), channel_id=1, source_target_pairs={{0,2},{2,0},{4,6},{6,4},{8,10},{10,8},{12,14},{14,12},{1,3},{3,1},... | collective-permute-start | bytes 688136 | tf_op jit(solution)/shard_map/ppermute | solution.py:235
  8.3 0.9 %collective-permute-done.refs_3_ = bf16[64,896]{1,0:T(8,128)(2,1)S(1)} collective-permute-done((bf16[64,896]{1,0:T(8,128)(2,1)S(1)}, bf16[64,896]{1,0:T(8,128)(2,1)S(1)}, u32[]{:S(2)}, u32[]{:S(2)}) %collective-permute-start) | collective-permute-done | bytes 114720 | tf_op jit(solution)/shard_map/ppermute | solution.py:235
  9.2 1.2 %collective-permute-start.1 = (bf16[64,896]{1,0:T(8,128)(2,1)S(1)}, bf16[64,896]{1,0:T(8,128)(2,1)S(1)}, u32[]{:S(2)}, u32[]{:S(2)}) collective-permute-start(bf16[64,896]{1,0:T(8,128)(2,1)S(1)} %collective-permute-done.refs_3_), channel_id=1, source_target_pairs={{0,4},{2,6},{4,12},{6,14},{12,8},{14,10},{8,0},{10,2},{1,5},{3,7},... | collective-permute-start | bytes 344072 | tf_op jit(solution)/shard_map/ppermute | solution.py:235
  10.8 2.9 %collective-permute-start.6 = (bf16[64,896]{1,0:T(8,128)(2,1)S(1)}, bf16[64,896]{1,0:T(8,128)(2,1)S(1)}, u32[]{:S(2)}, u32[]{:S(2)}) collective-permute-start(bf16[64,896]{1,0:T(8,128)(2,1)S(1)} %collective-permute-done.3.refs_4_), channel_id=1, source_target_pairs={{0,4},{2,6},{4,12},{6,14},{12,8},{14,10},{8,0},{10,2},{1,5},{3,7},... | collective-permute-start | bytes 344072 | tf_op jit(solution)/shard_map/ppermute | solution.py:235
  13.7 1.6 %collective-permute-start.5 = (bf16[64,1792]{1,0:T(8,128)(2,1)S(1)}, bf16[64,1792]{1,0:T(8,128)(2,1)S(1)}, u32[]{:S(2)}, u32[]{:S(2)}) collective-permute-start(bf16[64,1792]{1,0:T(8,128)(2,1)S(1)} %pad_maximum_fusion), channel_id=1, source_target_pairs={{0,2},{2,0},{4,6},{6,4},{8,10},{10,8},{12,14},{14,12},{1,3},{3,1},... | collective-permute-start | bytes 688136 | tf_op jit(solution)/shard_map/ppermute | solution.py:235
  15.3 0.8 %collective-permute-done.1.refs_6_ = bf16[64,896]{1,0:T(8,128)(2,1)S(1)} collective-permute-done((bf16[64,896]{1,0:T(8,128)(2,1)S(1)}, bf16[64,896]{1,0:T(8,128)(2,1)S(1)}, u32[]{:S(2)}, u32[]{:S(2)}) %collective-permute-start.1) | collective-permute-done | bytes 114720 | tf_op jit(solution)/shard_map/ppermute | solution.py:235
  16.1 0.8 %collective-permute-start.4 = (bf16[64,896]{1,0:T(8,128)(2,1)S(1)}, bf16[64,896]{1,0:T(8,128)(2,1)S(1)}, u32[]{:S(2)}, u32[]{:S(2)}) collective-permute-start(bf16[64,896]{1,0:T(8,128)(2,1)S(1)} %collective-permute-done.1.refs_6_), channel_id=1, source_target_pairs={{0,4},{2,6},{4,12},{6,14},{12,8},{14,10},{8,0},{10,2},{1,5},{3,7},... | collective-permute-start | bytes 344072 | tf_op jit(solution)/shard_map/ppermute | solution.py:235
  16.9 1.6 %collective-permute-done.6.refs_7_ = bf16[64,896]{1,0:T(8,128)(2,1)S(1)} collective-permute-done((bf16[64,896]{1,0:T(8,128)(2,1)S(1)}, bf16[64,896]{1,0:T(8,128)(2,1)S(1)}, u32[]{:S(2)}, u32[]{:S(2)}) %collective-permute-start.6) | collective-permute-done | bytes 114720 | tf_op jit(solution)/shard_map/ppermute | solution.py:235
  18.5 1.3 %collective-permute-start.8 = (bf16[64,1792]{1,0:T(8,128)(2,1)S(1)}, bf16[64,1792]{1,0:T(8,128)(2,1)S(1)}, u32[]{:S(2)}, u32[]{:S(2)}) collective-permute-start(bf16[64,1792]{1,0:T(8,128)(2,1)S(1)} %pad_maximum_fusion.1), channel_id=1, source_target_pairs={{0,2},{2,0},{4,6},{6,4},{8,10},{10,8},{12,14},{14,12},{1,3},{3,1},... | collective-permute-start | bytes 688136 | tf_op jit(solution)/shard_map/ppermute | solution.py:235
  19.8 2.0 %collective-permute-start.7 = (bf16[64,896]{1,0:T(8,128)(2,1)S(1)}, bf16[64,896]{1,0:T(8,128)(2,1)S(1)}, u32[]{:S(2)}, u32[]{:S(2)}) collective-permute-start(bf16[64,896]{1,0:T(8,128)(2,1)S(1)} %collective-permute-done.6.refs_7_), channel_id=1, source_target_pairs={{0,4},{2,6},{4,12},{6,14},{12,8},{14,10},{8,0},{10,2},{1,5},{3,7},... | collective-permute-start | bytes 344072 | tf_op jit(solution)/shard_map/ppermute | solution.py:235
  21.8 0.7 %collective-permute-done.4.refs_0_ = bf16[64,896]{1,0:T(8,128)(2,1)S(1)} collective-permute-done((bf16[64,896]{1,0:T(8,128)(2,1)S(1)}, bf16[64,896]{1,0:T(8,128)(2,1)S(1)}, u32[]{:S(2)}, u32[]{:S(2)}) %collective-permute-start.4) | collective-permute-done | bytes 114720 | tf_op jit(solution)/shard_map/ppermute | solution.py:235
  22.5 1.4 %collective-permute-start.9 = (bf16[64,896]{1,0:T(8,128)(2,1)S(1)}, bf16[64,896]{1,0:T(8,128)(2,1)S(1)}, u32[]{:S(2)}, u32[]{:S(2)}) collective-permute-start(bf16[64,896]{1,0:T(8,128)(2,1)S(1)} %collective-permute-done.4.refs_0_), channel_id=1, source_target_pairs={{0,2},{2,0},{4,6},{6,4},{8,10},{10,8},{12,14},{14,12},{1,3},{3,1},... | collective-permute-start | bytes 344072 | tf_op jit(solution)/shard_map/ppermute | solution.py:235
  23.9 1.6 %collective-permute-done.7.refs_1_ = bf16[64,896]{1,0:T(8,128)(2,1)S(1)} collective-permute-done((bf16[64,896]{1,0:T(8,128)(2,1)S(1)}, bf16[64,896]{1,0:T(8,128)(2,1)S(1)}, u32[]{:S(2)}, u32[]{:S(2)}) %collective-permute-start.7) | collective-permute-done | bytes 114720 | tf_op jit(solution)/shard_map/ppermute | solution.py:235
  25.5 0.8 %collective-permute-start.10 = (bf16[64,896]{1,0:T(8,128)(2,1)S(1)}, bf16[64,896]{1,0:T(8,128)(2,1)S(1)}, u32[]{:S(2)}, u32[]{:S(2)}) collective-permute-start(bf16[64,896]{1,0:T(8,128)(2,1)S(1)} %collective-permute-done.7.refs_1_), channel_id=1, source_target_pairs={{0,2},{2,0},{4,6},{6,4},{8,10},{10,8},{12,14},{14,12},{1,3},{3,1},... | collective-permute-start | bytes 344072 | tf_op jit(solution)/shard_map/ppermute | solution.py:235
  26.3 0.7 %copy-done.4 = s32[2,64,1]{1,2,0:T(1,128)S(1)} copy-done((s32[2,64,1]{1,2,0:T(1,128)S(1)}, s32[2,64,1]{1,2,0:T(1,128)}, u32[]{:S(2)}) %copy-start.4) | copy-done | bytes 536
  27.0 0.7 %copy-done.5 = s32[2,64]{1,0:T(2,128)S(1)} copy-done((s32[2,64]{1,0:T(2,128)S(1)}, s32[2,64]{1,0:T(2,128)}, u32[]{:S(2)}) %copy-start.5) | copy-done | bytes 536
  27.7 0.6 %shard_map.65 = (s32[128,1]{1,0:T(8,128)S(1)}, bf16[128,1792]{1,0:T(8,128)(2,1)S(1)}) custom-call(s32[2,1,64]{2,1,0:T(1,128)S(1)} %bitcast.3, s32[2,64]{1,0:T(2,128)S(1)} %copy-done.5, bf16[64,896]{1,0:T(8,128)(2,1)S(1)} %get-tuple-element.14.refs_0_, bf16[64,896]{1,0:T(8,128)(2,1)S(1)} %get-tuple-element.15.refs_1_, ...), custom_call_target="tpu_custom_call" | custom-call | flops 146800640 | bytes 458752 | tf_op jit(solution)/shard_map/pallas_call | solution.py:104
  28.4 1.9 %collective-permute-done.10.refs_4_ = bf16[64,896]{1,0:T(8,128)(2,1)S(1)} collective-permute-done((bf16[64,896]{1,0:T(8,128)(2,1)S(1)}, bf16[64,896]{1,0:T(8,128)(2,1)S(1)}, u32[]{:S(2)}, u32[]{:S(2)}) %collective-permute-start.10) | collective-permute-done | bytes 114720 | tf_op jit(solution)/shard_map/ppermute | solution.py:235
  30.8 0.7 %shard_map.68.values_ref = bf16[256,1024]{1,0:T(8,128)(2,1)S(1)} custom-call(bf16[128,1792]{1,0:T(8,128)(2,1)S(1)} %shard_map.66.picked_ref, bf16[896,1024]{1,0:T(8,128)(2,1)S(1)} %copy-done.1), custom_call_target="tpu_custom_call" | custom-call | tf_op jit(solution)/shard_map/pallas_call | solution.py:188
  31.8 1.0 %shard_map.67.first_ref = f32[16,64,128]{2,1,0:T(8,128)S(1)} custom-call(bf16[128,1792]{1,0:T(8,128)(2,1)S(1)} %shard_map.66.picked_ref, bf16[896,1024]{1,0:T(8,128)(2,1)S(1)} %copy-done, bf16[128,1024]{1,0:T(8,128)(2,1)S(1)} %copy-done.2), custom_call_target="tpu_custom_call" | custom-call | tf_op jit(solution)/shard_map/pallas_call | solution.py:172
  32.8 3.3 %shard_map.69 = bf16[128,1024]{1,0:T(8,128)(2,1)} custom-call(bf16[128,1792]{1,0:T(8,128)(2,1)S(1)} %collective-permute-done.11.other_ref, bf16[896,1024]{1,0:T(8,128)(2,1)S(1)} %copy-done, bf16[896,1024]{1,0:T(8,128)(2,1)S(1)} %copy-done.1, bf16[128,1024]{1,0:T(8,128)(2,1)S(1)} %copy-done.2, f32[16,64,128]{2,1,0:T(8,128)S(1)} %shard_map.67.first_ref, ...), custom_call_target="tpu_custom_call" | custom-call | tf_op jit(solution)/shard_map/pallas_call | solution.py:224
  (20 shorter events, 1.5 us)
Async XLA Ops:
  0.0 1.0 %copy-start.3 = (bf16[64,3584]{1,0:T(8,128)(2,1)S(1)}, bf16[64,3584]{1,0:T(8,128)(2,1)}, u32[]{:S(2)}) copy-start(bf16[64,3584]{1,0:T(8,128)(2,1)} %enc_ref.1) | copy-start | bytes 1376260
  1.1 8.1 %collective-permute-start = (bf16[64,896]{1,0:T(8,128)(2,1)S(1)}, bf16[64,896]{1,0:T(8,128)(2,1)S(1)}, u32[]{:S(2)}, u32[]{:S(2)}) collective-permute-start(bf16[64,896]{1,0:T(8,128)(2,1)S(1)} %get-tuple-element.14.refs_0_), channel_id=1, source_target_pairs={{0,4},{2,6},{4,12},{6,14},{12,8},{14,10},{8,0},{10,2},{1,5},{3,7},... | collective-permute-start | bytes 344072 | tf_op jit(solution)/shard_map/ppermute | solution.py:235
  4.2 6.6 %collective-permute-start.3 = (bf16[64,896]{1,0:T(8,128)(2,1)S(1)}, bf16[64,896]{1,0:T(8,128)(2,1)S(1)}, u32[]{:S(2)}, u32[]{:S(2)}) collective-permute-start(bf16[64,896]{1,0:T(8,128)(2,1)S(1)} %get-tuple-element.15.refs_1_), channel_id=1, source_target_pairs={{0,4},{2,6},{4,12},{6,14},{12,8},{14,10},{8,0},{10,2},{1,5},{3,7},... | collective-permute-start | bytes 344072 | tf_op jit(solution)/shard_map/ppermute | solution.py:235
  6.8 24.0 %copy-start.1 = (bf16[896,1024]{1,0:T(8,128)(2,1)S(1)}, bf16[896,1024]{1,0:T(8,128)(2,1)}, u32[]{:S(2)}) copy-start(bf16[896,1024]{1,0:T(8,128)(2,1)} %wv_ref.3) | copy-start | bytes 5505028
  6.8 9.3 %collective-permute-start.2 = (bf16[64,1792]{1,0:T(8,128)(2,1)S(1)}, bf16[64,1792]{1,0:T(8,128)(2,1)S(1)}, u32[]{:S(2)}, u32[]{:S(2)}) collective-permute-start(bf16[64,1792]{1,0:T(8,128)(2,1)S(1)} %get-tuple-element.16), channel_id=1, source_target_pairs={{0,2},{2,0},{4,6},{6,4},{8,10},{10,8},{12,14},{14,12},{1,3},{3,1},... | collective-permute-start | bytes 688136 | tf_op jit(solution)/shard_map/ppermute | solution.py:235
  9.2 6.9 %collective-permute-start.1 = (bf16[64,896]{1,0:T(8,128)(2,1)S(1)}, bf16[64,896]{1,0:T(8,128)(2,1)S(1)}, u32[]{:S(2)}, u32[]{:S(2)}) collective-permute-start(bf16[64,896]{1,0:T(8,128)(2,1)S(1)} %collective-permute-done.refs_3_), channel_id=1, source_target_pairs={{0,4},{2,6},{4,12},{6,14},{12,8},{14,10},{8,0},{10,2},{1,5},{3,7},... | collective-permute-start | bytes 344072 | tf_op jit(solution)/shard_map/ppermute | solution.py:235
  10.8 7.7 %collective-permute-start.6 = (bf16[64,896]{1,0:T(8,128)(2,1)S(1)}, bf16[64,896]{1,0:T(8,128)(2,1)S(1)}, u32[]{:S(2)}, u32[]{:S(2)}) collective-permute-start(bf16[64,896]{1,0:T(8,128)(2,1)S(1)} %collective-permute-done.3.refs_4_), channel_id=1, source_target_pairs={{0,4},{2,6},{4,12},{6,14},{12,8},{14,10},{8,0},{10,2},{1,5},{3,7},... | collective-permute-start | bytes 344072 | tf_op jit(solution)/shard_map/ppermute | solution.py:235
  13.7 8.8 %collective-permute-start.5 = (bf16[64,1792]{1,0:T(8,128)(2,1)S(1)}, bf16[64,1792]{1,0:T(8,128)(2,1)S(1)}, u32[]{:S(2)}, u32[]{:S(2)}) collective-permute-start(bf16[64,1792]{1,0:T(8,128)(2,1)S(1)} %pad_maximum_fusion), channel_id=1, source_target_pairs={{0,2},{2,0},{4,6},{6,4},{8,10},{10,8},{12,14},{14,12},{1,3},{3,1},... | collective-permute-start | bytes 688136 | tf_op jit(solution)/shard_map/ppermute | solution.py:235
  16.1 6.4 %collective-permute-start.4 = (bf16[64,896]{1,0:T(8,128)(2,1)S(1)}, bf16[64,896]{1,0:T(8,128)(2,1)S(1)}, u32[]{:S(2)}, u32[]{:S(2)}) collective-permute-start(bf16[64,896]{1,0:T(8,128)(2,1)S(1)} %collective-permute-done.1.refs_6_), channel_id=1, source_target_pairs={{0,4},{2,6},{4,12},{6,14},{12,8},{14,10},{8,0},{10,2},{1,5},{3,7},... | collective-permute-start | bytes 344072 | tf_op jit(solution)/shard_map/ppermute | solution.py:235
  18.5 9.8 %collective-permute-start.8 = (bf16[64,1792]{1,0:T(8,128)(2,1)S(1)}, bf16[64,1792]{1,0:T(8,128)(2,1)S(1)}, u32[]{:S(2)}, u32[]{:S(2)}) collective-permute-start(bf16[64,1792]{1,0:T(8,128)(2,1)S(1)} %pad_maximum_fusion.1), channel_id=1, source_target_pairs={{0,2},{2,0},{4,6},{6,4},{8,10},{10,8},{12,14},{14,12},{1,3},{3,1},... | collective-permute-start | bytes 688136 | tf_op jit(solution)/shard_map/ppermute | solution.py:235
  19.8 5.7 %collective-permute-start.7 = (bf16[64,896]{1,0:T(8,128)(2,1)S(1)}, bf16[64,896]{1,0:T(8,128)(2,1)S(1)}, u32[]{:S(2)}, u32[]{:S(2)}) collective-permute-start(bf16[64,896]{1,0:T(8,128)(2,1)S(1)} %collective-permute-done.6.refs_7_), channel_id=1, source_target_pairs={{0,4},{2,6},{4,12},{6,14},{12,8},{14,10},{8,0},{10,2},{1,5},{3,7},... | collective-permute-start | bytes 344072 | tf_op jit(solution)/shard_map/ppermute | solution.py:235
  22.5 5.9 %collective-permute-start.9 = (bf16[64,896]{1,0:T(8,128)(2,1)S(1)}, bf16[64,896]{1,0:T(8,128)(2,1)S(1)}, u32[]{:S(2)}, u32[]{:S(2)}) collective-permute-start(bf16[64,896]{1,0:T(8,128)(2,1)S(1)} %collective-permute-done.4.refs_0_), channel_id=1, source_target_pairs={{0,2},{2,0},{4,6},{6,4},{8,10},{10,8},{12,14},{14,12},{1,3},{3,1},... | collective-permute-start | bytes 344072 | tf_op jit(solution)/shard_map/ppermute | solution.py:235
  25.5 4.8 %collective-permute-start.10 = (bf16[64,896]{1,0:T(8,128)(2,1)S(1)}, bf16[64,896]{1,0:T(8,128)(2,1)S(1)}, u32[]{:S(2)}, u32[]{:S(2)}) collective-permute-start(bf16[64,896]{1,0:T(8,128)(2,1)S(1)} %collective-permute-done.7.refs_1_), channel_id=1, source_target_pairs={{0,2},{2,0},{4,6},{6,4},{8,10},{10,8},{12,14},{14,12},{1,3},{3,1},... | collective-permute-start | bytes 344072 | tf_op jit(solution)/shard_map/ppermute | solution.py:235
  26.3 0.7 %copy-start.4 = (s32[2,64,1]{1,2,0:T(1,128)S(1)}, s32[2,64,1]{1,2,0:T(1,128)}, u32[]{:S(2)}) copy-start(s32[2,64,1]{1,2,0:T(1,128)} %param.10) | copy-start | bytes 1540
  27.0 0.7 %copy-start.5 = (s32[2,64]{1,0:T(2,128)S(1)}, s32[2,64]{1,0:T(2,128)}, u32[]{:S(2)}) copy-start(s32[2,64]{1,0:T(2,128)} %stored_ref.1) | copy-start | bytes 1540
  30.3 1.5 %copy-start = (bf16[896,1024]{1,0:T(8,128)(2,1)S(1)}, bf16[896,1024]{1,0:T(8,128)(2,1)}, u32[]{:S(2)}) copy-start(bf16[896,1024]{1,0:T(8,128)(2,1)} %wk_ref.3) | copy-start | bytes 5505028
  30.3 1.5 %copy-start.2 = (bf16[128,1024]{1,0:T(8,128)(2,1)S(1)}, bf16[128,1024]{1,0:T(8,128)(2,1)}, u32[]{:S(2)}) copy-start(bf16[128,1024]{1,0:T(8,128)(2,1)} %query_ref.3) | copy-start | bytes 786436
  30.7 2.2 %collective-permute-start.11 = (bf16[128,1792]{1,0:T(8,128)(2,1)S(1)}, bf16[128,1792]{1,0:T(8,128)(2,1)S(1)}, u32[]{:S(2)}, u32[]{:S(2)}) collective-permute-start(bf16[128,1792]{1,0:T(8,128)(2,1)S(1)} %shard_map.66.picked_ref), channel_id=1, source_target_pairs={{0,1},{1,0},{2,3},{3,2},{4,5},{5,4},{6,7},{7,6},{8,9},{9,8},{10,11... | collective-permute-start | bytes 1376264 | tf_op jit(solution)/shard_map/ppermute | solution.py:271

commit v6 on v5

--- a/solution.py
+++ b/solution.py
@@ -91,31 +91,47 @@
     return jnp.concatenate(columns, axis=0).astype(jnp.int32)
 
 
-def early_kernel(order, turns, chunks, owner_ref, stored_ref, *refs):
-    sources, index_ref, out_ref = refs[:-2], refs[-2], refs[-1]
-    index_ref[...] = wanted_rows(order, turns, sources[0].shape[0], owner_ref, stored_ref)
-    out_ref[...] = chosen_rows(index_ref[...], chunks, sources, 0).astype(out_ref.dtype)
-
-
-def early(order, turns, owners, stored, sources, width):
+def places_kernel(order, turns, owner_ref, stored_ref, piece_ref, index_ref, piece_out, sem):
+    copy = pltpu.make_async_copy(piece_ref, piece_out, sem)
+    copy.start()
+    index_ref[...] = wanted_rows(order, turns, piece_ref.shape[0], owner_ref, stored_ref)
+    copy.wait()
+
+
+def places(order, turns, owners, stored, piece):
+    return pl.pallas_call(
+        functools.partial(places_kernel, order, turns),
+        out_shape=(
+            jax.ShapeDtypeStruct((stored.size, 1), jnp.int32),
+            jax.ShapeDtypeStruct(piece.shape, piece.dtype),
+        ),
+        in_specs=[VMEM] * 3,
+        out_specs=(VMEM, VMEM),
+        scratch_shapes=[pltpu.SemaphoreType.DMA],
+        compiler_params=params(),
+    )(owners, stored, piece)
+
+
+def early_kernel(chunks, index_ref, *refs):
+    refs[-1][...] = chosen_rows(index_ref[...], chunks, refs[:-1], 0).astype(refs[-1].dtype)
+
+
+def early(index, sources, width):
     rows = sources[0][0].shape[0]
-    requests = stored.size
+    requests = index.shape[0]
     arrays = [array for chunk in sources for array in chunk]
     return pl.pallas_call(
-        functools.partial(early_kernel, order, turns, [len(chunk) for chunk in sources]),
-        out_shape=(
-            jax.ShapeDtypeStruct((requests, 1), jnp.int32),
-            jax.ShapeDtypeStruct((requests, width), arrays[0].dtype),
-        ),
-        in_specs=[VMEM] * (2 + len(arrays)),
-        out_specs=(VMEM, VMEM),
+        functools.partial(early_kernel, [len(chunk) for chunk in sources]),
+        out_shape=jax.ShapeDtypeStruct((requests, width), arrays[0].dtype),
+        in_specs=[VMEM] * (1 + len(arrays)),
+        out_specs=VMEM,
         compiler_params=params(),
         cost_estimate=pl.CostEstimate(
             flops=2 * requests * width * rows * len(sources),
             bytes_accessed=2 * requests * width,
             transcendentals=0,
         ),
-    )(owners, stored, *arrays)
+    )(index, *arrays)
 
 
 def pick_kernel(chunks, first, index_ref, begun_ref, *refs):
@@ -195,28 +211,22 @@
 
 
 def attend_kernel(
-    spans, other_ref, wk_ref, wv_ref, query_ref, first_ref, values_ref, out_ref, second_ref
+    spans, other_ref, wk_ref, wv_ref, query_ref, first_ref, values_ref, out_ref, second_ref, probs_ref
 ):
     other = by_span(other_ref[...], spans, wk_ref.shape[0])
+    score(spans, other, wk_ref, query_ref, second_ref)
     per = other.shape[0] // spans
-    columns = wk_ref.shape[1]
-    heads = columns // HD
-    group = 2 if heads % 2 == 0 else 1
-    score(spans, other, wk_ref, query_ref, second_ref)
-    for at in range(0, heads, group):
-        lanes = slice(at * HD, (at + group) * HD)
-        more = jnp.dot(other, wv_ref[:, lanes], preferred_element_type=jnp.float32).astype(jnp.bfloat16)
-        for c in range(spans):
-            rows = slice(c * per, (c + 1) * per)
-            for h in range(group):
-                n = c * heads + at + h
-                scores = jnp.concatenate([first_ref[n], second_ref[n]], axis=1)
-                raised = jnp.exp2((scores - jnp.max(scores, axis=-1, keepdims=True)) * EXPONENT)
-                probs = (raised * (1.0 / jnp.sum(raised, axis=-1, keepdims=True))).astype(jnp.bfloat16)
-                head = slice((at + h) * HD, (at + h + 1) * HD)
-                values = jnp.concatenate([values_ref[rows, head], more[rows, h * HD : (h + 1) * HD]], axis=0)
-                mixed = jnp.dot(probs, values, preferred_element_type=jnp.float32)
-                out_ref[c * SPAN : (c + 1) * SPAN, head] = mixed.astype(out_ref.dtype)
+    more = jnp.dot(other, wv_ref[...], preferred_element_type=jnp.float32).astype(jnp.bfloat16)
+    places = head_places(spans, more.shape[1])
+    for c, lanes, n in places:
+        scores = jnp.concatenate([first_ref[n], second_ref[n]], axis=1)
+        raised = jnp.exp2((scores - jnp.max(scores, axis=-1, keepdims=True)) * EXPONENT)
+        probs_ref[n] = (raised * (1.0 / jnp.sum(raised, axis=-1, keepdims=True))).astype(jnp.bfloat16)
+    for c, lanes, n in places:
+        rows = slice(c * per, (c + 1) * per)
+        values = jnp.concatenate([values_ref[rows, lanes], more[rows, lanes]], axis=0)
+        mixed = jnp.dot(probs_ref[n], values, preferred_element_type=jnp.float32)
+        out_ref[c * SPAN : (c + 1) * SPAN, lanes] = mixed.astype(out_ref.dtype)
 
 
 def attend(other, w_key, w_value, queries, first, values, spans):
@@ -226,7 +236,7 @@
         out_shape=jax.ShapeDtypeStruct(queries.shape, queries.dtype),
         in_specs=[VMEM] * 6,
         out_specs=VMEM,
-        scratch_shapes=[pltpu.VMEM(each, jnp.float32)],
+        scratch_shapes=[pltpu.VMEM(each, jnp.float32), pltpu.VMEM(each[:2] + (2 * each[2],), jnp.bfloat16)],
         compiler_params=params(),
     )(other, w_key, w_value, queries, first, values)
 
@@ -246,6 +256,11 @@
     ]
     across = [(n, n + 1 if n % SIDE == 0 else n - 1) for n in range(wide_count)]
     *pieces, whole = half_columns(encodings)
+    order = [(0, 0)]
+    for k in range(1, turns):
+        order += [(k, 0), (k - 1, 1)]
+    order.append((turns - 1, 1))
+    index, pieces[-1] = places(order, turns, jnp.transpose(block_owner, (0, 2, 1)), block_row, pieces[-1])
     held = {(0, 0): pieces}
     for k in range(1, turns):
         behind = held[k - 1, 0]
@@ -256,18 +271,10 @@
             steps[0], held[k - 2, 1][0] = lax.optimization_barrier((steps[0], held[k - 2, 1][0]))
         held[k, 0] = steps
     held[turns - 1, 1] = [send(piece, across) for piece in held[turns - 1, 0]]
-    late = [(turns - 1, 0), (turns - 2, 1), (turns - 1, 1)]
-    order = [chunk for chunk in held if chunk not in late] + late
-    there = len(order) - len(late)
-    index, begun = early(
-        order,
-        turns,
-        jnp.transpose(block_owner, (0, 2, 1)),
-        block_row,
-        [held[chunk] for chunk in order[:there]],
-        whole.shape[1],
-    )
-    picked = pick(index, begun, [held[chunk] for chunk in late], there * rows)
+    late = 3
+    sources = [held[chunk] for chunk in order]
+    begun = early(index, sources[:-late], whole.shape[1])
+    picked = pick(index, begun, sources[-late:], (len(order) - late) * rows)
     other = lax.ppermute(picked, "heads", [(0, 1), (1, 0)])
     first = own_scores(picked, w_key, queries, spans)
     values = own_values(picked, w_value, spans)

time: 36.4 us -> 35.4 us (0.973)
  starting transfers between devices: 19.1 us -> 16.7 us
  waiting for transfers between devices: 8.1 us -> 10.5 us
  Pallas kernels: 6.13 us -> 5.48 us
    ppermute x11, starting transfers between devices: 19 us -> 16.6 us  [send(): return lax.ppermute(chunk, 'wide', pairs)]
    ppermute x11, waiting for transfers between devices: 8.1 us -> 10.5 us  [send(): return lax.ppermute(chunk, 'wide', pairs)]
    pallas_call x1, Pallas kernels: 3.35 us -> 2.56 us  [attend(): pl.pallas_call(functools.partial(attend_kernel, spans), out_shape=jax.Sha...]
    pallas_call x1 -> x2, Pallas kernels: 0.61 us -> 0.75 us  [the longest x1 0.48 us: early(): pl.pallas_call(functools.partial(early_kernel, [len(chunk) for chunk in s...]
  transfers between devices with their start and end apart: 12 -> 12, of which waited for: 8 -> 9; matrix products, arithmetic and copies ran while one was open for 0% -> 0% of each run, Pallas kernels for 6% -> 7%
where the time goes in v6:
time: 35.4 us; the launch traced here: 35.2 us
  starting transfers between devices  16.7 us (47%)
  waiting for transfers between devices  10.5 us (30%)
  Pallas kernels  5.48 us (15%)
  local copies, waits for them, and re-layouts  2.39 us (7%)
    ppermute x11, starting transfers between devices, send(): return lax.ppermute(chunk, 'wide', pairs)  16.6 us
    ppermute x11, waiting for transfers between devices, send(): return lax.ppermute(chunk, 'wide', pairs)  10.5 us
    pallas_call x1, Pallas kernels, attend(): pl.pallas_call(functools.partial(attend_kernel, spans), out_shape=jax.Sha...  2.56 us
    unnamed x12, local copies, waits for them, and re-layouts  2.39 us
    pallas_call x1, Pallas kernels, own_scores(): pl.pallas_call(functools.partial(score_kernel, spans), out_shape=jax.Shap...  1.02 us
  transfers between devices with their start and end apart: 12, of which 9 were waited for; matrix products, arithmetic and copies ran while one was open for 0% of the time, Pallas kernels for 7%

profile of v6, /device:TPU:0, one launch (start us, length us, event | category | flops | bytes accessed | tf_op | source)
XLA Modules:
  0.0 35.2 jit_solution(10251382885560106053)
XLA Ops:
  0.0 1.0 %copy-done.3 = bf16[64,3584]{1,0:T(8,128)(2,1)S(1)} copy-done((bf16[64,3584]{1,0:T(8,128)(2,1)S(1)}, bf16[64,3584]{1,0:T(8,128)(2,1)}, u32[]{:S(2)}) %copy-start.3) | copy-done | bytes 458776
  1.1 3.1 %collective-permute-start = (bf16[64,896]{1,0:T(8,128)(2,1)S(1)}, bf16[64,896]{1,0:T(8,128)(2,1)S(1)}, u32[]{:S(2)}, u32[]{:S(2)}) collective-permute-start(bf16[64,896]{1,0:T(8,128)(2,1)S(1)} %get-tuple-element.16.refs_0_), channel_id=1, source_target_pairs={{0,4},{2,6},{4,12},{6,14},{12,8},{14,10},{8,0},{10,2},{1,5},{3,7},... | collective-permute-start | bytes 344072 | tf_op jit(solution)/shard_map/ppermute | solution.py:245
  4.2 0.7 %copy-done.4 = s32[2,64,1]{1,2,0:T(1,128)S(1)} copy-done((s32[2,64,1]{1,2,0:T(1,128)S(1)}, s32[2,64,1]{1,2,0:T(1,128)}, u32[]{:S(2)}) %copy-start.4) | copy-done | bytes 536
  4.9 0.7 %copy-done.5 = s32[2,64]{1,0:T(2,128)S(1)} copy-done((s32[2,64]{1,0:T(2,128)S(1)}, s32[2,64]{1,0:T(2,128)}, u32[]{:S(2)}) %copy-start.5) | copy-done | bytes 536
  5.8 2.6 %collective-permute-start.1 = (bf16[64,896]{1,0:T(8,128)(2,1)S(1)}, bf16[64,896]{1,0:T(8,128)(2,1)S(1)}, u32[]{:S(2)}, u32[]{:S(2)}) collective-permute-start(bf16[64,896]{1,0:T(8,128)(2,1)S(1)} %get-tuple-element.17.refs_1_), channel_id=1, source_target_pairs={{0,4},{2,6},{4,12},{6,14},{12,8},{14,10},{8,0},{10,2},{1,5},{3,7},... | collective-permute-start | bytes 344072 | tf_op jit(solution)/shard_map/ppermute | solution.py:245
  8.5 1.5 %collective-permute-start.3 = (bf16[64,1792]{1,0:T(8,128)(2,1)S(1)}, bf16[64,1792]{1,0:T(8,128)(2,1)S(1)}, u32[]{:S(2)}, u32[]{:S(2)}) collective-permute-start(bf16[64,1792]{1,0:T(8,128)(2,1)S(1)} %get-tuple-element.18), channel_id=1, source_target_pairs={{0,2},{2,0},{4,6},{6,4},{8,10},{10,8},{12,14},{14,12},{1,3},{3,1},... | collective-permute-start | bytes 688136 | tf_op jit(solution)/shard_map/ppermute | solution.py:245
  10.0 0.5 %collective-permute-start.2 = (bf16[64,896]{1,0:T(8,128)(2,1)S(1)}, bf16[64,896]{1,0:T(8,128)(2,1)S(1)}, u32[]{:S(2)}, u32[]{:S(2)}) collective-permute-start(bf16[64,896]{1,0:T(8,128)(2,1)S(1)} %collective-permute-done.refs_2_), channel_id=1, source_target_pairs={{0,4},{2,6},{4,12},{6,14},{12,8},{14,10},{8,0},{10,2},{1,5},{3,7},... | collective-permute-start | bytes 344072 | tf_op jit(solution)/shard_map/ppermute | solution.py:245
  10.4 1.6 %collective-permute-done.1.refs_3_ = bf16[64,896]{1,0:T(8,128)(2,1)S(1)} collective-permute-done((bf16[64,896]{1,0:T(8,128)(2,1)S(1)}, bf16[64,896]{1,0:T(8,128)(2,1)S(1)}, u32[]{:S(2)}, u32[]{:S(2)}) %collective-permute-start.1) | collective-permute-done | bytes 114720 | tf_op jit(solution)/shard_map/ppermute | solution.py:245
  12.0 2.5 %collective-permute-start.4 = (bf16[64,896]{1,0:T(8,128)(2,1)S(1)}, bf16[64,896]{1,0:T(8,128)(2,1)S(1)}, u32[]{:S(2)}, u32[]{:S(2)}) collective-permute-start(bf16[64,896]{1,0:T(8,128)(2,1)S(1)} %collective-permute-done.1.refs_3_), channel_id=1, source_target_pairs={{0,4},{2,6},{4,12},{6,14},{12,8},{14,10},{8,0},{10,2},{1,5},{3,7},... | collective-permute-start | bytes 344072 | tf_op jit(solution)/shard_map/ppermute | solution.py:245
  14.5 1.4 %collective-permute-start.6 = (bf16[64,1792]{1,0:T(8,128)(2,1)S(1)}, bf16[64,1792]{1,0:T(8,128)(2,1)S(1)}, u32[]{:S(2)}, u32[]{:S(2)}) collective-permute-start(bf16[64,1792]{1,0:T(8,128)(2,1)S(1)} %pad_maximum_fusion), channel_id=1, source_target_pairs={{0,2},{2,0},{4,6},{6,4},{8,10},{10,8},{12,14},{14,12},{1,3},{3,1},... | collective-permute-start | bytes 688136 | tf_op jit(solution)/shard_map/ppermute | solution.py:245
  16.4 0.6 %collective-permute-start.5 = (bf16[64,896]{1,0:T(8,128)(2,1)S(1)}, bf16[64,896]{1,0:T(8,128)(2,1)S(1)}, u32[]{:S(2)}, u32[]{:S(2)}) collective-permute-start(bf16[64,896]{1,0:T(8,128)(2,1)S(1)} %collective-permute-done.2.refs_5_), channel_id=1, source_target_pairs={{0,4},{2,6},{4,12},{6,14},{12,8},{14,10},{8,0},{10,2},{1,5},{3,7},... | collective-permute-start | bytes 344072 | tf_op jit(solution)/shard_map/ppermute | solution.py:245
  16.9 1.4 %collective-permute-done.4.refs_6_ = bf16[64,896]{1,0:T(8,128)(2,1)S(1)} collective-permute-done((bf16[64,896]{1,0:T(8,128)(2,1)S(1)}, bf16[64,896]{1,0:T(8,128)(2,1)S(1)}, u32[]{:S(2)}, u32[]{:S(2)}) %collective-permute-start.4) | collective-permute-done | bytes 114720 | tf_op jit(solution)/shard_map/ppermute | solution.py:245
  18.4 1.2 %collective-permute-start.8 = (bf16[64,1792]{1,0:T(8,128)(2,1)S(1)}, bf16[64,1792]{1,0:T(8,128)(2,1)S(1)}, u32[]{:S(2)}, u32[]{:S(2)}) collective-permute-start(bf16[64,1792]{1,0:T(8,128)(2,1)S(1)} %pad_maximum_fusion.1), channel_id=1, source_target_pairs={{0,2},{2,0},{4,6},{6,4},{8,10},{10,8},{12,14},{14,12},{1,3},{3,1},... | collective-permute-start | bytes 688136 | tf_op jit(solution)/shard_map/ppermute | solution.py:245
  19.5 2.1 %collective-permute-start.7 = (bf16[64,896]{1,0:T(8,128)(2,1)S(1)}, bf16[64,896]{1,0:T(8,128)(2,1)S(1)}, u32[]{:S(2)}, u32[]{:S(2)}) collective-permute-start(bf16[64,896]{1,0:T(8,128)(2,1)S(1)} %collective-permute-done.4.refs_6_), channel_id=1, source_target_pairs={{0,4},{2,6},{4,12},{6,14},{12,8},{14,10},{8,0},{10,2},{1,5},{3,7},... | collective-permute-start | bytes 344072 | tf_op jit(solution)/shard_map/ppermute | solution.py:245
  21.6 1.6 %collective-permute-done.5.refs_0_ = bf16[64,896]{1,0:T(8,128)(2,1)S(1)} collective-permute-done((bf16[64,896]{1,0:T(8,128)(2,1)S(1)}, bf16[64,896]{1,0:T(8,128)(2,1)S(1)}, u32[]{:S(2)}, u32[]{:S(2)}) %collective-permute-start.5) | collective-permute-done | bytes 114720 | tf_op jit(solution)/shard_map/ppermute | solution.py:245
  23.7 1.6 %collective-permute-done.7.refs_1_ = bf16[64,896]{1,0:T(8,128)(2,1)S(1)} collective-permute-done((bf16[64,896]{1,0:T(8,128)(2,1)S(1)}, bf16[64,896]{1,0:T(8,128)(2,1)S(1)}, u32[]{:S(2)}, u32[]{:S(2)}) %collective-permute-start.7) | collective-permute-done | bytes 114720 | tf_op jit(solution)/shard_map/ppermute | solution.py:245
  25.2 0.9 %collective-permute-start.10 = (bf16[64,896]{1,0:T(8,128)(2,1)S(1)}, bf16[64,896]{1,0:T(8,128)(2,1)S(1)}, u32[]{:S(2)}, u32[]{:S(2)}) collective-permute-start(bf16[64,896]{1,0:T(8,128)(2,1)S(1)} %collective-permute-done.7.refs_1_), channel_id=1, source_target_pairs={{0,2},{2,0},{4,6},{6,4},{8,10},{10,8},{12,14},{14,12},{1,3},{3,1},... | collective-permute-start | bytes 344072 | tf_op jit(solution)/shard_map/ppermute | solution.py:245
  26.2 0.5 %shard_map.66.begun_ref = bf16[128,1792]{1,0:T(8,128)(2,1)S(1)} custom-call(s32[128,1]{1,0:T(8,128)S(1)} %get-tuple-element.15.index_ref, bf16[64,896]{1,0:T(8,128)(2,1)S(1)} %get-tuple-element.16.refs_0_, bf16[64,896]{1,0:T(8,128)(2,1)S(1)} %get-tuple-element.17.refs_1_, bf16[64,896]{1,0:T(8,128)(2,1)S(1)} %collective-permute-done.refs_2_, ...), custom_call_target="tpu_custom_call" | custom-call | flops 146800640 | bytes 458752 | tf_op jit(solution)/shard_map/pallas_call | solution.py:123
  26.7 0.8 %collective-permute-done.8.refs_2_ = bf16[64,1792]{1,0:T(8,128)(2,1)S(1)} collective-permute-done((bf16[64,1792]{1,0:T(8,128)(2,1)S(1)}, bf16[64,1792]{1,0:T(8,128)(2,1)S(1)}, u32[]{:S(2)}, u32[]{:S(2)}) %collective-permute-start.8) | collective-permute-done | bytes 229408 | tf_op jit(solution)/shard_map/ppermute | solution.py:245
  27.5 1.7 %collective-permute-done.9.refs_3_ = bf16[64,896]{1,0:T(8,128)(2,1)S(1)} collective-permute-done((bf16[64,896]{1,0:T(8,128)(2,1)S(1)}, bf16[64,896]{1,0:T(8,128)(2,1)S(1)}, u32[]{:S(2)}, u32[]{:S(2)}) %collective-permute-start.9) | collective-permute-done | bytes 114720 | tf_op jit(solution)/shard_map/ppermute | solution.py:245
  29.2 1.2 %collective-permute-done.10.refs_4_ = bf16[64,896]{1,0:T(8,128)(2,1)S(1)} collective-permute-done((bf16[64,896]{1,0:T(8,128)(2,1)S(1)}, bf16[64,896]{1,0:T(8,128)(2,1)S(1)}, u32[]{:S(2)}, u32[]{:S(2)}) %collective-permute-start.10) | collective-permute-done | bytes 114720 | tf_op jit(solution)/shard_map/ppermute | solution.py:245
  30.9 0.7 %shard_map.69.values_ref = bf16[256,1024]{1,0:T(8,128)(2,1)S(1)} custom-call(bf16[128,1792]{1,0:T(8,128)(2,1)S(1)} %shard_map.67.picked_ref, bf16[896,1024]{1,0:T(8,128)(2,1)S(1)} %copy-done.1), custom_call_target="tpu_custom_call" | custom-call | tf_op jit(solution)/shard_map/pallas_call | solution.py:204
  31.6 1.0 %shard_map.68.first_ref = f32[16,64,128]{2,1,0:T(8,128)S(1)} custom-call(bf16[128,1792]{1,0:T(8,128)(2,1)S(1)} %shard_map.67.picked_ref, bf16[896,1024]{1,0:T(8,128)(2,1)S(1)} %copy-done, bf16[128,1024]{1,0:T(8,128)(2,1)S(1)} %copy-done.2), custom_call_target="tpu_custom_call" | custom-call | tf_op jit(solution)/shard_map/pallas_call | solution.py:188
  32.7 2.6 %shard_map.70 = bf16[128,1024]{1,0:T(8,128)(2,1)} custom-call(bf16[128,1792]{1,0:T(8,128)(2,1)S(1)} %collective-permute-done.11.other_ref, bf16[896,1024]{1,0:T(8,128)(2,1)S(1)} %copy-done, bf16[896,1024]{1,0:T(8,128)(2,1)S(1)} %copy-done.1, bf16[128,1024]{1,0:T(8,128)(2,1)S(1)} %copy-done.2, f32[16,64,128]{2,1,0:T(8,128)S(1)} %shard_map.68.first_ref, ...), custom_call_target="tpu_custom_call" | custom-call | tf_op jit(solution)/shard_map/pallas_call | solution.py:234
  (21 shorter events, 1.7 us)
Async XLA Ops:
  0.0 1.0 %copy-start.3 = (bf16[64,3584]{1,0:T(8,128)(2,1)S(1)}, bf16[64,3584]{1,0:T(8,128)(2,1)}, u32[]{:S(2)}) copy-start(bf16[64,3584]{1,0:T(8,128)(2,1)} %enc_ref.1) | copy-start | bytes 1376260
  1.1 8.8 %collective-permute-start = (bf16[64,896]{1,0:T(8,128)(2,1)S(1)}, bf16[64,896]{1,0:T(8,128)(2,1)S(1)}, u32[]{:S(2)}, u32[]{:S(2)}) collective-permute-start(bf16[64,896]{1,0:T(8,128)(2,1)S(1)} %get-tuple-element.16.refs_0_), channel_id=1, source_target_pairs={{0,4},{2,6},{4,12},{6,14},{12,8},{14,10},{8,0},{10,2},{1,5},{3,7},... | collective-permute-start | bytes 344072 | tf_op jit(solution)/shard_map/ppermute | solution.py:245
  4.2 0.7 %copy-start.4 = (s32[2,64,1]{1,2,0:T(1,128)S(1)}, s32[2,64,1]{1,2,0:T(1,128)}, u32[]{:S(2)}) copy-start(s32[2,64,1]{1,2,0:T(1,128)} %param.10) | copy-start | bytes 1540
  4.9 0.7 %copy-start.5 = (s32[2,64]{1,0:T(2,128)S(1)}, s32[2,64]{1,0:T(2,128)}, u32[]{:S(2)}) copy-start(s32[2,64]{1,0:T(2,128)} %stored_ref.1) | copy-start | bytes 1540
  5.8 6.2 %collective-permute-start.1 = (bf16[64,896]{1,0:T(8,128)(2,1)S(1)}, bf16[64,896]{1,0:T(8,128)(2,1)S(1)}, u32[]{:S(2)}, u32[]{:S(2)}) collective-permute-start(bf16[64,896]{1,0:T(8,128)(2,1)S(1)} %get-tuple-element.17.refs_1_), channel_id=1, source_target_pairs={{0,4},{2,6},{4,12},{6,14},{12,8},{14,10},{8,0},{10,2},{1,5},{3,7},... | collective-permute-start | bytes 344072 | tf_op jit(solution)/shard_map/ppermute | solution.py:245
  8.5 7.9 %collective-permute-start.3 = (bf16[64,1792]{1,0:T(8,128)(2,1)S(1)}, bf16[64,1792]{1,0:T(8,128)(2,1)S(1)}, u32[]{:S(2)}, u32[]{:S(2)}) collective-permute-start(bf16[64,1792]{1,0:T(8,128)(2,1)S(1)} %get-tuple-element.18), channel_id=1, source_target_pairs={{0,2},{2,0},{4,6},{6,4},{8,10},{10,8},{12,14},{14,12},{1,3},{3,1},... | collective-permute-start | bytes 688136 | tf_op jit(solution)/shard_map/ppermute | solution.py:245
  10.0 6.2 %collective-permute-start.2 = (bf16[64,896]{1,0:T(8,128)(2,1)S(1)}, bf16[64,896]{1,0:T(8,128)(2,1)S(1)}, u32[]{:S(2)}, u32[]{:S(2)}) collective-permute-start(bf16[64,896]{1,0:T(8,128)(2,1)S(1)} %collective-permute-done.refs_2_), channel_id=1, source_target_pairs={{0,4},{2,6},{4,12},{6,14},{12,8},{14,10},{8,0},{10,2},{1,5},{3,7},... | collective-permute-start | bytes 344072 | tf_op jit(solution)/shard_map/ppermute | solution.py:245
  12.0 6.3 %collective-permute-start.4 = (bf16[64,896]{1,0:T(8,128)(2,1)S(1)}, bf16[64,896]{1,0:T(8,128)(2,1)S(1)}, u32[]{:S(2)}, u32[]{:S(2)}) collective-permute-start(bf16[64,896]{1,0:T(8,128)(2,1)S(1)} %collective-permute-done.1.refs_3_), channel_id=1, source_target_pairs={{0,4},{2,6},{4,12},{6,14},{12,8},{14,10},{8,0},{10,2},{1,5},{3,7},... | collective-permute-start | bytes 344072 | tf_op jit(solution)/shard_map/ppermute | solution.py:245
  14.5 16.4 %copy-start.1 = (bf16[896,1024]{1,0:T(8,128)(2,1)S(1)}, bf16[896,1024]{1,0:T(8,128)(2,1)}, u32[]{:S(2)}) copy-start(bf16[896,1024]{1,0:T(8,128)(2,1)} %wv_ref.3) | copy-start | bytes 5505028
  14.5 8.7 %collective-permute-start.6 = (bf16[64,1792]{1,0:T(8,128)(2,1)S(1)}, bf16[64,1792]{1,0:T(8,128)(2,1)S(1)}, u32[]{:S(2)}, u32[]{:S(2)}) collective-permute-start(bf16[64,1792]{1,0:T(8,128)(2,1)S(1)} %pad_maximum_fusion), channel_id=1, source_target_pairs={{0,2},{2,0},{4,6},{6,4},{8,10},{10,8},{12,14},{14,12},{1,3},{3,1},... | collective-permute-start | bytes 688136 | tf_op jit(solution)/shard_map/ppermute | solution.py:245
  16.4 6.9 %collective-permute-start.5 = (bf16[64,896]{1,0:T(8,128)(2,1)S(1)}, bf16[64,896]{1,0:T(8,128)(2,1)S(1)}, u32[]{:S(2)}, u32[]{:S(2)}) collective-permute-start(bf16[64,896]{1,0:T(8,128)(2,1)S(1)} %collective-permute-done.2.refs_5_), channel_id=1, source_target_pairs={{0,4},{2,6},{4,12},{6,14},{12,8},{14,10},{8,0},{10,2},{1,5},{3,7},... | collective-permute-start | bytes 344072 | tf_op jit(solution)/shard_map/ppermute | solution.py:245
  18.4 9.1 %collective-permute-start.8 = (bf16[64,1792]{1,0:T(8,128)(2,1)S(1)}, bf16[64,1792]{1,0:T(8,128)(2,1)S(1)}, u32[]{:S(2)}, u32[]{:S(2)}) collective-permute-start(bf16[64,1792]{1,0:T(8,128)(2,1)S(1)} %pad_maximum_fusion.1), channel_id=1, source_target_pairs={{0,2},{2,0},{4,6},{6,4},{8,10},{10,8},{12,14},{14,12},{1,3},{3,1},... | collective-permute-start | bytes 688136 | tf_op jit(solution)/shard_map/ppermute | solution.py:245
  19.5 5.7 %collective-permute-start.7 = (bf16[64,896]{1,0:T(8,128)(2,1)S(1)}, bf16[64,896]{1,0:T(8,128)(2,1)S(1)}, u32[]{:S(2)}, u32[]{:S(2)}) collective-permute-start(bf16[64,896]{1,0:T(8,128)(2,1)S(1)} %collective-permute-done.4.refs_6_), channel_id=1, source_target_pairs={{0,4},{2,6},{4,12},{6,14},{12,8},{14,10},{8,0},{10,2},{1,5},{3,7},... | collective-permute-start | bytes 344072 | tf_op jit(solution)/shard_map/ppermute | solution.py:245
  23.3 5.9 %collective-permute-start.9 = (bf16[64,896]{1,0:T(8,128)(2,1)S(1)}, bf16[64,896]{1,0:T(8,128)(2,1)S(1)}, u32[]{:S(2)}, u32[]{:S(2)}) collective-permute-start(bf16[64,896]{1,0:T(8,128)(2,1)S(1)} %collective-permute-done.5.refs_0_), channel_id=1, source_target_pairs={{0,2},{2,0},{4,6},{6,4},{8,10},{10,8},{12,14},{14,12},{1,3},{3,1},... | collective-permute-start | bytes 344072 | tf_op jit(solution)/shard_map/ppermute | solution.py:245
  25.2 5.2 %collective-permute-start.10 = (bf16[64,896]{1,0:T(8,128)(2,1)S(1)}, bf16[64,896]{1,0:T(8,128)(2,1)S(1)}, u32[]{:S(2)}, u32[]{:S(2)}) collective-permute-start(bf16[64,896]{1,0:T(8,128)(2,1)S(1)} %collective-permute-done.7.refs_1_), channel_id=1, source_target_pairs={{0,2},{2,0},{4,6},{6,4},{8,10},{10,8},{12,14},{14,12},{1,3},{3,1},... | collective-permute-start | bytes 344072 | tf_op jit(solution)/shard_map/ppermute | solution.py:245
  26.7 5.0 %copy-start = (bf16[896,1024]{1,0:T(8,128)(2,1)S(1)}, bf16[896,1024]{1,0:T(8,128)(2,1)}, u32[]{:S(2)}) copy-start(bf16[896,1024]{1,0:T(8,128)(2,1)} %wk_ref.3) | copy-start | bytes 5505028
  26.7 5.0 %copy-start.2 = (bf16[128,1024]{1,0:T(8,128)(2,1)S(1)}, bf16[128,1024]{1,0:T(8,128)(2,1)}, u32[]{:S(2)}) copy-start(bf16[128,1024]{1,0:T(8,128)(2,1)} %query_ref.3) | copy-start | bytes 786436
  30.8 1.9 %collective-permute-start.11 = (bf16[128,1792]{1,0:T(8,128)(2,1)S(1)}, bf16[128,1792]{1,0:T(8,128)(2,1)S(1)}, u32[]{:S(2)}, u32[]{:S(2)}) collective-permute-start(bf16[128,1792]{1,0:T(8,128)(2,1)S(1)} %shard_map.67.picked_ref), channel_id=1, source_target_pairs={{0,1},{1,0},{2,3},{3,2},{4,5},{5,4},{6,7},{7,6},{8,9},{9,8},{10,11... | collective-permute-start | bytes 1376264 | tf_op jit(solution)/shard_map/ppermute | solution.py:278

commit v7 on v6

--- a/solution.py
+++ b/solution.py
@@ -265,10 +265,10 @@
     for k in range(1, turns):
         behind = held[k - 1, 0]
         steps = [send(piece, onward) for piece in behind]
-        joined = whole if k == 1 else jnp.concatenate(behind, axis=1)
-        held[k - 1, 1] = [send(joined, across)]
-        if k > 1:
-            steps[0], held[k - 2, 1][0] = lax.optimization_barrier((steps[0], held[k - 2, 1][0]))
+        if k < turns - 1:
+            held[k - 1, 1] = [send(whole if k == 1 else jnp.concatenate(behind, axis=1), across)]
+        else:
+            held[k - 1, 1] = [send(piece, across) for piece in behind]
         held[k, 0] = steps
     held[turns - 1, 1] = [send(piece, across) for piece in held[turns - 1, 0]]
     late = 3

time: 35.4 us -> 35.4 us (level)
  starting transfers between devices: 16.7 us -> 19 us
  waiting for transfers between devices: 10.5 us -> 8.2 us
    ppermute x11 -> x12, starting transfers between devices: 16.6 us -> 19 us  [send(): return lax.ppermute(chunk, 'wide', pairs)]
    ppermute x11 -> x12, waiting for transfers between devices: 10.5 us -> 8.16 us  [send(): return lax.ppermute(chunk, 'wide', pairs)]
  transfers between devices with their start and end apart: 12 -> 13, of which waited for: 9 -> 8; matrix products, arithmetic and copies ran while one was open for 0% -> 0% of each run, Pallas kernels for 7% -> 7%
where the time goes in v7:
time: 35.4 us; the launch traced here: 35.2 us
  starting transfers between devices  19 us (54%)
  waiting for transfers between devices  8.2 us (23%)
  Pallas kernels  5.48 us (15%)
  local copies, waits for them, and re-layouts  2.39 us (7%)
    ppermute x12, starting transfers between devices, send(): return lax.ppermute(chunk, 'wide', pairs)  19 us
    ppermute x12, waiting for transfers between devices, send(): return lax.ppermute(chunk, 'wide', pairs)  8.16 us
    pallas_call x1, Pallas kernels, attend(): pl.pallas_call(functools.partial(attend_kernel, spans), out_shape=jax.Sha...  2.56 us
    unnamed x12, local copies, waits for them, and re-layouts  2.39 us
    pallas_call x1, Pallas kernels, own_scores(): pl.pallas_call(functools.partial(score_kernel, spans), out_shape=jax.Shap...  1.02 us
  transfers between devices with their start and end apart: 13, of which 8 were waited for; matrix products, arithmetic and copies ran while one was open for 0% of the time, Pallas kernels for 7%

profile of v7, /device:TPU:0, one launch (start us, length us, event | category | flops | bytes accessed | tf_op | source)
XLA Modules:
  0.0 35.2 jit_solution(11069431404833205278)
XLA Ops:
  0.0 1.0 %copy-done.3 = bf16[64,3584]{1,0:T(8,128)(2,1)S(1)} copy-done((bf16[64,3584]{1,0:T(8,128)(2,1)S(1)}, bf16[64,3584]{1,0:T(8,128)(2,1)}, u32[]{:S(2)}) %copy-start.3) | copy-done | bytes 458776
  1.1 3.1 %collective-permute-start = (bf16[64,896]{1,0:T(8,128)(2,1)S(1)}, bf16[64,896]{1,0:T(8,128)(2,1)S(1)}, u32[]{:S(2)}, u32[]{:S(2)}) collective-permute-start(bf16[64,896]{1,0:T(8,128)(2,1)S(1)} %get-tuple-element.12.refs_0_), channel_id=1, source_target_pairs={{0,4},{2,6},{4,12},{6,14},{12,8},{14,10},{8,0},{10,2},{1,5},{3,7},... | collective-permute-start | bytes 344072 | tf_op jit(solution)/shard_map/ppermute | solution.py:245
  4.2 0.7 %copy-done.4 = s32[2,64,1]{1,2,0:T(1,128)S(1)} copy-done((s32[2,64,1]{1,2,0:T(1,128)S(1)}, s32[2,64,1]{1,2,0:T(1,128)}, u32[]{:S(2)}) %copy-start.4) | copy-done | bytes 536
  4.9 0.7 %copy-done.5 = s32[2,64]{1,0:T(2,128)S(1)} copy-done((s32[2,64]{1,0:T(2,128)S(1)}, s32[2,64]{1,0:T(2,128)}, u32[]{:S(2)}) %copy-start.5) | copy-done | bytes 536
  5.8 2.6 %collective-permute-start.1 = (bf16[64,896]{1,0:T(8,128)(2,1)S(1)}, bf16[64,896]{1,0:T(8,128)(2,1)S(1)}, u32[]{:S(2)}, u32[]{:S(2)}) collective-permute-start(bf16[64,896]{1,0:T(8,128)(2,1)S(1)} %get-tuple-element.13.refs_1_), channel_id=1, source_target_pairs={{0,4},{2,6},{4,12},{6,14},{12,8},{14,10},{8,0},{10,2},{1,5},{3,7},... | collective-permute-start | bytes 344072 | tf_op jit(solution)/shard_map/ppermute | solution.py:245
  8.5 1.5 %collective-permute-start.2 = (bf16[64,1792]{1,0:T(8,128)(2,1)S(1)}, bf16[64,1792]{1,0:T(8,128)(2,1)S(1)}, u32[]{:S(2)}, u32[]{:S(2)}) collective-permute-start(bf16[64,1792]{1,0:T(8,128)(2,1)S(1)} %get-tuple-element.14), channel_id=1, source_target_pairs={{0,2},{2,0},{4,6},{6,4},{8,10},{10,8},{12,14},{14,12},{1,3},{3,1},... | collective-permute-start | bytes 688136 | tf_op jit(solution)/shard_map/ppermute | solution.py:245
  10.4 1.6 %collective-permute-done.1.refs_3_ = bf16[64,896]{1,0:T(8,128)(2,1)S(1)} collective-permute-done((bf16[64,896]{1,0:T(8,128)(2,1)S(1)}, bf16[64,896]{1,0:T(8,128)(2,1)S(1)}, u32[]{:S(2)}, u32[]{:S(2)}) %collective-permute-start.1) | collective-permute-done | bytes 114720 | tf_op jit(solution)/shard_map/ppermute | solution.py:245
  12.0 2.5 %collective-permute-start.4 = (bf16[64,896]{1,0:T(8,128)(2,1)S(1)}, bf16[64,896]{1,0:T(8,128)(2,1)S(1)}, u32[]{:S(2)}, u32[]{:S(2)}) collective-permute-start(bf16[64,896]{1,0:T(8,128)(2,1)S(1)} %collective-permute-done.1.refs_3_), channel_id=1, source_target_pairs={{0,4},{2,6},{4,12},{6,14},{12,8},{14,10},{8,0},{10,2},{1,5},{3,7},... | collective-permute-start | bytes 344072 | tf_op jit(solution)/shard_map/ppermute | solution.py:245
  14.5 1.4 %collective-permute-start.5 = (bf16[64,1792]{1,0:T(8,128)(2,1)S(1)}, bf16[64,1792]{1,0:T(8,128)(2,1)S(1)}, u32[]{:S(2)}, u32[]{:S(2)}) collective-permute-start(bf16[64,1792]{1,0:T(8,128)(2,1)S(1)} %pad_maximum_fusion), channel_id=1, source_target_pairs={{0,2},{2,0},{4,6},{6,4},{8,10},{10,8},{12,14},{14,12},{1,3},{3,1},... | collective-permute-start | bytes 688136 | tf_op jit(solution)/shard_map/ppermute | solution.py:245
  16.1 0.8 %collective-permute-start.6 = (bf16[64,896]{1,0:T(8,128)(2,1)S(1)}, bf16[64,896]{1,0:T(8,128)(2,1)S(1)}, u32[]{:S(2)}, u32[]{:S(2)}) collective-permute-start(bf16[64,896]{1,0:T(8,128)(2,1)S(1)} %collective-permute-done.3.refs_5_), channel_id=1, source_target_pairs={{0,4},{2,6},{4,12},{6,14},{12,8},{14,10},{8,0},{10,2},{1,5},{3,7},... | collective-permute-start | bytes 344072 | tf_op jit(solution)/shard_map/ppermute | solution.py:245
  16.9 1.6 %collective-permute-done.4.refs_6_ = bf16[64,896]{1,0:T(8,128)(2,1)S(1)} collective-permute-done((bf16[64,896]{1,0:T(8,128)(2,1)S(1)}, bf16[64,896]{1,0:T(8,128)(2,1)S(1)}, u32[]{:S(2)}, u32[]{:S(2)}) %collective-permute-start.4) | collective-permute-done | bytes 114720 | tf_op jit(solution)/shard_map/ppermute | solution.py:245
  18.5 2.0 %collective-permute-start.7 = (bf16[64,896]{1,0:T(8,128)(2,1)S(1)}, bf16[64,896]{1,0:T(8,128)(2,1)S(1)}, u32[]{:S(2)}, u32[]{:S(2)}) collective-permute-start(bf16[64,896]{1,0:T(8,128)(2,1)S(1)} %collective-permute-done.4.refs_6_), channel_id=1, source_target_pairs={{0,4},{2,6},{4,12},{6,14},{12,8},{14,10},{8,0},{10,2},{1,5},{3,7},... | collective-permute-start | bytes 344072 | tf_op jit(solution)/shard_map/ppermute | solution.py:245
  20.5 1.0 %collective-permute-start.8 = (bf16[64,896]{1,0:T(8,128)(2,1)S(1)}, bf16[64,896]{1,0:T(8,128)(2,1)S(1)}, u32[]{:S(2)}, u32[]{:S(2)}) collective-permute-start(bf16[64,896]{1,0:T(8,128)(2,1)S(1)} %collective-permute-done.3.refs_5_), channel_id=1, source_target_pairs={{0,2},{2,0},{4,6},{6,4},{8,10},{10,8},{12,14},{14,12},{1,3},{3,1},... | collective-permute-start | bytes 344072 | tf_op jit(solution)/shard_map/ppermute | solution.py:245
  21.5 1.0 %collective-permute-start.9 = (bf16[64,896]{1,0:T(8,128)(2,1)S(1)}, bf16[64,896]{1,0:T(8,128)(2,1)S(1)}, u32[]{:S(2)}, u32[]{:S(2)}) collective-permute-start(bf16[64,896]{1,0:T(8,128)(2,1)S(1)} %collective-permute-done.4.refs_6_), channel_id=1, source_target_pairs={{0,2},{2,0},{4,6},{6,4},{8,10},{10,8},{12,14},{14,12},{1,3},{3,1},... | collective-permute-start | bytes 344072 | tf_op jit(solution)/shard_map/ppermute | solution.py:245
  22.5 1.0 %collective-permute-start.10 = (bf16[64,896]{1,0:T(8,128)(2,1)S(1)}, bf16[64,896]{1,0:T(8,128)(2,1)S(1)}, u32[]{:S(2)}, u32[]{:S(2)}) collective-permute-start(bf16[64,896]{1,0:T(8,128)(2,1)S(1)} %collective-permute-done.6.refs_0_), channel_id=1, source_target_pairs={{0,2},{2,0},{4,6},{6,4},{8,10},{10,8},{12,14},{14,12},{1,3},{3,1},... | collective-permute-start | bytes 344072 | tf_op jit(solution)/shard_map/ppermute | solution.py:245
  23.6 0.6 %collective-permute-done.7.refs_1_ = bf16[64,896]{1,0:T(8,128)(2,1)S(1)} collective-permute-done((bf16[64,896]{1,0:T(8,128)(2,1)S(1)}, bf16[64,896]{1,0:T(8,128)(2,1)S(1)}, u32[]{:S(2)}, u32[]{:S(2)}) %collective-permute-start.7) | collective-permute-done | bytes 114720 | tf_op jit(solution)/shard_map/ppermute | solution.py:245
  24.2 1.6 %collective-permute-start.11 = (bf16[64,896]{1,0:T(8,128)(2,1)S(1)}, bf16[64,896]{1,0:T(8,128)(2,1)S(1)}, u32[]{:S(2)}, u32[]{:S(2)}) collective-permute-start(bf16[64,896]{1,0:T(8,128)(2,1)S(1)} %collective-permute-done.7.refs_1_), channel_id=1, source_target_pairs={{0,2},{2,0},{4,6},{6,4},{8,10},{10,8},{12,14},{14,12},{1,3},{3,1},... | collective-permute-start | bytes 344072 | tf_op jit(solution)/shard_map/ppermute | solution.py:245
  25.8 0.5 %shard_map.66.begun_ref = bf16[128,1792]{1,0:T(8,128)(2,1)S(1)} custom-call(s32[128,1]{1,0:T(8,128)S(1)} %get-tuple-element.11.index_ref, bf16[64,896]{1,0:T(8,128)(2,1)S(1)} %get-tuple-element.12.refs_0_, bf16[64,896]{1,0:T(8,128)(2,1)S(1)} %get-tuple-element.13.refs_1_, bf16[64,896]{1,0:T(8,128)(2,1)S(1)} %collective-permute-done.refs_2_, ...), custom_call_target="tpu_custom_call" | custom-call | flops 146800640 | bytes 458752 | tf_op jit(solution)/shard_map/pallas_call | solution.py:123
  26.6 1.4 %collective-permute-done.9.refs_3_ = bf16[64,896]{1,0:T(8,128)(2,1)S(1)} collective-permute-done((bf16[64,896]{1,0:T(8,128)(2,1)S(1)}, bf16[64,896]{1,0:T(8,128)(2,1)S(1)}, u32[]{:S(2)}, u32[]{:S(2)}) %collective-permute-start.9) | collective-permute-done | bytes 114720 | tf_op jit(solution)/shard_map/ppermute | solution.py:245
  28.0 1.2 %collective-permute-done.10.refs_4_ = bf16[64,896]{1,0:T(8,128)(2,1)S(1)} collective-permute-done((bf16[64,896]{1,0:T(8,128)(2,1)S(1)}, bf16[64,896]{1,0:T(8,128)(2,1)S(1)}, u32[]{:S(2)}, u32[]{:S(2)}) %collective-permute-start.10) | collective-permute-done | bytes 114720 | tf_op jit(solution)/shard_map/ppermute | solution.py:245
  29.2 1.2 %collective-permute-done.11.refs_5_ = bf16[64,896]{1,0:T(8,128)(2,1)S(1)} collective-permute-done((bf16[64,896]{1,0:T(8,128)(2,1)S(1)}, bf16[64,896]{1,0:T(8,128)(2,1)S(1)}, u32[]{:S(2)}, u32[]{:S(2)}) %collective-permute-start.11) | collective-permute-done | bytes 114720 | tf_op jit(solution)/shard_map/ppermute | solution.py:245
  30.9 0.7 %shard_map.69.values_ref = bf16[256,1024]{1,0:T(8,128)(2,1)S(1)} custom-call(bf16[128,1792]{1,0:T(8,128)(2,1)S(1)} %shard_map.67.picked_ref, bf16[896,1024]{1,0:T(8,128)(2,1)S(1)} %copy-done.1), custom_call_target="tpu_custom_call" | custom-call | tf_op jit(solution)/shard_map/pallas_call | solution.py:204
  31.6 1.0 %shard_map.68.first_ref = f32[16,64,128]{2,1,0:T(8,128)S(1)} custom-call(bf16[128,1792]{1,0:T(8,128)(2,1)S(1)} %shard_map.67.picked_ref, bf16[896,1024]{1,0:T(8,128)(2,1)S(1)} %copy-done, bf16[128,1024]{1,0:T(8,128)(2,1)S(1)} %copy-done.2), custom_call_target="tpu_custom_call" | custom-call | tf_op jit(solution)/shard_map/pallas_call | solution.py:188
  32.7 2.6 %shard_map.70 = bf16[128,1024]{1,0:T(8,128)(2,1)} custom-call(bf16[128,1792]{1,0:T(8,128)(2,1)S(1)} %collective-permute-done.12.other_ref, bf16[896,1024]{1,0:T(8,128)(2,1)S(1)} %copy-done, bf16[896,1024]{1,0:T(8,128)(2,1)S(1)} %copy-done.1, bf16[128,1024]{1,0:T(8,128)(2,1)S(1)} %copy-done.2, f32[16,64,128]{2,1,0:T(8,128)S(1)} %shard_map.68.first_ref, ...), custom_call_target="tpu_custom_call" | custom-call | tf_op jit(solution)/shard_map/pallas_call | solution.py:234
  (22 shorter events, 1.9 us)
Async XLA Ops:
  0.0 1.0 %copy-start.3 = (bf16[64,3584]{1,0:T(8,128)(2,1)S(1)}, bf16[64,3584]{1,0:T(8,128)(2,1)}, u32[]{:S(2)}) copy-start(bf16[64,3584]{1,0:T(8,128)(2,1)} %enc_ref.1) | copy-start | bytes 1376260
  1.1 8.8 %collective-permute-start = (bf16[64,896]{1,0:T(8,128)(2,1)S(1)}, bf16[64,896]{1,0:T(8,128)(2,1)S(1)}, u32[]{:S(2)}, u32[]{:S(2)}) collective-permute-start(bf16[64,896]{1,0:T(8,128)(2,1)S(1)} %get-tuple-element.12.refs_0_), channel_id=1, source_target_pairs={{0,4},{2,6},{4,12},{6,14},{12,8},{14,10},{8,0},{10,2},{1,5},{3,7},... | collective-permute-start | bytes 344072 | tf_op jit(solution)/shard_map/ppermute | solution.py:245
  4.2 0.7 %copy-start.4 = (s32[2,64,1]{1,2,0:T(1,128)S(1)}, s32[2,64,1]{1,2,0:T(1,128)}, u32[]{:S(2)}) copy-start(s32[2,64,1]{1,2,0:T(1,128)} %param.10) | copy-start | bytes 1540
  4.9 0.7 %copy-start.5 = (s32[2,64]{1,0:T(2,128)S(1)}, s32[2,64]{1,0:T(2,128)}, u32[]{:S(2)}) copy-start(s32[2,64]{1,0:T(2,128)} %stored_ref.1) | copy-start | bytes 1540
  5.8 6.2 %collective-permute-start.1 = (bf16[64,896]{1,0:T(8,128)(2,1)S(1)}, bf16[64,896]{1,0:T(8,128)(2,1)S(1)}, u32[]{:S(2)}, u32[]{:S(2)}) collective-permute-start(bf16[64,896]{1,0:T(8,128)(2,1)S(1)} %get-tuple-element.13.refs_1_), channel_id=1, source_target_pairs={{0,4},{2,6},{4,12},{6,14},{12,8},{14,10},{8,0},{10,2},{1,5},{3,7},... | collective-permute-start | bytes 344072 | tf_op jit(solution)/shard_map/ppermute | solution.py:245
  8.5 22.4 %copy-start.1 = (bf16[896,1024]{1,0:T(8,128)(2,1)S(1)}, bf16[896,1024]{1,0:T(8,128)(2,1)}, u32[]{:S(2)}) copy-start(bf16[896,1024]{1,0:T(8,128)(2,1)} %wv_ref.3) | copy-start | bytes 5505028
  8.5 13.1 %collective-permute-start.2 = (bf16[64,1792]{1,0:T(8,128)(2,1)S(1)}, bf16[64,1792]{1,0:T(8,128)(2,1)S(1)}, u32[]{:S(2)}, u32[]{:S(2)}) collective-permute-start(bf16[64,1792]{1,0:T(8,128)(2,1)S(1)} %get-tuple-element.14), channel_id=1, source_target_pairs={{0,2},{2,0},{4,6},{6,4},{8,10},{10,8},{12,14},{14,12},{1,3},{3,1},... | collective-permute-start | bytes 688136 | tf_op jit(solution)/shard_map/ppermute | solution.py:245
  10.0 6.2 %collective-permute-start.3 = (bf16[64,896]{1,0:T(8,128)(2,1)S(1)}, bf16[64,896]{1,0:T(8,128)(2,1)S(1)}, u32[]{:S(2)}, u32[]{:S(2)}) collective-permute-start(bf16[64,896]{1,0:T(8,128)(2,1)S(1)} %collective-permute-done.refs_2_), channel_id=1, source_target_pairs={{0,4},{2,6},{4,12},{6,14},{12,8},{14,10},{8,0},{10,2},{1,5},{3,7},... | collective-permute-start | bytes 344072 | tf_op jit(solution)/shard_map/ppermute | solution.py:245
  12.0 6.5 %collective-permute-start.4 = (bf16[64,896]{1,0:T(8,128)(2,1)S(1)}, bf16[64,896]{1,0:T(8,128)(2,1)S(1)}, u32[]{:S(2)}, u32[]{:S(2)}) collective-permute-start(bf16[64,896]{1,0:T(8,128)(2,1)S(1)} %collective-permute-done.1.refs_3_), channel_id=1, source_target_pairs={{0,4},{2,6},{4,12},{6,14},{12,8},{14,10},{8,0},{10,2},{1,5},{3,7},... | collective-permute-start | bytes 344072 | tf_op jit(solution)/shard_map/ppermute | solution.py:245
  14.5 11.2 %collective-permute-start.5 = (bf16[64,1792]{1,0:T(8,128)(2,1)S(1)}, bf16[64,1792]{1,0:T(8,128)(2,1)S(1)}, u32[]{:S(2)}, u32[]{:S(2)}) collective-permute-start(bf16[64,1792]{1,0:T(8,128)(2,1)S(1)} %pad_maximum_fusion), channel_id=1, source_target_pairs={{0,2},{2,0},{4,6},{6,4},{8,10},{10,8},{12,14},{14,12},{1,3},{3,1},... | collective-permute-start | bytes 688136 | tf_op jit(solution)/shard_map/ppermute | solution.py:245
  16.1 6.4 %collective-permute-start.6 = (bf16[64,896]{1,0:T(8,128)(2,1)S(1)}, bf16[64,896]{1,0:T(8,128)(2,1)S(1)}, u32[]{:S(2)}, u32[]{:S(2)}) collective-permute-start(bf16[64,896]{1,0:T(8,128)(2,1)S(1)} %collective-permute-done.3.refs_5_), channel_id=1, source_target_pairs={{0,4},{2,6},{4,12},{6,14},{12,8},{14,10},{8,0},{10,2},{1,5},{3,7},... | collective-permute-start | bytes 344072 | tf_op jit(solution)/shard_map/ppermute | solution.py:245
  18.5 5.7 %collective-permute-start.7 = (bf16[64,896]{1,0:T(8,128)(2,1)S(1)}, bf16[64,896]{1,0:T(8,128)(2,1)S(1)}, u32[]{:S(2)}, u32[]{:S(2)}) collective-permute-start(bf16[64,896]{1,0:T(8,128)(2,1)S(1)} %collective-permute-done.4.refs_6_), channel_id=1, source_target_pairs={{0,4},{2,6},{4,12},{6,14},{12,8},{14,10},{8,0},{10,2},{1,5},{3,7},... | collective-permute-start | bytes 344072 | tf_op jit(solution)/shard_map/ppermute | solution.py:245
  20.5 6.1 %collective-permute-start.8 = (bf16[64,896]{1,0:T(8,128)(2,1)S(1)}, bf16[64,896]{1,0:T(8,128)(2,1)S(1)}, u32[]{:S(2)}, u32[]{:S(2)}) collective-permute-start(bf16[64,896]{1,0:T(8,128)(2,1)S(1)} %collective-permute-done.3.refs_5_), channel_id=1, source_target_pairs={{0,2},{2,0},{4,6},{6,4},{8,10},{10,8},{12,14},{14,12},{1,3},{3,1},... | collective-permute-start | bytes 344072 | tf_op jit(solution)/shard_map/ppermute | solution.py:245
  21.5 6.4 %collective-permute-start.9 = (bf16[64,896]{1,0:T(8,128)(2,1)S(1)}, bf16[64,896]{1,0:T(8,128)(2,1)S(1)}, u32[]{:S(2)}, u32[]{:S(2)}) collective-permute-start(bf16[64,896]{1,0:T(8,128)(2,1)S(1)} %collective-permute-done.4.refs_6_), channel_id=1, source_target_pairs={{0,2},{2,0},{4,6},{6,4},{8,10},{10,8},{12,14},{14,12},{1,3},{3,1},... | collective-permute-start | bytes 344072 | tf_op jit(solution)/shard_map/ppermute | solution.py:245
  22.5 6.7 %collective-permute-start.10 = (bf16[64,896]{1,0:T(8,128)(2,1)S(1)}, bf16[64,896]{1,0:T(8,128)(2,1)S(1)}, u32[]{:S(2)}, u32[]{:S(2)}) collective-permute-start(bf16[64,896]{1,0:T(8,128)(2,1)S(1)} %collective-permute-done.6.refs_0_), channel_id=1, source_target_pairs={{0,2},{2,0},{4,6},{6,4},{8,10},{10,8},{12,14},{14,12},{1,3},{3,1},... | collective-permute-start | bytes 344072 | tf_op jit(solution)/shard_map/ppermute | solution.py:245
  24.2 6.3 %collective-permute-start.11 = (bf16[64,896]{1,0:T(8,128)(2,1)S(1)}, bf16[64,896]{1,0:T(8,128)(2,1)S(1)}, u32[]{:S(2)}, u32[]{:S(2)}) collective-permute-start(bf16[64,896]{1,0:T(8,128)(2,1)S(1)} %collective-permute-done.7.refs_1_), channel_id=1, source_target_pairs={{0,2},{2,0},{4,6},{6,4},{8,10},{10,8},{12,14},{14,12},{1,3},{3,1},... | collective-permute-start | bytes 344072 | tf_op jit(solution)/shard_map/ppermute | solution.py:245
  26.3 5.3 %copy-start = (bf16[896,1024]{1,0:T(8,128)(2,1)S(1)}, bf16[896,1024]{1,0:T(8,128)(2,1)}, u32[]{:S(2)}) copy-start(bf16[896,1024]{1,0:T(8,128)(2,1)} %wk_ref.3) | copy-start | bytes 5505028
  26.3 5.3 %copy-start.2 = (bf16[128,1024]{1,0:T(8,128)(2,1)S(1)}, bf16[128,1024]{1,0:T(8,128)(2,1)}, u32[]{:S(2)}) copy-start(bf16[128,1024]{1,0:T(8,128)(2,1)} %query_ref.3) | copy-start | bytes 786436
  30.8 1.9 %collective-permute-start.12 = (bf16[128,1792]{1,0:T(8,128)(2,1)S(1)}, bf16[128,1792]{1,0:T(8,128)(2,1)S(1)}, u32[]{:S(2)}, u32[]{:S(2)}) collective-permute-start(bf16[128,1792]{1,0:T(8,128)(2,1)S(1)} %shard_map.67.picked_ref), channel_id=1, source_target_pairs={{0,1},{1,0},{2,3},{3,2},{4,5},{5,4},{6,7},{7,6},{8,9},{9,8},{10,11... | collective-permute-start | bytes 1376264 | tf_op jit(solution)/shard_map/ppermute | solution.py:278

commit v8 on v6

--- a/solution.py
+++ b/solution.py
@@ -91,25 +91,18 @@
     return jnp.concatenate(columns, axis=0).astype(jnp.int32)
 
 
-def places_kernel(order, turns, owner_ref, stored_ref, piece_ref, index_ref, piece_out, sem):
-    copy = pltpu.make_async_copy(piece_ref, piece_out, sem)
-    copy.start()
-    index_ref[...] = wanted_rows(order, turns, piece_ref.shape[0], owner_ref, stored_ref)
-    copy.wait()
-
-
-def places(order, turns, owners, stored, piece):
-    return pl.pallas_call(
-        functools.partial(places_kernel, order, turns),
-        out_shape=(
-            jax.ShapeDtypeStruct((stored.size, 1), jnp.int32),
-            jax.ShapeDtypeStruct(piece.shape, piece.dtype),
-        ),
-        in_specs=[VMEM] * 3,
-        out_specs=(VMEM, VMEM),
-        scratch_shapes=[pltpu.SemaphoreType.DMA],
-        compiler_params=params(),
-    )(owners, stored, piece)
+def places_kernel(order, turns, rows, owner_ref, stored_ref, index_ref):
+    index_ref[...] = wanted_rows(order, turns, rows, owner_ref, stored_ref)
+
+
+def places(order, turns, rows, owners, stored):
+    return pl.pallas_call(
+        functools.partial(places_kernel, order, turns, rows),
+        out_shape=jax.ShapeDtypeStruct((stored.size, 1), jnp.int32),
+        in_specs=[VMEM] * 2,
+        out_specs=VMEM,
+        compiler_params=params(),
+    )(owners, stored)
 
 
 def early_kernel(chunks, index_ref, *refs):
@@ -255,22 +248,22 @@
         (here * SIDE + x, there * SIDE + x) for here, there in zip(line, line[1:] + line[:1]) for x in range(SIDE)
     ]
     across = [(n, n + 1 if n % SIDE == 0 else n - 1) for n in range(wide_count)]
+    backward = [(there, here) for here, there in onward]
     *pieces, whole = half_columns(encodings)
-    order = [(0, 0)]
-    for k in range(1, turns):
-        order += [(k, 0), (k - 1, 1)]
-    order.append((turns - 1, 1))
-    index, pieces[-1] = places(order, turns, jnp.transpose(block_owner, (0, 2, 1)), block_row, pieces[-1])
     held = {(0, 0): pieces}
-    for k in range(1, turns):
-        behind = held[k - 1, 0]
-        steps = [send(piece, onward) for piece in behind]
-        joined = whole if k == 1 else jnp.concatenate(behind, axis=1)
+    ahead = turns // 2
+    for k in range(1, ahead + 1):
+        held[k, 0] = [send(piece, onward) for piece in held[k - 1, 0]]
+        joined = whole if k == 1 else jnp.concatenate(held[k - 1, 0], axis=1)
         held[k - 1, 1] = [send(joined, across)]
-        if k > 1:
-            steps[0], held[k - 2, 1][0] = lax.optimization_barrier((steps[0], held[k - 2, 1][0]))
-        held[k, 0] = steps
-    held[turns - 1, 1] = [send(piece, across) for piece in held[turns - 1, 0]]
+    returned = whole
+    for k in range(turns - 1, ahead, -1):
+        returned = send(returned, backward)
+        held[k, 0], held[k, 1] = [returned], [send(returned, across)]
+    held[ahead, 1] = [send(piece, across) for piece in held[ahead, 0]]
+    last = [(ahead, 0), (ahead + 1, 1), (ahead, 1)]
+    order = [chunk for chunk in held if chunk not in last] + last
+    index = places(order, turns, rows, jnp.transpose(block_owner, (0, 2, 1)), block_row)
     late = 3
     sources = [held[chunk] for chunk in order]
     begun = early(index, sources[:-late], whole.shape[1])

time: 35.4 us -> 35.9 us (1.014)
  starting transfers between devices: 16.7 us -> 20.8 us
  waiting for transfers between devices: 10.5 us -> 7.08 us
    ppermute x11 -> x10, starting transfers between devices: 16.6 us -> 20.7 us  [send(): return lax.ppermute(chunk, 'wide', pairs)]
    ppermute x11 -> x10, waiting for transfers between devices: 10.5 us -> 7.04 us  [send(): return lax.ppermute(chunk, 'wide', pairs)]
  transfers between devices with their start and end apart: 12 -> 11, of which waited for: 9 -> 5; matrix products, arithmetic and copies ran while one was open for 0% -> 0% of each run, Pallas kernels for 7% -> 7%
where the time goes in v8:
time: 35.9 us; the launch traced here: 35.7 us
  starting transfers between devices  20.8 us (58%)
  waiting for transfers between devices  7.08 us (20%)
  Pallas kernels  5.33 us (15%)
  local copies, waits for them, and re-layouts  2.39 us (7%)
    ppermute x10, starting transfers between devices, send(): return lax.ppermute(chunk, 'wide', pairs)  20.7 us
    ppermute x10, waiting for transfers between devices, send(): return lax.ppermute(chunk, 'wide', pairs)  7.04 us
    pallas_call x1, Pallas kernels, attend(): pl.pallas_call(functools.partial(attend_kernel, spans), out_shape=jax.Sha...  2.56 us
    unnamed x12, local copies, waits for them, and re-layouts  2.39 us
    pallas_call x1, Pallas kernels, own_scores(): pl.pallas_call(functools.partial(score_kernel, spans), out_shape=jax.Shap...  1.02 us
  transfers between devices with their start and end apart: 11, of which 5 were waited for; matrix products, arithmetic and copies ran while one was open for 0% of the time, Pallas kernels for 7%

profile of v8, /device:TPU:0, one launch (start us, length us, event | category | flops | bytes accessed | tf_op | source)
XLA Modules:
  0.0 35.7 jit_solution(1753041482012773412)
XLA Ops:
  0.0 1.0 %copy-done.3 = bf16[64,3584]{1,0:T(8,128)(2,1)S(1)} copy-done((bf16[64,3584]{1,0:T(8,128)(2,1)S(1)}, bf16[64,3584]{1,0:T(8,128)(2,1)}, u32[]{:S(2)}) %copy-start.3) | copy-done | bytes 458776
  1.1 3.1 %collective-permute-start = (bf16[64,896]{1,0:T(8,128)(2,1)S(1)}, bf16[64,896]{1,0:T(8,128)(2,1)S(1)}, u32[]{:S(2)}, u32[]{:S(2)}) collective-permute-start(bf16[64,896]{1,0:T(8,128)(2,1)S(1)} %get-tuple-element.8.refs_0_), channel_id=1, source_target_pairs={{0,4},{2,6},{4,12},{6,14},{12,8},{14,10},{8,0},{10,2},{1,5},{3,7},... | collective-permute-start | bytes 344072 | tf_op jit(solution)/shard_map/ppermute | solution.py:238
  4.2 2.6 %collective-permute-start.1 = (bf16[64,896]{1,0:T(8,128)(2,1)S(1)}, bf16[64,896]{1,0:T(8,128)(2,1)S(1)}, u32[]{:S(2)}, u32[]{:S(2)}) collective-permute-start(bf16[64,896]{1,0:T(8,128)(2,1)S(1)} %get-tuple-element.9.refs_1_), channel_id=1, source_target_pairs={{0,4},{2,6},{4,12},{6,14},{12,8},{14,10},{8,0},{10,2},{1,5},{3,7},... | collective-permute-start | bytes 344072 | tf_op jit(solution)/shard_map/ppermute | solution.py:238
  6.8 1.5 %collective-permute-start.2 = (bf16[64,1792]{1,0:T(8,128)(2,1)S(1)}, bf16[64,1792]{1,0:T(8,128)(2,1)S(1)}, u32[]{:S(2)}, u32[]{:S(2)}) collective-permute-start(bf16[64,1792]{1,0:T(8,128)(2,1)S(1)} %get-tuple-element.10), channel_id=1, source_target_pairs={{0,2},{2,0},{4,6},{6,4},{8,10},{10,8},{12,14},{14,12},{1,3},{3,1},... | collective-permute-start | bytes 688136 | tf_op jit(solution)/shard_map/ppermute | solution.py:238
  8.3 0.3 collective-permute-start.4
  8.6 0.6 %collective-permute-done.refs_2_ = bf16[64,896]{1,0:T(8,128)(2,1)S(1)} collective-permute-done((bf16[64,896]{1,0:T(8,128)(2,1)S(1)}, bf16[64,896]{1,0:T(8,128)(2,1)S(1)}, u32[]{:S(2)}, u32[]{:S(2)}) %collective-permute-start) | collective-permute-done | bytes 114720 | tf_op jit(solution)/shard_map/ppermute | solution.py:238
  9.2 1.7 %collective-permute-done.1.refs_3_ = bf16[64,896]{1,0:T(8,128)(2,1)S(1)} collective-permute-done((bf16[64,896]{1,0:T(8,128)(2,1)S(1)}, bf16[64,896]{1,0:T(8,128)(2,1)S(1)}, u32[]{:S(2)}, u32[]{:S(2)}) %collective-permute-start.1) | collective-permute-done | bytes 114720 | tf_op jit(solution)/shard_map/ppermute | solution.py:238
  10.9 1.6 %collective-permute-start.3 = (bf16[64,1792]{1,0:T(8,128)(2,1)S(1)}, bf16[64,1792]{1,0:T(8,128)(2,1)S(1)}, u32[]{:S(2)}, u32[]{:S(2)}) collective-permute-start(bf16[64,1792]{1,0:T(8,128)(2,1)S(1)} %pad_maximum_fusion), channel_id=1, source_target_pairs={{0,2},{2,0},{4,6},{6,4},{8,10},{10,8},{12,14},{14,12},{1,3},{3,1},... | collective-permute-start | bytes 688136 | tf_op jit(solution)/shard_map/ppermute | solution.py:238
  12.6 5.3 %collective-permute-start.5 = (bf16[64,896]{1,0:T(8,128)(2,1)S(1)}, bf16[64,896]{1,0:T(8,128)(2,1)S(1)}, u32[]{:S(2)}, u32[]{:S(2)}) collective-permute-start(bf16[64,896]{1,0:T(8,128)(2,1)S(1)} %collective-permute-done.refs_2_), channel_id=1, source_target_pairs={{0,4},{2,6},{4,12},{6,14},{12,8},{14,10},{8,0},{10,2},{1,5},{3,7},... | collective-permute-start | bytes 344072 | tf_op jit(solution)/shard_map/ppermute | solution.py:238
  17.9 3.5 %collective-permute-start.6 = (bf16[64,896]{1,0:T(8,128)(2,1)S(1)}, bf16[64,896]{1,0:T(8,128)(2,1)S(1)}, u32[]{:S(2)}, u32[]{:S(2)}) collective-permute-start(bf16[64,896]{1,0:T(8,128)(2,1)S(1)} %collective-permute-done.1.refs_3_), channel_id=1, source_target_pairs={{0,4},{2,6},{4,12},{6,14},{12,8},{14,10},{8,0},{10,2},{1,5},{3,7},... | collective-permute-start | bytes 344072 | tf_op jit(solution)/shard_map/ppermute | solution.py:238
  21.4 0.7 %collective-permute-start.7 = (bf16[64,1792]{1,0:T(8,128)(2,1)S(1)}, bf16[64,1792]{1,0:T(8,128)(2,1)S(1)}, u32[]{:S(2)}, u32[]{:S(2)}) collective-permute-start(bf16[64,1792]{1,0:T(8,128)(2,1)S(1)} %collective-permute-done.4.refs_6_), channel_id=1, source_target_pairs={{0,2},{2,0},{4,6},{6,4},{8,10},{10,8},{12,14},{14,12},{1,3},{3,1},... | collective-permute-start | bytes 688136 | tf_op jit(solution)/shard_map/ppermute | solution.py:238
  22.1 1.3 %collective-permute-start.8 = (bf16[64,896]{1,0:T(8,128)(2,1)S(1)}, bf16[64,896]{1,0:T(8,128)(2,1)S(1)}, u32[]{:S(2)}, u32[]{:S(2)}) collective-permute-start(bf16[64,896]{1,0:T(8,128)(2,1)S(1)} %collective-permute-done.5.refs_0_), channel_id=1, source_target_pairs={{0,2},{2,0},{4,6},{6,4},{8,10},{10,8},{12,14},{14,12},{1,3},{3,1},... | collective-permute-start | bytes 344072 | tf_op jit(solution)/shard_map/ppermute | solution.py:238
  23.4 0.3 collective-permute-done.6.refs_1_
  23.8 0.7 %collective-permute-start.9 = (bf16[64,896]{1,0:T(8,128)(2,1)S(1)}, bf16[64,896]{1,0:T(8,128)(2,1)S(1)}, u32[]{:S(2)}, u32[]{:S(2)}) collective-permute-start(bf16[64,896]{1,0:T(8,128)(2,1)S(1)} %collective-permute-done.6.refs_1_), channel_id=1, source_target_pairs={{0,2},{2,0},{4,6},{6,4},{8,10},{10,8},{12,14},{14,12},{1,3},{3,1},... | collective-permute-start | bytes 344072 | tf_op jit(solution)/shard_map/ppermute | solution.py:238
  24.5 0.7 %copy-done.4 = s32[2,64,1]{1,2,0:T(1,128)S(1)} copy-done((s32[2,64,1]{1,2,0:T(1,128)S(1)}, s32[2,64,1]{1,2,0:T(1,128)}, u32[]{:S(2)}) %copy-start.4) | copy-done | bytes 536
  25.2 0.7 %copy-done.5 = s32[2,64]{1,0:T(2,128)S(1)} copy-done((s32[2,64]{1,0:T(2,128)S(1)}, s32[2,64]{1,0:T(2,128)}, u32[]{:S(2)}) %copy-start.5) | copy-done | bytes 536
  25.8 0.1 shard_map.64.index_ref
  26.0 0.5 %shard_map.66.begun_ref = bf16[128,1792]{1,0:T(8,128)(2,1)S(1)} custom-call(s32[128,1]{1,0:T(8,128)S(1)} %shard_map.64.index_ref, bf16[64,896]{1,0:T(8,128)(2,1)S(1)} %get-tuple-element.8.refs_0_, bf16[64,896]{1,0:T(8,128)(2,1)S(1)} %get-tuple-element.9.refs_1_, bf16[64,896]{1,0:T(8,128)(2,1)S(1)} %collective-permute-done.refs_2_, ...), custom_call_target="tpu_custom_call" | custom-call | flops 146800640 | bytes 458752 | tf_op jit(solution)/shard_map/pallas_call | solution.py:116
  26.5 3.2 %collective-permute-done.8.refs_3_ = bf16[64,896]{1,0:T(8,128)(2,1)S(1)} collective-permute-done((bf16[64,896]{1,0:T(8,128)(2,1)S(1)}, bf16[64,896]{1,0:T(8,128)(2,1)S(1)}, u32[]{:S(2)}, u32[]{:S(2)}) %collective-permute-start.8) | collective-permute-done | bytes 114720 | tf_op jit(solution)/shard_map/ppermute | solution.py:238
  29.7 1.2 %collective-permute-done.9.refs_4_ = bf16[64,896]{1,0:T(8,128)(2,1)S(1)} collective-permute-done((bf16[64,896]{1,0:T(8,128)(2,1)S(1)}, bf16[64,896]{1,0:T(8,128)(2,1)S(1)}, u32[]{:S(2)}, u32[]{:S(2)}) %collective-permute-start.9) | collective-permute-done | bytes 114720 | tf_op jit(solution)/shard_map/ppermute | solution.py:238
  30.9 0.3 shard_map.67.picked_ref
  31.3 0.7 %shard_map.69.values_ref = bf16[256,1024]{1,0:T(8,128)(2,1)S(1)} custom-call(bf16[128,1792]{1,0:T(8,128)(2,1)S(1)} %shard_map.67.picked_ref, bf16[896,1024]{1,0:T(8,128)(2,1)S(1)} %copy-done.1), custom_call_target="tpu_custom_call" | custom-call | tf_op jit(solution)/shard_map/pallas_call | solution.py:197
  32.1 1.0 %shard_map.68.first_ref = f32[16,64,128]{2,1,0:T(8,128)S(1)} custom-call(bf16[128,1792]{1,0:T(8,128)(2,1)S(1)} %shard_map.67.picked_ref, bf16[896,1024]{1,0:T(8,128)(2,1)S(1)} %copy-done, bf16[128,1024]{1,0:T(8,128)(2,1)S(1)} %copy-done.2), custom_call_target="tpu_custom_call" | custom-call | tf_op jit(solution)/shard_map/pallas_call | solution.py:181
  33.1 2.6 %shard_map.70 = bf16[128,1024]{1,0:T(8,128)(2,1)} custom-call(bf16[128,1792]{1,0:T(8,128)(2,1)S(1)} %collective-permute-done.10.other_ref, bf16[896,1024]{1,0:T(8,128)(2,1)S(1)} %copy-done, bf16[896,1024]{1,0:T(8,128)(2,1)S(1)} %copy-done.1, bf16[128,1024]{1,0:T(8,128)(2,1)S(1)} %copy-done.2, f32[16,64,128]{2,1,0:T(8,128)S(1)} %shard_map.68.first_ref, ...), custom_call_target="tpu_custom_call" | custom-call | tf_op jit(solution)/shard_map/pallas_call | solution.py:227
  (18 shorter events, 0.3 us)
Async XLA Ops:
  0.0 1.0 %copy-start.3 = (bf16[64,3584]{1,0:T(8,128)(2,1)S(1)}, bf16[64,3584]{1,0:T(8,128)(2,1)}, u32[]{:S(2)}) copy-start(bf16[64,3584]{1,0:T(8,128)(2,1)} %enc_ref.1) | copy-start | bytes 1376260
  1.1 8.1 %collective-permute-start = (bf16[64,896]{1,0:T(8,128)(2,1)S(1)}, bf16[64,896]{1,0:T(8,128)(2,1)S(1)}, u32[]{:S(2)}, u32[]{:S(2)}) collective-permute-start(bf16[64,896]{1,0:T(8,128)(2,1)S(1)} %get-tuple-element.8.refs_0_), channel_id=1, source_target_pairs={{0,4},{2,6},{4,12},{6,14},{12,8},{14,10},{8,0},{10,2},{1,5},{3,7},... | collective-permute-start | bytes 344072 | tf_op jit(solution)/shard_map/ppermute | solution.py:238
  4.2 6.7 %collective-permute-start.1 = (bf16[64,896]{1,0:T(8,128)(2,1)S(1)}, bf16[64,896]{1,0:T(8,128)(2,1)S(1)}, u32[]{:S(2)}, u32[]{:S(2)}) collective-permute-start(bf16[64,896]{1,0:T(8,128)(2,1)S(1)} %get-tuple-element.9.refs_1_), channel_id=1, source_target_pairs={{0,4},{2,6},{4,12},{6,14},{12,8},{14,10},{8,0},{10,2},{1,5},{3,7},... | collective-permute-start | bytes 344072 | tf_op jit(solution)/shard_map/ppermute | solution.py:238
  6.8 24.5 %copy-start.1 = (bf16[896,1024]{1,0:T(8,128)(2,1)S(1)}, bf16[896,1024]{1,0:T(8,128)(2,1)}, u32[]{:S(2)}) copy-start(bf16[896,1024]{1,0:T(8,128)(2,1)} %wv_ref.3) | copy-start | bytes 5505028
  6.8 19.2 %collective-permute-start.2 = (bf16[64,1792]{1,0:T(8,128)(2,1)S(1)}, bf16[64,1792]{1,0:T(8,128)(2,1)S(1)}, u32[]{:S(2)}, u32[]{:S(2)}) collective-permute-start(bf16[64,1792]{1,0:T(8,128)(2,1)S(1)} %get-tuple-element.10), channel_id=1, source_target_pairs={{0,2},{2,0},{4,6},{6,4},{8,10},{10,8},{12,14},{14,12},{1,3},{3,1},... | collective-permute-start | bytes 688136 | tf_op jit(solution)/shard_map/ppermute | solution.py:238
  8.3 13.1 %collective-permute-start.4 = (bf16[64,1792]{1,0:T(8,128)(2,1)S(1)}, bf16[64,1792]{1,0:T(8,128)(2,1)S(1)}, u32[]{:S(2)}, u32[]{:S(2)}) collective-permute-start(bf16[64,1792]{1,0:T(8,128)(2,1)S(1)} %get-tuple-element.10), channel_id=1, source_target_pairs={{4,0},{6,2},{12,4},{14,6},{8,12},{10,14},{0,8},{2,10},{5,1},{7,3},... | collective-permute-start | bytes 688136 | tf_op jit(solution)/shard_map/ppermute | solution.py:238
  10.9 15.0 %collective-permute-start.3 = (bf16[64,1792]{1,0:T(8,128)(2,1)S(1)}, bf16[64,1792]{1,0:T(8,128)(2,1)S(1)}, u32[]{:S(2)}, u32[]{:S(2)}) collective-permute-start(bf16[64,1792]{1,0:T(8,128)(2,1)S(1)} %pad_maximum_fusion), channel_id=1, source_target_pairs={{0,2},{2,0},{4,6},{6,4},{8,10},{10,8},{12,14},{14,12},{1,3},{3,1},... | collective-permute-start | bytes 688136 | tf_op jit(solution)/shard_map/ppermute | solution.py:238
  12.6 9.6 %collective-permute-start.5 = (bf16[64,896]{1,0:T(8,128)(2,1)S(1)}, bf16[64,896]{1,0:T(8,128)(2,1)S(1)}, u32[]{:S(2)}, u32[]{:S(2)}) collective-permute-start(bf16[64,896]{1,0:T(8,128)(2,1)S(1)} %collective-permute-done.refs_2_), channel_id=1, source_target_pairs={{0,4},{2,6},{4,12},{6,14},{12,8},{14,10},{8,0},{10,2},{1,5},{3,7},... | collective-permute-start | bytes 344072 | tf_op jit(solution)/shard_map/ppermute | solution.py:238
  17.9 5.9 %collective-permute-start.6 = (bf16[64,896]{1,0:T(8,128)(2,1)S(1)}, bf16[64,896]{1,0:T(8,128)(2,1)S(1)}, u32[]{:S(2)}, u32[]{:S(2)}) collective-permute-start(bf16[64,896]{1,0:T(8,128)(2,1)S(1)} %collective-permute-done.1.refs_3_), channel_id=1, source_target_pairs={{0,4},{2,6},{4,12},{6,14},{12,8},{14,10},{8,0},{10,2},{1,5},{3,7},... | collective-permute-start | bytes 344072 | tf_op jit(solution)/shard_map/ppermute | solution.py:238
  21.4 9.5 %collective-permute-start.7 = (bf16[64,1792]{1,0:T(8,128)(2,1)S(1)}, bf16[64,1792]{1,0:T(8,128)(2,1)S(1)}, u32[]{:S(2)}, u32[]{:S(2)}) collective-permute-start(bf16[64,1792]{1,0:T(8,128)(2,1)S(1)} %collective-permute-done.4.refs_6_), channel_id=1, source_target_pairs={{0,2},{2,0},{4,6},{6,4},{8,10},{10,8},{12,14},{14,12},{1,3},{3,1},... | collective-permute-start | bytes 688136 | tf_op jit(solution)/shard_map/ppermute | solution.py:238
  22.1 7.6 %collective-permute-start.8 = (bf16[64,896]{1,0:T(8,128)(2,1)S(1)}, bf16[64,896]{1,0:T(8,128)(2,1)S(1)}, u32[]{:S(2)}, u32[]{:S(2)}) collective-permute-start(bf16[64,896]{1,0:T(8,128)(2,1)S(1)} %collective-permute-done.5.refs_0_), channel_id=1, source_target_pairs={{0,2},{2,0},{4,6},{6,4},{8,10},{10,8},{12,14},{14,12},{1,3},{3,1},... | collective-permute-start | bytes 344072 | tf_op jit(solution)/shard_map/ppermute | solution.py:238
  23.8 7.1 %collective-permute-start.9 = (bf16[64,896]{1,0:T(8,128)(2,1)S(1)}, bf16[64,896]{1,0:T(8,128)(2,1)S(1)}, u32[]{:S(2)}, u32[]{:S(2)}) collective-permute-start(bf16[64,896]{1,0:T(8,128)(2,1)S(1)} %collective-permute-done.6.refs_1_), channel_id=1, source_target_pairs={{0,2},{2,0},{4,6},{6,4},{8,10},{10,8},{12,14},{14,12},{1,3},{3,1},... | collective-permute-start | bytes 344072 | tf_op jit(solution)/shard_map/ppermute | solution.py:238
  24.5 0.7 %copy-start.4 = (s32[2,64,1]{1,2,0:T(1,128)S(1)}, s32[2,64,1]{1,2,0:T(1,128)}, u32[]{:S(2)}) copy-start(s32[2,64,1]{1,2,0:T(1,128)} %param.10) | copy-start | bytes 1540
  25.2 0.7 %copy-start.5 = (s32[2,64]{1,0:T(2,128)S(1)}, s32[2,64]{1,0:T(2,128)}, u32[]{:S(2)}) copy-start(s32[2,64]{1,0:T(2,128)} %stored_ref.1) | copy-start | bytes 1540
  26.5 5.6 %copy-start = (bf16[896,1024]{1,0:T(8,128)(2,1)S(1)}, bf16[896,1024]{1,0:T(8,128)(2,1)}, u32[]{:S(2)}) copy-start(bf16[896,1024]{1,0:T(8,128)(2,1)} %wk_ref.3) | copy-start | bytes 5505028
  26.5 5.6 %copy-start.2 = (bf16[128,1024]{1,0:T(8,128)(2,1)S(1)}, bf16[128,1024]{1,0:T(8,128)(2,1)}, u32[]{:S(2)}) copy-start(bf16[128,1024]{1,0:T(8,128)(2,1)} %query_ref.3) | copy-start | bytes 786436
  31.3 1.9 %collective-permute-start.10 = (bf16[128,1792]{1,0:T(8,128)(2,1)S(1)}, bf16[128,1792]{1,0:T(8,128)(2,1)S(1)}, u32[]{:S(2)}, u32[]{:S(2)}) collective-permute-start(bf16[128,1792]{1,0:T(8,128)(2,1)S(1)} %shard_map.67.picked_ref), channel_id=1, source_target_pairs={{0,1},{1,0},{2,3},{3,2},{4,5},{5,4},{6,7},{7,6},{8,9},{9,8},{10,11... | collective-permute-start | bytes 1376264 | tf_op jit(solution)/shard_map/ppermute | solution.py:271

commit v9 on v7

--- a/solution.py
+++ b/solution.py
@@ -91,25 +91,18 @@
     return jnp.concatenate(columns, axis=0).astype(jnp.int32)
 
 
-def places_kernel(order, turns, owner_ref, stored_ref, piece_ref, index_ref, piece_out, sem):
-    copy = pltpu.make_async_copy(piece_ref, piece_out, sem)
-    copy.start()
-    index_ref[...] = wanted_rows(order, turns, piece_ref.shape[0], owner_ref, stored_ref)
-    copy.wait()
-
-
-def places(order, turns, owners, stored, piece):
-    return pl.pallas_call(
-        functools.partial(places_kernel, order, turns),
-        out_shape=(
-            jax.ShapeDtypeStruct((stored.size, 1), jnp.int32),
-            jax.ShapeDtypeStruct(piece.shape, piece.dtype),
-        ),
-        in_specs=[VMEM] * 3,
-        out_specs=(VMEM, VMEM),
-        scratch_shapes=[pltpu.SemaphoreType.DMA],
-        compiler_params=params(),
-    )(owners, stored, piece)
+def places_kernel(order, turns, rows, owner_ref, stored_ref, index_ref):
+    index_ref[...] = wanted_rows(order, turns, rows, owner_ref, stored_ref)
+
+
+def places(order, turns, rows, owners, stored):
+    return pl.pallas_call(
+        functools.partial(places_kernel, order, turns, rows),
+        out_shape=jax.ShapeDtypeStruct((stored.size, 1), jnp.int32),
+        in_specs=[VMEM] * 2,
+        out_specs=VMEM,
+        compiler_params=params(),
+    )(owners, stored)
 
 
 def early_kernel(chunks, index_ref, *refs):
@@ -159,18 +152,30 @@
     return jnp.concatenate(parts, axis=0)
 
 
-def head_places(spans, columns):
-    heads = columns // HD
-    return [(c, slice(h * HD, (h + 1) * HD), c * heads + h) for c in range(spans) for h in range(heads)]
+PAIR = 2
+
+
+def pair_places(spans, columns):
+    pairs = columns // (PAIR * HD)
+    return [
+        (c, slice(p * PAIR * HD, (p + 1) * PAIR * HD), c * pairs + p) for c in range(spans) for p in range(pairs)
+    ]
+
+
+def apart(query):
+    none = jnp.zeros((query.shape[0], HD), query.dtype)
+    upper = jnp.concatenate([query[:, :HD], none], axis=1)
+    lower = jnp.concatenate([none, query[:, HD:]], axis=1)
+    return jnp.concatenate([upper, lower], axis=0)
 
 
 def score(spans, source, wk_ref, query_ref, scores_ref):
     keys = jnp.dot(source, wk_ref[...], preferred_element_type=jnp.float32).astype(jnp.bfloat16)
     per = keys.shape[0] // spans
-    for c, lanes, n in head_places(spans, keys.shape[1]):
+    for c, lanes, n in pair_places(spans, keys.shape[1]):
         scores_ref[n] = lax.dot_general(
-            query_ref[c * SPAN : (c + 1) * SPAN, lanes],
             keys[c * per : (c + 1) * per, lanes],
+            apart(query_ref[c * SPAN : (c + 1) * SPAN, lanes]),
             (((1,), (1,)), ((), ())),
             preferred_element_type=jnp.float32,
         )
@@ -181,7 +186,7 @@
 
 
 def scores_shape(picked, queries, channels, spans):
-    return spans * (queries.shape[1] // HD), SPAN, picked.size // channels // spans
+    return spans * (queries.shape[1] // (PAIR * HD)), picked.size // channels // spans, PAIR * SPAN
 
 
 def own_scores(picked, w_key, queries, spans):
@@ -217,16 +222,19 @@
     score(spans, other, wk_ref, query_ref, second_ref)
     per = other.shape[0] // spans
     more = jnp.dot(other, wv_ref[...], preferred_element_type=jnp.float32).astype(jnp.bfloat16)
-    places = head_places(spans, more.shape[1])
-    for c, lanes, n in places:
-        scores = jnp.concatenate([first_ref[n], second_ref[n]], axis=1)
-        raised = jnp.exp2((scores - jnp.max(scores, axis=-1, keepdims=True)) * EXPONENT)
-        probs_ref[n] = (raised * (1.0 / jnp.sum(raised, axis=-1, keepdims=True))).astype(jnp.bfloat16)
-    for c, lanes, n in places:
+    everything = pair_places(spans, more.shape[1])
+    for c, lanes, n in everything:
+        scores = jnp.concatenate([first_ref[n], second_ref[n]], axis=0)
+        raised = jnp.exp2((scores - jnp.max(scores, axis=0, keepdims=True)) * EXPONENT)
+        probs_ref[n] = (raised * (1.0 / jnp.sum(raised, axis=0, keepdims=True))).astype(jnp.bfloat16)
+    for c, lanes, n in everything:
         rows = slice(c * per, (c + 1) * per)
         values = jnp.concatenate([values_ref[rows, lanes], more[rows, lanes]], axis=0)
-        mixed = jnp.dot(probs_ref[n], values, preferred_element_type=jnp.float32)
-        out_ref[c * SPAN : (c + 1) * SPAN, lanes] = mixed.astype(out_ref.dtype)
+        mixed = lax.dot_general(
+            probs_ref[n], values, (((0,), (0,)), ((), ())), preferred_element_type=jnp.float32
+        ).astype(out_ref.dtype)
+        own = [mixed[h * SPAN : (h + 1) * SPAN, h * HD : (h + 1) * HD] for h in range(PAIR)]
+        out_ref[c * SPAN : (c + 1) * SPAN, lanes] = jnp.concatenate(own, axis=1)
 
 
 def attend(other, w_key, w_value, queries, first, values, spans):
@@ -236,7 +244,7 @@
         out_shape=jax.ShapeDtypeStruct(queries.shape, queries.dtype),
         in_specs=[VMEM] * 6,
         out_specs=VMEM,
-        scratch_shapes=[pltpu.VMEM(each, jnp.float32), pltpu.VMEM(each[:2] + (2 * each[2],), jnp.bfloat16)],
+        scratch_shapes=[pltpu.VMEM(each, jnp.float32), pltpu.VMEM((each[0], 2 * each[1], each[2]), jnp.bfloat16)],
         compiler_params=params(),
     )(other, w_key, w_value, queries, first, values)
 
@@ -260,7 +268,7 @@
     for k in range(1, turns):
         order += [(k, 0), (k - 1, 1)]
     order.append((turns - 1, 1))
-    index, pieces[-1] = places(order, turns, jnp.transpose(block_owner, (0, 2, 1)), block_row, pieces[-1])
+    index = places(order, turns, rows, jnp.transpose(block_owner, (0, 2, 1)), block_row)
     held = {(0, 0): pieces}
     for k in range(1, turns):
         behind = held[k - 1, 0]

time: 35.4 us -> 34.9 us (0.986)
  waiting for transfers between devices: 8.2 us -> 6.9 us
  starting transfers between devices: 19 us -> 20.1 us
    ppermute x12, waiting for transfers between devices: 8.16 us -> 6.71 us  [send(): return lax.ppermute(chunk, 'wide', pairs)]
    ppermute x12, starting transfers between devices: 19 us -> 20 us  [send(): return lax.ppermute(chunk, 'wide', pairs)]
  transfers between devices with their start and end apart: 13 -> 13, of which waited for: 8 -> 8; matrix products, arithmetic and copies ran while one was open for 0% -> 0% of each run, Pallas kernels for 7% -> 6%
where the time goes in v9:
time: 34.9 us; the launch traced here: 34.7 us
  starting transfers between devices  20.1 us (58%)
  waiting for transfers between devices  6.9 us (20%)
  Pallas kernels  5.13 us (15%)
  local copies, waits for them, and re-layouts  2.39 us (7%)
    ppermute x12, starting transfers between devices, send(): return lax.ppermute(chunk, 'wide', pairs)  20 us
    ppermute x12, waiting for transfers between devices, send(): return lax.ppermute(chunk, 'wide', pairs)  6.71 us
    pallas_call x1, Pallas kernels, attend(): pl.pallas_call(functools.partial(attend_kernel, spans), out_shape=jax.Sha...  2.51 us
    unnamed x12, local copies, waits for them, and re-layouts  2.39 us
    pallas_call x1, Pallas kernels, own_scores(): pl.pallas_call(functools.partial(score_kernel, spans), out_shape=jax.Shap...  0.87 us
    pallas_call x1, Pallas kernels, own_values(): pl.pallas_call(functools.partial(values_kernel, spans), out_shape=jax.Sha...  0.71 us
  transfers between devices with their start and end apart: 13, of which 8 were waited for; matrix products, arithmetic and copies ran while one was open for 0% of the time, Pallas kernels for 6%

profile of v9, /device:TPU:0, one launch (start us, length us, event | category | flops | bytes accessed | tf_op | source)
XLA Modules:
  0.0 34.7 jit_solution(2978418590092284754)
XLA Ops:
  0.0 1.0 %copy-done.3 = bf16[64,3584]{1,0:T(8,128)(2,1)S(1)} copy-done((bf16[64,3584]{1,0:T(8,128)(2,1)S(1)}, bf16[64,3584]{1,0:T(8,128)(2,1)}, u32[]{:S(2)}) %copy-start.3) | copy-done | bytes 458776
  1.1 3.1 %collective-permute-start = (bf16[64,896]{1,0:T(8,128)(2,1)S(1)}, bf16[64,896]{1,0:T(8,128)(2,1)S(1)}, u32[]{:S(2)}, u32[]{:S(2)}) collective-permute-start(bf16[64,896]{1,0:T(8,128)(2,1)S(1)} %get-tuple-element.8.refs_0_), channel_id=1, source_target_pairs={{0,4},{2,6},{4,12},{6,14},{12,8},{14,10},{8,0},{10,2},{1,5},{3,7},... | collective-permute-start | bytes 344072 | tf_op jit(solution)/shard_map/ppermute | solution.py:253
  4.2 2.6 %collective-permute-start.1 = (bf16[64,896]{1,0:T(8,128)(2,1)S(1)}, bf16[64,896]{1,0:T(8,128)(2,1)S(1)}, u32[]{:S(2)}, u32[]{:S(2)}) collective-permute-start(bf16[64,896]{1,0:T(8,128)(2,1)S(1)} %get-tuple-element.9.refs_1_), channel_id=1, source_target_pairs={{0,4},{2,6},{4,12},{6,14},{12,8},{14,10},{8,0},{10,2},{1,5},{3,7},... | collective-permute-start | bytes 344072 | tf_op jit(solution)/shard_map/ppermute | solution.py:253
  6.8 1.5 %collective-permute-start.2 = (bf16[64,1792]{1,0:T(8,128)(2,1)S(1)}, bf16[64,1792]{1,0:T(8,128)(2,1)S(1)}, u32[]{:S(2)}, u32[]{:S(2)}) collective-permute-start(bf16[64,1792]{1,0:T(8,128)(2,1)S(1)} %get-tuple-element.10), channel_id=1, source_target_pairs={{0,2},{2,0},{4,6},{6,4},{8,10},{10,8},{12,14},{14,12},{1,3},{3,1},... | collective-permute-start | bytes 688136 | tf_op jit(solution)/shard_map/ppermute | solution.py:253
  8.3 0.9 %collective-permute-done.refs_2_ = bf16[64,896]{1,0:T(8,128)(2,1)S(1)} collective-permute-done((bf16[64,896]{1,0:T(8,128)(2,1)S(1)}, bf16[64,896]{1,0:T(8,128)(2,1)S(1)}, u32[]{:S(2)}, u32[]{:S(2)}) %collective-permute-start) | collective-permute-done | bytes 114720 | tf_op jit(solution)/shard_map/ppermute | solution.py:253
  9.2 1.2 %collective-permute-start.3 = (bf16[64,896]{1,0:T(8,128)(2,1)S(1)}, bf16[64,896]{1,0:T(8,128)(2,1)S(1)}, u32[]{:S(2)}, u32[]{:S(2)}) collective-permute-start(bf16[64,896]{1,0:T(8,128)(2,1)S(1)} %collective-permute-done.refs_2_), channel_id=1, source_target_pairs={{0,4},{2,6},{4,12},{6,14},{12,8},{14,10},{8,0},{10,2},{1,5},{3,7},... | collective-permute-start | bytes 344072 | tf_op jit(solution)/shard_map/ppermute | solution.py:253
  10.8 2.9 %collective-permute-start.4 = (bf16[64,896]{1,0:T(8,128)(2,1)S(1)}, bf16[64,896]{1,0:T(8,128)(2,1)S(1)}, u32[]{:S(2)}, u32[]{:S(2)}) collective-permute-start(bf16[64,896]{1,0:T(8,128)(2,1)S(1)} %collective-permute-done.1.refs_3_), channel_id=1, source_target_pairs={{0,4},{2,6},{4,12},{6,14},{12,8},{14,10},{8,0},{10,2},{1,5},{3,7},... | collective-permute-start | bytes 344072 | tf_op jit(solution)/shard_map/ppermute | solution.py:253
  13.7 1.6 %collective-permute-start.5 = (bf16[64,1792]{1,0:T(8,128)(2,1)S(1)}, bf16[64,1792]{1,0:T(8,128)(2,1)S(1)}, u32[]{:S(2)}, u32[]{:S(2)}) collective-permute-start(bf16[64,1792]{1,0:T(8,128)(2,1)S(1)} %pad_maximum_fusion), channel_id=1, source_target_pairs={{0,2},{2,0},{4,6},{6,4},{8,10},{10,8},{12,14},{14,12},{1,3},{3,1},... | collective-permute-start | bytes 688136 | tf_op jit(solution)/shard_map/ppermute | solution.py:253
  15.3 0.8 %collective-permute-done.3.refs_5_ = bf16[64,896]{1,0:T(8,128)(2,1)S(1)} collective-permute-done((bf16[64,896]{1,0:T(8,128)(2,1)S(1)}, bf16[64,896]{1,0:T(8,128)(2,1)S(1)}, u32[]{:S(2)}, u32[]{:S(2)}) %collective-permute-start.3) | collective-permute-done | bytes 114720 | tf_op jit(solution)/shard_map/ppermute | solution.py:253
  16.1 0.8 %collective-permute-start.6 = (bf16[64,896]{1,0:T(8,128)(2,1)S(1)}, bf16[64,896]{1,0:T(8,128)(2,1)S(1)}, u32[]{:S(2)}, u32[]{:S(2)}) collective-permute-start(bf16[64,896]{1,0:T(8,128)(2,1)S(1)} %collective-permute-done.3.refs_5_), channel_id=1, source_target_pairs={{0,4},{2,6},{4,12},{6,14},{12,8},{14,10},{8,0},{10,2},{1,5},{3,7},... | collective-permute-start | bytes 344072 | tf_op jit(solution)/shard_map/ppermute | solution.py:253
  16.9 1.6 %collective-permute-done.4.refs_6_ = bf16[64,896]{1,0:T(8,128)(2,1)S(1)} collective-permute-done((bf16[64,896]{1,0:T(8,128)(2,1)S(1)}, bf16[64,896]{1,0:T(8,128)(2,1)S(1)}, u32[]{:S(2)}, u32[]{:S(2)}) %collective-permute-start.4) | collective-permute-done | bytes 114720 | tf_op jit(solution)/shard_map/ppermute | solution.py:253
  18.5 1.8 %collective-permute-start.7 = (bf16[64,896]{1,0:T(8,128)(2,1)S(1)}, bf16[64,896]{1,0:T(8,128)(2,1)S(1)}, u32[]{:S(2)}, u32[]{:S(2)}) collective-permute-start(bf16[64,896]{1,0:T(8,128)(2,1)S(1)} %collective-permute-done.4.refs_6_), channel_id=1, source_target_pairs={{0,4},{2,6},{4,12},{6,14},{12,8},{14,10},{8,0},{10,2},{1,5},{3,7},... | collective-permute-start | bytes 344072 | tf_op jit(solution)/shard_map/ppermute | solution.py:253
  20.3 1.5 %collective-permute-start.8 = (bf16[64,896]{1,0:T(8,128)(2,1)S(1)}, bf16[64,896]{1,0:T(8,128)(2,1)S(1)}, u32[]{:S(2)}, u32[]{:S(2)}) collective-permute-start(bf16[64,896]{1,0:T(8,128)(2,1)S(1)} %collective-permute-done.3.refs_5_), channel_id=1, source_target_pairs={{0,2},{2,0},{4,6},{6,4},{8,10},{10,8},{12,14},{14,12},{1,3},{3,1},... | collective-permute-start | bytes 344072 | tf_op jit(solution)/shard_map/ppermute | solution.py:253
  21.8 0.5 %collective-permute-start.9 = (bf16[64,896]{1,0:T(8,128)(2,1)S(1)}, bf16[64,896]{1,0:T(8,128)(2,1)S(1)}, u32[]{:S(2)}, u32[]{:S(2)}) collective-permute-start(bf16[64,896]{1,0:T(8,128)(2,1)S(1)} %collective-permute-done.4.refs_6_), channel_id=1, source_target_pairs={{0,2},{2,0},{4,6},{6,4},{8,10},{10,8},{12,14},{14,12},{1,3},{3,1},... | collective-permute-start | bytes 344072 | tf_op jit(solution)/shard_map/ppermute | solution.py:253
  22.3 1.5 %collective-permute-start.10 = (bf16[64,896]{1,0:T(8,128)(2,1)S(1)}, bf16[64,896]{1,0:T(8,128)(2,1)S(1)}, u32[]{:S(2)}, u32[]{:S(2)}) collective-permute-start(bf16[64,896]{1,0:T(8,128)(2,1)S(1)} %collective-permute-done.6.refs_0_), channel_id=1, source_target_pairs={{0,2},{2,0},{4,6},{6,4},{8,10},{10,8},{12,14},{14,12},{1,3},{3,1},... | collective-permute-start | bytes 344072 | tf_op jit(solution)/shard_map/ppermute | solution.py:253
  24.2 1.2 %collective-permute-start.11 = (bf16[64,896]{1,0:T(8,128)(2,1)S(1)}, bf16[64,896]{1,0:T(8,128)(2,1)S(1)}, u32[]{:S(2)}, u32[]{:S(2)}) collective-permute-start(bf16[64,896]{1,0:T(8,128)(2,1)S(1)} %collective-permute-done.7.refs_1_), channel_id=1, source_target_pairs={{0,2},{2,0},{4,6},{6,4},{8,10},{10,8},{12,14},{14,12},{1,3},{3,1},... | collective-permute-start | bytes 344072 | tf_op jit(solution)/shard_map/ppermute | solution.py:253
  25.4 0.7 %copy-done.4 = s32[2,64,1]{1,2,0:T(1,128)S(1)} copy-done((s32[2,64,1]{1,2,0:T(1,128)S(1)}, s32[2,64,1]{1,2,0:T(1,128)}, u32[]{:S(2)}) %copy-start.4) | copy-done | bytes 536
  26.1 0.7 %copy-done.5 = s32[2,64]{1,0:T(2,128)S(1)} copy-done((s32[2,64]{1,0:T(2,128)S(1)}, s32[2,64]{1,0:T(2,128)}, u32[]{:S(2)}) %copy-start.5) | copy-done | bytes 536
  26.9 0.5 %shard_map.66.begun_ref = bf16[128,1792]{1,0:T(8,128)(2,1)S(1)} custom-call(s32[128,1]{1,0:T(8,128)S(1)} %shard_map.64.index_ref, bf16[64,896]{1,0:T(8,128)(2,1)S(1)} %get-tuple-element.8.refs_0_, bf16[64,896]{1,0:T(8,128)(2,1)S(1)} %get-tuple-element.9.refs_1_, bf16[64,896]{1,0:T(8,128)(2,1)S(1)} %collective-permute-done.refs_2_, ...), custom_call_target="tpu_custom_call" | custom-call | flops 146800640 | bytes 458752 | tf_op jit(solution)/shard_map/pallas_call | solution.py:116
  27.5 1.2 %collective-permute-done.10.refs_4_ = bf16[64,896]{1,0:T(8,128)(2,1)S(1)} collective-permute-done((bf16[64,896]{1,0:T(8,128)(2,1)S(1)}, bf16[64,896]{1,0:T(8,128)(2,1)S(1)}, u32[]{:S(2)}, u32[]{:S(2)}) %collective-permute-start.10) | collective-permute-done | bytes 114720 | tf_op jit(solution)/shard_map/ppermute | solution.py:253
  28.7 1.2 %collective-permute-done.11.refs_5_ = bf16[64,896]{1,0:T(8,128)(2,1)S(1)} collective-permute-done((bf16[64,896]{1,0:T(8,128)(2,1)S(1)}, bf16[64,896]{1,0:T(8,128)(2,1)S(1)}, u32[]{:S(2)}, u32[]{:S(2)}) %collective-permute-start.11) | collective-permute-done | bytes 114720 | tf_op jit(solution)/shard_map/ppermute | solution.py:253
  30.4 0.7 %shard_map.69.values_ref = bf16[256,1024]{1,0:T(8,128)(2,1)S(1)} custom-call(bf16[128,1792]{1,0:T(8,128)(2,1)S(1)} %shard_map.67.picked_ref, bf16[896,1024]{1,0:T(8,128)(2,1)S(1)} %copy-done.1), custom_call_target="tpu_custom_call" | custom-call | tf_op jit(solution)/shard_map/pallas_call | solution.py:209
  31.1 0.9 %shard_map.68.first_ref = f32[8,128,128]{2,1,0:T(8,128)S(1)} custom-call(bf16[128,1792]{1,0:T(8,128)(2,1)S(1)} %shard_map.67.picked_ref, bf16[896,1024]{1,0:T(8,128)(2,1)S(1)} %copy-done, bf16[128,1024]{1,0:T(8,128)(2,1)S(1)} %copy-done.2), custom_call_target="tpu_custom_call" | custom-call | tf_op jit(solution)/shard_map/pallas_call | solution.py:193
  32.2 2.5 %shard_map.70 = bf16[128,1024]{1,0:T(8,128)(2,1)} custom-call(bf16[128,1792]{1,0:T(8,128)(2,1)S(1)} %collective-permute-done.12.other_ref, bf16[896,1024]{1,0:T(8,128)(2,1)S(1)} %copy-done, bf16[896,1024]{1,0:T(8,128)(2,1)S(1)} %copy-done.1, bf16[128,1024]{1,0:T(8,128)(2,1)S(1)} %copy-done.2, f32[8,128,128]{2,1,0:T(8,128)S(1)} %shard_map.68.first_ref, ...), custom_call_target="tpu_custom_call" | custom-call | tf_op jit(solution)/shard_map/pallas_call | solution.py:242
  (22 shorter events, 1.8 us)
Async XLA Ops:
  0.0 1.0 %copy-start.3 = (bf16[64,3584]{1,0:T(8,128)(2,1)S(1)}, bf16[64,3584]{1,0:T(8,128)(2,1)}, u32[]{:S(2)}) copy-start(bf16[64,3584]{1,0:T(8,128)(2,1)} %enc_ref.1) | copy-start | bytes 1376260
  1.1 8.1 %collective-permute-start = (bf16[64,896]{1,0:T(8,128)(2,1)S(1)}, bf16[64,896]{1,0:T(8,128)(2,1)S(1)}, u32[]{:S(2)}, u32[]{:S(2)}) collective-permute-start(bf16[64,896]{1,0:T(8,128)(2,1)S(1)} %get-tuple-element.8.refs_0_), channel_id=1, source_target_pairs={{0,4},{2,6},{4,12},{6,14},{12,8},{14,10},{8,0},{10,2},{1,5},{3,7},... | collective-permute-start | bytes 344072 | tf_op jit(solution)/shard_map/ppermute | solution.py:253
  4.2 6.6 %collective-permute-start.1 = (bf16[64,896]{1,0:T(8,128)(2,1)S(1)}, bf16[64,896]{1,0:T(8,128)(2,1)S(1)}, u32[]{:S(2)}, u32[]{:S(2)}) collective-permute-start(bf16[64,896]{1,0:T(8,128)(2,1)S(1)} %get-tuple-element.9.refs_1_), channel_id=1, source_target_pairs={{0,4},{2,6},{4,12},{6,14},{12,8},{14,10},{8,0},{10,2},{1,5},{3,7},... | collective-permute-start | bytes 344072 | tf_op jit(solution)/shard_map/ppermute | solution.py:253
  6.8 23.6 %copy-start.1 = (bf16[896,1024]{1,0:T(8,128)(2,1)S(1)}, bf16[896,1024]{1,0:T(8,128)(2,1)}, u32[]{:S(2)}) copy-start(bf16[896,1024]{1,0:T(8,128)(2,1)} %wv_ref.3) | copy-start | bytes 5505028
  6.8 15.0 %collective-permute-start.2 = (bf16[64,1792]{1,0:T(8,128)(2,1)S(1)}, bf16[64,1792]{1,0:T(8,128)(2,1)S(1)}, u32[]{:S(2)}, u32[]{:S(2)}) collective-permute-start(bf16[64,1792]{1,0:T(8,128)(2,1)S(1)} %get-tuple-element.10), channel_id=1, source_target_pairs={{0,2},{2,0},{4,6},{6,4},{8,10},{10,8},{12,14},{14,12},{1,3},{3,1},... | collective-permute-start | bytes 688136 | tf_op jit(solution)/shard_map/ppermute | solution.py:253
  9.2 6.9 %collective-permute-start.3 = (bf16[64,896]{1,0:T(8,128)(2,1)S(1)}, bf16[64,896]{1,0:T(8,128)(2,1)S(1)}, u32[]{:S(2)}, u32[]{:S(2)}) collective-permute-start(bf16[64,896]{1,0:T(8,128)(2,1)S(1)} %collective-permute-done.refs_2_), channel_id=1, source_target_pairs={{0,4},{2,6},{4,12},{6,14},{12,8},{14,10},{8,0},{10,2},{1,5},{3,7},... | collective-permute-start | bytes 344072 | tf_op jit(solution)/shard_map/ppermute | solution.py:253
  10.8 7.7 %collective-permute-start.4 = (bf16[64,896]{1,0:T(8,128)(2,1)S(1)}, bf16[64,896]{1,0:T(8,128)(2,1)S(1)}, u32[]{:S(2)}, u32[]{:S(2)}) collective-permute-start(bf16[64,896]{1,0:T(8,128)(2,1)S(1)} %collective-permute-done.1.refs_3_), channel_id=1, source_target_pairs={{0,4},{2,6},{4,12},{6,14},{12,8},{14,10},{8,0},{10,2},{1,5},{3,7},... | collective-permute-start | bytes 344072 | tf_op jit(solution)/shard_map/ppermute | solution.py:253
  13.7 13.2 %collective-permute-start.5 = (bf16[64,1792]{1,0:T(8,128)(2,1)S(1)}, bf16[64,1792]{1,0:T(8,128)(2,1)S(1)}, u32[]{:S(2)}, u32[]{:S(2)}) collective-permute-start(bf16[64,1792]{1,0:T(8,128)(2,1)S(1)} %pad_maximum_fusion), channel_id=1, source_target_pairs={{0,2},{2,0},{4,6},{6,4},{8,10},{10,8},{12,14},{14,12},{1,3},{3,1},... | collective-permute-start | bytes 688136 | tf_op jit(solution)/shard_map/ppermute | solution.py:253
  16.1 6.2 %collective-permute-start.6 = (bf16[64,896]{1,0:T(8,128)(2,1)S(1)}, bf16[64,896]{1,0:T(8,128)(2,1)S(1)}, u32[]{:S(2)}, u32[]{:S(2)}) collective-permute-start(bf16[64,896]{1,0:T(8,128)(2,1)S(1)} %collective-permute-done.3.refs_5_), channel_id=1, source_target_pairs={{0,4},{2,6},{4,12},{6,14},{12,8},{14,10},{8,0},{10,2},{1,5},{3,7},... | collective-permute-start | bytes 344072 | tf_op jit(solution)/shard_map/ppermute | solution.py:253
  18.5 5.7 %collective-permute-start.7 = (bf16[64,896]{1,0:T(8,128)(2,1)S(1)}, bf16[64,896]{1,0:T(8,128)(2,1)S(1)}, u32[]{:S(2)}, u32[]{:S(2)}) collective-permute-start(bf16[64,896]{1,0:T(8,128)(2,1)S(1)} %collective-permute-done.4.refs_6_), channel_id=1, source_target_pairs={{0,4},{2,6},{4,12},{6,14},{12,8},{14,10},{8,0},{10,2},{1,5},{3,7},... | collective-permute-start | bytes 344072 | tf_op jit(solution)/shard_map/ppermute | solution.py:253
  20.3 7.2 %collective-permute-start.8 = (bf16[64,896]{1,0:T(8,128)(2,1)S(1)}, bf16[64,896]{1,0:T(8,128)(2,1)S(1)}, u32[]{:S(2)}, u32[]{:S(2)}) collective-permute-start(bf16[64,896]{1,0:T(8,128)(2,1)S(1)} %collective-permute-done.3.refs_5_), channel_id=1, source_target_pairs={{0,2},{2,0},{4,6},{6,4},{8,10},{10,8},{12,14},{14,12},{1,3},{3,1},... | collective-permute-start | bytes 344072 | tf_op jit(solution)/shard_map/ppermute | solution.py:253
  21.8 5.7 %collective-permute-start.9 = (bf16[64,896]{1,0:T(8,128)(2,1)S(1)}, bf16[64,896]{1,0:T(8,128)(2,1)S(1)}, u32[]{:S(2)}, u32[]{:S(2)}) collective-permute-start(bf16[64,896]{1,0:T(8,128)(2,1)S(1)} %collective-permute-done.4.refs_6_), channel_id=1, source_target_pairs={{0,2},{2,0},{4,6},{6,4},{8,10},{10,8},{12,14},{14,12},{1,3},{3,1},... | collective-permute-start | bytes 344072 | tf_op jit(solution)/shard_map/ppermute | solution.py:253
  22.3 6.4 %collective-permute-start.10 = (bf16[64,896]{1,0:T(8,128)(2,1)S(1)}, bf16[64,896]{1,0:T(8,128)(2,1)S(1)}, u32[]{:S(2)}, u32[]{:S(2)}) collective-permute-start(bf16[64,896]{1,0:T(8,128)(2,1)S(1)} %collective-permute-done.6.refs_0_), channel_id=1, source_target_pairs={{0,2},{2,0},{4,6},{6,4},{8,10},{10,8},{12,14},{14,12},{1,3},{3,1},... | collective-permute-start | bytes 344072 | tf_op jit(solution)/shard_map/ppermute | solution.py:253
  24.2 5.7 %collective-permute-start.11 = (bf16[64,896]{1,0:T(8,128)(2,1)S(1)}, bf16[64,896]{1,0:T(8,128)(2,1)S(1)}, u32[]{:S(2)}, u32[]{:S(2)}) collective-permute-start(bf16[64,896]{1,0:T(8,128)(2,1)S(1)} %collective-permute-done.7.refs_1_), channel_id=1, source_target_pairs={{0,2},{2,0},{4,6},{6,4},{8,10},{10,8},{12,14},{14,12},{1,3},{3,1},... | collective-permute-start | bytes 344072 | tf_op jit(solution)/shard_map/ppermute | solution.py:253
  25.4 0.7 %copy-start.4 = (s32[2,64,1]{1,2,0:T(1,128)S(1)}, s32[2,64,1]{1,2,0:T(1,128)}, u32[]{:S(2)}) copy-start(s32[2,64,1]{1,2,0:T(1,128)} %param.10) | copy-start | bytes 1540
  26.1 0.7 %copy-start.5 = (s32[2,64]{1,0:T(2,128)S(1)}, s32[2,64]{1,0:T(2,128)}, u32[]{:S(2)}) copy-start(s32[2,64]{1,0:T(2,128)} %stored_ref.1) | copy-start | bytes 1540
  27.4 3.7 %copy-start = (bf16[896,1024]{1,0:T(8,128)(2,1)S(1)}, bf16[896,1024]{1,0:T(8,128)(2,1)}, u32[]{:S(2)}) copy-start(bf16[896,1024]{1,0:T(8,128)(2,1)} %wk_ref.3) | copy-start | bytes 5505028
  27.4 3.7 %copy-start.2 = (bf16[128,1024]{1,0:T(8,128)(2,1)S(1)}, bf16[128,1024]{1,0:T(8,128)(2,1)}, u32[]{:S(2)}) copy-start(bf16[128,1024]{1,0:T(8,128)(2,1)} %query_ref.3) | copy-start | bytes 786436
  30.3 1.9 %collective-permute-start.12 = (bf16[128,1792]{1,0:T(8,128)(2,1)S(1)}, bf16[128,1792]{1,0:T(8,128)(2,1)S(1)}, u32[]{:S(2)}, u32[]{:S(2)}) collective-permute-start(bf16[128,1792]{1,0:T(8,128)(2,1)S(1)} %shard_map.67.picked_ref), channel_id=1, source_target_pairs={{0,1},{1,0},{2,3},{3,2},{4,5},{5,4},{6,7},{7,6},{8,9},{9,8},{10,11... | collective-permute-start | bytes 1376264 | tf_op jit(solution)/shard_map/ppermute | solution.py:286

commit v10 on v9

--- a/solution.py
+++ b/solution.py
@@ -48,20 +48,11 @@
     )(encodings)
 
 
-def chosen_rows(index, chunks, refs, first):
-    rows = refs[0].shape[0]
-    width = min(ref.shape[1] for ref in refs)
-    places = lax.broadcasted_iota(jnp.int32, (index.shape[0], len(chunks) * rows), 1) + first
-    chosen = jnp.where(places == index, 1.0, 0.0).astype(refs[0].dtype)
-    starts = [sum(chunks[:n]) for n in range(len(chunks))]
-    parts = []
-    for n in range(STREAMS):
-        held = [
-            refs[at + n][...] if arrays > 1 else refs[at][:, n * width : (n + 1) * width]
-            for at, arrays in zip(starts, chunks)
-        ]
-        parts.append(jnp.dot(chosen, jnp.concatenate(held, axis=0), preferred_element_type=jnp.float32))
-    return jnp.concatenate(parts, axis=1)
+def chosen_rows(index, sources, first):
+    held = jnp.concatenate(sources, axis=0)
+    places = lax.broadcasted_iota(jnp.int32, (index.shape[0], held.shape[0]), 1) + first
+    chosen = jnp.where(places == index, 1.0, 0.0).astype(held.dtype)
+    return jnp.dot(chosen, held, preferred_element_type=jnp.float32)
 
 
 def ring_order(turns):
@@ -106,7 +97,14 @@
 
 
 def early_kernel(chunks, index_ref, *refs):
-    refs[-1][...] = chosen_rows(index_ref[...], chunks, refs[:-1], 0).astype(refs[-1].dtype)
+    sources, outs = refs[:-STREAMS], refs[-STREAMS:]
+    starts = [sum(chunks[:n]) for n in range(len(chunks))]
+    for n, out in enumerate(outs):
+        lanes = slice(n * out.shape[1], (n + 1) * out.shape[1])
+        held = [
+            sources[at + n][...] if arrays > 1 else sources[at][:, lanes] for at, arrays in zip(starts, chunks)
+        ]
+        out[...] = chosen_rows(index_ref[...], held, 0).astype(out.dtype)
 
 
 def early(index, sources, width):
@@ -115,9 +113,9 @@
     arrays = [array for chunk in sources for array in chunk]
     return pl.pallas_call(
         functools.partial(early_kernel, [len(chunk) for chunk in sources]),
-        out_shape=jax.ShapeDtypeStruct((requests, width), arrays[0].dtype),
+        out_shape=[jax.ShapeDtypeStruct((requests, width // STREAMS), arrays[0].dtype)] * STREAMS,
         in_specs=[VMEM] * (1 + len(arrays)),
-        out_specs=VMEM,
+        out_specs=[VMEM] * STREAMS,
         compiler_params=params(),
         cost_estimate=pl.CostEstimate(
             flops=2 * requests * width * rows * len(sources),
@@ -127,28 +125,28 @@
     )(index, *arrays)
 
 
-def pick_kernel(chunks, first, index_ref, begun_ref, *refs):
-    picked = chosen_rows(index_ref[...], chunks, refs[:-1], first)
-    refs[-1][...] = (picked + begun_ref[...].astype(jnp.float32)).astype(begun_ref.dtype)
-
-
-def pick(index, begun, sources, first):
-    arrays = [array for chunk in sources for array in chunk]
-    return pl.pallas_call(
-        functools.partial(pick_kernel, [len(chunk) for chunk in sources], first),
+def pick_kernel(first, index_ref, begun_ref, last_ref, out_ref):
+    picked = chosen_rows(index_ref[...], [last_ref[...]], first)
+    out_ref[...] = (picked + begun_ref[...].astype(jnp.float32)).astype(out_ref.dtype)
+
+
+def pick(index, begun, last, first):
+    return pl.pallas_call(
+        functools.partial(pick_kernel, first),
         out_shape=jax.ShapeDtypeStruct(begun.shape, begun.dtype),
-        in_specs=[VMEM] * (2 + len(arrays)),
+        in_specs=[VMEM] * 3,
         out_specs=VMEM,
         compiler_params=params(),
-    )(index, begun, *arrays)
+    )(index, begun, last)
 
 
 def by_span(picked, spans, channels):
-    per = picked.shape[0] // spans
+    per = picked[0].shape[0] // spans
     parts = []
     for c in range(spans):
-        for t in range(picked.shape[1] // channels):
-            parts.append(picked[c * per : (c + 1) * per, t * channels : (t + 1) * channels])
+        for array in picked:
+            for t in range(array.shape[1] // channels):
+                parts.append(array[c * per : (c + 1) * per, t * channels : (t + 1) * channels])
     return jnp.concatenate(parts, axis=0)
 
 
@@ -181,44 +179,48 @@
         )
 
 
-def score_kernel(spans, picked_ref, wk_ref, query_ref, scores_ref):
-    score(spans, by_span(picked_ref[...], spans, wk_ref.shape[0]), wk_ref, query_ref, scores_ref)
+def score_kernel(spans, *refs):
+    *picked, wk_ref, query_ref, scores_ref = refs
+    score(spans, by_span(picked, spans, wk_ref.shape[0]), wk_ref, query_ref, scores_ref)
+
+
+def tokens(picked, channels):
+    return sum(array.size for array in picked) // channels
 
 
 def scores_shape(picked, queries, channels, spans):
-    return spans * (queries.shape[1] // (PAIR * HD)), picked.size // channels // spans, PAIR * SPAN
+    return spans * (queries.shape[1] // (PAIR * HD)), tokens(picked, channels) // spans, PAIR * SPAN
 
 
 def own_scores(picked, w_key, queries, spans):
     return pl.pallas_call(
         functools.partial(score_kernel, spans),
         out_shape=jax.ShapeDtypeStruct(scores_shape(picked, queries, w_key.shape[0], spans), jnp.float32),
-        in_specs=[VMEM] * 3,
+        in_specs=[VMEM] * (2 + len(picked)),
         out_specs=VMEM,
         compiler_params=params(),
-    )(picked, w_key, queries)
-
-
-def values_kernel(spans, picked_ref, wv_ref, values_ref):
-    source = by_span(picked_ref[...], spans, wv_ref.shape[0])
+    )(*picked, w_key, queries)
+
+
+def values_kernel(spans, *refs):
+    *picked, wv_ref, values_ref = refs
+    source = by_span(picked, spans, wv_ref.shape[0])
     values_ref[...] = jnp.dot(source, wv_ref[...], preferred_element_type=jnp.float32).astype(values_ref.dtype)
 
 
 def own_values(picked, w_value, spans):
-    rows = picked.size // w_value.shape[0]
     return pl.pallas_call(
         functools.partial(values_kernel, spans),
-        out_shape=jax.ShapeDtypeStruct((rows, w_value.shape[1]), picked.dtype),
-        in_specs=[VMEM] * 2,
+        out_shape=jax.ShapeDtypeStruct((tokens(picked, w_value.shape[0]), w_value.shape[1]), picked[0].dtype),
+        in_specs=[VMEM] * (1 + len(picked)),
         out_specs=VMEM,
         compiler_params=params(),
-    )(picked, w_value)
-
-
-def attend_kernel(
-    spans, other_ref, wk_ref, wv_ref, query_ref, first_ref, values_ref, out_ref, second_ref, probs_ref
-):
-    other = by_span(other_ref[...], spans, wk_ref.shape[0])
+    )(*picked, w_value)
+
+
+def attend_kernel(spans, *refs):
+    *others, wk_ref, wv_ref, query_ref, first_ref, values_ref, out_ref, second_ref, probs_ref, held_ref, sems = refs
+    other = by_span(others, spans, wk_ref.shape[0])
     score(spans, other, wk_ref, query_ref, second_ref)
     per = other.shape[0] // spans
     more = jnp.dot(other, wv_ref[...], preferred_element_type=jnp.float32).astype(jnp.bfloat16)
@@ -227,26 +229,40 @@
         scores = jnp.concatenate([first_ref[n], second_ref[n]], axis=0)
         raised = jnp.exp2((scores - jnp.max(scores, axis=0, keepdims=True)) * EXPONENT)
         probs_ref[n] = (raised * (1.0 / jnp.sum(raised, axis=0, keepdims=True))).astype(jnp.bfloat16)
-    for c, lanes, n in everything:
-        rows = slice(c * per, (c + 1) * per)
-        values = jnp.concatenate([values_ref[rows, lanes], more[rows, lanes]], axis=0)
-        mixed = lax.dot_general(
-            probs_ref[n], values, (((0,), (0,)), ((), ())), preferred_element_type=jnp.float32
-        ).astype(out_ref.dtype)
-        own = [mixed[h * SPAN : (h + 1) * SPAN, h * HD : (h + 1) * HD] for h in range(PAIR)]
-        out_ref[c * SPAN : (c + 1) * SPAN, lanes] = jnp.concatenate(own, axis=1)
-
-
-def attend(other, w_key, w_value, queries, first, values, spans):
-    each = scores_shape(other, queries, w_key.shape[0], spans)
+    copies = []
+    for c in range(spans):
+        here = pl.ds(c * SPAN, SPAN)
+        for at, lanes, n in everything:
+            if at != c:
+                continue
+            rows = slice(c * per, (c + 1) * per)
+            values = jnp.concatenate([values_ref[rows, lanes], more[rows, lanes]], axis=0)
+            mixed = lax.dot_general(
+                probs_ref[n], values, (((0,), (0,)), ((), ())), preferred_element_type=jnp.float32
+            ).astype(out_ref.dtype)
+            own = [mixed[h * SPAN : (h + 1) * SPAN, h * HD : (h + 1) * HD] for h in range(PAIR)]
+            held_ref[here, lanes] = jnp.concatenate(own, axis=1)
+        copies.append(pltpu.make_async_copy(held_ref.at[here, :], out_ref.at[here, :], sems.at[c]))
+        copies[-1].start()
+    for copy in copies:
+        copy.wait()
+
+
+def attend(others, w_key, w_value, queries, first, values, spans):
+    each = scores_shape(others, queries, w_key.shape[0], spans)
     return pl.pallas_call(
         functools.partial(attend_kernel, spans),
         out_shape=jax.ShapeDtypeStruct(queries.shape, queries.dtype),
-        in_specs=[VMEM] * 6,
-        out_specs=VMEM,
-        scratch_shapes=[pltpu.VMEM(each, jnp.float32), pltpu.VMEM((each[0], 2 * each[1], each[2]), jnp.bfloat16)],
-        compiler_params=params(),
-    )(other, w_key, w_value, queries, first, values)
+        in_specs=[VMEM] * (5 + len(others)),
+        out_specs=pl.BlockSpec(memory_space=pl.ANY),
+        scratch_shapes=[
+            pltpu.VMEM(each, jnp.float32),
+            pltpu.VMEM((each[0], 2 * each[1], each[2]), jnp.bfloat16),
+            pltpu.VMEM(queries.shape, queries.dtype),
+            pltpu.SemaphoreType.DMA((spans,)),
+        ],
+        compiler_params=params(),
+    )(*others, w_key, w_value, queries, first, values)
 
 
 def send(chunk, pairs):
@@ -279,14 +295,13 @@
             held[k - 1, 1] = [send(piece, across) for piece in behind]
         held[k, 0] = steps
     held[turns - 1, 1] = [send(piece, across) for piece in held[turns - 1, 0]]
-    late = 3
     sources = [held[chunk] for chunk in order]
-    begun = early(index, sources[:-late], whole.shape[1])
-    picked = pick(index, begun, sources[-late:], (len(order) - late) * rows)
-    other = lax.ppermute(picked, "heads", [(0, 1), (1, 0)])
+    begun = early(index, sources[:-1], whole.shape[1])
+    picked = [pick(index, *pieces, (len(order) - 1) * rows) for pieces in zip(begun, sources[-1])]
+    others = [lax.ppermute(piece, "heads", [(0, 1), (1, 0)]) for piece in picked]
     first = own_scores(picked, w_key, queries, spans)
     values = own_values(picked, w_value, spans)
-    return attend(other, w_key, w_value, queries, first, values, spans)
+    return attend(others, w_key, w_value, queries, first, values, spans)
 
 
 def exchange(encodings, owners, stored, capacity):

time: 34.9 us -> 36 us (1.032)
  starting transfers between devices: 20.1 us -> 21.3 us
    ppermute x12, starting transfers between devices: 20 us -> 21.1 us  [send(): return lax.ppermute(chunk, 'wide', pairs)]
  transfers between devices with their start and end apart: 13 -> 14, of which waited for: 8 -> 8; matrix products, arithmetic and copies ran while one was open for 0% -> 0% of each run, Pallas kernels for 6% -> 8%
where the time goes in v10:
time: 36 us; the launch traced here: 35.8 us
  starting transfers between devices  21.3 us (59%)
  waiting for transfers between devices  6.66 us (18%)
  Pallas kernels  5.27 us (15%)
  local copies, waits for them, and re-layouts  2.39 us (7%)
    ppermute x12, starting transfers between devices, send(): return lax.ppermute(chunk, 'wide', pairs)  21.1 us
    ppermute x12, waiting for transfers between devices, send(): return lax.ppermute(chunk, 'wide', pairs)  6.65 us
    pallas_call x1, Pallas kernels, attend(): pl.pallas_call(functools.partial(attend_kernel, spans), out_shape=jax.Sha...  2.48 us
    unnamed x12, local copies, waits for them, and re-layouts  2.39 us
    pallas_call x1, Pallas kernels, own_scores(): pl.pallas_call(functools.partial(score_kernel, spans), out_shape=jax.Shap...  0.87 us
  transfers between devices with their start and end apart: 14, of which 8 were waited for; matrix products, arithmetic and copies ran while one was open for 0% of the time, Pallas kernels for 8%

profile of v10, /device:TPU:0, one launch (start us, length us, event | category | flops | bytes accessed | tf_op | source)
XLA Modules:
  0.0 35.8 jit_solution(6411468481751366886)
XLA Ops:
  0.0 1.0 %copy-done.3 = bf16[64,3584]{1,0:T(8,128)(2,1)S(1)} copy-done((bf16[64,3584]{1,0:T(8,128)(2,1)S(1)}, bf16[64,3584]{1,0:T(8,128)(2,1)}, u32[]{:S(2)}) %copy-start.3) | copy-done | bytes 458776
  1.1 3.1 %collective-permute-start = (bf16[64,896]{1,0:T(8,128)(2,1)S(1)}, bf16[64,896]{1,0:T(8,128)(2,1)S(1)}, u32[]{:S(2)}, u32[]{:S(2)}) collective-permute-start(bf16[64,896]{1,0:T(8,128)(2,1)S(1)} %get-tuple-element.10.refs_0_), channel_id=1, source_target_pairs={{0,4},{2,6},{4,12},{6,14},{12,8},{14,10},{8,0},{10,2},{1,5},{3,7},... | collective-permute-start | bytes 344072 | tf_op jit(solution)/shard_map/ppermute | solution.py:269
  4.2 2.6 %collective-permute-start.1 = (bf16[64,896]{1,0:T(8,128)(2,1)S(1)}, bf16[64,896]{1,0:T(8,128)(2,1)S(1)}, u32[]{:S(2)}, u32[]{:S(2)}) collective-permute-start(bf16[64,896]{1,0:T(8,128)(2,1)S(1)} %get-tuple-element.11.refs_1_), channel_id=1, source_target_pairs={{0,4},{2,6},{4,12},{6,14},{12,8},{14,10},{8,0},{10,2},{1,5},{3,7},... | collective-permute-start | bytes 344072 | tf_op jit(solution)/shard_map/ppermute | solution.py:269
  6.8 1.5 %collective-permute-start.2 = (bf16[64,1792]{1,0:T(8,128)(2,1)S(1)}, bf16[64,1792]{1,0:T(8,128)(2,1)S(1)}, u32[]{:S(2)}, u32[]{:S(2)}) collective-permute-start(bf16[64,1792]{1,0:T(8,128)(2,1)S(1)} %get-tuple-element.12), channel_id=1, source_target_pairs={{0,2},{2,0},{4,6},{6,4},{8,10},{10,8},{12,14},{14,12},{1,3},{3,1},... | collective-permute-start | bytes 688136 | tf_op jit(solution)/shard_map/ppermute | solution.py:269
  8.3 0.9 %collective-permute-done.refs_2_ = bf16[64,896]{1,0:T(8,128)(2,1)S(1)} collective-permute-done((bf16[64,896]{1,0:T(8,128)(2,1)S(1)}, bf16[64,896]{1,0:T(8,128)(2,1)S(1)}, u32[]{:S(2)}, u32[]{:S(2)}) %collective-permute-start) | collective-permute-done | bytes 114720 | tf_op jit(solution)/shard_map/ppermute | solution.py:269
  9.2 1.2 %collective-permute-start.3 = (bf16[64,896]{1,0:T(8,128)(2,1)S(1)}, bf16[64,896]{1,0:T(8,128)(2,1)S(1)}, u32[]{:S(2)}, u32[]{:S(2)}) collective-permute-start(bf16[64,896]{1,0:T(8,128)(2,1)S(1)} %collective-permute-done.refs_2_), channel_id=1, source_target_pairs={{0,4},{2,6},{4,12},{6,14},{12,8},{14,10},{8,0},{10,2},{1,5},{3,7},... | collective-permute-start | bytes 344072 | tf_op jit(solution)/shard_map/ppermute | solution.py:269
  10.8 2.9 %collective-permute-start.4 = (bf16[64,896]{1,0:T(8,128)(2,1)S(1)}, bf16[64,896]{1,0:T(8,128)(2,1)S(1)}, u32[]{:S(2)}, u32[]{:S(2)}) collective-permute-start(bf16[64,896]{1,0:T(8,128)(2,1)S(1)} %collective-permute-done.1.refs_3_), channel_id=1, source_target_pairs={{0,4},{2,6},{4,12},{6,14},{12,8},{14,10},{8,0},{10,2},{1,5},{3,7},... | collective-permute-start | bytes 344072 | tf_op jit(solution)/shard_map/ppermute | solution.py:269
  13.8 1.6 %collective-permute-start.5 = (bf16[64,1792]{1,0:T(8,128)(2,1)S(1)}, bf16[64,1792]{1,0:T(8,128)(2,1)S(1)}, u32[]{:S(2)}, u32[]{:S(2)}) collective-permute-start(bf16[64,1792]{1,0:T(8,128)(2,1)S(1)} %pad_maximum_fusion), channel_id=1, source_target_pairs={{0,2},{2,0},{4,6},{6,4},{8,10},{10,8},{12,14},{14,12},{1,3},{3,1},... | collective-permute-start | bytes 688136 | tf_op jit(solution)/shard_map/ppermute | solution.py:269
  15.3 2.0 %collective-permute-done.4.refs_6_ = bf16[64,896]{1,0:T(8,128)(2,1)S(1)} collective-permute-done((bf16[64,896]{1,0:T(8,128)(2,1)S(1)}, bf16[64,896]{1,0:T(8,128)(2,1)S(1)}, u32[]{:S(2)}, u32[]{:S(2)}) %collective-permute-start.4) | collective-permute-done | bytes 114720 | tf_op jit(solution)/shard_map/ppermute | solution.py:269
  17.3 1.2 %collective-permute-start.7 = (bf16[64,896]{1,0:T(8,128)(2,1)S(1)}, bf16[64,896]{1,0:T(8,128)(2,1)S(1)}, u32[]{:S(2)}, u32[]{:S(2)}) collective-permute-start(bf16[64,896]{1,0:T(8,128)(2,1)S(1)} %collective-permute-done.4.refs_6_), channel_id=1, source_target_pairs={{0,4},{2,6},{4,12},{6,14},{12,8},{14,10},{8,0},{10,2},{1,5},{3,7},... | collective-permute-start | bytes 344072 | tf_op jit(solution)/shard_map/ppermute | solution.py:269
  18.5 2.7 %collective-permute-start.6 = (bf16[64,896]{1,0:T(8,128)(2,1)S(1)}, bf16[64,896]{1,0:T(8,128)(2,1)S(1)}, u32[]{:S(2)}, u32[]{:S(2)}) collective-permute-start(bf16[64,896]{1,0:T(8,128)(2,1)S(1)} %collective-permute-done.3.refs_5_), channel_id=1, source_target_pairs={{0,4},{2,6},{4,12},{6,14},{12,8},{14,10},{8,0},{10,2},{1,5},{3,7},... | collective-permute-start | bytes 344072 | tf_op jit(solution)/shard_map/ppermute | solution.py:269
  21.2 1.5 %collective-permute-start.8 = (bf16[64,896]{1,0:T(8,128)(2,1)S(1)}, bf16[64,896]{1,0:T(8,128)(2,1)S(1)}, u32[]{:S(2)}, u32[]{:S(2)}) collective-permute-start(bf16[64,896]{1,0:T(8,128)(2,1)S(1)} %collective-permute-done.3.refs_5_), channel_id=1, source_target_pairs={{0,2},{2,0},{4,6},{6,4},{8,10},{10,8},{12,14},{14,12},{1,3},{3,1},... | collective-permute-start | bytes 344072 | tf_op jit(solution)/shard_map/ppermute | solution.py:269
  22.7 0.5 %collective-permute-start.9 = (bf16[64,896]{1,0:T(8,128)(2,1)S(1)}, bf16[64,896]{1,0:T(8,128)(2,1)S(1)}, u32[]{:S(2)}, u32[]{:S(2)}) collective-permute-start(bf16[64,896]{1,0:T(8,128)(2,1)S(1)} %collective-permute-done.4.refs_6_), channel_id=1, source_target_pairs={{0,2},{2,0},{4,6},{6,4},{8,10},{10,8},{12,14},{14,12},{1,3},{3,1},... | collective-permute-start | bytes 344072 | tf_op jit(solution)/shard_map/ppermute | solution.py:269
  23.3 1.4 %collective-permute-start.12 = (bf16[64,896]{1,0:T(8,128)(2,1)S(1)}, bf16[64,896]{1,0:T(8,128)(2,1)S(1)}, u32[]{:S(2)}, u32[]{:S(2)}) collective-permute-start(bf16[64,896]{1,0:T(8,128)(2,1)S(1)} %collective-permute-done.7.refs_9_), channel_id=1, source_target_pairs={{0,2},{2,0},{4,6},{6,4},{8,10},{10,8},{12,14},{14,12},{1,3},{3,1},... | collective-permute-start | bytes 344072 | tf_op jit(solution)/shard_map/ppermute | solution.py:269
  24.7 1.0 %collective-permute-start.10 = (bf16[64,896]{1,0:T(8,128)(2,1)S(1)}, bf16[64,896]{1,0:T(8,128)(2,1)S(1)}, u32[]{:S(2)}, u32[]{:S(2)}) collective-permute-start(bf16[64,896]{1,0:T(8,128)(2,1)S(1)} %collective-permute-done.6.refs_8_), channel_id=1, source_target_pairs={{0,2},{2,0},{4,6},{6,4},{8,10},{10,8},{12,14},{14,12},{1,3},{3,1},... | collective-permute-start | bytes 344072 | tf_op jit(solution)/shard_map/ppermute | solution.py:269
  25.7 0.7 %copy-done.4 = s32[2,64,1]{1,2,0:T(1,128)S(1)} copy-done((s32[2,64,1]{1,2,0:T(1,128)S(1)}, s32[2,64,1]{1,2,0:T(1,128)}, u32[]{:S(2)}) %copy-start.4) | copy-done | bytes 536
  26.4 0.7 %copy-done.5 = s32[2,64]{1,0:T(2,128)S(1)} copy-done((s32[2,64]{1,0:T(2,128)S(1)}, s32[2,64]{1,0:T(2,128)}, u32[]{:S(2)}) %copy-start.5) | copy-done | bytes 536
  27.3 1.6 %collective-permute-done.9.refs_11_ = bf16[64,896]{1,0:T(8,128)(2,1)S(1)} collective-permute-done((bf16[64,896]{1,0:T(8,128)(2,1)S(1)}, bf16[64,896]{1,0:T(8,128)(2,1)S(1)}, u32[]{:S(2)}, u32[]{:S(2)}) %collective-permute-start.9) | collective-permute-done | bytes 114720 | tf_op jit(solution)/shard_map/ppermute | solution.py:269
  28.8 0.5 %shard_map.66 = (bf16[128,896]{1,0:T(8,128)(2,1)S(1)}, bf16[128,896]{1,0:T(8,128)(2,1)S(1)}) custom-call(s32[128,1]{1,0:T(8,128)S(1)} %shard_map.64.index_ref, bf16[64,896]{1,0:T(8,128)(2,1)S(1)} %get-tuple-element.10.refs_0_, bf16[64,896]{1,0:T(8,128)(2,1)S(1)} %get-tuple-element.11.refs_1_, bf16[64,896]{1,0:T(8,128)(2,1)S(1)} %collective-permute-done.refs_2_, ...), custom_call_target="tpu_custom_call" | custom-call | flops 205520896 | bytes 458752 | tf_op jit(solution)/shard_map/pallas_call | solution.py:114
  29.3 0.7 %collective-permute-done.12.last_ref = bf16[64,896]{1,0:T(8,128)(2,1)S(1)} collective-permute-done((bf16[64,896]{1,0:T(8,128)(2,1)S(1)}, bf16[64,896]{1,0:T(8,128)(2,1)S(1)}, u32[]{:S(2)}, u32[]{:S(2)}) %collective-permute-start.12) | collective-permute-done | bytes 114720 | tf_op jit(solution)/shard_map/ppermute | solution.py:269
  30.4 0.9 %collective-permute-done.10.last_ref = bf16[64,896]{1,0:T(8,128)(2,1)S(1)} collective-permute-done((bf16[64,896]{1,0:T(8,128)(2,1)S(1)}, bf16[64,896]{1,0:T(8,128)(2,1)S(1)}, u32[]{:S(2)}, u32[]{:S(2)}) %collective-permute-start.10) | collective-permute-done | bytes 114720 | tf_op jit(solution)/shard_map/ppermute | solution.py:269
  31.6 0.7 %shard_map.70.refs_6_ = bf16[256,1024]{1,0:T(8,128)(2,1)S(1)} custom-call(bf16[128,896]{1,0:T(8,128)(2,1)S(1)} %shard_map.67.refs_0_, bf16[128,896]{1,0:T(8,128)(2,1)S(1)} %shard_map.68.refs_1_, bf16[896,1024]{1,0:T(8,128)(2,1)S(1)} %copy-done.1), custom_call_target="tpu_custom_call" | custom-call | tf_op jit(solution)/shard_map/pallas_call | solution.py:212
  32.4 0.9 %shard_map.69.refs_5_ = f32[8,128,128]{2,1,0:T(8,128)S(1)} custom-call(bf16[128,896]{1,0:T(8,128)(2,1)S(1)} %shard_map.67.refs_0_, bf16[128,896]{1,0:T(8,128)(2,1)S(1)} %shard_map.68.refs_1_, bf16[896,1024]{1,0:T(8,128)(2,1)S(1)} %copy-done, bf16[128,1024]{1,0:T(8,128)(2,1)S(1)} %copy-done.2), custom_call_target="tpu_custom_call" | custom-call | tf_op jit(solution)/shard_map/pallas_call | solution.py:196
  33.3 2.5 %shard_map.71 = bf16[128,1024]{1,0:T(8,128)(2,1)} custom-call(bf16[128,896]{1,0:T(8,128)(2,1)S(1)} %collective-permute-done.11.refs_0_, bf16[128,896]{1,0:T(8,128)(2,1)S(1)} %collective-permute-done.13.refs_1_, bf16[896,1024]{1,0:T(8,128)(2,1)S(1)} %copy-done, bf16[896,1024]{1,0:T(8,128)(2,1)S(1)} %copy-done.1, bf16[128,1024]{1,0:T(8,128)(2,1)S(1)} %copy-done.2, ...), custom_call_target="tpu_custom_call" | custom-call | tf_op jit(solution)/shard_map/pallas_call | solution.py:253
  (25 shorter events, 1.5 us)
Async XLA Ops:
  0.0 1.0 %copy-start.3 = (bf16[64,3584]{1,0:T(8,128)(2,1)S(1)}, bf16[64,3584]{1,0:T(8,128)(2,1)}, u32[]{:S(2)}) copy-start(bf16[64,3584]{1,0:T(8,128)(2,1)} %enc_ref.1) | copy-start | bytes 1376260
  1.1 30.5 %copy-start.1 = (bf16[896,1024]{1,0:T(8,128)(2,1)S(1)}, bf16[896,1024]{1,0:T(8,128)(2,1)}, u32[]{:S(2)}) copy-start(bf16[896,1024]{1,0:T(8,128)(2,1)} %refs_3_.3) | copy-start | bytes 5505028
  1.1 8.1 %collective-permute-start = (bf16[64,896]{1,0:T(8,128)(2,1)S(1)}, bf16[64,896]{1,0:T(8,128)(2,1)S(1)}, u32[]{:S(2)}, u32[]{:S(2)}) collective-permute-start(bf16[64,896]{1,0:T(8,128)(2,1)S(1)} %get-tuple-element.10.refs_0_), channel_id=1, source_target_pairs={{0,4},{2,6},{4,12},{6,14},{12,8},{14,10},{8,0},{10,2},{1,5},{3,7},... | collective-permute-start | bytes 344072 | tf_op jit(solution)/shard_map/ppermute | solution.py:269
  4.2 6.6 %collective-permute-start.1 = (bf16[64,896]{1,0:T(8,128)(2,1)S(1)}, bf16[64,896]{1,0:T(8,128)(2,1)S(1)}, u32[]{:S(2)}, u32[]{:S(2)}) collective-permute-start(bf16[64,896]{1,0:T(8,128)(2,1)S(1)} %get-tuple-element.11.refs_1_), channel_id=1, source_target_pairs={{0,4},{2,6},{4,12},{6,14},{12,8},{14,10},{8,0},{10,2},{1,5},{3,7},... | collective-permute-start | bytes 344072 | tf_op jit(solution)/shard_map/ppermute | solution.py:269
  6.8 15.9 %collective-permute-start.2 = (bf16[64,1792]{1,0:T(8,128)(2,1)S(1)}, bf16[64,1792]{1,0:T(8,128)(2,1)S(1)}, u32[]{:S(2)}, u32[]{:S(2)}) collective-permute-start(bf16[64,1792]{1,0:T(8,128)(2,1)S(1)} %get-tuple-element.12), channel_id=1, source_target_pairs={{0,2},{2,0},{4,6},{6,4},{8,10},{10,8},{12,14},{14,12},{1,3},{3,1},... | collective-permute-start | bytes 688136 | tf_op jit(solution)/shard_map/ppermute | solution.py:269
  9.2 9.3 %collective-permute-start.3 = (bf16[64,896]{1,0:T(8,128)(2,1)S(1)}, bf16[64,896]{1,0:T(8,128)(2,1)S(1)}, u32[]{:S(2)}, u32[]{:S(2)}) collective-permute-start(bf16[64,896]{1,0:T(8,128)(2,1)S(1)} %collective-permute-done.refs_2_), channel_id=1, source_target_pairs={{0,4},{2,6},{4,12},{6,14},{12,8},{14,10},{8,0},{10,2},{1,5},{3,7},... | collective-permute-start | bytes 344072 | tf_op jit(solution)/shard_map/ppermute | solution.py:269
  10.8 6.5 %collective-permute-start.4 = (bf16[64,896]{1,0:T(8,128)(2,1)S(1)}, bf16[64,896]{1,0:T(8,128)(2,1)S(1)}, u32[]{:S(2)}, u32[]{:S(2)}) collective-permute-start(bf16[64,896]{1,0:T(8,128)(2,1)S(1)} %collective-permute-done.1.refs_3_), channel_id=1, source_target_pairs={{0,4},{2,6},{4,12},{6,14},{12,8},{14,10},{8,0},{10,2},{1,5},{3,7},... | collective-permute-start | bytes 344072 | tf_op jit(solution)/shard_map/ppermute | solution.py:269
  13.8 13.5 %collective-permute-start.5 = (bf16[64,1792]{1,0:T(8,128)(2,1)S(1)}, bf16[64,1792]{1,0:T(8,128)(2,1)S(1)}, u32[]{:S(2)}, u32[]{:S(2)}) collective-permute-start(bf16[64,1792]{1,0:T(8,128)(2,1)S(1)} %pad_maximum_fusion), channel_id=1, source_target_pairs={{0,2},{2,0},{4,6},{6,4},{8,10},{10,8},{12,14},{14,12},{1,3},{3,1},... | collective-permute-start | bytes 688136 | tf_op jit(solution)/shard_map/ppermute | solution.py:269
  17.3 6.0 %collective-permute-start.7 = (bf16[64,896]{1,0:T(8,128)(2,1)S(1)}, bf16[64,896]{1,0:T(8,128)(2,1)S(1)}, u32[]{:S(2)}, u32[]{:S(2)}) collective-permute-start(bf16[64,896]{1,0:T(8,128)(2,1)S(1)} %collective-permute-done.4.refs_6_), channel_id=1, source_target_pairs={{0,4},{2,6},{4,12},{6,14},{12,8},{14,10},{8,0},{10,2},{1,5},{3,7},... | collective-permute-start | bytes 344072 | tf_op jit(solution)/shard_map/ppermute | solution.py:269
  18.5 6.2 %collective-permute-start.6 = (bf16[64,896]{1,0:T(8,128)(2,1)S(1)}, bf16[64,896]{1,0:T(8,128)(2,1)S(1)}, u32[]{:S(2)}, u32[]{:S(2)}) collective-permute-start(bf16[64,896]{1,0:T(8,128)(2,1)S(1)} %collective-permute-done.3.refs_5_), channel_id=1, source_target_pairs={{0,4},{2,6},{4,12},{6,14},{12,8},{14,10},{8,0},{10,2},{1,5},{3,7},... | collective-permute-start | bytes 344072 | tf_op jit(solution)/shard_map/ppermute | solution.py:269
  21.2 6.1 %collective-permute-start.8 = (bf16[64,896]{1,0:T(8,128)(2,1)S(1)}, bf16[64,896]{1,0:T(8,128)(2,1)S(1)}, u32[]{:S(2)}, u32[]{:S(2)}) collective-permute-start(bf16[64,896]{1,0:T(8,128)(2,1)S(1)} %collective-permute-done.3.refs_5_), channel_id=1, source_target_pairs={{0,2},{2,0},{4,6},{6,4},{8,10},{10,8},{12,14},{14,12},{1,3},{3,1},... | collective-permute-start | bytes 344072 | tf_op jit(solution)/shard_map/ppermute | solution.py:269
  22.7 6.1 %collective-permute-start.9 = (bf16[64,896]{1,0:T(8,128)(2,1)S(1)}, bf16[64,896]{1,0:T(8,128)(2,1)S(1)}, u32[]{:S(2)}, u32[]{:S(2)}) collective-permute-start(bf16[64,896]{1,0:T(8,128)(2,1)S(1)} %collective-permute-done.4.refs_6_), channel_id=1, source_target_pairs={{0,2},{2,0},{4,6},{6,4},{8,10},{10,8},{12,14},{14,12},{1,3},{3,1},... | collective-permute-start | bytes 344072 | tf_op jit(solution)/shard_map/ppermute | solution.py:269
  23.3 6.8 %collective-permute-start.12 = (bf16[64,896]{1,0:T(8,128)(2,1)S(1)}, bf16[64,896]{1,0:T(8,128)(2,1)S(1)}, u32[]{:S(2)}, u32[]{:S(2)}) collective-permute-start(bf16[64,896]{1,0:T(8,128)(2,1)S(1)} %collective-permute-done.7.refs_9_), channel_id=1, source_target_pairs={{0,2},{2,0},{4,6},{6,4},{8,10},{10,8},{12,14},{14,12},{1,3},{3,1},... | collective-permute-start | bytes 344072 | tf_op jit(solution)/shard_map/ppermute | solution.py:269
  24.7 6.6 %collective-permute-start.10 = (bf16[64,896]{1,0:T(8,128)(2,1)S(1)}, bf16[64,896]{1,0:T(8,128)(2,1)S(1)}, u32[]{:S(2)}, u32[]{:S(2)}) collective-permute-start(bf16[64,896]{1,0:T(8,128)(2,1)S(1)} %collective-permute-done.6.refs_8_), channel_id=1, source_target_pairs={{0,2},{2,0},{4,6},{6,4},{8,10},{10,8},{12,14},{14,12},{1,3},{3,1},... | collective-permute-start | bytes 344072 | tf_op jit(solution)/shard_map/ppermute | solution.py:269
  25.7 0.7 %copy-start.4 = (s32[2,64,1]{1,2,0:T(1,128)S(1)}, s32[2,64,1]{1,2,0:T(1,128)}, u32[]{:S(2)}) copy-start(s32[2,64,1]{1,2,0:T(1,128)} %param.10) | copy-start | bytes 1540
  26.4 0.7 %copy-start.5 = (s32[2,64]{1,0:T(2,128)S(1)}, s32[2,64]{1,0:T(2,128)}, u32[]{:S(2)}) copy-start(s32[2,64]{1,0:T(2,128)} %stored_ref.1) | copy-start | bytes 1540
  30.3 2.0 %copy-start = (bf16[896,1024]{1,0:T(8,128)(2,1)S(1)}, bf16[896,1024]{1,0:T(8,128)(2,1)}, u32[]{:S(2)}) copy-start(bf16[896,1024]{1,0:T(8,128)(2,1)} %refs_2_.5) | copy-start | bytes 5505028
  30.3 2.0 %copy-start.2 = (bf16[128,1024]{1,0:T(8,128)(2,1)S(1)}, bf16[128,1024]{1,0:T(8,128)(2,1)}, u32[]{:S(2)}) copy-start(bf16[128,1024]{1,0:T(8,128)(2,1)} %refs_4_.1) | copy-start | bytes 786436
  30.3 2.9 %collective-permute-start.13 = (bf16[128,896]{1,0:T(8,128)(2,1)S(1)}, bf16[128,896]{1,0:T(8,128)(2,1)S(1)}, u32[]{:S(2)}, u32[]{:S(2)}) collective-permute-start(bf16[128,896]{1,0:T(8,128)(2,1)S(1)} %shard_map.68.refs_1_), channel_id=1, source_target_pairs={{0,1},{1,0},{2,3},{3,2},{4,5},{5,4},{6,7},{7,6},{8,9},{9,8},{10,11... | collective-permute-start | bytes 688136 | tf_op jit(solution)/shard_map/ppermute | solution.py:301
  31.6 1.7 %collective-permute-start.11 = (bf16[128,896]{1,0:T(8,128)(2,1)S(1)}, bf16[128,896]{1,0:T(8,128)(2,1)S(1)}, u32[]{:S(2)}, u32[]{:S(2)}) collective-permute-start(bf16[128,896]{1,0:T(8,128)(2,1)S(1)} %shard_map.67.refs_0_), channel_id=1, source_target_pairs={{0,1},{1,0},{2,3},{3,2},{4,5},{5,4},{6,7},{7,6},{8,9},{9,8},{10,11... | collective-permute-start | bytes 688136 | tf_op jit(solution)/shard_map/ppermute | solution.py:301

commit v11 on v10

--- a/solution.py
+++ b/solution.py
@@ -297,7 +297,7 @@
     held[turns - 1, 1] = [send(piece, across) for piece in held[turns - 1, 0]]
     sources = [held[chunk] for chunk in order]
     begun = early(index, sources[:-1], whole.shape[1])
-    picked = [pick(index, *pieces, (len(order) - 1) * rows) for pieces in zip(begun, sources[-1])]
+    picked = [pick(index, *pieces, (len(order) - 1) * rows) for pieces in zip(begun[::-1], sources[-1][::-1])]
     others = [lax.ppermute(piece, "heads", [(0, 1), (1, 0)]) for piece in picked]
     first = own_scores(picked, w_key, queries, spans)
     values = own_values(picked, w_value, spans)

time: 36 us -> 34.6 us (0.961)
  starting transfers between devices: 21.3 us -> 20.2 us
    ppermute x12, starting transfers between devices: 21.1 us -> 20 us  [send(): return lax.ppermute(chunk, 'wide', pairs)]
where the time goes in v11:
time: 34.6 us; the launch traced here: 34.4 us
  starting transfers between devices  20.2 us (58%)
  waiting for transfers between devices  6.38 us (18%)
  Pallas kernels  5.27 us (15%)
  local copies, waits for them, and re-layouts  2.39 us (7%)
    ppermute x12, starting transfers between devices, send(): return lax.ppermute(chunk, 'wide', pairs)  20 us
    ppermute x12, waiting for transfers between devices, send(): return lax.ppermute(chunk, 'wide', pairs)  6.37 us
    pallas_call x1, Pallas kernels, attend(): pl.pallas_call(functools.partial(attend_kernel, spans), out_shape=jax.Sha...  2.48 us
    unnamed x12, local copies, waits for them, and re-layouts  2.39 us
    pallas_call x1, Pallas kernels, own_scores(): pl.pallas_call(functools.partial(score_kernel, spans), out_shape=jax.Shap...  0.87 us
    pallas_call x1, Pallas kernels, own_values(): pl.pallas_call(functools.partial(values_kernel, spans), out_shape=jax.Sha...  0.71 us
  transfers between devices with their start and end apart: 14, of which 8 were waited for; matrix products, arithmetic and copies ran while one was open for 0% of the time, Pallas kernels for 8%

profile of v11, /device:TPU:0, one launch (start us, length us, event | category | flops | bytes accessed | tf_op | source)
XLA Modules:
  0.0 34.4 jit_solution(115991258617183700)
XLA Ops:
  0.0 1.0 %copy-done.3 = bf16[64,3584]{1,0:T(8,128)(2,1)S(1)} copy-done((bf16[64,3584]{1,0:T(8,128)(2,1)S(1)}, bf16[64,3584]{1,0:T(8,128)(2,1)}, u32[]{:S(2)}) %copy-start.3) | copy-done | bytes 458776
  1.1 3.1 %collective-permute-start = (bf16[64,896]{1,0:T(8,128)(2,1)S(1)}, bf16[64,896]{1,0:T(8,128)(2,1)S(1)}, u32[]{:S(2)}, u32[]{:S(2)}) collective-permute-start(bf16[64,896]{1,0:T(8,128)(2,1)S(1)} %get-tuple-element.10.refs_0_), channel_id=1, source_target_pairs={{0,4},{2,6},{4,12},{6,14},{12,8},{14,10},{8,0},{10,2},{1,5},{3,7},... | collective-permute-start | bytes 344072 | tf_op jit(solution)/shard_map/ppermute | solution.py:269
  4.2 2.6 %collective-permute-start.1 = (bf16[64,896]{1,0:T(8,128)(2,1)S(1)}, bf16[64,896]{1,0:T(8,128)(2,1)S(1)}, u32[]{:S(2)}, u32[]{:S(2)}) collective-permute-start(bf16[64,896]{1,0:T(8,128)(2,1)S(1)} %get-tuple-element.11.refs_1_), channel_id=1, source_target_pairs={{0,4},{2,6},{4,12},{6,14},{12,8},{14,10},{8,0},{10,2},{1,5},{3,7},... | collective-permute-start | bytes 344072 | tf_op jit(solution)/shard_map/ppermute | solution.py:269
  6.8 1.5 %collective-permute-start.2 = (bf16[64,1792]{1,0:T(8,128)(2,1)S(1)}, bf16[64,1792]{1,0:T(8,128)(2,1)S(1)}, u32[]{:S(2)}, u32[]{:S(2)}) collective-permute-start(bf16[64,1792]{1,0:T(8,128)(2,1)S(1)} %get-tuple-element.12), channel_id=1, source_target_pairs={{0,2},{2,0},{4,6},{6,4},{8,10},{10,8},{12,14},{14,12},{1,3},{3,1},... | collective-permute-start | bytes 688136 | tf_op jit(solution)/shard_map/ppermute | solution.py:269
  8.3 0.9 %collective-permute-done.refs_2_ = bf16[64,896]{1,0:T(8,128)(2,1)S(1)} collective-permute-done((bf16[64,896]{1,0:T(8,128)(2,1)S(1)}, bf16[64,896]{1,0:T(8,128)(2,1)S(1)}, u32[]{:S(2)}, u32[]{:S(2)}) %collective-permute-start) | collective-permute-done | bytes 114720 | tf_op jit(solution)/shard_map/ppermute | solution.py:269
  9.2 1.2 %collective-permute-start.3 = (bf16[64,896]{1,0:T(8,128)(2,1)S(1)}, bf16[64,896]{1,0:T(8,128)(2,1)S(1)}, u32[]{:S(2)}, u32[]{:S(2)}) collective-permute-start(bf16[64,896]{1,0:T(8,128)(2,1)S(1)} %collective-permute-done.refs_2_), channel_id=1, source_target_pairs={{0,4},{2,6},{4,12},{6,14},{12,8},{14,10},{8,0},{10,2},{1,5},{3,7},... | collective-permute-start | bytes 344072 | tf_op jit(solution)/shard_map/ppermute | solution.py:269
  10.8 2.9 %collective-permute-start.4 = (bf16[64,896]{1,0:T(8,128)(2,1)S(1)}, bf16[64,896]{1,0:T(8,128)(2,1)S(1)}, u32[]{:S(2)}, u32[]{:S(2)}) collective-permute-start(bf16[64,896]{1,0:T(8,128)(2,1)S(1)} %collective-permute-done.1.refs_3_), channel_id=1, source_target_pairs={{0,4},{2,6},{4,12},{6,14},{12,8},{14,10},{8,0},{10,2},{1,5},{3,7},... | collective-permute-start | bytes 344072 | tf_op jit(solution)/shard_map/ppermute | solution.py:269
  13.8 1.6 %collective-permute-start.5 = (bf16[64,1792]{1,0:T(8,128)(2,1)S(1)}, bf16[64,1792]{1,0:T(8,128)(2,1)S(1)}, u32[]{:S(2)}, u32[]{:S(2)}) collective-permute-start(bf16[64,1792]{1,0:T(8,128)(2,1)S(1)} %pad_maximum_fusion), channel_id=1, source_target_pairs={{0,2},{2,0},{4,6},{6,4},{8,10},{10,8},{12,14},{14,12},{1,3},{3,1},... | collective-permute-start | bytes 688136 | tf_op jit(solution)/shard_map/ppermute | solution.py:269
  15.3 0.8 %collective-permute-done.3.refs_5_ = bf16[64,896]{1,0:T(8,128)(2,1)S(1)} collective-permute-done((bf16[64,896]{1,0:T(8,128)(2,1)S(1)}, bf16[64,896]{1,0:T(8,128)(2,1)S(1)}, u32[]{:S(2)}, u32[]{:S(2)}) %collective-permute-start.3) | collective-permute-done | bytes 114720 | tf_op jit(solution)/shard_map/ppermute | solution.py:269
  16.1 0.8 %collective-permute-start.6 = (bf16[64,896]{1,0:T(8,128)(2,1)S(1)}, bf16[64,896]{1,0:T(8,128)(2,1)S(1)}, u32[]{:S(2)}, u32[]{:S(2)}) collective-permute-start(bf16[64,896]{1,0:T(8,128)(2,1)S(1)} %collective-permute-done.3.refs_5_), channel_id=1, source_target_pairs={{0,4},{2,6},{4,12},{6,14},{12,8},{14,10},{8,0},{10,2},{1,5},{3,7},... | collective-permute-start | bytes 344072 | tf_op jit(solution)/shard_map/ppermute | solution.py:269
  16.9 1.6 %collective-permute-done.4.refs_6_ = bf16[64,896]{1,0:T(8,128)(2,1)S(1)} collective-permute-done((bf16[64,896]{1,0:T(8,128)(2,1)S(1)}, bf16[64,896]{1,0:T(8,128)(2,1)S(1)}, u32[]{:S(2)}, u32[]{:S(2)}) %collective-permute-start.4) | collective-permute-done | bytes 114720 | tf_op jit(solution)/shard_map/ppermute | solution.py:269
  18.5 1.8 %collective-permute-start.7 = (bf16[64,896]{1,0:T(8,128)(2,1)S(1)}, bf16[64,896]{1,0:T(8,128)(2,1)S(1)}, u32[]{:S(2)}, u32[]{:S(2)}) collective-permute-start(bf16[64,896]{1,0:T(8,128)(2,1)S(1)} %collective-permute-done.4.refs_6_), channel_id=1, source_target_pairs={{0,4},{2,6},{4,12},{6,14},{12,8},{14,10},{8,0},{10,2},{1,5},{3,7},... | collective-permute-start | bytes 344072 | tf_op jit(solution)/shard_map/ppermute | solution.py:269
  20.3 1.5 %collective-permute-start.8 = (bf16[64,896]{1,0:T(8,128)(2,1)S(1)}, bf16[64,896]{1,0:T(8,128)(2,1)S(1)}, u32[]{:S(2)}, u32[]{:S(2)}) collective-permute-start(bf16[64,896]{1,0:T(8,128)(2,1)S(1)} %collective-permute-done.3.refs_5_), channel_id=1, source_target_pairs={{0,2},{2,0},{4,6},{6,4},{8,10},{10,8},{12,14},{14,12},{1,3},{3,1},... | collective-permute-start | bytes 344072 | tf_op jit(solution)/shard_map/ppermute | solution.py:269
  21.8 0.5 %collective-permute-start.9 = (bf16[64,896]{1,0:T(8,128)(2,1)S(1)}, bf16[64,896]{1,0:T(8,128)(2,1)S(1)}, u32[]{:S(2)}, u32[]{:S(2)}) collective-permute-start(bf16[64,896]{1,0:T(8,128)(2,1)S(1)} %collective-permute-done.4.refs_6_), channel_id=1, source_target_pairs={{0,2},{2,0},{4,6},{6,4},{8,10},{10,8},{12,14},{14,12},{1,3},{3,1},... | collective-permute-start | bytes 344072 | tf_op jit(solution)/shard_map/ppermute | solution.py:269
  22.3 1.5 %collective-permute-start.12 = (bf16[64,896]{1,0:T(8,128)(2,1)S(1)}, bf16[64,896]{1,0:T(8,128)(2,1)S(1)}, u32[]{:S(2)}, u32[]{:S(2)}) collective-permute-start(bf16[64,896]{1,0:T(8,128)(2,1)S(1)} %collective-permute-done.6.refs_8_), channel_id=1, source_target_pairs={{0,2},{2,0},{4,6},{6,4},{8,10},{10,8},{12,14},{14,12},{1,3},{3,1},... | collective-permute-start | bytes 344072 | tf_op jit(solution)/shard_map/ppermute | solution.py:269
  24.2 1.2 %collective-permute-start.10 = (bf16[64,896]{1,0:T(8,128)(2,1)S(1)}, bf16[64,896]{1,0:T(8,128)(2,1)S(1)}, u32[]{:S(2)}, u32[]{:S(2)}) collective-permute-start(bf16[64,896]{1,0:T(8,128)(2,1)S(1)} %collective-permute-done.7.refs_9_), channel_id=1, source_target_pairs={{0,2},{2,0},{4,6},{6,4},{8,10},{10,8},{12,14},{14,12},{1,3},{3,1},... | collective-permute-start | bytes 344072 | tf_op jit(solution)/shard_map/ppermute | solution.py:269
  25.4 0.7 %copy-done.4 = s32[2,64,1]{1,2,0:T(1,128)S(1)} copy-done((s32[2,64,1]{1,2,0:T(1,128)S(1)}, s32[2,64,1]{1,2,0:T(1,128)}, u32[]{:S(2)}) %copy-start.4) | copy-done | bytes 536
  26.1 0.7 %copy-done.5 = s32[2,64]{1,0:T(2,128)S(1)} copy-done((s32[2,64]{1,0:T(2,128)S(1)}, s32[2,64]{1,0:T(2,128)}, u32[]{:S(2)}) %copy-start.5) | copy-done | bytes 536
  26.9 0.6 %collective-permute-done.9.refs_11_ = bf16[64,896]{1,0:T(8,128)(2,1)S(1)} collective-permute-done((bf16[64,896]{1,0:T(8,128)(2,1)S(1)}, bf16[64,896]{1,0:T(8,128)(2,1)S(1)}, u32[]{:S(2)}, u32[]{:S(2)}) %collective-permute-start.9) | collective-permute-done | bytes 114720 | tf_op jit(solution)/shard_map/ppermute | solution.py:269
  28.0 0.7 %collective-permute-done.12.last_ref = bf16[64,896]{1,0:T(8,128)(2,1)S(1)} collective-permute-done((bf16[64,896]{1,0:T(8,128)(2,1)S(1)}, bf16[64,896]{1,0:T(8,128)(2,1)S(1)}, u32[]{:S(2)}, u32[]{:S(2)}) %collective-permute-start.12) | collective-permute-done | bytes 114720 | tf_op jit(solution)/shard_map/ppermute | solution.py:269
  29.1 0.9 %collective-permute-done.10.last_ref = bf16[64,896]{1,0:T(8,128)(2,1)S(1)} collective-permute-done((bf16[64,896]{1,0:T(8,128)(2,1)S(1)}, bf16[64,896]{1,0:T(8,128)(2,1)S(1)}, u32[]{:S(2)}, u32[]{:S(2)}) %collective-permute-start.10) | collective-permute-done | bytes 114720 | tf_op jit(solution)/shard_map/ppermute | solution.py:269
  30.3 0.7 %shard_map.70.refs_6_ = bf16[256,1024]{1,0:T(8,128)(2,1)S(1)} custom-call(bf16[128,896]{1,0:T(8,128)(2,1)S(1)} %shard_map.67.refs_0_, bf16[128,896]{1,0:T(8,128)(2,1)S(1)} %shard_map.68.refs_1_, bf16[896,1024]{1,0:T(8,128)(2,1)S(1)} %copy-done.1), custom_call_target="tpu_custom_call" | custom-call | tf_op jit(solution)/shard_map/pallas_call | solution.py:212
  31.0 0.9 %shard_map.69.refs_5_ = f32[8,128,128]{2,1,0:T(8,128)S(1)} custom-call(bf16[128,896]{1,0:T(8,128)(2,1)S(1)} %shard_map.67.refs_0_, bf16[128,896]{1,0:T(8,128)(2,1)S(1)} %shard_map.68.refs_1_, bf16[896,1024]{1,0:T(8,128)(2,1)S(1)} %copy-done, bf16[128,1024]{1,0:T(8,128)(2,1)S(1)} %copy-done.2), custom_call_target="tpu_custom_call" | custom-call | tf_op jit(solution)/shard_map/pallas_call | solution.py:196
  31.9 2.5 %shard_map.71 = bf16[128,1024]{1,0:T(8,128)(2,1)} custom-call(bf16[128,896]{1,0:T(8,128)(2,1)S(1)} %collective-permute-done.11.refs_0_, bf16[128,896]{1,0:T(8,128)(2,1)S(1)} %collective-permute-done.13.refs_1_, bf16[896,1024]{1,0:T(8,128)(2,1)S(1)} %copy-done, bf16[896,1024]{1,0:T(8,128)(2,1)S(1)} %copy-done.1, bf16[128,1024]{1,0:T(8,128)(2,1)S(1)} %copy-done.2, ...), custom_call_target="tpu_custom_call" | custom-call | tf_op jit(solution)/shard_map/pallas_call | solution.py:253
  (25 shorter events, 2.3 us)
Async XLA Ops:
  0.0 1.0 %copy-start.3 = (bf16[64,3584]{1,0:T(8,128)(2,1)S(1)}, bf16[64,3584]{1,0:T(8,128)(2,1)}, u32[]{:S(2)}) copy-start(bf16[64,3584]{1,0:T(8,128)(2,1)} %enc_ref.1) | copy-start | bytes 1376260
  1.1 29.2 %copy-start.1 = (bf16[896,1024]{1,0:T(8,128)(2,1)S(1)}, bf16[896,1024]{1,0:T(8,128)(2,1)}, u32[]{:S(2)}) copy-start(bf16[896,1024]{1,0:T(8,128)(2,1)} %refs_3_.3) | copy-start | bytes 5505028
  1.1 8.1 %collective-permute-start = (bf16[64,896]{1,0:T(8,128)(2,1)S(1)}, bf16[64,896]{1,0:T(8,128)(2,1)S(1)}, u32[]{:S(2)}, u32[]{:S(2)}) collective-permute-start(bf16[64,896]{1,0:T(8,128)(2,1)S(1)} %get-tuple-element.10.refs_0_), channel_id=1, source_target_pairs={{0,4},{2,6},{4,12},{6,14},{12,8},{14,10},{8,0},{10,2},{1,5},{3,7},... | collective-permute-start | bytes 344072 | tf_op jit(solution)/shard_map/ppermute | solution.py:269
  4.2 6.6 %collective-permute-start.1 = (bf16[64,896]{1,0:T(8,128)(2,1)S(1)}, bf16[64,896]{1,0:T(8,128)(2,1)S(1)}, u32[]{:S(2)}, u32[]{:S(2)}) collective-permute-start(bf16[64,896]{1,0:T(8,128)(2,1)S(1)} %get-tuple-element.11.refs_1_), channel_id=1, source_target_pairs={{0,4},{2,6},{4,12},{6,14},{12,8},{14,10},{8,0},{10,2},{1,5},{3,7},... | collective-permute-start | bytes 344072 | tf_op jit(solution)/shard_map/ppermute | solution.py:269
  6.8 15.0 %collective-permute-start.2 = (bf16[64,1792]{1,0:T(8,128)(2,1)S(1)}, bf16[64,1792]{1,0:T(8,128)(2,1)S(1)}, u32[]{:S(2)}, u32[]{:S(2)}) collective-permute-start(bf16[64,1792]{1,0:T(8,128)(2,1)S(1)} %get-tuple-element.12), channel_id=1, source_target_pairs={{0,2},{2,0},{4,6},{6,4},{8,10},{10,8},{12,14},{14,12},{1,3},{3,1},... | collective-permute-start | bytes 688136 | tf_op jit(solution)/shard_map/ppermute | solution.py:269
  9.2 6.9 %collective-permute-start.3 = (bf16[64,896]{1,0:T(8,128)(2,1)S(1)}, bf16[64,896]{1,0:T(8,128)(2,1)S(1)}, u32[]{:S(2)}, u32[]{:S(2)}) collective-permute-start(bf16[64,896]{1,0:T(8,128)(2,1)S(1)} %collective-permute-done.refs_2_), channel_id=1, source_target_pairs={{0,4},{2,6},{4,12},{6,14},{12,8},{14,10},{8,0},{10,2},{1,5},{3,7},... | collective-permute-start | bytes 344072 | tf_op jit(solution)/shard_map/ppermute | solution.py:269
  10.8 7.7 %collective-permute-start.4 = (bf16[64,896]{1,0:T(8,128)(2,1)S(1)}, bf16[64,896]{1,0:T(8,128)(2,1)S(1)}, u32[]{:S(2)}, u32[]{:S(2)}) collective-permute-start(bf16[64,896]{1,0:T(8,128)(2,1)S(1)} %collective-permute-done.1.refs_3_), channel_id=1, source_target_pairs={{0,4},{2,6},{4,12},{6,14},{12,8},{14,10},{8,0},{10,2},{1,5},{3,7},... | collective-permute-start | bytes 344072 | tf_op jit(solution)/shard_map/ppermute | solution.py:269
  13.8 13.2 %collective-permute-start.5 = (bf16[64,1792]{1,0:T(8,128)(2,1)S(1)}, bf16[64,1792]{1,0:T(8,128)(2,1)S(1)}, u32[]{:S(2)}, u32[]{:S(2)}) collective-permute-start(bf16[64,1792]{1,0:T(8,128)(2,1)S(1)} %pad_maximum_fusion), channel_id=1, source_target_pairs={{0,2},{2,0},{4,6},{6,4},{8,10},{10,8},{12,14},{14,12},{1,3},{3,1},... | collective-permute-start | bytes 688136 | tf_op jit(solution)/shard_map/ppermute | solution.py:269
  16.1 6.2 %collective-permute-start.6 = (bf16[64,896]{1,0:T(8,128)(2,1)S(1)}, bf16[64,896]{1,0:T(8,128)(2,1)S(1)}, u32[]{:S(2)}, u32[]{:S(2)}) collective-permute-start(bf16[64,896]{1,0:T(8,128)(2,1)S(1)} %collective-permute-done.3.refs_5_), channel_id=1, source_target_pairs={{0,4},{2,6},{4,12},{6,14},{12,8},{14,10},{8,0},{10,2},{1,5},{3,7},... | collective-permute-start | bytes 344072 | tf_op jit(solution)/shard_map/ppermute | solution.py:269
  18.5 5.7 %collective-permute-start.7 = (bf16[64,896]{1,0:T(8,128)(2,1)S(1)}, bf16[64,896]{1,0:T(8,128)(2,1)S(1)}, u32[]{:S(2)}, u32[]{:S(2)}) collective-permute-start(bf16[64,896]{1,0:T(8,128)(2,1)S(1)} %collective-permute-done.4.refs_6_), channel_id=1, source_target_pairs={{0,4},{2,6},{4,12},{6,14},{12,8},{14,10},{8,0},{10,2},{1,5},{3,7},... | collective-permute-start | bytes 344072 | tf_op jit(solution)/shard_map/ppermute | solution.py:269
  20.3 6.7 %collective-permute-start.8 = (bf16[64,896]{1,0:T(8,128)(2,1)S(1)}, bf16[64,896]{1,0:T(8,128)(2,1)S(1)}, u32[]{:S(2)}, u32[]{:S(2)}) collective-permute-start(bf16[64,896]{1,0:T(8,128)(2,1)S(1)} %collective-permute-done.3.refs_5_), channel_id=1, source_target_pairs={{0,2},{2,0},{4,6},{6,4},{8,10},{10,8},{12,14},{14,12},{1,3},{3,1},... | collective-permute-start | bytes 344072 | tf_op jit(solution)/shard_map/ppermute | solution.py:269
  21.8 5.7 %collective-permute-start.9 = (bf16[64,896]{1,0:T(8,128)(2,1)S(1)}, bf16[64,896]{1,0:T(8,128)(2,1)S(1)}, u32[]{:S(2)}, u32[]{:S(2)}) collective-permute-start(bf16[64,896]{1,0:T(8,128)(2,1)S(1)} %collective-permute-done.4.refs_6_), channel_id=1, source_target_pairs={{0,2},{2,0},{4,6},{6,4},{8,10},{10,8},{12,14},{14,12},{1,3},{3,1},... | collective-permute-start | bytes 344072 | tf_op jit(solution)/shard_map/ppermute | solution.py:269
  22.3 6.4 %collective-permute-start.12 = (bf16[64,896]{1,0:T(8,128)(2,1)S(1)}, bf16[64,896]{1,0:T(8,128)(2,1)S(1)}, u32[]{:S(2)}, u32[]{:S(2)}) collective-permute-start(bf16[64,896]{1,0:T(8,128)(2,1)S(1)} %collective-permute-done.6.refs_8_), channel_id=1, source_target_pairs={{0,2},{2,0},{4,6},{6,4},{8,10},{10,8},{12,14},{14,12},{1,3},{3,1},... | collective-permute-start | bytes 344072 | tf_op jit(solution)/shard_map/ppermute | solution.py:269
  24.2 5.7 %collective-permute-start.10 = (bf16[64,896]{1,0:T(8,128)(2,1)S(1)}, bf16[64,896]{1,0:T(8,128)(2,1)S(1)}, u32[]{:S(2)}, u32[]{:S(2)}) collective-permute-start(bf16[64,896]{1,0:T(8,128)(2,1)S(1)} %collective-permute-done.7.refs_9_), channel_id=1, source_target_pairs={{0,2},{2,0},{4,6},{6,4},{8,10},{10,8},{12,14},{14,12},{1,3},{3,1},... | collective-permute-start | bytes 344072 | tf_op jit(solution)/shard_map/ppermute | solution.py:269
  25.4 0.7 %copy-start.4 = (s32[2,64,1]{1,2,0:T(1,128)S(1)}, s32[2,64,1]{1,2,0:T(1,128)}, u32[]{:S(2)}) copy-start(s32[2,64,1]{1,2,0:T(1,128)} %param.10) | copy-start | bytes 1540
  26.1 0.7 %copy-start.5 = (s32[2,64]{1,0:T(2,128)S(1)}, s32[2,64]{1,0:T(2,128)}, u32[]{:S(2)}) copy-start(s32[2,64]{1,0:T(2,128)} %stored_ref.1) | copy-start | bytes 1540
  29.0 2.0 %copy-start = (bf16[896,1024]{1,0:T(8,128)(2,1)S(1)}, bf16[896,1024]{1,0:T(8,128)(2,1)}, u32[]{:S(2)}) copy-start(bf16[896,1024]{1,0:T(8,128)(2,1)} %refs_2_.5) | copy-start | bytes 5505028
  29.0 2.0 %copy-start.2 = (bf16[128,1024]{1,0:T(8,128)(2,1)S(1)}, bf16[128,1024]{1,0:T(8,128)(2,1)}, u32[]{:S(2)}) copy-start(bf16[128,1024]{1,0:T(8,128)(2,1)} %refs_4_.1) | copy-start | bytes 786436
  29.0 2.9 %collective-permute-start.13 = (bf16[128,896]{1,0:T(8,128)(2,1)S(1)}, bf16[128,896]{1,0:T(8,128)(2,1)S(1)}, u32[]{:S(2)}, u32[]{:S(2)}) collective-permute-start(bf16[128,896]{1,0:T(8,128)(2,1)S(1)} %shard_map.68.refs_1_), channel_id=1, source_target_pairs={{0,1},{1,0},{2,3},{3,2},{4,5},{5,4},{6,7},{7,6},{8,9},{9,8},{10,11... | collective-permute-start | bytes 688136 | tf_op jit(solution)/shard_map/ppermute | solution.py:301
  30.2 1.7 %collective-permute-start.11 = (bf16[128,896]{1,0:T(8,128)(2,1)S(1)}, bf16[128,896]{1,0:T(8,128)(2,1)S(1)}, u32[]{:S(2)}, u32[]{:S(2)}) collective-permute-start(bf16[128,896]{1,0:T(8,128)(2,1)S(1)} %shard_map.67.refs_0_), channel_id=1, source_target_pairs={{0,1},{1,0},{2,3},{3,2},{4,5},{5,4},{6,7},{7,6},{8,9},{9,8},{10,11... | collective-permute-start | bytes 688136 | tf_op jit(solution)/shard_map/ppermute | solution.py:301

commit v12 on v11

--- a/solution.py
+++ b/solution.py
@@ -294,6 +294,8 @@
         else:
             held[k - 1, 1] = [send(piece, across) for piece in behind]
         held[k, 0] = steps
+    straight, crossed = held[turns - 1, 0], held[turns - 2, 1]
+    straight[0], crossed[0] = lax.optimization_barrier((straight[0], crossed[0]))
     held[turns - 1, 1] = [send(piece, across) for piece in held[turns - 1, 0]]
     sources = [held[chunk] for chunk in order]
     begun = early(index, sources[:-1], whole.shape[1])

time: 34.6 us -> 34.5 us (level)
  waiting for transfers between devices: 6.38 us -> 4.46 us
  starting transfers between devices: 20.2 us -> 21.8 us
    ppermute x12, waiting for transfers between devices: 6.37 us -> 4.45 us  [send(): return lax.ppermute(chunk, 'wide', pairs)]
    ppermute x12, starting transfers between devices: 20 us -> 21.6 us  [send(): return lax.ppermute(chunk, 'wide', pairs)]
where the time goes in v12:
time: 34.5 us; the launch traced here: 34.1 us
  starting transfers between devices  21.8 us (63%)
  Pallas kernels  5.27 us (15%)
  waiting for transfers between devices  4.46 us (13%)
  local copies, waits for them, and re-layouts  2.39 us (7%)
    ppermute x12, starting transfers between devices, send(): return lax.ppermute(chunk, 'wide', pairs)  21.6 us
    ppermute x12, waiting for transfers between devices, send(): return lax.ppermute(chunk, 'wide', pairs)  4.45 us
    pallas_call x1, Pallas kernels, attend(): pl.pallas_call(functools.partial(attend_kernel, spans), out_shape=jax.Sha...  2.48 us
    unnamed x12, local copies, waits for them, and re-layouts  2.39 us
    pallas_call x1, Pallas kernels, own_scores(): pl.pallas_call(functools.partial(score_kernel, spans), out_shape=jax.Shap...  0.87 us
    pallas_call x1, Pallas kernels, own_values(): pl.pallas_call(functools.partial(values_kernel, spans), out_shape=jax.Sha...  0.71 us
  transfers between devices with their start and end apart: 14, of which 8 were waited for; matrix products, arithmetic and copies ran while one was open for 0% of the time, Pallas kernels for 8%

profile of v12, /device:TPU:0, one launch (start us, length us, event | category | flops | bytes accessed | tf_op | source)
XLA Modules:
  0.0 34.1 jit_solution(2567129992073110251)
XLA Ops:
  0.0 1.0 %copy-done.3 = bf16[64,3584]{1,0:T(8,128)(2,1)S(1)} copy-done((bf16[64,3584]{1,0:T(8,128)(2,1)S(1)}, bf16[64,3584]{1,0:T(8,128)(2,1)}, u32[]{:S(2)}) %copy-start.3) | copy-done | bytes 458776
  1.1 3.1 %collective-permute-start = (bf16[64,896]{1,0:T(8,128)(2,1)S(1)}, bf16[64,896]{1,0:T(8,128)(2,1)S(1)}, u32[]{:S(2)}, u32[]{:S(2)}) collective-permute-start(bf16[64,896]{1,0:T(8,128)(2,1)S(1)} %get-tuple-element.12.refs_0_), channel_id=1, source_target_pairs={{0,4},{2,6},{4,12},{6,14},{12,8},{14,10},{8,0},{10,2},{1,5},{3,7},... | collective-permute-start | bytes 344072 | tf_op jit(solution)/shard_map/ppermute | solution.py:269
  4.2 2.6 %collective-permute-start.1 = (bf16[64,896]{1,0:T(8,128)(2,1)S(1)}, bf16[64,896]{1,0:T(8,128)(2,1)S(1)}, u32[]{:S(2)}, u32[]{:S(2)}) collective-permute-start(bf16[64,896]{1,0:T(8,128)(2,1)S(1)} %get-tuple-element.13.refs_1_), channel_id=1, source_target_pairs={{0,4},{2,6},{4,12},{6,14},{12,8},{14,10},{8,0},{10,2},{1,5},{3,7},... | collective-permute-start | bytes 344072 | tf_op jit(solution)/shard_map/ppermute | solution.py:269
  6.8 1.5 %collective-permute-start.2 = (bf16[64,1792]{1,0:T(8,128)(2,1)S(1)}, bf16[64,1792]{1,0:T(8,128)(2,1)S(1)}, u32[]{:S(2)}, u32[]{:S(2)}) collective-permute-start(bf16[64,1792]{1,0:T(8,128)(2,1)S(1)} %get-tuple-element.14), channel_id=1, source_target_pairs={{0,2},{2,0},{4,6},{6,4},{8,10},{10,8},{12,14},{14,12},{1,3},{3,1},... | collective-permute-start | bytes 688136 | tf_op jit(solution)/shard_map/ppermute | solution.py:269
  8.3 0.9 %collective-permute-done.refs_2_ = bf16[64,896]{1,0:T(8,128)(2,1)S(1)} collective-permute-done((bf16[64,896]{1,0:T(8,128)(2,1)S(1)}, bf16[64,896]{1,0:T(8,128)(2,1)S(1)}, u32[]{:S(2)}, u32[]{:S(2)}) %collective-permute-start) | collective-permute-done | bytes 114720 | tf_op jit(solution)/shard_map/ppermute | solution.py:269
  9.2 1.2 %collective-permute-start.3 = (bf16[64,896]{1,0:T(8,128)(2,1)S(1)}, bf16[64,896]{1,0:T(8,128)(2,1)S(1)}, u32[]{:S(2)}, u32[]{:S(2)}) collective-permute-start(bf16[64,896]{1,0:T(8,128)(2,1)S(1)} %collective-permute-done.refs_2_), channel_id=1, source_target_pairs={{0,4},{2,6},{4,12},{6,14},{12,8},{14,10},{8,0},{10,2},{1,5},{3,7},... | collective-permute-start | bytes 344072 | tf_op jit(solution)/shard_map/ppermute | solution.py:269
  10.4 0.5 %collective-permute-done.1.refs_3_ = bf16[64,896]{1,0:T(8,128)(2,1)S(1)} collective-permute-done((bf16[64,896]{1,0:T(8,128)(2,1)S(1)}, bf16[64,896]{1,0:T(8,128)(2,1)S(1)}, u32[]{:S(2)}, u32[]{:S(2)}) %collective-permute-start.1) | collective-permute-done | bytes 114720 | tf_op jit(solution)/shard_map/ppermute | solution.py:269
  10.8 2.9 %collective-permute-start.4 = (bf16[64,896]{1,0:T(8,128)(2,1)S(1)}, bf16[64,896]{1,0:T(8,128)(2,1)S(1)}, u32[]{:S(2)}, u32[]{:S(2)}) collective-permute-start(bf16[64,896]{1,0:T(8,128)(2,1)S(1)} %collective-permute-done.1.refs_3_), channel_id=1, source_target_pairs={{0,4},{2,6},{4,12},{6,14},{12,8},{14,10},{8,0},{10,2},{1,5},{3,7},... | collective-permute-start | bytes 344072 | tf_op jit(solution)/shard_map/ppermute | solution.py:269
  13.8 1.6 %collective-permute-start.5 = (bf16[64,1792]{1,0:T(8,128)(2,1)S(1)}, bf16[64,1792]{1,0:T(8,128)(2,1)S(1)}, u32[]{:S(2)}, u32[]{:S(2)}) collective-permute-start(bf16[64,1792]{1,0:T(8,128)(2,1)S(1)} %pad_maximum_fusion), channel_id=1, source_target_pairs={{0,2},{2,0},{4,6},{6,4},{8,10},{10,8},{12,14},{14,12},{1,3},{3,1},... | collective-permute-start | bytes 688136 | tf_op jit(solution)/shard_map/ppermute | solution.py:269
  15.3 0.8 %collective-permute-done.3.refs_5_ = bf16[64,896]{1,0:T(8,128)(2,1)S(1)} collective-permute-done((bf16[64,896]{1,0:T(8,128)(2,1)S(1)}, bf16[64,896]{1,0:T(8,128)(2,1)S(1)}, u32[]{:S(2)}, u32[]{:S(2)}) %collective-permute-start.3) | collective-permute-done | bytes 114720 | tf_op jit(solution)/shard_map/ppermute | solution.py:269
  16.1 0.8 %collective-permute-start.6 = (bf16[64,896]{1,0:T(8,128)(2,1)S(1)}, bf16[64,896]{1,0:T(8,128)(2,1)S(1)}, u32[]{:S(2)}, u32[]{:S(2)}) collective-permute-start(bf16[64,896]{1,0:T(8,128)(2,1)S(1)} %collective-permute-done.3.refs_5_), channel_id=1, source_target_pairs={{0,4},{2,6},{4,12},{6,14},{12,8},{14,10},{8,0},{10,2},{1,5},{3,7},... | collective-permute-start | bytes 344072 | tf_op jit(solution)/shard_map/ppermute | solution.py:269
  16.9 1.5 %collective-permute-start.7 = (bf16[64,896]{1,0:T(8,128)(2,1)S(1)}, bf16[64,896]{1,0:T(8,128)(2,1)S(1)}, u32[]{:S(2)}, u32[]{:S(2)}) collective-permute-start(bf16[64,896]{1,0:T(8,128)(2,1)S(1)} %collective-permute-done.3.refs_5_), channel_id=1, source_target_pairs={{0,2},{2,0},{4,6},{6,4},{8,10},{10,8},{12,14},{14,12},{1,3},{3,1},... | collective-permute-start | bytes 344072 | tf_op jit(solution)/shard_map/ppermute | solution.py:269
  18.5 3.2 %collective-permute-start.8 = (bf16[64,896]{1,0:T(8,128)(2,1)S(1)}, bf16[64,896]{1,0:T(8,128)(2,1)S(1)}, u32[]{:S(2)}, u32[]{:S(2)}) collective-permute-start(bf16[64,896]{1,0:T(8,128)(2,1)S(1)} %collective-permute-done.4.refs_6_), channel_id=1, source_target_pairs={{0,4},{2,6},{4,12},{6,14},{12,8},{14,10},{8,0},{10,2},{1,5},{3,7},... | collective-permute-start | bytes 344072 | tf_op jit(solution)/shard_map/ppermute | solution.py:269
  22.1 1.2 %collective-permute-start.9 = (bf16[64,896]{1,0:T(8,128)(2,1)S(1)}, bf16[64,896]{1,0:T(8,128)(2,1)S(1)}, u32[]{:S(2)}, u32[]{:S(2)}) collective-permute-start(bf16[64,896]{1,0:T(8,128)(2,1)S(1)} %collective-permute-done.4.refs_6_), channel_id=1, source_target_pairs={{0,2},{2,0},{4,6},{6,4},{8,10},{10,8},{12,14},{14,12},{1,3},{3,1},... | collective-permute-start | bytes 344072 | tf_op jit(solution)/shard_map/ppermute | solution.py:269
  23.3 0.9 %collective-permute-start.12 = (bf16[64,896]{1,0:T(8,128)(2,1)S(1)}, bf16[64,896]{1,0:T(8,128)(2,1)S(1)}, u32[]{:S(2)}, u32[]{:S(2)}) collective-permute-start(bf16[64,896]{1,0:T(8,128)(2,1)S(1)} %collective-permute-done.6.refs_8_), channel_id=1, source_target_pairs={{0,2},{2,0},{4,6},{6,4},{8,10},{10,8},{12,14},{14,12},{1,3},{3,1},... | collective-permute-start | bytes 344072 | tf_op jit(solution)/shard_map/ppermute | solution.py:269
  24.2 1.2 %collective-permute-start.10 = (bf16[64,896]{1,0:T(8,128)(2,1)S(1)}, bf16[64,896]{1,0:T(8,128)(2,1)S(1)}, u32[]{:S(2)}, u32[]{:S(2)}) collective-permute-start(bf16[64,896]{1,0:T(8,128)(2,1)S(1)} %collective-permute-done.8.refs_9_), channel_id=1, source_target_pairs={{0,2},{2,0},{4,6},{6,4},{8,10},{10,8},{12,14},{14,12},{1,3},{3,1},... | collective-permute-start | bytes 344072 | tf_op jit(solution)/shard_map/ppermute | solution.py:269
  25.4 0.7 %copy-done.4 = s32[2,64,1]{1,2,0:T(1,128)S(1)} copy-done((s32[2,64,1]{1,2,0:T(1,128)S(1)}, s32[2,64,1]{1,2,0:T(1,128)}, u32[]{:S(2)}) %copy-start.4) | copy-done | bytes 536
  26.1 0.7 %copy-done.5 = s32[2,64]{1,0:T(2,128)S(1)} copy-done((s32[2,64]{1,0:T(2,128)S(1)}, s32[2,64]{1,0:T(2,128)}, u32[]{:S(2)}) %copy-start.5) | copy-done | bytes 536
  27.2 0.5 %shard_map.66 = (bf16[128,896]{1,0:T(8,128)(2,1)S(1)}, bf16[128,896]{1,0:T(8,128)(2,1)S(1)}) custom-call(s32[128,1]{1,0:T(8,128)S(1)} %shard_map.64.index_ref, bf16[64,896]{1,0:T(8,128)(2,1)S(1)} %get-tuple-element.12.refs_0_, bf16[64,896]{1,0:T(8,128)(2,1)S(1)} %get-tuple-element.13.refs_1_, bf16[64,896]{1,0:T(8,128)(2,1)S(1)} %collective-permute-done.refs_2_, ...), custom_call_target="tpu_custom_call" | custom-call | flops 205520896 | bytes 458752 | tf_op jit(solution)/shard_map/pallas_call | solution.py:114
  27.7 0.7 %collective-permute-done.12.last_ref = bf16[64,896]{1,0:T(8,128)(2,1)S(1)} collective-permute-done((bf16[64,896]{1,0:T(8,128)(2,1)S(1)}, bf16[64,896]{1,0:T(8,128)(2,1)S(1)}, u32[]{:S(2)}, u32[]{:S(2)}) %collective-permute-start.12) | collective-permute-done | bytes 114720 | tf_op jit(solution)/shard_map/ppermute | solution.py:269
  28.8 0.9 %collective-permute-done.10.last_ref = bf16[64,896]{1,0:T(8,128)(2,1)S(1)} collective-permute-done((bf16[64,896]{1,0:T(8,128)(2,1)S(1)}, bf16[64,896]{1,0:T(8,128)(2,1)S(1)}, u32[]{:S(2)}, u32[]{:S(2)}) %collective-permute-start.10) | collective-permute-done | bytes 114720 | tf_op jit(solution)/shard_map/ppermute | solution.py:269
  30.0 0.7 %shard_map.70.refs_6_ = bf16[256,1024]{1,0:T(8,128)(2,1)S(1)} custom-call(bf16[128,896]{1,0:T(8,128)(2,1)S(1)} %shard_map.67.refs_0_, bf16[128,896]{1,0:T(8,128)(2,1)S(1)} %shard_map.68.refs_1_, bf16[896,1024]{1,0:T(8,128)(2,1)S(1)} %copy-done.1), custom_call_target="tpu_custom_call" | custom-call | tf_op jit(solution)/shard_map/pallas_call | solution.py:212
  30.7 0.9 %shard_map.69.refs_5_ = f32[8,128,128]{2,1,0:T(8,128)S(1)} custom-call(bf16[128,896]{1,0:T(8,128)(2,1)S(1)} %shard_map.67.refs_0_, bf16[128,896]{1,0:T(8,128)(2,1)S(1)} %shard_map.68.refs_1_, bf16[896,1024]{1,0:T(8,128)(2,1)S(1)} %copy-done, bf16[128,1024]{1,0:T(8,128)(2,1)S(1)} %copy-done.2), custom_call_target="tpu_custom_call" | custom-call | tf_op jit(solution)/shard_map/pallas_call | solution.py:196
  31.6 2.5 %shard_map.71 = bf16[128,1024]{1,0:T(8,128)(2,1)} custom-call(bf16[128,896]{1,0:T(8,128)(2,1)S(1)} %collective-permute-done.11.refs_0_, bf16[128,896]{1,0:T(8,128)(2,1)S(1)} %collective-permute-done.13.refs_1_, bf16[896,1024]{1,0:T(8,128)(2,1)S(1)} %copy-done, bf16[896,1024]{1,0:T(8,128)(2,1)S(1)} %copy-done.1, bf16[128,1024]{1,0:T(8,128)(2,1)S(1)} %copy-done.2, ...), custom_call_target="tpu_custom_call" | custom-call | tf_op jit(solution)/shard_map/pallas_call | solution.py:253
  (25 shorter events, 1.6 us)
Async XLA Ops:
  0.0 1.0 %copy-start.3 = (bf16[64,3584]{1,0:T(8,128)(2,1)S(1)}, bf16[64,3584]{1,0:T(8,128)(2,1)}, u32[]{:S(2)}) copy-start(bf16[64,3584]{1,0:T(8,128)(2,1)} %enc_ref.1) | copy-start | bytes 1376260
  1.1 28.9 %copy-start.1 = (bf16[896,1024]{1,0:T(8,128)(2,1)S(1)}, bf16[896,1024]{1,0:T(8,128)(2,1)}, u32[]{:S(2)}) copy-start(bf16[896,1024]{1,0:T(8,128)(2,1)} %refs_3_.3) | copy-start | bytes 5505028
  1.1 8.1 %collective-permute-start = (bf16[64,896]{1,0:T(8,128)(2,1)S(1)}, bf16[64,896]{1,0:T(8,128)(2,1)S(1)}, u32[]{:S(2)}, u32[]{:S(2)}) collective-permute-start(bf16[64,896]{1,0:T(8,128)(2,1)S(1)} %get-tuple-element.12.refs_0_), channel_id=1, source_target_pairs={{0,4},{2,6},{4,12},{6,14},{12,8},{14,10},{8,0},{10,2},{1,5},{3,7},... | collective-permute-start | bytes 344072 | tf_op jit(solution)/shard_map/ppermute | solution.py:269
  4.2 6.6 %collective-permute-start.1 = (bf16[64,896]{1,0:T(8,128)(2,1)S(1)}, bf16[64,896]{1,0:T(8,128)(2,1)S(1)}, u32[]{:S(2)}, u32[]{:S(2)}) collective-permute-start(bf16[64,896]{1,0:T(8,128)(2,1)S(1)} %get-tuple-element.13.refs_1_), channel_id=1, source_target_pairs={{0,4},{2,6},{4,12},{6,14},{12,8},{14,10},{8,0},{10,2},{1,5},{3,7},... | collective-permute-start | bytes 344072 | tf_op jit(solution)/shard_map/ppermute | solution.py:269
  6.8 20.1 %collective-permute-start.2 = (bf16[64,1792]{1,0:T(8,128)(2,1)S(1)}, bf16[64,1792]{1,0:T(8,128)(2,1)S(1)}, u32[]{:S(2)}, u32[]{:S(2)}) collective-permute-start(bf16[64,1792]{1,0:T(8,128)(2,1)S(1)} %get-tuple-element.14), channel_id=1, source_target_pairs={{0,2},{2,0},{4,6},{6,4},{8,10},{10,8},{12,14},{14,12},{1,3},{3,1},... | collective-permute-start | bytes 688136 | tf_op jit(solution)/shard_map/ppermute | solution.py:269
  9.2 6.9 %collective-permute-start.3 = (bf16[64,896]{1,0:T(8,128)(2,1)S(1)}, bf16[64,896]{1,0:T(8,128)(2,1)S(1)}, u32[]{:S(2)}, u32[]{:S(2)}) collective-permute-start(bf16[64,896]{1,0:T(8,128)(2,1)S(1)} %collective-permute-done.refs_2_), channel_id=1, source_target_pairs={{0,4},{2,6},{4,12},{6,14},{12,8},{14,10},{8,0},{10,2},{1,5},{3,7},... | collective-permute-start | bytes 344072 | tf_op jit(solution)/shard_map/ppermute | solution.py:269
  10.8 7.7 %collective-permute-start.4 = (bf16[64,896]{1,0:T(8,128)(2,1)S(1)}, bf16[64,896]{1,0:T(8,128)(2,1)S(1)}, u32[]{:S(2)}, u32[]{:S(2)}) collective-permute-start(bf16[64,896]{1,0:T(8,128)(2,1)S(1)} %collective-permute-done.1.refs_3_), channel_id=1, source_target_pairs={{0,4},{2,6},{4,12},{6,14},{12,8},{14,10},{8,0},{10,2},{1,5},{3,7},... | collective-permute-start | bytes 344072 | tf_op jit(solution)/shard_map/ppermute | solution.py:269
  13.8 13.2 %collective-permute-start.5 = (bf16[64,1792]{1,0:T(8,128)(2,1)S(1)}, bf16[64,1792]{1,0:T(8,128)(2,1)S(1)}, u32[]{:S(2)}, u32[]{:S(2)}) collective-permute-start(bf16[64,1792]{1,0:T(8,128)(2,1)S(1)} %pad_maximum_fusion), channel_id=1, source_target_pairs={{0,2},{2,0},{4,6},{6,4},{8,10},{10,8},{12,14},{14,12},{1,3},{3,1},... | collective-permute-start | bytes 688136 | tf_op jit(solution)/shard_map/ppermute | solution.py:269
  16.1 6.0 %collective-permute-start.6 = (bf16[64,896]{1,0:T(8,128)(2,1)S(1)}, bf16[64,896]{1,0:T(8,128)(2,1)S(1)}, u32[]{:S(2)}, u32[]{:S(2)}) collective-permute-start(bf16[64,896]{1,0:T(8,128)(2,1)S(1)} %collective-permute-done.3.refs_5_), channel_id=1, source_target_pairs={{0,4},{2,6},{4,12},{6,14},{12,8},{14,10},{8,0},{10,2},{1,5},{3,7},... | collective-permute-start | bytes 344072 | tf_op jit(solution)/shard_map/ppermute | solution.py:269
  16.9 6.4 %collective-permute-start.7 = (bf16[64,896]{1,0:T(8,128)(2,1)S(1)}, bf16[64,896]{1,0:T(8,128)(2,1)S(1)}, u32[]{:S(2)}, u32[]{:S(2)}) collective-permute-start(bf16[64,896]{1,0:T(8,128)(2,1)S(1)} %collective-permute-done.3.refs_5_), channel_id=1, source_target_pairs={{0,2},{2,0},{4,6},{6,4},{8,10},{10,8},{12,14},{14,12},{1,3},{3,1},... | collective-permute-start | bytes 344072 | tf_op jit(solution)/shard_map/ppermute | solution.py:269
  18.5 5.7 %collective-permute-start.8 = (bf16[64,896]{1,0:T(8,128)(2,1)S(1)}, bf16[64,896]{1,0:T(8,128)(2,1)S(1)}, u32[]{:S(2)}, u32[]{:S(2)}) collective-permute-start(bf16[64,896]{1,0:T(8,128)(2,1)S(1)} %collective-permute-done.4.refs_6_), channel_id=1, source_target_pairs={{0,4},{2,6},{4,12},{6,14},{12,8},{14,10},{8,0},{10,2},{1,5},{3,7},... | collective-permute-start | bytes 344072 | tf_op jit(solution)/shard_map/ppermute | solution.py:269
  22.1 5.1 %collective-permute-start.9 = (bf16[64,896]{1,0:T(8,128)(2,1)S(1)}, bf16[64,896]{1,0:T(8,128)(2,1)S(1)}, u32[]{:S(2)}, u32[]{:S(2)}) collective-permute-start(bf16[64,896]{1,0:T(8,128)(2,1)S(1)} %collective-permute-done.4.refs_6_), channel_id=1, source_target_pairs={{0,2},{2,0},{4,6},{6,4},{8,10},{10,8},{12,14},{14,12},{1,3},{3,1},... | collective-permute-start | bytes 344072 | tf_op jit(solution)/shard_map/ppermute | solution.py:269
  23.3 5.1 %collective-permute-start.12 = (bf16[64,896]{1,0:T(8,128)(2,1)S(1)}, bf16[64,896]{1,0:T(8,128)(2,1)S(1)}, u32[]{:S(2)}, u32[]{:S(2)}) collective-permute-start(bf16[64,896]{1,0:T(8,128)(2,1)S(1)} %collective-permute-done.6.refs_8_), channel_id=1, source_target_pairs={{0,2},{2,0},{4,6},{6,4},{8,10},{10,8},{12,14},{14,12},{1,3},{3,1},... | collective-permute-start | bytes 344072 | tf_op jit(solution)/shard_map/ppermute | solution.py:269
  24.2 5.4 %collective-permute-start.10 = (bf16[64,896]{1,0:T(8,128)(2,1)S(1)}, bf16[64,896]{1,0:T(8,128)(2,1)S(1)}, u32[]{:S(2)}, u32[]{:S(2)}) collective-permute-start(bf16[64,896]{1,0:T(8,128)(2,1)S(1)} %collective-permute-done.8.refs_9_), channel_id=1, source_target_pairs={{0,2},{2,0},{4,6},{6,4},{8,10},{10,8},{12,14},{14,12},{1,3},{3,1},... | collective-permute-start | bytes 344072 | tf_op jit(solution)/shard_map/ppermute | solution.py:269
  25.4 0.7 %copy-start.4 = (s32[2,64,1]{1,2,0:T(1,128)S(1)}, s32[2,64,1]{1,2,0:T(1,128)}, u32[]{:S(2)}) copy-start(s32[2,64,1]{1,2,0:T(1,128)} %param.10) | copy-start | bytes 1540
  26.1 0.7 %copy-start.5 = (s32[2,64]{1,0:T(2,128)S(1)}, s32[2,64]{1,0:T(2,128)}, u32[]{:S(2)}) copy-start(s32[2,64]{1,0:T(2,128)} %stored_ref.1) | copy-start | bytes 1540
  28.7 2.0 %copy-start = (bf16[896,1024]{1,0:T(8,128)(2,1)S(1)}, bf16[896,1024]{1,0:T(8,128)(2,1)}, u32[]{:S(2)}) copy-start(bf16[896,1024]{1,0:T(8,128)(2,1)} %refs_2_.5) | copy-start | bytes 5505028
  28.7 2.0 %copy-start.2 = (bf16[128,1024]{1,0:T(8,128)(2,1)S(1)}, bf16[128,1024]{1,0:T(8,128)(2,1)}, u32[]{:S(2)}) copy-start(bf16[128,1024]{1,0:T(8,128)(2,1)} %refs_4_.1) | copy-start | bytes 786436
  28.7 2.9 %collective-permute-start.13 = (bf16[128,896]{1,0:T(8,128)(2,1)S(1)}, bf16[128,896]{1,0:T(8,128)(2,1)S(1)}, u32[]{:S(2)}, u32[]{:S(2)}) collective-permute-start(bf16[128,896]{1,0:T(8,128)(2,1)S(1)} %shard_map.68.refs_1_), channel_id=1, source_target_pairs={{0,1},{1,0},{2,3},{3,2},{4,5},{5,4},{6,7},{7,6},{8,9},{9,8},{10,11... | collective-permute-start | bytes 688136 | tf_op jit(solution)/shard_map/ppermute | solution.py:303
  29.9 1.7 %collective-permute-start.11 = (bf16[128,896]{1,0:T(8,128)(2,1)S(1)}, bf16[128,896]{1,0:T(8,128)(2,1)S(1)}, u32[]{:S(2)}, u32[]{:S(2)}) collective-permute-start(bf16[128,896]{1,0:T(8,128)(2,1)S(1)} %shard_map.67.refs_0_), channel_id=1, source_target_pairs={{0,1},{1,0},{2,3},{3,2},{4,5},{5,4},{6,7},{7,6},{8,9},{9,8},{10,11... | collective-permute-start | bytes 688136 | tf_op jit(solution)/shard_map/ppermute | solution.py:303

commit v13 on v12

--- a/solution.py
+++ b/solution.py
@@ -225,16 +225,15 @@
     per = other.shape[0] // spans
     more = jnp.dot(other, wv_ref[...], preferred_element_type=jnp.float32).astype(jnp.bfloat16)
     everything = pair_places(spans, more.shape[1])
-    for c, lanes, n in everything:
-        scores = jnp.concatenate([first_ref[n], second_ref[n]], axis=0)
-        raised = jnp.exp2((scores - jnp.max(scores, axis=0, keepdims=True)) * EXPONENT)
-        probs_ref[n] = (raised * (1.0 / jnp.sum(raised, axis=0, keepdims=True))).astype(jnp.bfloat16)
     copies = []
     for c in range(spans):
         here = pl.ds(c * SPAN, SPAN)
-        for at, lanes, n in everything:
-            if at != c:
-                continue
+        ours = [(lanes, n) for at, lanes, n in everything if at == c]
+        for lanes, n in ours:
+            scores = jnp.concatenate([first_ref[n], second_ref[n]], axis=0)
+            raised = jnp.exp2((scores - jnp.max(scores, axis=0, keepdims=True)) * EXPONENT)
+            probs_ref[n] = (raised * (1.0 / jnp.sum(raised, axis=0, keepdims=True))).astype(jnp.bfloat16)
+        for lanes, n in ours:
             rows = slice(c * per, (c + 1) * per)
             values = jnp.concatenate([values_ref[rows, lanes], more[rows, lanes]], axis=0)
             mixed = lax.dot_general(

time: 34.5 us -> 34.5 us (level)
  no operation moved by 1% of the time
where the time goes in v13:
time: 34.5 us; the launch traced here: 34.1 us
  starting transfers between devices  21.8 us (63%)
  Pallas kernels  5.27 us (15%)
  waiting for transfers between devices  4.46 us (13%)
  local copies, waits for them, and re-layouts  2.39 us (7%)
    ppermute x12, starting transfers between devices, send(): return lax.ppermute(chunk, 'wide', pairs)  21.6 us
    ppermute x12, waiting for transfers between devices, send(): return lax.ppermute(chunk, 'wide', pairs)  4.45 us
    pallas_call x1, Pallas kernels, attend(): pl.pallas_call(functools.partial(attend_kernel, spans), out_shape=jax.Sha...  2.48 us
    unnamed x12, local copies, waits for them, and re-layouts  2.39 us
    pallas_call x1, Pallas kernels, own_scores(): pl.pallas_call(functools.partial(score_kernel, spans), out_shape=jax.Shap...  0.87 us
    pallas_call x1, Pallas kernels, own_values(): pl.pallas_call(functools.partial(values_kernel, spans), out_shape=jax.Sha...  0.71 us
  transfers between devices with their start and end apart: 14, of which 8 were waited for; matrix products, arithmetic and copies ran while one was open for 0% of the time, Pallas kernels for 8%

profile of v13, /device:TPU:0, one launch (start us, length us, event | category | flops | bytes accessed | tf_op | source)
XLA Modules:
  0.0 34.1 jit_solution(2567129992073110251)
XLA Ops:
  0.0 1.0 %copy-done.3 = bf16[64,3584]{1,0:T(8,128)(2,1)S(1)} copy-done((bf16[64,3584]{1,0:T(8,128)(2,1)S(1)}, bf16[64,3584]{1,0:T(8,128)(2,1)}, u32[]{:S(2)}) %copy-start.3) | copy-done | bytes 458776
  1.1 3.1 %collective-permute-start = (bf16[64,896]{1,0:T(8,128)(2,1)S(1)}, bf16[64,896]{1,0:T(8,128)(2,1)S(1)}, u32[]{:S(2)}, u32[]{:S(2)}) collective-permute-start(bf16[64,896]{1,0:T(8,128)(2,1)S(1)} %get-tuple-element.12.refs_0_), channel_id=1, source_target_pairs={{0,4},{2,6},{4,12},{6,14},{12,8},{14,10},{8,0},{10,2},{1,5},{3,7},... | collective-permute-start | bytes 344072 | tf_op jit(solution)/shard_map/ppermute | solution.py:268
  4.2 2.6 %collective-permute-start.1 = (bf16[64,896]{1,0:T(8,128)(2,1)S(1)}, bf16[64,896]{1,0:T(8,128)(2,1)S(1)}, u32[]{:S(2)}, u32[]{:S(2)}) collective-permute-start(bf16[64,896]{1,0:T(8,128)(2,1)S(1)} %get-tuple-element.13.refs_1_), channel_id=1, source_target_pairs={{0,4},{2,6},{4,12},{6,14},{12,8},{14,10},{8,0},{10,2},{1,5},{3,7},... | collective-permute-start | bytes 344072 | tf_op jit(solution)/shard_map/ppermute | solution.py:268
  6.8 1.5 %collective-permute-start.2 = (bf16[64,1792]{1,0:T(8,128)(2,1)S(1)}, bf16[64,1792]{1,0:T(8,128)(2,1)S(1)}, u32[]{:S(2)}, u32[]{:S(2)}) collective-permute-start(bf16[64,1792]{1,0:T(8,128)(2,1)S(1)} %get-tuple-element.14), channel_id=1, source_target_pairs={{0,2},{2,0},{4,6},{6,4},{8,10},{10,8},{12,14},{14,12},{1,3},{3,1},... | collective-permute-start | bytes 688136 | tf_op jit(solution)/shard_map/ppermute | solution.py:268
  8.3 0.9 %collective-permute-done.refs_2_ = bf16[64,896]{1,0:T(8,128)(2,1)S(1)} collective-permute-done((bf16[64,896]{1,0:T(8,128)(2,1)S(1)}, bf16[64,896]{1,0:T(8,128)(2,1)S(1)}, u32[]{:S(2)}, u32[]{:S(2)}) %collective-permute-start) | collective-permute-done | bytes 114720 | tf_op jit(solution)/shard_map/ppermute | solution.py:268
  9.2 1.2 %collective-permute-start.3 = (bf16[64,896]{1,0:T(8,128)(2,1)S(1)}, bf16[64,896]{1,0:T(8,128)(2,1)S(1)}, u32[]{:S(2)}, u32[]{:S(2)}) collective-permute-start(bf16[64,896]{1,0:T(8,128)(2,1)S(1)} %collective-permute-done.refs_2_), channel_id=1, source_target_pairs={{0,4},{2,6},{4,12},{6,14},{12,8},{14,10},{8,0},{10,2},{1,5},{3,7},... | collective-permute-start | bytes 344072 | tf_op jit(solution)/shard_map/ppermute | solution.py:268
  10.4 0.5 %collective-permute-done.1.refs_3_ = bf16[64,896]{1,0:T(8,128)(2,1)S(1)} collective-permute-done((bf16[64,896]{1,0:T(8,128)(2,1)S(1)}, bf16[64,896]{1,0:T(8,128)(2,1)S(1)}, u32[]{:S(2)}, u32[]{:S(2)}) %collective-permute-start.1) | collective-permute-done | bytes 114720 | tf_op jit(solution)/shard_map/ppermute | solution.py:268
  10.8 2.9 %collective-permute-start.4 = (bf16[64,896]{1,0:T(8,128)(2,1)S(1)}, bf16[64,896]{1,0:T(8,128)(2,1)S(1)}, u32[]{:S(2)}, u32[]{:S(2)}) collective-permute-start(bf16[64,896]{1,0:T(8,128)(2,1)S(1)} %collective-permute-done.1.refs_3_), channel_id=1, source_target_pairs={{0,4},{2,6},{4,12},{6,14},{12,8},{14,10},{8,0},{10,2},{1,5},{3,7},... | collective-permute-start | bytes 344072 | tf_op jit(solution)/shard_map/ppermute | solution.py:268
  13.8 1.6 %collective-permute-start.5 = (bf16[64,1792]{1,0:T(8,128)(2,1)S(1)}, bf16[64,1792]{1,0:T(8,128)(2,1)S(1)}, u32[]{:S(2)}, u32[]{:S(2)}) collective-permute-start(bf16[64,1792]{1,0:T(8,128)(2,1)S(1)} %pad_maximum_fusion), channel_id=1, source_target_pairs={{0,2},{2,0},{4,6},{6,4},{8,10},{10,8},{12,14},{14,12},{1,3},{3,1},... | collective-permute-start | bytes 688136 | tf_op jit(solution)/shard_map/ppermute | solution.py:268
  15.3 0.8 %collective-permute-done.3.refs_5_ = bf16[64,896]{1,0:T(8,128)(2,1)S(1)} collective-permute-done((bf16[64,896]{1,0:T(8,128)(2,1)S(1)}, bf16[64,896]{1,0:T(8,128)(2,1)S(1)}, u32[]{:S(2)}, u32[]{:S(2)}) %collective-permute-start.3) | collective-permute-done | bytes 114720 | tf_op jit(solution)/shard_map/ppermute | solution.py:268
  16.1 0.8 %collective-permute-start.6 = (bf16[64,896]{1,0:T(8,128)(2,1)S(1)}, bf16[64,896]{1,0:T(8,128)(2,1)S(1)}, u32[]{:S(2)}, u32[]{:S(2)}) collective-permute-start(bf16[64,896]{1,0:T(8,128)(2,1)S(1)} %collective-permute-done.3.refs_5_), channel_id=1, source_target_pairs={{0,4},{2,6},{4,12},{6,14},{12,8},{14,10},{8,0},{10,2},{1,5},{3,7},... | collective-permute-start | bytes 344072 | tf_op jit(solution)/shard_map/ppermute | solution.py:268
  16.9 1.5 %collective-permute-start.7 = (bf16[64,896]{1,0:T(8,128)(2,1)S(1)}, bf16[64,896]{1,0:T(8,128)(2,1)S(1)}, u32[]{:S(2)}, u32[]{:S(2)}) collective-permute-start(bf16[64,896]{1,0:T(8,128)(2,1)S(1)} %collective-permute-done.3.refs_5_), channel_id=1, source_target_pairs={{0,2},{2,0},{4,6},{6,4},{8,10},{10,8},{12,14},{14,12},{1,3},{3,1},... | collective-permute-start | bytes 344072 | tf_op jit(solution)/shard_map/ppermute | solution.py:268
  18.5 3.2 %collective-permute-start.8 = (bf16[64,896]{1,0:T(8,128)(2,1)S(1)}, bf16[64,896]{1,0:T(8,128)(2,1)S(1)}, u32[]{:S(2)}, u32[]{:S(2)}) collective-permute-start(bf16[64,896]{1,0:T(8,128)(2,1)S(1)} %collective-permute-done.4.refs_6_), channel_id=1, source_target_pairs={{0,4},{2,6},{4,12},{6,14},{12,8},{14,10},{8,0},{10,2},{1,5},{3,7},... | collective-permute-start | bytes 344072 | tf_op jit(solution)/shard_map/ppermute | solution.py:268
  22.1 1.2 %collective-permute-start.9 = (bf16[64,896]{1,0:T(8,128)(2,1)S(1)}, bf16[64,896]{1,0:T(8,128)(2,1)S(1)}, u32[]{:S(2)}, u32[]{:S(2)}) collective-permute-start(bf16[64,896]{1,0:T(8,128)(2,1)S(1)} %collective-permute-done.4.refs_6_), channel_id=1, source_target_pairs={{0,2},{2,0},{4,6},{6,4},{8,10},{10,8},{12,14},{14,12},{1,3},{3,1},... | collective-permute-start | bytes 344072 | tf_op jit(solution)/shard_map/ppermute | solution.py:268
  23.3 0.9 %collective-permute-start.12 = (bf16[64,896]{1,0:T(8,128)(2,1)S(1)}, bf16[64,896]{1,0:T(8,128)(2,1)S(1)}, u32[]{:S(2)}, u32[]{:S(2)}) collective-permute-start(bf16[64,896]{1,0:T(8,128)(2,1)S(1)} %collective-permute-done.6.refs_8_), channel_id=1, source_target_pairs={{0,2},{2,0},{4,6},{6,4},{8,10},{10,8},{12,14},{14,12},{1,3},{3,1},... | collective-permute-start | bytes 344072 | tf_op jit(solution)/shard_map/ppermute | solution.py:268
  24.2 1.2 %collective-permute-start.10 = (bf16[64,896]{1,0:T(8,128)(2,1)S(1)}, bf16[64,896]{1,0:T(8,128)(2,1)S(1)}, u32[]{:S(2)}, u32[]{:S(2)}) collective-permute-start(bf16[64,896]{1,0:T(8,128)(2,1)S(1)} %collective-permute-done.8.refs_9_), channel_id=1, source_target_pairs={{0,2},{2,0},{4,6},{6,4},{8,10},{10,8},{12,14},{14,12},{1,3},{3,1},... | collective-permute-start | bytes 344072 | tf_op jit(solution)/shard_map/ppermute | solution.py:268
  25.4 0.7 %copy-done.4 = s32[2,64,1]{1,2,0:T(1,128)S(1)} copy-done((s32[2,64,1]{1,2,0:T(1,128)S(1)}, s32[2,64,1]{1,2,0:T(1,128)}, u32[]{:S(2)}) %copy-start.4) | copy-done | bytes 536
  26.1 0.7 %copy-done.5 = s32[2,64]{1,0:T(2,128)S(1)} copy-done((s32[2,64]{1,0:T(2,128)S(1)}, s32[2,64]{1,0:T(2,128)}, u32[]{:S(2)}) %copy-start.5) | copy-done | bytes 536
  27.2 0.5 %shard_map.66 = (bf16[128,896]{1,0:T(8,128)(2,1)S(1)}, bf16[128,896]{1,0:T(8,128)(2,1)S(1)}) custom-call(s32[128,1]{1,0:T(8,128)S(1)} %shard_map.64.index_ref, bf16[64,896]{1,0:T(8,128)(2,1)S(1)} %get-tuple-element.12.refs_0_, bf16[64,896]{1,0:T(8,128)(2,1)S(1)} %get-tuple-element.13.refs_1_, bf16[64,896]{1,0:T(8,128)(2,1)S(1)} %collective-permute-done.refs_2_, ...), custom_call_target="tpu_custom_call" | custom-call | flops 205520896 | bytes 458752 | tf_op jit(solution)/shard_map/pallas_call | solution.py:114
  27.7 0.7 %collective-permute-done.12.last_ref = bf16[64,896]{1,0:T(8,128)(2,1)S(1)} collective-permute-done((bf16[64,896]{1,0:T(8,128)(2,1)S(1)}, bf16[64,896]{1,0:T(8,128)(2,1)S(1)}, u32[]{:S(2)}, u32[]{:S(2)}) %collective-permute-start.12) | collective-permute-done | bytes 114720 | tf_op jit(solution)/shard_map/ppermute | solution.py:268
  28.8 0.9 %collective-permute-done.10.last_ref = bf16[64,896]{1,0:T(8,128)(2,1)S(1)} collective-permute-done((bf16[64,896]{1,0:T(8,128)(2,1)S(1)}, bf16[64,896]{1,0:T(8,128)(2,1)S(1)}, u32[]{:S(2)}, u32[]{:S(2)}) %collective-permute-start.10) | collective-permute-done | bytes 114720 | tf_op jit(solution)/shard_map/ppermute | solution.py:268
  30.0 0.7 %shard_map.70.refs_6_ = bf16[256,1024]{1,0:T(8,128)(2,1)S(1)} custom-call(bf16[128,896]{1,0:T(8,128)(2,1)S(1)} %shard_map.67.refs_0_, bf16[128,896]{1,0:T(8,128)(2,1)S(1)} %shard_map.68.refs_1_, bf16[896,1024]{1,0:T(8,128)(2,1)S(1)} %copy-done.1), custom_call_target="tpu_custom_call" | custom-call | tf_op jit(solution)/shard_map/pallas_call | solution.py:212
  30.7 0.9 %shard_map.69.refs_5_ = f32[8,128,128]{2,1,0:T(8,128)S(1)} custom-call(bf16[128,896]{1,0:T(8,128)(2,1)S(1)} %shard_map.67.refs_0_, bf16[128,896]{1,0:T(8,128)(2,1)S(1)} %shard_map.68.refs_1_, bf16[896,1024]{1,0:T(8,128)(2,1)S(1)} %copy-done, bf16[128,1024]{1,0:T(8,128)(2,1)S(1)} %copy-done.2), custom_call_target="tpu_custom_call" | custom-call | tf_op jit(solution)/shard_map/pallas_call | solution.py:196
  31.6 2.5 %shard_map.71 = bf16[128,1024]{1,0:T(8,128)(2,1)} custom-call(bf16[128,896]{1,0:T(8,128)(2,1)S(1)} %collective-permute-done.11.refs_0_, bf16[128,896]{1,0:T(8,128)(2,1)S(1)} %collective-permute-done.13.refs_1_, bf16[896,1024]{1,0:T(8,128)(2,1)S(1)} %copy-done, bf16[896,1024]{1,0:T(8,128)(2,1)S(1)} %copy-done.1, bf16[128,1024]{1,0:T(8,128)(2,1)S(1)} %copy-done.2, ...), custom_call_target="tpu_custom_call" | custom-call | tf_op jit(solution)/shard_map/pallas_call | solution.py:252
  (25 shorter events, 1.6 us)
Async XLA Ops:
  0.0 1.0 %copy-start.3 = (bf16[64,3584]{1,0:T(8,128)(2,1)S(1)}, bf16[64,3584]{1,0:T(8,128)(2,1)}, u32[]{:S(2)}) copy-start(bf16[64,3584]{1,0:T(8,128)(2,1)} %enc_ref.1) | copy-start | bytes 1376260
  1.1 28.9 %copy-start.1 = (bf16[896,1024]{1,0:T(8,128)(2,1)S(1)}, bf16[896,1024]{1,0:T(8,128)(2,1)}, u32[]{:S(2)}) copy-start(bf16[896,1024]{1,0:T(8,128)(2,1)} %refs_3_.3) | copy-start | bytes 5505028
  1.1 8.1 %collective-permute-start = (bf16[64,896]{1,0:T(8,128)(2,1)S(1)}, bf16[64,896]{1,0:T(8,128)(2,1)S(1)}, u32[]{:S(2)}, u32[]{:S(2)}) collective-permute-start(bf16[64,896]{1,0:T(8,128)(2,1)S(1)} %get-tuple-element.12.refs_0_), channel_id=1, source_target_pairs={{0,4},{2,6},{4,12},{6,14},{12,8},{14,10},{8,0},{10,2},{1,5},{3,7},... | collective-permute-start | bytes 344072 | tf_op jit(solution)/shard_map/ppermute | solution.py:268
  4.2 6.6 %collective-permute-start.1 = (bf16[64,896]{1,0:T(8,128)(2,1)S(1)}, bf16[64,896]{1,0:T(8,128)(2,1)S(1)}, u32[]{:S(2)}, u32[]{:S(2)}) collective-permute-start(bf16[64,896]{1,0:T(8,128)(2,1)S(1)} %get-tuple-element.13.refs_1_), channel_id=1, source_target_pairs={{0,4},{2,6},{4,12},{6,14},{12,8},{14,10},{8,0},{10,2},{1,5},{3,7},... | collective-permute-start | bytes 344072 | tf_op jit(solution)/shard_map/ppermute | solution.py:268
  6.8 20.1 %collective-permute-start.2 = (bf16[64,1792]{1,0:T(8,128)(2,1)S(1)}, bf16[64,1792]{1,0:T(8,128)(2,1)S(1)}, u32[]{:S(2)}, u32[]{:S(2)}) collective-permute-start(bf16[64,1792]{1,0:T(8,128)(2,1)S(1)} %get-tuple-element.14), channel_id=1, source_target_pairs={{0,2},{2,0},{4,6},{6,4},{8,10},{10,8},{12,14},{14,12},{1,3},{3,1},... | collective-permute-start | bytes 688136 | tf_op jit(solution)/shard_map/ppermute | solution.py:268
  9.2 6.9 %collective-permute-start.3 = (bf16[64,896]{1,0:T(8,128)(2,1)S(1)}, bf16[64,896]{1,0:T(8,128)(2,1)S(1)}, u32[]{:S(2)}, u32[]{:S(2)}) collective-permute-start(bf16[64,896]{1,0:T(8,128)(2,1)S(1)} %collective-permute-done.refs_2_), channel_id=1, source_target_pairs={{0,4},{2,6},{4,12},{6,14},{12,8},{14,10},{8,0},{10,2},{1,5},{3,7},... | collective-permute-start | bytes 344072 | tf_op jit(solution)/shard_map/ppermute | solution.py:268
  10.8 7.7 %collective-permute-start.4 = (bf16[64,896]{1,0:T(8,128)(2,1)S(1)}, bf16[64,896]{1,0:T(8,128)(2,1)S(1)}, u32[]{:S(2)}, u32[]{:S(2)}) collective-permute-start(bf16[64,896]{1,0:T(8,128)(2,1)S(1)} %collective-permute-done.1.refs_3_), channel_id=1, source_target_pairs={{0,4},{2,6},{4,12},{6,14},{12,8},{14,10},{8,0},{10,2},{1,5},{3,7},... | collective-permute-start | bytes 344072 | tf_op jit(solution)/shard_map/ppermute | solution.py:268
  13.8 13.2 %collective-permute-start.5 = (bf16[64,1792]{1,0:T(8,128)(2,1)S(1)}, bf16[64,1792]{1,0:T(8,128)(2,1)S(1)}, u32[]{:S(2)}, u32[]{:S(2)}) collective-permute-start(bf16[64,1792]{1,0:T(8,128)(2,1)S(1)} %pad_maximum_fusion), channel_id=1, source_target_pairs={{0,2},{2,0},{4,6},{6,4},{8,10},{10,8},{12,14},{14,12},{1,3},{3,1},... | collective-permute-start | bytes 688136 | tf_op jit(solution)/shard_map/ppermute | solution.py:268
  16.1 6.0 %collective-permute-start.6 = (bf16[64,896]{1,0:T(8,128)(2,1)S(1)}, bf16[64,896]{1,0:T(8,128)(2,1)S(1)}, u32[]{:S(2)}, u32[]{:S(2)}) collective-permute-start(bf16[64,896]{1,0:T(8,128)(2,1)S(1)} %collective-permute-done.3.refs_5_), channel_id=1, source_target_pairs={{0,4},{2,6},{4,12},{6,14},{12,8},{14,10},{8,0},{10,2},{1,5},{3,7},... | collective-permute-start | bytes 344072 | tf_op jit(solution)/shard_map/ppermute | solution.py:268
  16.9 6.4 %collective-permute-start.7 = (bf16[64,896]{1,0:T(8,128)(2,1)S(1)}, bf16[64,896]{1,0:T(8,128)(2,1)S(1)}, u32[]{:S(2)}, u32[]{:S(2)}) collective-permute-start(bf16[64,896]{1,0:T(8,128)(2,1)S(1)} %collective-permute-done.3.refs_5_), channel_id=1, source_target_pairs={{0,2},{2,0},{4,6},{6,4},{8,10},{10,8},{12,14},{14,12},{1,3},{3,1},... | collective-permute-start | bytes 344072 | tf_op jit(solution)/shard_map/ppermute | solution.py:268
  18.5 5.7 %collective-permute-start.8 = (bf16[64,896]{1,0:T(8,128)(2,1)S(1)}, bf16[64,896]{1,0:T(8,128)(2,1)S(1)}, u32[]{:S(2)}, u32[]{:S(2)}) collective-permute-start(bf16[64,896]{1,0:T(8,128)(2,1)S(1)} %collective-permute-done.4.refs_6_), channel_id=1, source_target_pairs={{0,4},{2,6},{4,12},{6,14},{12,8},{14,10},{8,0},{10,2},{1,5},{3,7},... | collective-permute-start | bytes 344072 | tf_op jit(solution)/shard_map/ppermute | solution.py:268
  22.1 5.1 %collective-permute-start.9 = (bf16[64,896]{1,0:T(8,128)(2,1)S(1)}, bf16[64,896]{1,0:T(8,128)(2,1)S(1)}, u32[]{:S(2)}, u32[]{:S(2)}) collective-permute-start(bf16[64,896]{1,0:T(8,128)(2,1)S(1)} %collective-permute-done.4.refs_6_), channel_id=1, source_target_pairs={{0,2},{2,0},{4,6},{6,4},{8,10},{10,8},{12,14},{14,12},{1,3},{3,1},... | collective-permute-start | bytes 344072 | tf_op jit(solution)/shard_map/ppermute | solution.py:268
  23.3 5.1 %collective-permute-start.12 = (bf16[64,896]{1,0:T(8,128)(2,1)S(1)}, bf16[64,896]{1,0:T(8,128)(2,1)S(1)}, u32[]{:S(2)}, u32[]{:S(2)}) collective-permute-start(bf16[64,896]{1,0:T(8,128)(2,1)S(1)} %collective-permute-done.6.refs_8_), channel_id=1, source_target_pairs={{0,2},{2,0},{4,6},{6,4},{8,10},{10,8},{12,14},{14,12},{1,3},{3,1},... | collective-permute-start | bytes 344072 | tf_op jit(solution)/shard_map/ppermute | solution.py:268
  24.2 5.4 %collective-permute-start.10 = (bf16[64,896]{1,0:T(8,128)(2,1)S(1)}, bf16[64,896]{1,0:T(8,128)(2,1)S(1)}, u32[]{:S(2)}, u32[]{:S(2)}) collective-permute-start(bf16[64,896]{1,0:T(8,128)(2,1)S(1)} %collective-permute-done.8.refs_9_), channel_id=1, source_target_pairs={{0,2},{2,0},{4,6},{6,4},{8,10},{10,8},{12,14},{14,12},{1,3},{3,1},... | collective-permute-start | bytes 344072 | tf_op jit(solution)/shard_map/ppermute | solution.py:268
  25.4 0.7 %copy-start.4 = (s32[2,64,1]{1,2,0:T(1,128)S(1)}, s32[2,64,1]{1,2,0:T(1,128)}, u32[]{:S(2)}) copy-start(s32[2,64,1]{1,2,0:T(1,128)} %param.10) | copy-start | bytes 1540
  26.1 0.7 %copy-start.5 = (s32[2,64]{1,0:T(2,128)S(1)}, s32[2,64]{1,0:T(2,128)}, u32[]{:S(2)}) copy-start(s32[2,64]{1,0:T(2,128)} %stored_ref.1) | copy-start | bytes 1540
  28.7 2.0 %copy-start = (bf16[896,1024]{1,0:T(8,128)(2,1)S(1)}, bf16[896,1024]{1,0:T(8,128)(2,1)}, u32[]{:S(2)}) copy-start(bf16[896,1024]{1,0:T(8,128)(2,1)} %refs_2_.5) | copy-start | bytes 5505028
  28.7 2.0 %copy-start.2 = (bf16[128,1024]{1,0:T(8,128)(2,1)S(1)}, bf16[128,1024]{1,0:T(8,128)(2,1)}, u32[]{:S(2)}) copy-start(bf16[128,1024]{1,0:T(8,128)(2,1)} %refs_4_.1) | copy-start | bytes 786436
  28.7 2.9 %collective-permute-start.13 = (bf16[128,896]{1,0:T(8,128)(2,1)S(1)}, bf16[128,896]{1,0:T(8,128)(2,1)S(1)}, u32[]{:S(2)}, u32[]{:S(2)}) collective-permute-start(bf16[128,896]{1,0:T(8,128)(2,1)S(1)} %shard_map.68.refs_1_), channel_id=1, source_target_pairs={{0,1},{1,0},{2,3},{3,2},{4,5},{5,4},{6,7},{7,6},{8,9},{9,8},{10,11... | collective-permute-start | bytes 688136 | tf_op jit(solution)/shard_map/ppermute | solution.py:302
  29.9 1.7 %collective-permute-start.11 = (bf16[128,896]{1,0:T(8,128)(2,1)S(1)}, bf16[128,896]{1,0:T(8,128)(2,1)S(1)}, u32[]{:S(2)}, u32[]{:S(2)}) collective-permute-start(bf16[128,896]{1,0:T(8,128)(2,1)S(1)} %shard_map.67.refs_0_), channel_id=1, source_target_pairs={{0,1},{1,0},{2,3},{3,2},{4,5},{5,4},{6,7},{7,6},{8,9},{9,8},{10,11... | collective-permute-start | bytes 688136 | tf_op jit(solution)/shard_map/ppermute | solution.py:302

commit v14 on v12

--- a/solution.py
+++ b/solution.py
@@ -219,7 +219,9 @@
 
 
 def attend_kernel(spans, *refs):
-    *others, wk_ref, wv_ref, query_ref, first_ref, values_ref, out_ref, second_ref, probs_ref, held_ref, sems = refs
+    others, refs = refs[:STREAMS], refs[STREAMS:]
+    values_refs, refs = refs[:STREAMS], refs[STREAMS:]
+    wk_ref, wv_ref, query_ref, first_ref, out_ref, second_ref, probs_ref, held_ref, sems = refs
     other = by_span(others, spans, wk_ref.shape[0])
     score(spans, other, wk_ref, query_ref, second_ref)
     per = other.shape[0] // spans
@@ -236,7 +238,8 @@
             if at != c:
                 continue
             rows = slice(c * per, (c + 1) * per)
-            values = jnp.concatenate([values_ref[rows, lanes], more[rows, lanes]], axis=0)
+            owned = [ref[c * ref.shape[0] // spans : (c + 1) * ref.shape[0] // spans, lanes] for ref in values_refs]
+            values = jnp.concatenate(owned + [more[rows, lanes]], axis=0)
             mixed = lax.dot_general(
                 probs_ref[n], values, (((0,), (0,)), ((), ())), preferred_element_type=jnp.float32
             ).astype(out_ref.dtype)
@@ -253,7 +256,7 @@
     return pl.pallas_call(
         functools.partial(attend_kernel, spans),
         out_shape=jax.ShapeDtypeStruct(queries.shape, queries.dtype),
-        in_specs=[VMEM] * (5 + len(others)),
+        in_specs=[VMEM] * (4 + len(others) + len(values)),
         out_specs=pl.BlockSpec(memory_space=pl.ANY),
         scratch_shapes=[
             pltpu.VMEM(each, jnp.float32),
@@ -262,7 +265,7 @@
             pltpu.SemaphoreType.DMA((spans,)),
         ],
         compiler_params=params(),
-    )(*others, w_key, w_value, queries, first, values)
+    )(*others, *values, w_key, w_value, queries, first)
 
 
 def send(chunk, pairs):
@@ -299,10 +302,14 @@
     held[turns - 1, 1] = [send(piece, across) for piece in held[turns - 1, 0]]
     sources = [held[chunk] for chunk in order]
     begun = early(index, sources[:-1], whole.shape[1])
-    picked = [pick(index, *pieces, (len(order) - 1) * rows) for pieces in zip(begun[::-1], sources[-1][::-1])]
-    others = [lax.ppermute(piece, "heads", [(0, 1), (1, 0)]) for piece in picked]
+    picked, values, others = [], [], []
+    for piece, last in zip(begun, sources[-1]):
+        if values:
+            last, values[-1] = lax.optimization_barrier((last, values[-1]))
+        picked.append(pick(index, piece, last, (len(order) - 1) * rows))
+        others.append(lax.ppermute(picked[-1], "heads", [(0, 1), (1, 0)]))
+        values.append(own_values(picked[-1:], w_value, spans))
     first = own_scores(picked, w_key, queries, spans)
-    values = own_values(picked, w_value, spans)
     return attend(others, w_key, w_value, queries, first, values, spans)
 
 

time: 34.5 us -> 34.6 us (level)
  starting transfers between devices: 21.8 us -> 22.2 us
  waiting for transfers between devices: 4.46 us -> 4.08 us
    ppermute x2, starting transfers between devices: 0.14 us -> 0.57 us  [gathered_plan(): others.append(lax.ppermute(picked[-1], 'heads', [(0, 1), (1, 0)]))]
    ppermute x12, waiting for transfers between devices: 4.45 us -> 4.07 us  [send(): return lax.ppermute(chunk, 'wide', pairs)]
    pallas_call x1 -> x2, Pallas kernels: 0.71 us -> 0.88 us  [own_values(): pl.pallas_call(functools.partial(values_kernel, spans), out_shape=jax.Sha...]
where the time goes in v14:
time: 34.6 us; the launch traced here: 34.4 us
  starting transfers between devices  22.2 us (64%)
  Pallas kernels  5.44 us (16%)
  waiting for transfers between devices  4.08 us (12%)
  local copies, waits for them, and re-layouts  2.53 us (7%)
    ppermute x12, starting transfers between devices, send(): return lax.ppermute(chunk, 'wide', pairs)  21.6 us
    ppermute x12, waiting for transfers between devices, send(): return lax.ppermute(chunk, 'wide', pairs)  4.07 us
    unnamed x12, local copies, waits for them, and re-layouts  2.53 us
    pallas_call x1, Pallas kernels, attend(): pl.pallas_call(functools.partial(attend_kernel, spans), out_shape=jax.Sha...  2.48 us
    pallas_call x2, Pallas kernels, own_values(): pl.pallas_call(functools.partial(values_kernel, spans), out_shape=jax.Sha...  0.88 us
    pallas_call x1, Pallas kernels, own_scores(): pl.pallas_call(functools.partial(score_kernel, spans), out_shape=jax.Shap...  0.87 us
  transfers between devices with their start and end apart: 14, of which 8 were waited for; matrix products, arithmetic and copies ran while one was open for 0% of the time, Pallas kernels for 8%

profile of v14, /device:TPU:0, one launch (start us, length us, event | category | flops | bytes accessed | tf_op | source)
XLA Modules:
  0.0 34.4 jit_solution(6553967401993209240)
XLA Ops:
  0.0 1.2 %copy-done.3 = bf16[64,3584]{1,0:T(8,128)(2,1)S(1)} copy-done((bf16[64,3584]{1,0:T(8,128)(2,1)S(1)}, bf16[64,3584]{1,0:T(8,128)(2,1)}, u32[]{:S(2)}) %copy-start.3) | copy-done | bytes 458776
  1.3 3.1 %collective-permute-start = (bf16[64,896]{1,0:T(8,128)(2,1)S(1)}, bf16[64,896]{1,0:T(8,128)(2,1)S(1)}, u32[]{:S(2)}, u32[]{:S(2)}) collective-permute-start(bf16[64,896]{1,0:T(8,128)(2,1)S(1)} %get-tuple-element.14.refs_0_), channel_id=1, source_target_pairs={{0,4},{2,6},{4,12},{6,14},{12,8},{14,10},{8,0},{10,2},{1,5},{3,7},... | collective-permute-start | bytes 344072 | tf_op jit(solution)/shard_map/ppermute | solution.py:272
  4.3 2.6 %collective-permute-start.1 = (bf16[64,896]{1,0:T(8,128)(2,1)S(1)}, bf16[64,896]{1,0:T(8,128)(2,1)S(1)}, u32[]{:S(2)}, u32[]{:S(2)}) collective-permute-start(bf16[64,896]{1,0:T(8,128)(2,1)S(1)} %get-tuple-element.15.refs_1_), channel_id=1, source_target_pairs={{0,4},{2,6},{4,12},{6,14},{12,8},{14,10},{8,0},{10,2},{1,5},{3,7},... | collective-permute-start | bytes 344072 | tf_op jit(solution)/shard_map/ppermute | solution.py:272
  6.9 1.5 %collective-permute-start.2 = (bf16[64,1792]{1,0:T(8,128)(2,1)S(1)}, bf16[64,1792]{1,0:T(8,128)(2,1)S(1)}, u32[]{:S(2)}, u32[]{:S(2)}) collective-permute-start(bf16[64,1792]{1,0:T(8,128)(2,1)S(1)} %get-tuple-element.16), channel_id=1, source_target_pairs={{0,2},{2,0},{4,6},{6,4},{8,10},{10,8},{12,14},{14,12},{1,3},{3,1},... | collective-permute-start | bytes 688136 | tf_op jit(solution)/shard_map/ppermute | solution.py:272
  8.4 0.9 %collective-permute-done.refs_2_ = bf16[64,896]{1,0:T(8,128)(2,1)S(1)} collective-permute-done((bf16[64,896]{1,0:T(8,128)(2,1)S(1)}, bf16[64,896]{1,0:T(8,128)(2,1)S(1)}, u32[]{:S(2)}, u32[]{:S(2)}) %collective-permute-start) | collective-permute-done | bytes 114720 | tf_op jit(solution)/shard_map/ppermute | solution.py:272
  9.3 1.2 %collective-permute-start.3 = (bf16[64,896]{1,0:T(8,128)(2,1)S(1)}, bf16[64,896]{1,0:T(8,128)(2,1)S(1)}, u32[]{:S(2)}, u32[]{:S(2)}) collective-permute-start(bf16[64,896]{1,0:T(8,128)(2,1)S(1)} %collective-permute-done.refs_2_), channel_id=1, source_target_pairs={{0,4},{2,6},{4,12},{6,14},{12,8},{14,10},{8,0},{10,2},{1,5},{3,7},... | collective-permute-start | bytes 344072 | tf_op jit(solution)/shard_map/ppermute | solution.py:272
  10.5 0.5 %collective-permute-done.1.refs_3_ = bf16[64,896]{1,0:T(8,128)(2,1)S(1)} collective-permute-done((bf16[64,896]{1,0:T(8,128)(2,1)S(1)}, bf16[64,896]{1,0:T(8,128)(2,1)S(1)}, u32[]{:S(2)}, u32[]{:S(2)}) %collective-permute-start.1) | collective-permute-done | bytes 114720 | tf_op jit(solution)/shard_map/ppermute | solution.py:272
  11.0 2.9 %collective-permute-start.4 = (bf16[64,896]{1,0:T(8,128)(2,1)S(1)}, bf16[64,896]{1,0:T(8,128)(2,1)S(1)}, u32[]{:S(2)}, u32[]{:S(2)}) collective-permute-start(bf16[64,896]{1,0:T(8,128)(2,1)S(1)} %collective-permute-done.1.refs_3_), channel_id=1, source_target_pairs={{0,4},{2,6},{4,12},{6,14},{12,8},{14,10},{8,0},{10,2},{1,5},{3,7},... | collective-permute-start | bytes 344072 | tf_op jit(solution)/shard_map/ppermute | solution.py:272
  13.9 1.6 %collective-permute-start.5 = (bf16[64,1792]{1,0:T(8,128)(2,1)S(1)}, bf16[64,1792]{1,0:T(8,128)(2,1)S(1)}, u32[]{:S(2)}, u32[]{:S(2)}) collective-permute-start(bf16[64,1792]{1,0:T(8,128)(2,1)S(1)} %pad_maximum_fusion), channel_id=1, source_target_pairs={{0,2},{2,0},{4,6},{6,4},{8,10},{10,8},{12,14},{14,12},{1,3},{3,1},... | collective-permute-start | bytes 688136 | tf_op jit(solution)/shard_map/ppermute | solution.py:272
  15.4 0.8 %collective-permute-done.3.refs_5_ = bf16[64,896]{1,0:T(8,128)(2,1)S(1)} collective-permute-done((bf16[64,896]{1,0:T(8,128)(2,1)S(1)}, bf16[64,896]{1,0:T(8,128)(2,1)S(1)}, u32[]{:S(2)}, u32[]{:S(2)}) %collective-permute-start.3) | collective-permute-done | bytes 114720 | tf_op jit(solution)/shard_map/ppermute | solution.py:272
  16.2 0.8 %collective-permute-start.6 = (bf16[64,896]{1,0:T(8,128)(2,1)S(1)}, bf16[64,896]{1,0:T(8,128)(2,1)S(1)}, u32[]{:S(2)}, u32[]{:S(2)}) collective-permute-start(bf16[64,896]{1,0:T(8,128)(2,1)S(1)} %collective-permute-done.3.refs_5_), channel_id=1, source_target_pairs={{0,4},{2,6},{4,12},{6,14},{12,8},{14,10},{8,0},{10,2},{1,5},{3,7},... | collective-permute-start | bytes 344072 | tf_op jit(solution)/shard_map/ppermute | solution.py:272
  17.0 1.5 %collective-permute-start.7 = (bf16[64,896]{1,0:T(8,128)(2,1)S(1)}, bf16[64,896]{1,0:T(8,128)(2,1)S(1)}, u32[]{:S(2)}, u32[]{:S(2)}) collective-permute-start(bf16[64,896]{1,0:T(8,128)(2,1)S(1)} %collective-permute-done.3.refs_5_), channel_id=1, source_target_pairs={{0,2},{2,0},{4,6},{6,4},{8,10},{10,8},{12,14},{14,12},{1,3},{3,1},... | collective-permute-start | bytes 344072 | tf_op jit(solution)/shard_map/ppermute | solution.py:272
  18.6 3.2 %collective-permute-start.8 = (bf16[64,896]{1,0:T(8,128)(2,1)S(1)}, bf16[64,896]{1,0:T(8,128)(2,1)S(1)}, u32[]{:S(2)}, u32[]{:S(2)}) collective-permute-start(bf16[64,896]{1,0:T(8,128)(2,1)S(1)} %collective-permute-done.4.refs_6_), channel_id=1, source_target_pairs={{0,4},{2,6},{4,12},{6,14},{12,8},{14,10},{8,0},{10,2},{1,5},{3,7},... | collective-permute-start | bytes 344072 | tf_op jit(solution)/shard_map/ppermute | solution.py:272
  22.2 1.2 %collective-permute-start.9 = (bf16[64,896]{1,0:T(8,128)(2,1)S(1)}, bf16[64,896]{1,0:T(8,128)(2,1)S(1)}, u32[]{:S(2)}, u32[]{:S(2)}) collective-permute-start(bf16[64,896]{1,0:T(8,128)(2,1)S(1)} %collective-permute-done.4.refs_6_), channel_id=1, source_target_pairs={{0,2},{2,0},{4,6},{6,4},{8,10},{10,8},{12,14},{14,12},{1,3},{3,1},... | collective-permute-start | bytes 344072 | tf_op jit(solution)/shard_map/ppermute | solution.py:272
  23.4 0.9 %collective-permute-start.10 = (bf16[64,896]{1,0:T(8,128)(2,1)S(1)}, bf16[64,896]{1,0:T(8,128)(2,1)S(1)}, u32[]{:S(2)}, u32[]{:S(2)}) collective-permute-start(bf16[64,896]{1,0:T(8,128)(2,1)S(1)} %collective-permute-done.6.refs_8_), channel_id=1, source_target_pairs={{0,2},{2,0},{4,6},{6,4},{8,10},{10,8},{12,14},{14,12},{1,3},{3,1},... | collective-permute-start | bytes 344072 | tf_op jit(solution)/shard_map/ppermute | solution.py:272
  24.3 1.2 %collective-permute-start.12 = (bf16[64,896]{1,0:T(8,128)(2,1)S(1)}, bf16[64,896]{1,0:T(8,128)(2,1)S(1)}, u32[]{:S(2)}, u32[]{:S(2)}) collective-permute-start(bf16[64,896]{1,0:T(8,128)(2,1)S(1)} %collective-permute-done.8.refs_9_), channel_id=1, source_target_pairs={{0,2},{2,0},{4,6},{6,4},{8,10},{10,8},{12,14},{14,12},{1,3},{3,1},... | collective-permute-start | bytes 344072 | tf_op jit(solution)/shard_map/ppermute | solution.py:272
  25.6 0.7 %copy-done.4 = s32[2,64,1]{1,2,0:T(1,128)S(1)} copy-done((s32[2,64,1]{1,2,0:T(1,128)S(1)}, s32[2,64,1]{1,2,0:T(1,128)}, u32[]{:S(2)}) %copy-start.4) | copy-done | bytes 536
  26.2 0.7 %copy-done.5 = s32[2,64]{1,0:T(2,128)S(1)} copy-done((s32[2,64]{1,0:T(2,128)S(1)}, s32[2,64]{1,0:T(2,128)}, u32[]{:S(2)}) %copy-start.5) | copy-done | bytes 536
  27.3 0.5 %shard_map.66 = (bf16[128,896]{1,0:T(8,128)(2,1)S(1)}, bf16[128,896]{1,0:T(8,128)(2,1)S(1)}) custom-call(s32[128,1]{1,0:T(8,128)S(1)} %shard_map.64.index_ref, bf16[64,896]{1,0:T(8,128)(2,1)S(1)} %get-tuple-element.14.refs_0_, bf16[64,896]{1,0:T(8,128)(2,1)S(1)} %get-tuple-element.15.refs_1_, bf16[64,896]{1,0:T(8,128)(2,1)S(1)} %collective-permute-done.refs_2_, ...), custom_call_target="tpu_custom_call" | custom-call | flops 205520896 | bytes 458752 | tf_op jit(solution)/shard_map/pallas_call | solution.py:114
  27.8 0.7 %collective-permute-done.10.last_ref = bf16[64,896]{1,0:T(8,128)(2,1)S(1)} collective-permute-done((bf16[64,896]{1,0:T(8,128)(2,1)S(1)}, bf16[64,896]{1,0:T(8,128)(2,1)S(1)}, u32[]{:S(2)}, u32[]{:S(2)}) %collective-permute-start.10) | collective-permute-done | bytes 114720 | tf_op jit(solution)/shard_map/ppermute | solution.py:272
  29.3 0.5 %collective-permute-done.12.last_ref = bf16[64,896]{1,0:T(8,128)(2,1)S(1)} collective-permute-done((bf16[64,896]{1,0:T(8,128)(2,1)S(1)}, bf16[64,896]{1,0:T(8,128)(2,1)S(1)}, u32[]{:S(2)}, u32[]{:S(2)}) %collective-permute-start.12) | collective-permute-done | bytes 114720 | tf_op jit(solution)/shard_map/ppermute | solution.py:272
  30.1 0.5 %collective-permute-start.11 = (bf16[128,896]{1,0:T(8,128)(2,1)S(1)}, bf16[128,896]{1,0:T(8,128)(2,1)S(1)}, u32[]{:S(2)}, u32[]{:S(2)}) collective-permute-start(bf16[128,896]{1,0:T(8,128)(2,1)S(1)} %shard_map.67.refs_0_), channel_id=1, source_target_pairs={{0,1},{1,0},{2,3},{3,2},{4,5},{5,4},{6,7},{7,6},{8,9},{9,8},{10,11... | collective-permute-start | bytes 688136 | tf_op jit(solution)/shard_map/ppermute | solution.py:310
  31.1 0.9 %shard_map.71.refs_7_ = f32[8,128,128]{2,1,0:T(8,128)S(1)} custom-call(bf16[128,896]{1,0:T(8,128)(2,1)S(1)} %shard_map.67.refs_0_, bf16[128,896]{1,0:T(8,128)(2,1)S(1)} %shard_map.69.refs_0_.refs_1_, bf16[896,1024]{1,0:T(8,128)(2,1)S(1)} %copy-done.1, bf16[128,1024]{1,0:T(8,128)(2,1)S(1)} %copy-done.2), custom_call_target="tpu_custom_call" | custom-call | tf_op jit(solution)/shard_map/pallas_call | solution.py:196
  32.0 2.5 %shard_map.72 = bf16[128,1024]{1,0:T(8,128)(2,1)} custom-call(bf16[128,896]{1,0:T(8,128)(2,1)S(1)} %collective-permute-done.11.refs_0_, bf16[128,896]{1,0:T(8,128)(2,1)S(1)} %collective-permute-done.13.refs_1_, bf16[128,1024]{1,0:T(8,128)(2,1)S(1)} %shard_map.68.refs_2_, bf16[128,1024]{1,0:T(8,128)(2,1)S(1)} %shard_map.70.refs_3_, ...), custom_call_target="tpu_custom_call" | custom-call | tf_op jit(solution)/shard_map/pallas_call | solution.py:256
  (26 shorter events, 2.4 us)
Async XLA Ops:
  0.0 28.8 %copy-start = (bf16[896,1024]{1,0:T(8,128)(2,1)S(1)}, bf16[896,1024]{1,0:T(8,128)(2,1)}, u32[]{:S(2)}) copy-start(bf16[896,1024]{1,0:T(8,128)(2,1)} %refs_5_.1) | copy-start | bytes 5505028
  0.0 1.2 %copy-start.3 = (bf16[64,3584]{1,0:T(8,128)(2,1)S(1)}, bf16[64,3584]{1,0:T(8,128)(2,1)}, u32[]{:S(2)}) copy-start(bf16[64,3584]{1,0:T(8,128)(2,1)} %enc_ref.1) | copy-start | bytes 1376260
  1.3 8.1 %collective-permute-start = (bf16[64,896]{1,0:T(8,128)(2,1)S(1)}, bf16[64,896]{1,0:T(8,128)(2,1)S(1)}, u32[]{:S(2)}, u32[]{:S(2)}) collective-permute-start(bf16[64,896]{1,0:T(8,128)(2,1)S(1)} %get-tuple-element.14.refs_0_), channel_id=1, source_target_pairs={{0,4},{2,6},{4,12},{6,14},{12,8},{14,10},{8,0},{10,2},{1,5},{3,7},... | collective-permute-start | bytes 344072 | tf_op jit(solution)/shard_map/ppermute | solution.py:272
  4.3 6.6 %collective-permute-start.1 = (bf16[64,896]{1,0:T(8,128)(2,1)S(1)}, bf16[64,896]{1,0:T(8,128)(2,1)S(1)}, u32[]{:S(2)}, u32[]{:S(2)}) collective-permute-start(bf16[64,896]{1,0:T(8,128)(2,1)S(1)} %get-tuple-element.15.refs_1_), channel_id=1, source_target_pairs={{0,4},{2,6},{4,12},{6,14},{12,8},{14,10},{8,0},{10,2},{1,5},{3,7},... | collective-permute-start | bytes 344072 | tf_op jit(solution)/shard_map/ppermute | solution.py:272
  6.9 20.1 %collective-permute-start.2 = (bf16[64,1792]{1,0:T(8,128)(2,1)S(1)}, bf16[64,1792]{1,0:T(8,128)(2,1)S(1)}, u32[]{:S(2)}, u32[]{:S(2)}) collective-permute-start(bf16[64,1792]{1,0:T(8,128)(2,1)S(1)} %get-tuple-element.16), channel_id=1, source_target_pairs={{0,2},{2,0},{4,6},{6,4},{8,10},{10,8},{12,14},{14,12},{1,3},{3,1},... | collective-permute-start | bytes 688136 | tf_op jit(solution)/shard_map/ppermute | solution.py:272
  9.3 6.9 %collective-permute-start.3 = (bf16[64,896]{1,0:T(8,128)(2,1)S(1)}, bf16[64,896]{1,0:T(8,128)(2,1)S(1)}, u32[]{:S(2)}, u32[]{:S(2)}) collective-permute-start(bf16[64,896]{1,0:T(8,128)(2,1)S(1)} %collective-permute-done.refs_2_), channel_id=1, source_target_pairs={{0,4},{2,6},{4,12},{6,14},{12,8},{14,10},{8,0},{10,2},{1,5},{3,7},... | collective-permute-start | bytes 344072 | tf_op jit(solution)/shard_map/ppermute | solution.py:272
  11.0 7.7 %collective-permute-start.4 = (bf16[64,896]{1,0:T(8,128)(2,1)S(1)}, bf16[64,896]{1,0:T(8,128)(2,1)S(1)}, u32[]{:S(2)}, u32[]{:S(2)}) collective-permute-start(bf16[64,896]{1,0:T(8,128)(2,1)S(1)} %collective-permute-done.1.refs_3_), channel_id=1, source_target_pairs={{0,4},{2,6},{4,12},{6,14},{12,8},{14,10},{8,0},{10,2},{1,5},{3,7},... | collective-permute-start | bytes 344072 | tf_op jit(solution)/shard_map/ppermute | solution.py:272
  13.9 13.2 %collective-permute-start.5 = (bf16[64,1792]{1,0:T(8,128)(2,1)S(1)}, bf16[64,1792]{1,0:T(8,128)(2,1)S(1)}, u32[]{:S(2)}, u32[]{:S(2)}) collective-permute-start(bf16[64,1792]{1,0:T(8,128)(2,1)S(1)} %pad_maximum_fusion), channel_id=1, source_target_pairs={{0,2},{2,0},{4,6},{6,4},{8,10},{10,8},{12,14},{14,12},{1,3},{3,1},... | collective-permute-start | bytes 688136 | tf_op jit(solution)/shard_map/ppermute | solution.py:272
  16.2 6.0 %collective-permute-start.6 = (bf16[64,896]{1,0:T(8,128)(2,1)S(1)}, bf16[64,896]{1,0:T(8,128)(2,1)S(1)}, u32[]{:S(2)}, u32[]{:S(2)}) collective-permute-start(bf16[64,896]{1,0:T(8,128)(2,1)S(1)} %collective-permute-done.3.refs_5_), channel_id=1, source_target_pairs={{0,4},{2,6},{4,12},{6,14},{12,8},{14,10},{8,0},{10,2},{1,5},{3,7},... | collective-permute-start | bytes 344072 | tf_op jit(solution)/shard_map/ppermute | solution.py:272
  17.0 6.4 %collective-permute-start.7 = (bf16[64,896]{1,0:T(8,128)(2,1)S(1)}, bf16[64,896]{1,0:T(8,128)(2,1)S(1)}, u32[]{:S(2)}, u32[]{:S(2)}) collective-permute-start(bf16[64,896]{1,0:T(8,128)(2,1)S(1)} %collective-permute-done.3.refs_5_), channel_id=1, source_target_pairs={{0,2},{2,0},{4,6},{6,4},{8,10},{10,8},{12,14},{14,12},{1,3},{3,1},... | collective-permute-start | bytes 344072 | tf_op jit(solution)/shard_map/ppermute | solution.py:272
  18.6 5.7 %collective-permute-start.8 = (bf16[64,896]{1,0:T(8,128)(2,1)S(1)}, bf16[64,896]{1,0:T(8,128)(2,1)S(1)}, u32[]{:S(2)}, u32[]{:S(2)}) collective-permute-start(bf16[64,896]{1,0:T(8,128)(2,1)S(1)} %collective-permute-done.4.refs_6_), channel_id=1, source_target_pairs={{0,4},{2,6},{4,12},{6,14},{12,8},{14,10},{8,0},{10,2},{1,5},{3,7},... | collective-permute-start | bytes 344072 | tf_op jit(solution)/shard_map/ppermute | solution.py:272
  22.2 5.1 %collective-permute-start.9 = (bf16[64,896]{1,0:T(8,128)(2,1)S(1)}, bf16[64,896]{1,0:T(8,128)(2,1)S(1)}, u32[]{:S(2)}, u32[]{:S(2)}) collective-permute-start(bf16[64,896]{1,0:T(8,128)(2,1)S(1)} %collective-permute-done.4.refs_6_), channel_id=1, source_target_pairs={{0,2},{2,0},{4,6},{6,4},{8,10},{10,8},{12,14},{14,12},{1,3},{3,1},... | collective-permute-start | bytes 344072 | tf_op jit(solution)/shard_map/ppermute | solution.py:272
  23.4 5.1 %collective-permute-start.10 = (bf16[64,896]{1,0:T(8,128)(2,1)S(1)}, bf16[64,896]{1,0:T(8,128)(2,1)S(1)}, u32[]{:S(2)}, u32[]{:S(2)}) collective-permute-start(bf16[64,896]{1,0:T(8,128)(2,1)S(1)} %collective-permute-done.6.refs_8_), channel_id=1, source_target_pairs={{0,2},{2,0},{4,6},{6,4},{8,10},{10,8},{12,14},{14,12},{1,3},{3,1},... | collective-permute-start | bytes 344072 | tf_op jit(solution)/shard_map/ppermute | solution.py:272
  24.3 5.4 %collective-permute-start.12 = (bf16[64,896]{1,0:T(8,128)(2,1)S(1)}, bf16[64,896]{1,0:T(8,128)(2,1)S(1)}, u32[]{:S(2)}, u32[]{:S(2)}) collective-permute-start(bf16[64,896]{1,0:T(8,128)(2,1)S(1)} %collective-permute-done.8.refs_9_), channel_id=1, source_target_pairs={{0,2},{2,0},{4,6},{6,4},{8,10},{10,8},{12,14},{14,12},{1,3},{3,1},... | collective-permute-start | bytes 344072 | tf_op jit(solution)/shard_map/ppermute | solution.py:272
  25.6 0.7 %copy-start.4 = (s32[2,64,1]{1,2,0:T(1,128)S(1)}, s32[2,64,1]{1,2,0:T(1,128)}, u32[]{:S(2)}) copy-start(s32[2,64,1]{1,2,0:T(1,128)} %param.10) | copy-start | bytes 1540
  26.2 0.7 %copy-start.5 = (s32[2,64]{1,0:T(2,128)S(1)}, s32[2,64]{1,0:T(2,128)}, u32[]{:S(2)}) copy-start(s32[2,64]{1,0:T(2,128)} %stored_ref.1) | copy-start | bytes 1540
  29.3 1.8 %copy-start.1 = (bf16[896,1024]{1,0:T(8,128)(2,1)S(1)}, bf16[896,1024]{1,0:T(8,128)(2,1)}, u32[]{:S(2)}) copy-start(bf16[896,1024]{1,0:T(8,128)(2,1)} %refs_4_.1) | copy-start | bytes 5505028
  29.3 1.8 %copy-start.2 = (bf16[128,1024]{1,0:T(8,128)(2,1)S(1)}, bf16[128,1024]{1,0:T(8,128)(2,1)}, u32[]{:S(2)}) copy-start(bf16[128,1024]{1,0:T(8,128)(2,1)} %refs_6_.1) | copy-start | bytes 786436
  30.0 1.9 %collective-permute-start.13 = (bf16[128,896]{1,0:T(8,128)(2,1)S(1)}, bf16[128,896]{1,0:T(8,128)(2,1)S(1)}, u32[]{:S(2)}, u32[]{:S(2)}) collective-permute-start(bf16[128,896]{1,0:T(8,128)(2,1)S(1)} %shard_map.69.refs_0_.refs_1_), channel_id=1, source_target_pairs={{0,1},{1,0},{2,3},{3,2},{4,5},{5,4},{6,7},{7,6},{8,9},{9,8},{10,11... | collective-permute-start | bytes 688136 | tf_op jit(solution)/shard_map/ppermute | solution.py:310
  30.1 1.9 %collective-permute-start.11 = (bf16[128,896]{1,0:T(8,128)(2,1)S(1)}, bf16[128,896]{1,0:T(8,128)(2,1)S(1)}, u32[]{:S(2)}, u32[]{:S(2)}) collective-permute-start(bf16[128,896]{1,0:T(8,128)(2,1)S(1)} %shard_map.67.refs_0_), channel_id=1, source_target_pairs={{0,1},{1,0},{2,3},{3,2},{4,5},{5,4},{6,7},{7,6},{8,9},{9,8},{10,11... | collective-permute-start | bytes 688136 | tf_op jit(solution)/shard_map/ppermute | solution.py:310
